TPU v7x, 32 devices: a whole 2x2x4 slice. The times are simulated.
32 devices in a mesh: fsdp: 4 (over z), seq: 8 (over y, x, core).
Axes of the slice: x: 2, y: 2, z: 4, core: 2. Of those that a mesh axis runs over, the one named last changes fastest.
Arguments:
- tokens: bfloat16 [8, 2048, 1024], P('fsdp', 'seq'), may hold values from -6 to 6
- segments: int32 [8, 2048], P('fsdp', 'seq'), may hold values from 0 to 2047, as said below
- norm_gain: bfloat16 [2, 1024], P(None, 'fsdp'), may hold values from 0.5 to 1.5
- in_weight: bfloat16 [2, 1024, 4352], P(None, 'fsdp'), may hold values from -0.1875 to 0.1875
- dt_weight: bfloat16 [2, 1024, 32], P(None, 'fsdp'), may hold values from -0.1875 to 0.1875
- conv_weight: bfloat16 [2, 4, 2304], P(None, None, 'fsdp'), may hold values from -3 to 3
- conv_bias: bfloat16 [2, 2304], P(None, 'fsdp'), may hold values from -1.5 to 1.5
- dt_bias: bfloat16 [2, 32], P(None, 'fsdp')
- a_log: bfloat16 [2, 32], P(None, 'fsdp'), may hold values from -0.5 to 0.5
- d_skip: bfloat16 [2, 32], P(None, 'fsdp'), may hold values from 0.5 to 1.5
- gate_gain: bfloat16 [2, 2048], P(None, 'fsdp'), may hold values from 0.5 to 1.5
- out_weight: bfloat16 [2, 2048, 1024], P(None, 'fsdp'), may hold values from -0.125 to 0.125
- cotangent: bfloat16 [8, 2048, 1024], P('fsdp', 'seq'), may hold values from -6 to 6
Outputs:
- output: float32 [8, 2048, 1024], P('fsdp', 'seq')
- input_grad: float32 [8, 2048, 1024], P('fsdp', 'seq')
- norm_gain_grad: float32 [2, 1024], P(None, 'fsdp')
- in_weight_grad: float32 [2, 1024, 4352], P(None, 'fsdp')
- dt_weight_grad: float32 [2, 1024, 32], P(None, 'fsdp')
- conv_weight_grad: float32 [2, 4, 2304], P(None, None, 'fsdp')
- conv_bias_grad: float32 [2, 2304], P(None, 'fsdp')
- dt_bias_grad: float32 [2, 32], P(None, 'fsdp')
- a_log_grad: float32 [2, 32], P(None, 'fsdp')
- d_skip_grad: float32 [2, 32], P(None, 'fsdp')
- gate_gain_grad: float32 [2, 2048], P(None, 'fsdp')
- out_weight_grad: float32 [2, 2048, 1024], P(None, 'fsdp')
Inputs may be any that keep to these rules, and one draw needn't show every extreme that they name: `segments`: A position's document number is the index, within its sequence, of the last position of its document, so numbers never fall along a sequence and every sequence ends with 2047; in every group of 2 sequences on one index of fsdp one sequence is a single document.
All inputs are finite; a program needn't handle non-finite values.
Results may differ from a plain program's by a relative error of at most 0.02.
Values may be sent and summed in bfloat16 or wider, within the bound.
No kernel may reach another device: no remote copies, remote signals or barrier semaphores. Data moves between devices by JAX's collectives and lax.ppermute only.
A program may use at most 448 MiB of HBM per device.

v0:
```python
import jax
import jax.numpy as jnp
from jax import lax
from jax.sharding import PartitionSpec as P

EPSILON = 1e-05
highest = lax.Precision.HIGHEST


def passed_along(block, axis, distance):
    devices = range(lax.axis_size(axis))
    route = [(i - distance, i) for i in devices if i - distance in devices]
    return lax.ppermute(block, axis, route)


def prefix(x, axis, combine, identity):
    peers, mine = (lax.axis_size(axis), lax.axis_index(axis))
    everything = jax.tree.map(
        lambda part, kind: lax.all_gather(part.astype(kind), axis), x, (jnp.bfloat16, jnp.bfloat16)
    )
    start = jax.tree.map(
        lambda part, zero: jnp.broadcast_to(jnp.asarray(zero, part.dtype), part.shape), x, identity
    )

    def turn(k, before):
        reached = k < mine
        new = combine(
            before, jax.tree.map(lambda part, own: part[k].astype(own.dtype), everything, x)
        )
        return jax.tree.map(lambda a, b: jnp.where(reached, a, b), new, before)

    return lax.fori_loop(0, peers, turn, start)


def prefix_2(x, axis, combine, identity):
    peers, mine = (lax.axis_size(axis), lax.axis_index(axis))
    everything = jax.tree.map(
        lambda part, kind: lax.all_gather(part.astype(kind), axis),
        x,
        jax.tree.map(lambda a: jnp.bfloat16 if a.dtype == jnp.float32 else a.dtype, x),
    )
    start = jax.tree.map(
        lambda part, zero: jnp.broadcast_to(jnp.asarray(zero, part.dtype), part.shape), x, identity
    )

    def turn(k, before):
        at = peers - 1 - k
        reached = at > mine
        new = combine(
            before, jax.tree.map(lambda part, own: part[at].astype(own.dtype), everything, x)
        )
        return jax.tree.map(lambda a, b: jnp.where(reached, a, b), new, before)

    return lax.fori_loop(0, peers, turn, start)


def normed(value, gain):
    return value * lax.rsqrt(jnp.mean(value * value, axis=-1, keepdims=True) + EPSILON) * gain


def split_parts(activated, heads, inner):
    state = (activated.shape[-1] - inner) // 2
    batch, width = (activated.shape[0], activated.shape[1])
    values = activated[..., :inner].reshape(batch, width, heads, inner // heads)
    return (values, activated[..., inner : inner + state], activated[..., inner + state :])


def conv_piece(
    mixed_in, step_raw, edge_rows, conv_taps, conv_offset, step_offset, rate_logs, conv_masks
):
    width = mixed_in.shape[1]
    padded = jnp.concatenate([edge_rows, mixed_in], axis=1)
    total = conv_offset + jnp.zeros_like(mixed_in)
    for offset in range(conv_taps.shape[0]):
        total = total + jnp.where(
            conv_masks[offset][:, :, None],
            padded[:, offset : offset + width] * conv_taps[offset],
            0.0,
        )
    activated = jax.nn.silu(total)
    step_size = jax.nn.softplus(step_raw + step_offset)
    decay_sum = jnp.cumsum(step_size * -jnp.exp(rate_logs), axis=1)
    return (activated, step_size, decay_sum)


def state_piece(activated, step_size, decay_sum, tail_same, cont_last, inner):
    values, keys_in, queries = split_parts(activated, step_size.shape[-1], inner)
    weight = (
        jnp.where(tail_same[:, :, None], jnp.exp(decay_sum[:, -1:, :] - decay_sum), 0.0) * step_size
    )
    carried = jnp.einsum("bsh,bshp,bsn->bhpn", weight, values, keys_in, precision=highest)
    factor = jnp.where(cont_last[:, None], jnp.exp(decay_sum[:, -1, :]), 0.0)
    return (carried, factor)


def mix_piece(
    activated, step_size, decay_sum, gate_in, state_in, skip_scale, gate_scale, pair_same, cont
):
    batch, width, heads = step_size.shape
    inner = gate_in.shape[-1]
    values, keys_in, queries = split_parts(activated, heads, inner)
    spread = decay_sum[:, :, None, :] - decay_sum[:, None, :, :]
    decay = jnp.where(
        pair_same[..., None], jnp.exp(jnp.where(pair_same[..., None], spread, 0.0)), 0.0
    )
    scores = jnp.einsum("btn,bsn->bts", queries, keys_in, precision=highest)
    weights = scores[..., None] * decay * step_size[:, None, :, :]
    mixed = jnp.einsum("btsh,bshp->bthp", weights, values, precision=highest)
    enter = jnp.where(cont[:, :, None], jnp.exp(decay_sum), 0.0)
    mixed = (
        mixed
        + jnp.einsum("btn,bhpn->bthp", queries, state_in, precision=highest) * enter[..., None]
    )
    mixed = mixed + skip_scale[:, None] * values
    return normed(mixed.reshape(batch, width, inner) * jax.nn.silu(gate_in), gate_scale)


def combine_maps(earlier, later):
    return (earlier[0] * later[0], later[0][:, :, None, None] * earlier[1] + later[1])


def make_masks(segments, edge_marks, conv_len):
    width = segments.shape[1]
    marks = (segments + 1).astype(jnp.float32)
    padded = jnp.concatenate([edge_marks, marks], axis=1)
    conv_masks = [padded[:, offset : offset + width] == marks for offset in range(conv_len)]
    order = jnp.arange(width)
    pair_same = (segments[:, :, None] == segments[:, None, :]) & (order[:, None] >= order[None, :])
    cont = marks == edge_marks[:, -1:]
    tail_same = segments == segments[:, -1:]
    return (conv_masks, pair_same, cont, tail_same, cont[:, -1])


def widen(gathered):
    return (
        gathered[0].astype(jnp.float32),
        gathered[1],
        gathered[2],
        gathered[3].astype(jnp.float32),
        gathered[4].astype(jnp.float32),
        gathered[5].astype(jnp.float32),
        gathered[6].astype(jnp.float32),
        gathered[7].astype(jnp.float32),
        gathered[8].astype(jnp.float32),
        gathered[9],
    )


def fetch_forward(
    norm_scale,
    proj_matrix,
    step_matrix,
    conv_taps,
    conv_offset,
    step_offset,
    rate_logs,
    skip_scale,
    gate_scale,
    out_matrix,
):
    return widen(
        (
            lax.all_gather(norm_scale, "fsdp", axis=0, tiled=True),
            lax.all_gather(proj_matrix, "fsdp", axis=0, tiled=True),
            lax.all_gather(step_matrix, "fsdp", axis=0, tiled=True),
            lax.all_gather(conv_taps, "fsdp", axis=1, tiled=True),
            lax.all_gather(conv_offset, "fsdp", axis=0, tiled=True),
            lax.all_gather(step_offset, "fsdp", axis=0, tiled=True),
            lax.all_gather(rate_logs, "fsdp", axis=0, tiled=True),
            lax.all_gather(skip_scale, "fsdp", axis=0, tiled=True),
            lax.all_gather(gate_scale, "fsdp", axis=0, tiled=True),
            lax.all_gather(out_matrix, "fsdp", axis=0, tiled=True),
        )
    )


def fetch_backward(
    norm_scale,
    proj_matrix,
    step_matrix,
    conv_taps,
    conv_offset,
    step_offset,
    rate_logs,
    skip_scale,
    gate_scale,
    out_matrix,
):
    return widen(
        (
            lax.all_gather(norm_scale, "fsdp", axis=0, tiled=True),
            lax.all_gather(proj_matrix, "fsdp", axis=0, tiled=True),
            lax.all_gather(step_matrix, "fsdp", axis=0, tiled=True),
            lax.all_gather(conv_taps, "fsdp", axis=1, tiled=True),
            lax.all_gather(conv_offset, "fsdp", axis=0, tiled=True),
            lax.all_gather(step_offset, "fsdp", axis=0, tiled=True),
            lax.all_gather(rate_logs, "fsdp", axis=0, tiled=True),
            lax.all_gather(skip_scale, "fsdp", axis=0, tiled=True),
            lax.all_gather(gate_scale, "fsdp", axis=0, tiled=True),
            lax.all_gather(out_matrix, "fsdp", axis=0, tiled=True),
        )
    )


def reduce_layer(
    gain_grad,
    proj_grad,
    step_grad,
    taps_grad,
    offset_grad,
    shift_grad,
    rate_grad,
    skip_grad,
    scale_grad,
    out_grad,
):
    shares = (
        lax.psum_scatter(
            gain_grad.astype(jnp.bfloat16), "fsdp", scatter_dimension=0, tiled=True
        ).astype(jnp.float32),
        lax.psum_scatter(
            proj_grad.astype(jnp.bfloat16), "fsdp", scatter_dimension=0, tiled=True
        ).astype(jnp.float32),
        lax.psum_scatter(
            step_grad.astype(jnp.bfloat16), "fsdp", scatter_dimension=0, tiled=True
        ).astype(jnp.float32),
        lax.psum_scatter(
            taps_grad.astype(jnp.bfloat16), "fsdp", scatter_dimension=1, tiled=True
        ).astype(jnp.float32),
        lax.psum_scatter(
            offset_grad.astype(jnp.bfloat16), "fsdp", scatter_dimension=0, tiled=True
        ).astype(jnp.float32),
        lax.psum_scatter(
            shift_grad.astype(jnp.bfloat16), "fsdp", scatter_dimension=0, tiled=True
        ).astype(jnp.float32),
        lax.psum_scatter(
            rate_grad.astype(jnp.bfloat16), "fsdp", scatter_dimension=0, tiled=True
        ).astype(jnp.float32),
        lax.psum_scatter(
            skip_grad.astype(jnp.bfloat16), "fsdp", scatter_dimension=0, tiled=True
        ).astype(jnp.float32),
        lax.psum_scatter(
            scale_grad.astype(jnp.bfloat16), "fsdp", scatter_dimension=0, tiled=True
        ).astype(jnp.float32),
        lax.psum_scatter(
            out_grad.astype(jnp.bfloat16), "fsdp", scatter_dimension=0, tiled=True
        ).astype(jnp.float32),
    )
    return (
        lax.psum(shares[0].astype(jnp.bfloat16), "seq").astype(jnp.float32),
        lax.psum(shares[1].astype(jnp.bfloat16), "seq").astype(jnp.float32),
        lax.psum(shares[2].astype(jnp.bfloat16), "seq").astype(jnp.float32),
        lax.psum(shares[3].astype(jnp.bfloat16), "seq").astype(jnp.float32),
        lax.psum(shares[4].astype(jnp.bfloat16), "seq").astype(jnp.float32),
        lax.psum(shares[5].astype(jnp.bfloat16), "seq").astype(jnp.float32),
        lax.psum(shares[6].astype(jnp.bfloat16), "seq").astype(jnp.float32),
        lax.psum(shares[7].astype(jnp.bfloat16), "seq").astype(jnp.float32),
        lax.psum(shares[8].astype(jnp.bfloat16), "seq").astype(jnp.float32),
        lax.psum(shares[9].astype(jnp.bfloat16), "seq").astype(jnp.float32),
    )


def on_device(
    tokens,
    segments,
    norm_gain,
    in_weight,
    dt_weight,
    conv_weight,
    conv_bias,
    dt_bias,
    a_log,
    d_skip,
    gate_gain,
    out_weight,
    cotangent,
):
    layers = in_weight.shape[0]
    batch, width, model = tokens.shape
    heads = dt_weight.shape[2]
    conv_len = conv_weight.shape[1]
    rows = batch * width
    cut = width - conv_len + 1

    def shards(layer):
        return (
            norm_gain[layer],
            in_weight[layer],
            dt_weight[layer],
            conv_weight[layer],
            conv_bias[layer],
            dt_bias[layer],
            a_log[layer],
            d_skip[layer],
            gate_gain[layer],
            out_weight[layer],
        )

    stream = tokens.astype(jnp.float32)
    kept_inputs, kept_edges, kept_states, kept_weights = ([], [], [], [])
    masks = None
    for layer in range(layers):
        weights = fetch_forward(*shards(layer))
        (
            norm_scale,
            proj_matrix,
            step_matrix,
            conv_taps,
            conv_offset,
            step_offset,
            rate_logs,
            skip_scale,
            gate_scale,
            out_matrix,
        ) = weights
        inner = out_matrix.shape[0]
        kept_inputs.append(stream)
        low_rows = normed(stream, norm_scale).astype(jnp.bfloat16).reshape(rows, model)
        projected = jnp.dot(low_rows, proj_matrix, preferred_element_type=jnp.float32).reshape(
            batch, width, -1
        )
        step_raw = jnp.dot(low_rows, step_matrix, preferred_element_type=jnp.float32).reshape(
            batch, width, heads
        )
        mixed_in = projected[..., inner:]
        tail_marks = (segments[:, cut:] + 1).astype(jnp.float32)
        edge_rows, edge_marks = passed_along((mixed_in[:, cut:], tail_marks), "seq", 1)
        kept_edges.append(edge_rows)
        if layer == 0:
            masks = make_masks(segments, edge_marks, conv_len)
        conv_masks, pair_same, cont, tail_same, cont_last = masks
        activated, step_size, decay_sum = conv_piece(
            mixed_in,
            step_raw,
            edge_rows,
            conv_taps,
            conv_offset,
            step_offset,
            rate_logs,
            conv_masks,
        )
        carried, factor = state_piece(activated, step_size, decay_sum, tail_same, cont_last, inner)
        identity = (jnp.ones_like(factor), jnp.zeros_like(carried))
        state_in = prefix((factor, carried), "seq", combine_maps, identity)[1]
        kept_states.append(state_in)
        gated = mix_piece(
            activated,
            step_size,
            decay_sum,
            projected[..., :inner],
            state_in,
            skip_scale,
            gate_scale,
            pair_same,
            cont,
        )
        branch = jnp.dot(
            gated.astype(jnp.bfloat16).reshape(rows, inner),
            out_matrix,
            preferred_element_type=jnp.float32,
        )
        stream = stream + branch.reshape(batch, width, model)
    conv_masks, pair_same, cont, tail_same, cont_last = masks
    grad_stream = cotangent.astype(jnp.float32)
    collected = []
    for layer in reversed(range(layers)):
        weights = fetch_backward(*shards(layer))
        (
            norm_scale,
            proj_matrix,
            step_matrix,
            conv_taps,
            conv_offset,
            step_offset,
            rate_logs,
            skip_scale,
            gate_scale,
            out_matrix,
        ) = weights
        inner = out_matrix.shape[0]
        state_in = kept_states[layer]
        normed_rows, pull_norm = jax.vjp(normed, kept_inputs[layer], norm_scale)
        low_rows = normed_rows.astype(jnp.bfloat16).reshape(rows, model)
        projected = jnp.dot(low_rows, proj_matrix, preferred_element_type=jnp.float32).reshape(
            batch, width, -1
        )
        step_raw = jnp.dot(low_rows, step_matrix, preferred_element_type=jnp.float32).reshape(
            batch, width, heads
        )

        def conv_local(mixed, raw, edge, taps, offset, shift, logs):
            return conv_piece(mixed, raw, edge, taps, offset, shift, logs, conv_masks)

        (activated, step_size, decay_sum), pull_conv = jax.vjp(
            conv_local,
            projected[..., inner:],
            step_raw,
            kept_edges[layer],
            conv_taps,
            conv_offset,
            step_offset,
            rate_logs,
        )

        def state_local(act, size, total):
            return state_piece(act, size, total, tail_same, cont_last, inner)

        (carried, factor), pull_state = jax.vjp(state_local, activated, step_size, decay_sum)

        def mix_local(act, size, total, gate, state, skip, scale):
            return mix_piece(act, size, total, gate, state, skip, scale, pair_same, cont)

        gated, pull_mix = jax.vjp(
            mix_local,
            activated,
            step_size,
            decay_sum,
            projected[..., :inner],
            state_in,
            skip_scale,
            gate_scale,
        )
        low_gated = gated.astype(jnp.bfloat16).reshape(rows, inner)
        grad_low = grad_stream.astype(jnp.bfloat16).reshape(rows, model)
        out_grad = jnp.einsum("ti,td->id", low_gated, grad_low, preferred_element_type=jnp.float32)
        grad_gated = jnp.einsum(
            "td,id->ti", grad_low, out_matrix, preferred_element_type=jnp.float32
        ).reshape(batch, width, inner)
        mix_act, mix_size, mix_total, grad_gate, grad_state, skip_grad, scale_grad = pull_mix(
            grad_gated
        )
        identity = (jnp.ones_like(factor), jnp.zeros_like(grad_state))
        state_out_grad = prefix_2((factor, grad_state), "seq", combine_maps, identity)[1]
        factor_grad = jnp.sum(state_out_grad * state_in, axis=(2, 3))
        state_act, state_size, state_total = pull_state((state_out_grad, factor_grad))
        grad_mixed, grad_raw, grad_edge, taps_grad, offset_grad, shift_grad, rate_grad = pull_conv(
            (mix_act + state_act, mix_size + state_size, mix_total + state_total)
        )
        from_next = passed_along(grad_edge.astype(jnp.bfloat16), "seq", -1).astype(grad_edge.dtype)
        grad_mixed = jnp.concatenate([grad_mixed[:, :cut], grad_mixed[:, cut:] + from_next], axis=1)
        grad_proj = (
            jnp.concatenate([grad_gate, grad_mixed], axis=-1).astype(jnp.bfloat16).reshape(rows, -1)
        )
        grad_step = grad_raw.astype(jnp.bfloat16).reshape(rows, heads)
        proj_grad = jnp.einsum("tk,tp->kp", low_rows, grad_proj, preferred_element_type=jnp.float32)
        step_grad = jnp.einsum("tk,th->kh", low_rows, grad_step, preferred_element_type=jnp.float32)
        grad_rows = jnp.einsum(
            "tp,kp->tk", grad_proj, proj_matrix, preferred_element_type=jnp.float32
        )
        grad_rows = grad_rows + jnp.einsum(
            "th,kh->tk", grad_step, step_matrix, preferred_element_type=jnp.float32
        )
        grad_input, gain_grad = pull_norm(grad_rows.reshape(batch, width, model))
        grad_stream = grad_stream + grad_input
        grads = (
            gain_grad,
            proj_grad,
            step_grad,
            taps_grad,
            offset_grad,
            shift_grad,
            rate_grad,
            skip_grad,
            scale_grad,
            out_grad,
        )
        collected.append(reduce_layer(*grads))
    collected = collected[::-1]
    stacked = tuple((jnp.stack([entry[index] for entry in collected]) for index in range(10)))
    return (stream, grad_stream) + tuple(stacked)


def solution(mesh):
    placed = (
        P("fsdp", "seq", None),
        P("fsdp", "seq"),
        P(None, "fsdp"),
        P(None, "fsdp", None),
        P(None, "fsdp", None),
        P(None, None, "fsdp"),
        P(None, "fsdp"),
        P(None, "fsdp"),
        P(None, "fsdp"),
        P(None, "fsdp"),
        P(None, "fsdp"),
        P(None, "fsdp", None),
        P("fsdp", "seq", None),
    )
    return jax.shard_map(
        on_device,
        mesh=mesh,
        in_specs=placed,
        out_specs=(
            P("fsdp", "seq", None),
            P("fsdp", "seq", None),
            P(None, "fsdp"),
            P(None, "fsdp", None),
            P(None, "fsdp", None),
            P(None, None, "fsdp"),
            P(None, "fsdp"),
            P(None, "fsdp"),
            P(None, "fsdp"),
            P(None, "fsdp"),
            P(None, "fsdp"),
            P(None, "fsdp", None),
        ),
        check_vma=False,
    )
```

profile of v0, /device:TPU:0, one launch (start us, length us, event | category | flops | bytes accessed | tf_op | source)
XLA Modules:
  0.0 1682.0 jit_solution(15970298688092459578)
XLA Ops:
  18.5 25.9 %all-reduce.53 = (bf16[32]{0:T(256)(128)(2,1)S(1)}, bf16[32]{0:T(256)(128)(2,1)S(1)}, bf16[2304]{0:T(1024)(128)(2,1)S(1)}, bf16[32]{0:T(256)(128)(2,1)}, bf16[32...) all-reduce(bf16[32]{0:T(256)(128)(2,1)S(1)} %dynamic-update-slice.1, ...), channel_id=7, replica_groups=mesh['fsdp'=4,'seq'=8] {'fsdp'}, use_global_device_ids=true, to_apply=%add.31 | all-reduce | flops 4800 | bytes 19200
  75.1 43.0 %all-gather.3 = bf16[1,4,2304]{1,0,2:T(2,128)(2,1)S(1)} all-gather(bf16[1,4,576]{1,0,2:T(2,128)(2,1)S(1)} %copy.259), channel_id=5, replica_groups=mesh['fsdp'=4,'seq'=8] {'fsdp'}, dimensions={2}, use_global_device_ids=true | all-gather | bytes 23040 | tf_op jit(solution)/shard_map/all_gather | solution.py:166
  121.1 47.8 %slice_reduce_fusion.7 = (f32[2304]{0:T(1024)S(1)}, f32[2304]{0:T(1024)S(1)}, f32[2304]{0:T(1024)S(1)}, f32[2304]{0:T(1024)S(1)}) fusion(f32[1,4,2304]{1,0,2:T(1,128)S(1)} %convert_element_type.457), kind=kLoop, calls=%fused_computation.275 | loop fusion | bytes 73728 | tf_op jit(solution)/shard_map/slice | solution.py:77
  170.1 23.4 %all-gather.33.cloned.1.call-done = bf16[1,1024,4352]{2,1,0:T(8,128)(2,1)} async-done(((bf16[1,256,4352]{2,1,0:T(8,128)(2,1)}), bf16[1,1024,4352]{2,1,0:T(8,128)(2,1)}) %all-gather.33.cloned.1.call-update) | async-done | bytes 8912912 | tf_op jit(solution)/shard_map/all_gather | solution.py:164
  252.2 22.3 %all-gather.14 = bf16[1,4,2304]{1,0,2:T(2,128)(2,1)S(1)} all-gather(bf16[1,4,576]{1,0,2:T(2,128)(2,1)S(1)} %copy.260), channel_id=16, replica_groups=mesh['fsdp'=4,'seq'=8] {'fsdp'}, dimensions={2}, use_global_device_ids=true | all-gather | bytes 23040 | tf_op jit(solution)/shard_map/all_gather | solution.py:166
  293.1 47.9 %slice_reduce_fusion.3 = (f32[2304]{0:T(1024)S(1)}, f32[2304]{0:T(1024)S(1)}, f32[2304]{0:T(1024)S(1)}, f32[2304]{0:T(1024)S(1)}) fusion(f32[1,4,2304]{1,0,2:T(1,128)S(1)} %convert_element_type.464), kind=kLoop, calls=%fused_computation.271 | loop fusion | bytes 73728 | tf_op jit(solution)/shard_map/slice | solution.py:77
  372.9 20.7 %fusion.110 = f32[2,256,32,64]{1,3,2,0:T(8,128)} fusion(f32[2,256,32,64]{1,3,2,0:T(8,128)S(1)} %fusion.229, f32[2,256,32,64]{1,3,2,0:T(8,128)S(1)} %bitcast.577, f32[2,256,32]{1,2,0:T(8,128)S(1)} %bitcast.611, f32[2,256,32]{1,2,0:T(8,128)S(1)} %copy-done.93, f32[2,256,256]{2,1,0:T(8,128)S(1)} %copy-done.54, pred[2,256,256]{2,1,0:T(8,128)(4,1)S(1)} %compare_and_fusion, ...), kind=kOutput, calls=%fused_computation.167 | convolution fusion | flops 3246391296 | bytes 13435008 | tf_op jit(solution)/shard_map/jvp(btsh,bshp->bthp)/dot_general | solution.py:108
  399.1 24.0 %fusion.121 = f32[2,256,32,64]{1,3,2,0:T(8,128)} fusion(f32[2,256,32,64]{1,3,2,0:T(8,128)} %copy-done.21, f32[2,256,32,64]{1,3,2,0:T(8,128)} %bitcast.574, f32[2,256,32]{1,2,0:T(8,128)S(1)} %copy-done.94, f32[2,256,32]{1,2,0:T(8,128)S(1)} %bitcast.618, f32[2,256,256]{2,1,0:T(8,128)S(1)} %copy-done.55, pred[2,256,256]{2,1,0:T(8,128)(4,1)S(1)} %compare_and_fusion, ...), kind=kOutput, calls=%fused_computation.182 | convolution fusion | flops 3246391296 | bytes 13435008 | tf_op jit(solution)/shard_map/btsh,bshp->bthp/dot_general | solution.py:108
  445.8 78.2 %all-gather.39.cloned.1.call-done = bf16[1,1024,4352]{2,1,0:T(8,128)(2,1)} async-done(((bf16[1,256,4352]{2,1,0:T(8,128)(2,1)}), bf16[1,1024,4352]{2,1,0:T(8,128)(2,1)}) %all-gather.39.cloned.1.call-update) | async-done | bytes 8912912 | tf_op jit(solution)/shard_map/all_gather | solution.py:164
  592.5 29.5 %all-gather.41.cloned.1.call-done = bf16[16,32,64,128]{3,2,1,0:T(8,128)(2,1)} async-done(((bf16[2,32,64,128]{3,2,1,0:T(8,128)(2,1)}), bf16[16,32,64,128]{3,2,1,0:T(8,128)(2,1)}) %all-gather.41.cloned.1.call-update) | async-done | bytes 8388624 | tf_op jit(solution)/shard_map/all_gather | solution.py:19
  641.8 20.8 %fusion.111 = f32[2,256,32,64]{1,3,2,0:T(8,128)} fusion(f32[2,256,32,64]{1,3,2,0:T(8,128)S(1)} %fusion.235, f32[2,256,32,64]{1,3,2,0:T(8,128)S(1)} %bitcast.580, f32[2,256,32]{1,2,0:T(8,128)S(1)} %bitcast_bitcast_fusion.3, f32[2,256,32]{1,2,0:T(8,128)S(1)} %get-tuple-element.727, f32[2,256,256]{2,1,0:T(8,128)S(1)} %fusion.240, ...), kind=kOutput, calls=%fused_computation.170 | convolution fusion | flops 3246391296 | bytes 13435008 | tf_op jit(solution)/shard_map/jvp(btsh,bshp->bthp)/dot_general | solution.py:108
  675.1 29.7 %all-gather.43.cloned.1.call-done = bf16[1,2048,1024]{2,1,0:T(8,128)(2,1)} async-done(((bf16[1,512,1024]{2,1,0:T(8,128)(2,1)}), bf16[1,2048,1024]{2,1,0:T(8,128)(2,1)}) %all-gather.43.cloned.1.call-update) | async-done | bytes 4194320 | tf_op jit(solution)/shard_map/all_gather | solution.py:172
  713.7 20.9 %fusion.116 = f32[2,256,32,64]{1,3,2,0:T(8,128)} fusion(f32[2,256,32,64]{1,3,2,0:T(8,128)S(1)} %copy-done.23, f32[2,256,32,64]{1,3,2,0:T(8,128)S(1)} %bitcast.581, f32[2,256,32]{1,2,0:T(8,128)S(1)} %get-tuple-element.727, f32[2,256,32]{1,2,0:T(8,128)S(1)} %bitcast_bitcast_fusion.4, f32[2,256,256]{2,1,0:T(8,128)S(1)} %fusion.240, ...), kind=kOutput, calls=%fused_computation.176 | convolution fusion | flops 3246391296 | bytes 13435008 | tf_op jit(solution)/shard_map/btsh,bshp->bthp/dot_general | solution.py:108
  775.2 18.2 %bitcast_add_fusion.2 = f32[2,256,32,64]{1,3,2,0:T(8,128)} fusion(f32[2,256,32,64]{1,3,2,0:T(8,128)} %bitcast.570, f32[2,32,64,256]{3,2,1,0:T(8,128)} %bitcast.569, f32[2,256,32]{1,2,0:T(8,128)S(1)} %bitcast_bitcast_fusion.3, f32[2,256,32]{1,2,0:T(8,128)S(1)} %get-tuple-element.727, f32[2,256,256]{2,1,0:T(8,128)S(1)} %fusion.240, ...), kind=kOutput, calls=%fused_computation.168 | convolution fusion | flops 3244294144 | bytes 13369472 | tf_op jit(solution)/shard_map/transpose(jvp(btsh,bshp->bthp))/dot_general | solution.py:108
  798.9 29.3 %fusion.43 = (f32[2,256,32]{1,2,0:T(8,128)S(1)}, f32[2,256,32]{1,2,0:T(8,128)}, f32[2,256,32]{1,2,0:T(8,128)S(1)}, f32[2,256,256]{2,1,0:T(8,128)S(1)}) fusion(f32[2,256,32]{1,2,0:T(8,128)S(1)} %bitcast_bitcast_fusion.3, f32[2,256,32]{1,2,0:T(8,128)S(1)} %get-tuple-element.727, f32[2,256,256]{2,1,0:T(8,128)S(1)} %fusion.240, ...), kind=kOutput, calls=%fused_computation.59 | convolution fusion | flops 3283959808 | bytes 9895936 | tf_op jit(solution)/shard_map/transpose(jvp(btsh,bshp->bthp))/dot_general | solution.py:108
  979.8 18.3 %bitcast_add_fusion = f32[2,256,32,64]{1,3,2,0:T(8,128)} fusion(f32[2,256,32,64]{1,3,2,0:T(8,128)} %bitcast.565, f32[2,32,64,256]{3,2,1,0:T(8,128)} %bitcast.564, f32[2,256,32]{1,2,0:T(8,128)S(1)} %bitcast.612, f32[2,256,32]{1,2,0:T(8,128)S(1)} %copy-done.95, f32[2,256,256]{2,1,0:T(8,128)S(1)} %copy-done.56, pred[2,256,256]{2,1,0:T(8,128)(4,1)S(1)} %copy-done.71, ...), kind=kOutput, calls=%fused_computation.165 | convolution fusion | flops 3244294144 | bytes 13369472 | tf_op jit(solution)/shard_map/transpose(jvp(btsh,bshp->bthp))/dot_general | solution.py:108
  1003.5 29.1 %fusion.45 = (f32[2,256,32]{1,2,0:T(8,128)}, f32[2,256,32]{1,2,0:T(8,128)}, f32[2,256,32]{1,2,0:T(8,128)}, f32[2,256,256]{2,1,0:T(8,128)S(1)}) fusion(f32[2,256,32]{1,2,0:T(8,128)S(1)} %bitcast.613, f32[2,256,32]{1,2,0:T(8,128)S(1)} %copy-done.95, f32[2,256,256]{2,1,0:T(8,128)S(1)} %copy-done.56, pred[2,256,256]{2,1,0:T(8,128)(4,1)S(1)} %copy-done.71, ...), kind=kOutput, calls=%fused_computation.61 | convolution fusion | flops 3283959808 | bytes 9895936 | tf_op jit(solution)/shard_map/transpose(jvp(btsh,bshp->bthp))/dot_general | solution.py:108
  1042.9 28.6 %while.63 = (s32[]{:T(128)}, f32[2,32,64,128]{3,2,1,0:T(8,128)}, s32[]{:T(128)}, bf16[8,2,32]{2,1,0:T(2,128)(2,1)S(1)}, bf16[8,2,32,64,128]{4,3,2,1,0:T(8,128)(2...) while((s32[]{:T(128)}, f32[2,32,64,128]{3,2,1,0:T(8,128)}, s32[]{:T(128)}, ...), condition=%wide.region_34.36_spmd.clone, body=%wide.region_33.35_spmd.clone.sunk | while | flops 2621512 | bytes 5243695 | solution.py:54
  1179.3 155.5 %reduce-scatter.15.cloned.1.call-done = bf16[256,4352]{1,0:T(8,128)(2,1)} async-done(((bf16[1024,4352]{1,0:T(8,128)(2,1)}), bf16[256,4352]{1,0:T(8,128)(2,1)}) %reduce-scatter.15.cloned.1.call-update) | async-done | bytes 2228240 | tf_op jit(solution)/shard_map/reduce_scatter | solution.py:221
  1334.8 156.6 %reduce-scatter.13.cloned.1.call-done = bf16[256,4352]{1,0:T(8,128)(2,1)} async-done(((bf16[1024,4352]{1,0:T(8,128)(2,1)}), bf16[256,4352]{1,0:T(8,128)(2,1)}) %reduce-scatter.13.cloned.1.call-update) | async-done | bytes 2228240 | tf_op jit(solution)/shard_map/reduce_scatter | solution.py:221
  1502.7 19.0 %all-reduce.52 = (bf16[1024]{0:T(1024)(128)(2,1)S(1)}, bf16[1024]{0:T(1024)(128)(2,1)S(1)}, bf16[2304]{0:T(1024)(128)(2,1)S(1)}, bf16[2304]{0:T(1024)(128)(2,1)S...) all-reduce(bf16[1024]{0:T(1024)(128)(2,1)S(1)} %copy-done.141, ...), channel_id=27, replica_groups=mesh['fsdp'=4,'seq'=8] {'fsdp'}, use_global_device_ids=true, to_apply=%region_48.50.clone | all-reduce | flops 10944 | bytes 43776
  1537.0 19.4 %reduce-scatter.17.cloned.1.call-done = bf16[256,32]{0,1:T(8,128)(2,1)} async-done(((bf16[1024,32]{0,1:T(8,128)(2,1)}), bf16[256,32]{0,1:T(8,128)(2,1)}) %reduce-scatter.17.cloned.1.call-update) | async-done | bytes 16400 | tf_op jit(solution)/shard_map/reduce_scatter | solution.py:224
  1556.5 24.4 %all-reduce.50 = (bf16[1,256]{1,0:T(2,128)(2,1)S(1)}, bf16[1,256]{1,0:T(2,128)(2,1)S(1)}, bf16[1,256,32]{1,2,0:T(8,128)(2,1)S(1)}, bf16[1,256,32]{1,2,0:T(8,128)...) all-reduce(bf16[1,256]{1,0:T(2,128)(2,1)S(1)} %stack.141, ...), channel_id=1, replica_groups=mesh['fsdp'=4,'seq'=8] {'seq'}, use_global_device_ids=true, to_apply=%region_49.51 | all-reduce | flops 23728 | bytes 94912 | tf_op jit(solution)/shard_map/psum | solution.py:250
  1585.7 80.7 %all-reduce.56.cloned.1.call-done = (bf16[1,256,4352]{2,1,0:T(8,128)(2,1)}, bf16[1,256,4352]{2,1,0:T(8,128)(2,1)}, bf16[1,512,1024]{2,1,0:T(8,128)(2,1)}, bf16[1,512,1024]{2,1,0:T(8,128)(2,1)}) async-done(((bf16[1,256,4352]{2,1,0:T(8,128)(2,1)}, bf16[1,256,4352]{2,1,0:T(8,128)(2,1)}, bf16[1,512,1024]{2,1,0:T(8,128)(2,1)}, bf16[1,512,1024]{2,1,0:T(8,128)(2,1)}), (bf16[1,256,4352]{2,1,0:T(8,128)(2,1)}, ...) | async-done | bytes 6553616 | tf_op jit(solution)/shard_map/psum | solution.py:251
  (750 shorter events, 719.3 us)
Async XLA Ops:
  7.3 186.2 %all-gather.33.cloned.1.call-start = ((), (), s32[]{:S(2)}) async-start(), calls=%async_computation.14 | async-start | bytes 11141120 | tf_op jit(solution)/shard_map/all_gather | solution.py:164
  12.1 341.4 %all-gather.35.cloned.1.call-start = ((), (), s32[]{:S(2)}) async-start(), calls=%async_computation.15 | async-start | bytes 9437184 | tf_op jit(solution)/shard_map/all_gather | solution.py:19
  12.3 156.7 %collective-permute-start = (f32[2,3]{1,0:T(2,128)S(1)}, f32[2,3]{1,0:T(2,128)S(1)}, u32[]{:S(2)}, u32[]{:S(2)}) collective-permute-start(f32[2,3]{1,0:T(2,128)S(1)} %add_convert_fusion.3), channel_id=1, source_target_pairs={{0,1},{1,2},{2,3},{3,4},{4,5},{5,6},{6,7},{8,9},{9,10},{10,11},{11... | collective-permute-start | bytes 80 | tf_op jit(solution)/shard_map/ppermute | solution.py:13
  169.3 374.7 %copy-start.100 = (pred[2,256]{1,0:T(4,128)(4,1)}, pred[2,256]{1,0:T(4,128)(4,1)S(1)}, u32[]{:S(2)}) copy-start(pred[2,256]{1,0:T(4,128)(4,1)S(1)} %get-tuple-element.739) | copy-start | bytes 1540
  201.2 3.5 collective-permute-start.1
  227.9 208.4 %all-gather.37.cloned.1.call-start = ((), (), s32[]{:S(2)}) async-start(), calls=%async_computation.16 | async-start | bytes 5242880 | tf_op jit(solution)/shard_map/all_gather | solution.py:172
  229.5 294.5 %all-gather.39.cloned.1.call-start = ((), (), s32[]{:S(2)}) async-start(), calls=%async_computation.17 | async-start | bytes 11141120 | tf_op jit(solution)/shard_map/all_gather | solution.py:164
  230.1 391.9 %all-gather.41.cloned.1.call-start = ((), (), s32[]{:S(2)}) async-start(), calls=%async_computation.18 | async-start | bytes 9437184 | tf_op jit(solution)/shard_map/all_gather | solution.py:19
  293.1 505.8 %copy-start.70 = (pred[2,256,256]{2,1,0:T(8,128)(4,1)}, pred[2,256,256]{2,1,0:T(8,128)(4,1)S(1)}, u32[]{:S(2)}) copy-start(pred[2,256,256]{2,1,0:T(8,128)(4,1)S(1)} %compare_and_fusion) | copy-start | bytes 393220
  535.0 8.9 collective-permute-start.2
  568.9 135.8 %all-gather.43.cloned.1.call-start = ((), (), s32[]{:S(2)}) async-start(), calls=%async_computation.19 | async-start | bytes 5242880 | tf_op jit(solution)/shard_map/all_gather | solution.py:172
  569.5 270.3 %all-gather.45.cloned.1.call-start = ((), (), s32[]{:S(2)}) async-start(), calls=%async_computation.20 | async-start | bytes 9437184 | tf_op jit(solution)/shard_map/all_gather | solution.py:38
  765.8 277.1 %all-gather.47.cloned.1.call-start = ((), (), s32[]{:S(2)}) async-start(), calls=%async_computation.21 | async-start | bytes 9437184 | tf_op jit(solution)/shard_map/all_gather | solution.py:38
  902.0 3.1 collective-permute-start.3
  942.4 205.3 %reduce-scatter.27.cloned.1.call-start = ((), (), s32[]{:S(2)}) async-start(), calls=%async_computation.23 | async-start | bytes 737280
  943.7 221.1 %reduce-scatter.23.cloned.1.call-start = ((), (), s32[]{:S(2)}) async-start(), calls=%async_computation.13 | async-start | bytes 5242880 | tf_op jit(solution)/shard_map/reduce_scatter | solution.py:245
  950.8 228.5 %reduce-scatter.21.cloned.1.call-start = ((), (), s32[]{:S(2)}) async-start(), calls=%async_computation.12 | async-start | bytes 5242880 | tf_op jit(solution)/shard_map/reduce_scatter | solution.py:245
  957.9 376.9 %reduce-scatter.15.cloned.1.call-start = ((), (), s32[]{:S(2)}) async-start(), calls=%async_computation.9 | async-start | bytes 11141120 | tf_op jit(solution)/shard_map/reduce_scatter | solution.py:221
  968.7 522.7 %reduce-scatter.13.cloned.1.call-start = ((), (), s32[]{:S(2)}) async-start(), calls=%async_computation.8 | async-start | bytes 11141120 | tf_op jit(solution)/shard_map/reduce_scatter | solution.py:221
  1112.6 3.4 collective-permute-start.4
  1125.3 400.8 %reduce-scatter.25.cloned.1.call-start = ((), (), s32[]{:S(2)}) async-start(), calls=%async_computation.22 | async-start | bytes 737280
  1140.3 396.8 %reduce-scatter.19.cloned.1.call-start = ((), (), s32[]{:S(2)}) async-start(), calls=%async_computation.11 | async-start | bytes 81920 | tf_op jit(solution)/shard_map/reduce_scatter | solution.py:224
  1140.9 415.6 %reduce-scatter.17.cloned.1.call-start = ((), (), s32[]{:S(2)}) async-start(), calls=%async_computation.10 | async-start | bytes 81920 | tf_op jit(solution)/shard_map/reduce_scatter | solution.py:224
  1164.5 501.9 %all-reduce.56.cloned.1.call-start = ((), (), s32[]{:S(2)}) async-start(), calls=%async_computation.24 | async-start | bytes 13107200 | tf_op jit(solution)/shard_map/psum | solution.py:251
  (181 other events, 6125.0 us)
Sparse Core Ops, SparseCore 0:
  12.2 181.1 all-gather.32
  228.1 54.7 all-gather.34
  285.0 80.7 all-gather.36
  367.2 156.7 all-gather.38
  569.1 52.8 all-gather.40
  623.9 80.7 all-gather.42
  765.9 52.9 all-gather.44
  942.5 55.4 all-gather.46
  1000.3 21.8 reduce-scatter.26
  1024.3 75.1 reduce-scatter.22
  1102.0 77.2 reduce-scatter.20
  1181.5 153.2 reduce-scatter.14
  1337.7 153.6 reduce-scatter.12
  1493.6 23.2 reduce-scatter.24
  1519.6 17.4 reduce-scatter.18
  1539.2 17.2 reduce-scatter.16
  1560.0 106.2 all-reduce.55
where the time goes:
time: 1690 us; the launch traced here: 1680 us
  waiting for transfers between devices  601 us (36%)
  matrix products  375 us (22%)
  blocking collectives  242 us (14%)
  other arithmetic  218 us (13%)
  local copies, waits for them, and re-layouts  213 us (13%)
  between operations  20.7 us (1%)
    reduce_scatter x2, waiting for transfers between devices, reduce_layer(): lax.psum_scatter(proj_grad.astype(jnp.bfloat16), 'fsdp', scatter_dimensio...  312 us
    dot_general x8, matrix products, mix_piece(): mixed = jnp.einsum('btsh,bshp->bthp', weights, values, precision=highest)  181 us
    all_gather x2, waiting for transfers between devices, fetch_forward(): lax.all_gather(proj_matrix, 'fsdp', axis=0, tiled=True)  102 us
    slice x2, local copies, waits for them, and re-layouts, conv_piece(): conv_taps[offset]  95.7 us
    psum x1, waiting for transfers between devices, reduce_layer(): lax.psum(shares[1].astype(jnp.bfloat16), 'seq').astype(jnp.float32)  80.7 us
    select_n x32, other arithmetic, turn(): return jax.tree.map(lambda a, b: jnp.where(reached, a, b), new, before)  71 us
    all_gather x2, blocking collectives, fetch_forward(): lax.all_gather(conv_taps, 'fsdp', axis=1, tiled=True)  65.4 us
    dot_general x6, matrix products, state_piece(): jnp.einsum('bsh,bshp,bsn->bhpn', weight, values, keys_in, precision=highest)  45.3 us
  transfers between devices with their start and end apart: 22, of which 12 were waited for; matrix products, arithmetic and copies ran while one was open for 33% of the time, Pallas kernels for 0%

commit v1 on v0

v1 whole, which is shorter than its diff:
```python
import functools

import jax
import jax.numpy as jnp
from jax import lax
from jax.experimental import pallas as pl
from jax.experimental.pallas import tpu as pltpu
from jax.sharding import PartitionSpec as P

EPSILON = 1e-05
F32, BF16 = jnp.float32, jnp.bfloat16
LANES = 128
EDGE = 8
FACTOR_ROWS = 16
VMEM = 48 * 1024 * 1024
NT = (((1,), (1,)), ((), ()))
TN = (((0,), (0,)), ((), ()))


def dot(a, b):
    return jnp.dot(a, b, preferred_element_type=F32)


def dot_nt(a, b):
    return lax.dot_general(a, b, NT, preferred_element_type=F32)


def dot_tn(a, b):
    return lax.dot_general(a, b, TN, preferred_element_type=F32)


def dot_exact(a, b):
    return jnp.dot(a, b, precision=lax.Precision.HIGHEST, preferred_element_type=F32)


def halves(v):
    high = v.astype(BF16)
    low = (v - high.astype(F32)).astype(BF16)
    return jnp.concatenate([high, low], axis=1)


def sigmoid(v):
    return 1.0 / (1.0 + jnp.exp(-v))


def softplus(v):
    return jnp.maximum(v, 0.0) + jnp.log1p(jnp.exp(-jnp.abs(v)))


def below(size):
    rows = lax.broadcasted_iota(jnp.int32, (size, size), 0)
    columns = lax.broadcasted_iota(jnp.int32, (size, size), 1)
    return rows >= columns


def head_column(table, head):
    return pltpu.roll(table, LANES - head, axis=1)[:, 0:1]


def conv_total(padded, taps, masks, at, wide, width):
    total = taps[4:5, pl.ds(at, wide)] + taps[3:4, pl.ds(at, wide)] * padded[EDGE:EDGE + width, pl.ds(at, wide)]
    for back in range(1, 4):
        tap = taps[3 - back:4 - back, pl.ds(at, wide)]
        total = total + (masks[back - 1] * tap) * padded[EDGE - back:EDGE - back + width, pl.ds(at, wide)]
    return total


def conv_kernel(inner, mixed, edge, marks, taps, raw, rates, spread, act, sizes, sums, sums_t, state, factor, padded):
    width, channels = mixed.shape[1:]
    padded[0:EDGE, :] = edge[0].astype(F32)
    padded[EDGE:EDGE + width, :] = mixed[0].astype(F32)
    marks_now = marks[0]
    masks = [marks_now[:, back:back + 1] for back in range(3)]
    wide = 256
    for at in range(0, channels, wide):
        total = conv_total(padded, taps, masks, at, wide, width)
        act[0, :, pl.ds(at, wide)] = (total * sigmoid(total)).astype(BF16)
    size = softplus(raw[0] + rates[0:1, :])
    tri = jnp.where(below(width), 1.0, 0.0).astype(F32)
    total_sum = dot_exact(tri, size * rates[1:2, :])
    last = total_sum[width - 1:width]
    sizes[0] = size
    sums[0] = total_sum
    sums_t[0] = total_sum.T[0:sums_t.shape[1]]
    weight = halves(marks_now[:, 4:5] * jnp.exp(last - total_sum) * size)
    gone = marks_now[width - 1:width, 3:4] * jnp.exp(last)
    gone = halves(jnp.broadcast_to(gone, (FACTOR_ROWS, LANES)))
    states = (channels - inner) // 2
    keys_t = act[0, :, inner:inner + states].T
    for at in range(0, inner, wide):
        part = spread[:, pl.ds(at, wide)]
        weighted = (dot(weight, part) * act[0, :, pl.ds(at, wide)].astype(F32)).astype(BF16)
        state[0, :, pl.ds(at, wide)] = dot(keys_t, weighted).astype(BF16)
        factor[0, :, pl.ds(at, wide)] = dot(gone, part)


def intra_kernel(inner, heads, act, sizes, sums, sums_t, marks, row_marks, skip, spread, out, scores, stepped):
    width = act.shape[1]
    states = (act.shape[2] - inner) // 2
    half = width // 2
    keys = act[0, :, inner:inner + states]
    queries = act[0, :, inner + states:]
    same = below(width) & (marks[0][:, 5:6] == row_marks[0, 0:1, :])
    scores[...] = jnp.where(same, dot_nt(queries, keys), 0.0)
    size = halves(sizes[0])
    wide = 256
    for at in range(0, inner, wide):
        part = dot(size, spread[:, pl.ds(at, wide)])
        stepped[:, pl.ds(at, wide)] = (part * act[0, :, pl.ds(at, wide)].astype(F32)).astype(BF16)
    per = LANES // (inner // heads)
    span = inner // heads
    lane = lax.broadcasted_iota(jnp.int32, (width, LANES), 1)

    def group(at, carry):
        place = pl.ds(pl.multiple_of(at * LANES, LANES), LANES)
        x = stepped[:, place]
        y_low = y_high = None
        for i in range(per):
            head = at * per + i
            column = head_column(sums[0], head)
            row = sums_t[0, pl.ds(head, 1), :]
            mine = (lane >= i * span) & (lane < (i + 1) * span)
            xh = jnp.where(mine, x, jnp.zeros_like(x))
            w_low = scores[0:half, 0:half] * jnp.exp(jnp.minimum(column[0:half] - row[:, 0:half], 0.0))
            w_high = scores[half:, :] * jnp.exp(jnp.minimum(column[half:] - row, 0.0))
            a = dot(w_low.astype(BF16), xh[0:half])
            b = dot(w_high.astype(BF16), xh)
            y_low = a if y_low is None else y_low + a
            y_high = b if y_high is None else y_high + b
        values = act[0, :, place].astype(F32) * skip[0:1, place]
        out[0, 0:half, place] = (y_low + values[0:half]).astype(out.dtype)
        out[0, half:, place] = (y_high + values[half:]).astype(out.dtype)
        return carry

    lax.fori_loop(0, inner // LANES, group, 0, unroll=2)


def post_kernel(inner, part_mixed, act, state, sums, marks, gate, gain, spread, mixed, gated, kept):
    states = (act.shape[2] - inner) // 2
    queries = act[0, :, inner + states:]
    enter = halves(marks[0][:, 3:4] * jnp.exp(sums[0]))
    wide = 256
    square = None
    for at in range(0, inner, wide):
        place = pl.ds(at, wide)
        whole = part_mixed[0, :, place].astype(F32) + dot(enter, spread[:, place]) * dot(queries, state[0, :, place])
        g = gate[0, :, place].astype(F32)
        w = whole * (g * sigmoid(g))
        mixed[0, :, place] = whole.astype(BF16)
        kept[:, place] = w
        square = w * w if square is None else square + w * w
    scale = lax.rsqrt(jnp.sum(square, axis=1, keepdims=True) / inner + EPSILON)
    for at in range(0, inner, wide):
        place = pl.ds(at, wide)
        gated[0, :, place] = (kept[:, place] * scale * gain[0:1, place]).astype(BF16)


def gate_back_kernel(
    inner, grad, mixed, gate, gain, act, state, sums, marks, spread,
    d_mixed, d_gate, d_state, d_queries, d_sums, row_grads, kept,
):
    states = (act.shape[2] - inner) // 2
    queries = act[0, :, inner + states:]
    queries_t = queries.T
    wide = 256

    @pl.when(pl.program_id(0) == 0)
    def _():
        row_grads[...] = jnp.zeros_like(row_grads)

    square = cross = None
    for at in range(0, inner, wide):
        place = pl.ds(at, wide)
        g = gate[0, :, place].astype(F32)
        w = mixed[0, :, place].astype(F32) * (g * sigmoid(g))
        gg = grad[0, :, place].astype(F32)
        kept[:, place] = w
        square = w * w if square is None else square + w * w
        more = w * gain[0:1, place] * gg
        cross = more if cross is None else cross + more
    scale = lax.rsqrt(jnp.sum(square, axis=1, keepdims=True) / inner + EPSILON)
    pulled = scale * scale * scale * (jnp.sum(cross, axis=1, keepdims=True) / inner)
    entered = marks[0][:, 3:4] * jnp.exp(sums[0])
    enter = halves(entered)
    grad_enter = dq = None
    for at in range(0, inner, wide):
        place = pl.ds(at, wide)
        g = gate[0, :, place].astype(F32)
        sig = sigmoid(g)
        silu = g * sig
        gg = grad[0, :, place].astype(F32)
        w = kept[:, place]
        whole = mixed[0, :, place].astype(F32)
        dw = scale * (gain[0:1, place] * gg) - pulled * w
        row_grads[0:1, place] += jnp.sum(gg * w * scale, axis=0, keepdims=True)
        dm = dw * silu
        d_gate[0, :, place] = (dw * whole * (sig + silu * (1.0 - sig))).astype(BF16)
        d_mixed[0, :, place] = dm.astype(BF16)
        row_grads[1:2, place] += jnp.sum(dm * act[0, :, place].astype(F32), axis=0, keepdims=True)
        part = spread[:, place]
        st = state[0, :, place]
        e = (dm * dot(enter, part)).astype(BF16)
        d_state[0, :, place] = dot(queries_t, e).astype(BF16)
        more_q = dot_nt(e, st)
        dq = more_q if dq is None else dq + more_q
        through = (dm * dot(queries, st)).astype(BF16)
        more_e = dot_nt(through, part[0:LANES])
        grad_enter = more_e if grad_enter is None else grad_enter + more_e
    d_queries[0] = dq
    d_sums[0] = grad_enter * entered


def intra_back_kernel(
    inner, heads, d_mixed, act, sizes, sums, sums_t, marks, row_marks, spread, d_queries, d_sums,
    d_stepped, d_pair, d_total, scores, d_scores, stepped, sums_rows, sums_columns,
):
    width = act.shape[1]
    states = (act.shape[2] - inner) // 2
    half = width // 2
    keys = act[0, :, inner:inner + states]
    queries = act[0, :, inner + states:]
    rows = lax.broadcasted_iota(jnp.int32, (width, width), 0)
    columns = lax.broadcasted_iota(jnp.int32, (width, width), 1)
    same = (rows <= columns) & (marks[0][:, 5:6] == row_marks[0, 0:1, :])
    scores[...] = jnp.where(same, dot_nt(keys, queries), 0.0)
    d_scores[...] = jnp.zeros_like(d_scores)
    sums_rows[...] = jnp.zeros_like(sums_rows)
    sums_columns[...] = jnp.zeros_like(sums_columns)
    size = halves(sizes[0])
    wide = 256
    for at in range(0, inner, wide):
        part = dot(size, spread[:, pl.ds(at, wide)])
        stepped[:, pl.ds(at, wide)] = (part * act[0, :, pl.ds(at, wide)].astype(F32)).astype(BF16)
    per = LANES // (inner // heads)
    span = inner // heads
    lane = lax.broadcasted_iota(jnp.int32, (width, LANES), 1)

    eighth = lax.broadcasted_iota(jnp.int32, (8, width), 0)

    def group(at, carry):
        place = pl.ds(pl.multiple_of(at * LANES, LANES), LANES)
        x = stepped[:, place]
        dy = d_mixed[0, :, place]
        dx_low = dx_high = None
        for i in range(per):
            head = at * per + i
            column = head_column(sums[0], head)
            row = sums_t[0, pl.ds(head, 1), :]
            mine = (lane >= i * span) & (lane < (i + 1) * span)
            xh = jnp.where(mine, x, jnp.zeros_like(x))
            dyh = jnp.where(mine, dy, jnp.zeros_like(dy))
            l_low = jnp.exp(jnp.minimum(row - column[0:half], 0.0))
            l_high = jnp.exp(jnp.minimum(row[:, half:] - column[half:], 0.0))
            w_low = scores[0:half, :] * l_low
            w_high = scores[half:, half:] * l_high
            dw_low = dot_nt(xh[0:half], dy)
            dw_high = dot_nt(xh[half:], dy[half:])
            d_scores[0:half, :] += dw_low * l_low
            d_scores[half:, half:] += dw_high * l_high
            g_low = dw_low * w_low
            g_high = dw_high * w_high
            over_low = jnp.sum(g_low, axis=0, keepdims=True)
            over_high = jnp.sum(g_high, axis=0, keepdims=True)
            eight = pl.ds(pl.multiple_of(head // 8 * 8, 8), 8)
            chosen = eighth == head % 8
            sums_rows[eight, :] += jnp.where(chosen, over_low, 0.0)
            sums_rows[eight, half:] += jnp.where(chosen[:, half:], over_high, 0.0)
            here = lane[0:half] == head
            sums_columns[0:half, :] += jnp.where(here, jnp.sum(g_low, axis=1, keepdims=True), 0.0)
            sums_columns[half:, :] += jnp.where(here, jnp.sum(g_high, axis=1, keepdims=True), 0.0)
            a = dot(w_low.astype(BF16), dyh)
            b = dot(w_high.astype(BF16), dyh[half:])
            dx_low = a if dx_low is None else dx_low + a
            dx_high = b if dx_high is None else dx_high + b
        d_stepped[0, 0:half, place] = dx_low.astype(BF16)
        d_stepped[0, half:, place] = dx_high.astype(BF16)
        return carry

    lax.fori_loop(0, inner // LANES, group, 0, unroll=2)
    grad = jnp.where(same, d_scores[...], 0.0).astype(BF16)
    d_pair[0, :, 0:states] = dot(grad, queries)
    d_pair[0, :, states:] = dot(grad.T, keys) + d_queries[0]
    d_total[0] = sums_rows[...].T - sums_columns[...] + d_sums[0]


def conv_back_kernel(
    inner, d_stepped, d_mixed, act, mixed_in, edge, marks, taps, raw, rates, skip, sizes, sums, spread,
    d_pair, d_total, d_state, state,
    d_mixed_in, d_edge, d_raw, tap_grads, head_grads, padded, shifted,
):
    width, channels = mixed_in.shape[1:]
    states = (channels - inner) // 2
    wide = 256

    @pl.when(pl.program_id(0) == 0)
    def _():
        tap_grads[...] = jnp.zeros_like(tap_grads)
        head_grads[...] = jnp.zeros_like(head_grads)

    padded[0:EDGE, :] = edge[0].astype(F32)
    padded[EDGE:EDGE + width, :] = mixed_in[0].astype(F32)
    marks_now = marks[0]
    masks = [marks_now[:, back:back + 1] for back in range(3)]
    total_sum = sums[0]
    size = sizes[0]
    last = total_sum[width - 1:width]
    faded = marks_now[:, 4:5] * jnp.exp(last - total_sum)
    weight = faded * size
    weight_pair = halves(weight)
    size_pair = halves(size)
    keys = act[0, :, inner:inner + states]
    for back in range(3):
        shifted[back, 0:EDGE, :] = jnp.zeros((EDGE, wide), F32)
        shifted[back, EDGE + width:, :] = jnp.zeros((EDGE, wide), F32)

    def through_conv(at, d_act):
        place = pl.ds(at, wide)
        total = conv_total(padded, taps, masks, at, wide, width)
        sig = sigmoid(total)
        d = d_act * (sig + total * sig * (1.0 - sig))
        tap_grads[4:5, place] += jnp.sum(d, axis=0, keepdims=True)
        tap_grads[3:4, place] += jnp.sum(d * padded[EDGE:EDGE + width, place], axis=0, keepdims=True)
        back_total = taps[3:4, place] * d
        edge_total = jnp.zeros((EDGE, wide), F32)
        for back in range(1, 4):
            u = masks[back - 1] * d
            tap_grads[3 - back:4 - back, place] += jnp.sum(
                u * padded[EDGE - back:EDGE - back + width, place], axis=0, keepdims=True
            )
            shifted[back - 1, EDGE:EDGE + width, :] = u
            tap = taps[3 - back:4 - back, place]
            back_total = back_total + tap * shifted[back - 1, EDGE + back:EDGE + back + width, :]
            edge_total = edge_total + tap * shifted[back - 1, back:back + EDGE, :]
        d_mixed_in[0, :, place] = back_total.astype(BF16)
        d_edge[0, :, place] = edge_total

    d_keys = d_pair[0, :, 0:states]
    d_size = d_weight = carried = None
    for at in range(0, inner, wide):
        place = pl.ds(at, wide)
        values = act[0, :, place].astype(F32)
        part = spread[:, place]
        ds = d_state[0, :, place]
        wide_weight = dot(weight_pair, part)
        d_weighted = dot(keys, ds)
        dx = d_stepped[0, :, place].astype(F32)
        d_act = dx * dot(size_pair, part) + d_weighted * wide_weight + skip[0:1, place] * d_mixed[0, :, place].astype(F32)
        d_keys = d_keys + dot_nt((wide_weight * values).astype(BF16), ds)
        a = dot_nt((dx * values).astype(BF16), part[0:LANES])
        b = dot_nt((d_weighted * values).astype(BF16), part[0:LANES])
        c = jnp.sum(ds.astype(F32) * state[0, :, place].astype(F32), axis=0, keepdims=True)
        c = dot_nt(jnp.broadcast_to(halves_rows(c), (EDGE, wide)), part[0:LANES])
        d_size = a if d_size is None else d_size + a
        d_weight = b if d_weight is None else d_weight + b
        carried = c if carried is None else carried + c
        through_conv(at, d_act)
    through_conv(inner, jnp.concatenate([d_keys, d_pair[0, :, states:]], axis=1))
    d_size = d_size + d_weight * faded
    pulled = d_weight * weight
    gone = marks_now[width - 1:width, 3:4] * jnp.exp(last)
    at_end = jnp.sum(pulled, axis=0, keepdims=True) + gone * carried[0:1]
    row = lax.broadcasted_iota(jnp.int32, (width, LANES), 0)
    d_sum = d_total[0] - pulled + jnp.where(row == width - 1, at_end, 0.0)
    order = lax.broadcasted_iota(jnp.int32, (width, width), 0) <= lax.broadcasted_iota(jnp.int32, (width, width), 1)
    d_rate = dot_exact(jnp.where(order, 1.0, 0.0).astype(F32), d_sum)
    d_size = d_size + d_rate * rates[1:2, :]
    d_step = d_size * sigmoid(raw[0] + rates[0:1, :])
    d_raw[0] = d_step.astype(BF16)
    head_grads[0:1, :] += jnp.sum(d_step, axis=0, keepdims=True)
    head_grads[1:2, :] += jnp.sum(d_rate * size * rates[1:2, :], axis=0, keepdims=True)


def halves_rows(v):
    return v.astype(BF16)


def call(kernel, batch, ins, outs, scratch, name):
    def spec(shape, whole):
        block = tuple(shape) if whole else (1,) + tuple(shape[1:])
        if whole:
            return pl.BlockSpec(block, lambda b: (0,) * len(block))
        return pl.BlockSpec(block, lambda b: (b,) + (0,) * (len(block) - 1))

    arrays = [a for a, _ in ins]
    return pl.pallas_call(
        kernel,
        grid=(batch,),
        in_specs=[spec(a.shape, whole) for a, whole in ins],
        out_specs=[spec(shape, whole) for shape, _, whole in outs],
        out_shape=[jax.ShapeDtypeStruct(shape, kind) for shape, kind, _ in outs],
        scratch_shapes=[pltpu.VMEM(shape, kind) for shape, kind in scratch],
        compiler_params=pltpu.CompilerParams(vmem_limit_bytes=VMEM),
        name=name,
    )(*arrays)


def exchange(state, factor, later_is_odd):
    peers = lax.axis_size("seq")
    odd = lax.axis_index("seq") % 2
    later = odd == 1 if later_is_odd else odd == 0
    states = state.shape[1]
    own = jnp.concatenate([state, factor.astype(BF16)], axis=1)
    other = lax.ppermute(own, "seq", [(i, i ^ 1) for i in range(peers)])
    mine = lax.dynamic_index_in_dim(own, odd, 0, keepdims=False).astype(F32)
    theirs = lax.dynamic_index_in_dim(other, odd, 0, keepdims=False).astype(F32)
    second = jnp.where(later, mine, theirs)
    first = jnp.where(later, theirs, mine)
    gain = second[states:states + 1]
    joined = jnp.concatenate(
        [gain * first[:states] + second[:states], gain * first[states:]], axis=0
    ).astype(BF16)
    before = jnp.zeros(joined[:states].shape, F32)
    for distance in range(peers // 2 - 1, 0, -1):
        step = 2 * distance if later_is_odd else -2 * distance
        route = [(i, i + step) for i in range(peers) if 0 <= i + step < peers]
        got = lax.ppermute(joined, "seq", route).astype(F32)
        before = got[states:states + 1] * before + got[:states]
    before = before.astype(BF16)
    partner = lax.ppermute(before, "seq", [(i, i ^ 1) for i in range(peers)])
    entering = jnp.where(odd == 0, jnp.stack([before, partner]), jnp.stack([partner, before])).astype(F32)
    gain = other[:, states:states + 1].astype(F32)
    through = gain * entering + other[:, :states].astype(F32)
    return jnp.where(later, through, entering).astype(BF16)


def gathered(block):
    peers = lax.axis_size("seq")
    rows = block.shape[0] // peers
    share = lax.dynamic_slice_in_dim(block, lax.axis_index("seq") * rows, rows, 0)
    return lax.all_gather(share, ("fsdp", "seq"), axis=0, tiled=True)


def reduced(grad):
    share = lax.psum_scatter(grad, ("fsdp", "seq"), scatter_dimension=0, tiled=True)
    return lax.all_gather(share, "seq", axis=0, tiled=True).astype(F32)


def norm_scale_of(stream):
    return lax.rsqrt(jnp.mean(stream * stream, axis=-1, keepdims=True) + EPSILON)


def on_device(
    tokens, segments, norm_gain, in_weight, dt_weight, conv_weight, conv_bias, dt_bias, a_log, d_skip,
    gate_gain, out_weight, cotangent,
):
    layers = in_weight.shape[0]
    batch, width, model = tokens.shape
    heads = dt_weight.shape[2]
    taps_len = conv_weight.shape[1]
    peers = lax.axis_size("seq")
    groups = lax.axis_size("fsdp")
    rows = batch * width
    inner = out_weight.shape[1] * groups
    channels = in_weight.shape[2] - inner
    states = (channels - inner) // 2
    span = inner // heads

    small = [norm_gain, conv_weight.reshape(layers, -1), conv_bias, dt_bias, a_log, d_skip, gate_gain, dt_weight.reshape(layers, -1)]
    sizes = [a.shape[1] for a in small]
    packed = lax.all_gather(jnp.concatenate(small, axis=1), "fsdp", axis=0)
    pieces, at = [], 0
    for size in sizes:
        pieces.append(packed[:, :, at:at + size])
        at += size

    def joined(piece):
        return jnp.moveaxis(piece, 0, 1).reshape(layers, -1)

    norm_all = joined(pieces[0]).astype(F32)
    taps_all = jnp.moveaxis(pieces[1].reshape(groups, layers, taps_len, -1), 0, 2).reshape(layers, taps_len, channels)
    taps_all = jnp.concatenate(
        [taps_all.astype(F32), joined(pieces[2]).astype(F32)[:, None], jnp.zeros((layers, 8 - taps_len - 1, channels), F32)], axis=1
    )
    pad_heads = ((0, 0), (0, LANES - heads))
    rates_all = jnp.stack(
        [jnp.pad(joined(pieces[3]).astype(F32), pad_heads), jnp.pad(-jnp.exp(joined(pieces[4]).astype(F32)), pad_heads)], axis=1
    )
    rates_all = jnp.pad(rates_all, ((0, 0), (0, 6), (0, 0)))
    skip_all = jnp.broadcast_to(jnp.repeat(joined(pieces[5]).astype(F32), span, axis=1)[:, None], (layers, 8, inner))
    gain_all = jnp.broadcast_to(joined(pieces[6]).astype(F32)[:, None], (layers, 8, inner))
    dt_all = jnp.moveaxis(pieces[7].reshape(groups, layers, -1, heads), 0, 1).reshape(layers, model, heads)
    dt_all = jnp.pad(dt_all, ((0, 0), (0, 0), (0, LANES - heads)))

    in_all = [gathered(in_weight[layer]) for layer in range(layers)]
    out_all = [gathered(out_weight[layer]) for layer in range(layers)]

    numbers = (segments + 1).astype(F32)
    before = lax.ppermute(numbers[:, width - EDGE:], "seq", [(i, i + 1) for i in range(peers - 1)])
    padded = jnp.concatenate([before, numbers], axis=1)
    columns = [padded[:, EDGE - back:EDGE - back + width] == numbers for back in range(1, taps_len)]
    columns += [numbers == before[:, EDGE - 1:], numbers == numbers[:, width - 1:]]
    marks = jnp.stack([c.astype(F32) for c in columns] + [numbers], axis=-1)
    marks = jnp.pad(marks, ((0, 0), (0, 0), (0, LANES - marks.shape[-1])))
    row_marks = jnp.broadcast_to(numbers[:, None, :], (batch, 8, width))
    lane_head = jnp.arange(inner) // span
    spread = (jnp.arange(2 * LANES)[:, None] % LANES == lane_head[None, :]).astype(BF16)

    stream = tokens.astype(F32)
    kept = []
    for layer in range(layers):
        norm_scale = norm_scale_of(stream)
        low = (stream * norm_scale * norm_all[layer]).astype(BF16).reshape(rows, model)
        w_in, w_out = in_all[layer], out_all[layer]
        mixed_in = dot(low, w_in[:, inner:]).astype(BF16).reshape(batch, width, channels)
        raw = dot(low, dt_all[layer]).reshape(batch, width, LANES)
        edge = lax.ppermute(mixed_in[:, width - EDGE:], "seq", [(i, i + 1) for i in range(peers - 1)])
        gate = dot(low, w_in[:, :inner]).astype(BF16).reshape(batch, width, inner)
        taps, rates, skip, gain = taps_all[layer], rates_all[layer], skip_all[layer], gain_all[layer]
        act, size, sums, sums_t, state, factor = call(
            functools.partial(conv_kernel, inner), batch,
            [(mixed_in, 0), (edge, 0), (marks, 0), (taps, 1), (raw, 0), (rates, 1), (spread, 1)],
            [
                ((batch, width, channels), BF16, 0), ((batch, width, LANES), F32, 0), ((batch, width, LANES), F32, 0),
                ((batch, heads, width), F32, 0), ((batch, states, inner), BF16, 0), ((batch, FACTOR_ROWS, inner), F32, 0),
            ],
            [((EDGE + width, channels), F32)], "conv_states",
        )
        entering = exchange(state, factor, True)
        (part,) = call(
            functools.partial(intra_kernel, inner, heads), batch,
            [(act, 0), (size, 0), (sums, 0), (sums_t, 0), (marks, 0), (row_marks, 0), (skip, 1), (spread, 1)],
            [((batch, width, inner), F32, 0)],
            [((width, width), F32), ((width, inner), BF16)], "mix_within",
        )
        mixed, gated = call(
            functools.partial(post_kernel, inner), batch,
            [(part, 0), (act, 0), (entering, 0), (sums, 0), (marks, 0), (gate, 0), (gain, 1), (spread, 1)],
            [((batch, width, inner), BF16, 0), ((batch, width, inner), BF16, 0)],
            [((width, inner), F32)], "mix_gate",
        )
        gated = gated.reshape(rows, inner)
        kept.append((stream, norm_scale, low, mixed_in, raw, edge, gate, act, size, sums, sums_t, factor, entering, mixed, gated))
        stream = stream + dot(gated, w_out).reshape(batch, width, model)

    grad_stream = cotangent.astype(F32)
    collected = []
    for layer in reversed(range(layers)):
        (entry, norm_scale, low, mixed_in, raw, edge, gate, act, size, sums, sums_t, factor, entering, mixed, gated) = kept[layer]
        w_in, w_out = in_all[layer], out_all[layer]
        taps, rates, skip, gain = taps_all[layer], rates_all[layer], skip_all[layer], gain_all[layer]
        grad_low = grad_stream.astype(BF16).reshape(rows, model)
        grad_gated = dot_nt(grad_low, w_out).astype(BF16).reshape(batch, width, inner)
        d_mixed, d_gate, d_state, d_queries, d_sums, row_grads = call(
            functools.partial(gate_back_kernel, inner), batch,
            [(grad_gated, 0), (mixed, 0), (gate, 0), (gain, 1), (act, 0), (entering, 0), (sums, 0), (marks, 0), (spread, 1)],
            [
                ((batch, width, inner), BF16, 0), ((batch, width, inner), BF16, 0), ((batch, states, inner), BF16, 0),
                ((batch, width, states), F32, 0), ((batch, width, LANES), F32, 0), ((8, inner), F32, 1),
            ],
            [((width, inner), F32)], "gate_back",
        )
        leaving = exchange(d_state, factor, False)
        out_grad = dot_tn(gated, grad_low).astype(BF16)
        out_share = reduced(out_grad)
        d_stepped, d_pair, d_total = call(
            functools.partial(intra_back_kernel, inner, heads), batch,
            [
                (d_mixed, 0), (act, 0), (size, 0), (sums, 0), (sums_t, 0), (marks, 0), (row_marks, 0), (spread, 1),
                (d_queries, 0), (d_sums, 0),
            ],
            [((batch, width, inner), BF16, 0), ((batch, width, 2 * states), F32, 0), ((batch, width, LANES), F32, 0)],
            [
                ((width, width), F32), ((width, width), F32), ((width, inner), BF16), ((LANES, width), F32), ((width, LANES), F32),
            ], "mix_within_back",
        )
        d_gate = d_gate.reshape(rows, inner)
        d_mixed_in, d_edge, d_raw, tap_grads, head_grads = call(
            functools.partial(conv_back_kernel, inner), batch,
            [
                (d_stepped, 0), (d_mixed, 0), (act, 0), (mixed_in, 0), (edge, 0), (marks, 0), (taps, 1), (raw, 0), (rates, 1),
                (skip, 1), (size, 0), (sums, 0), (spread, 1), (d_pair, 0), (d_total, 0), (leaving, 0), (entering, 0),
            ],
            [
                ((batch, width, channels), BF16, 0), ((batch, EDGE, channels), F32, 0), ((batch, width, LANES), BF16, 0),
                ((8, channels), F32, 1), ((8, LANES), F32, 1),
            ],
            [((EDGE + width, channels), F32), ((3, width + 2 * EDGE, 256), F32)], "conv_back",
        )
        from_next = lax.ppermute(d_edge.astype(BF16), "seq", [(i + 1, i) for i in range(peers - 1)])
        d_mixed_in = jnp.concatenate(
            [
                d_mixed_in[:, :width - EDGE],
                (d_mixed_in[:, width - EDGE:].astype(F32) + from_next.astype(F32)).astype(BF16),
            ], axis=1,
        ).reshape(rows, channels)
        d_raw = d_raw.reshape(rows, LANES)
        in_grad = jnp.concatenate([dot_tn(low, d_gate).astype(BF16), dot_tn(low, d_mixed_in).astype(BF16)], axis=1)
        in_share = reduced(in_grad)
        dt_grad = dot_tn(low, d_raw)[:, :heads]
        grad_rows = dot_nt(d_gate, w_in[:, :inner]) + dot_nt(d_mixed_in, w_in[:, inner:]) + dot_nt(d_raw, dt_all[layer])
        grad_rows = grad_rows.reshape(batch, width, model)
        scaled = grad_rows * norm_all[layer]
        inward = jnp.mean(scaled * entry, axis=-1, keepdims=True)
        gain_grad = jnp.sum(grad_rows * entry * norm_scale, axis=(0, 1))
        grad_stream = grad_stream + norm_scale * scaled - (norm_scale * norm_scale * norm_scale * inward) * entry
        skip_grad = jnp.sum(row_grads[1].reshape(heads, span), axis=1)
        small_grads = [
            gain_grad.reshape(groups, -1),
            jnp.moveaxis(tap_grads[:taps_len].reshape(taps_len, groups, -1), 1, 0).reshape(groups, -1),
            tap_grads[taps_len].reshape(groups, -1),
            head_grads[0, :heads].reshape(groups, -1),
            head_grads[1, :heads].reshape(groups, -1),
            skip_grad.reshape(groups, -1),
            row_grads[0].reshape(groups, -1),
            dt_grad.reshape(groups, -1),
        ]
        collected.append((in_share, out_share, jnp.concatenate(small_grads, axis=1)))
    collected = collected[::-1]
    small_sum = lax.psum(jnp.stack([c[2] for c in collected], axis=1), ("fsdp", "seq"))
    small_sum = lax.dynamic_index_in_dim(small_sum, lax.axis_index("fsdp"), 0, keepdims=False)
    pieces, at = [], 0
    for size in sizes:
        pieces.append(small_sum[:, at:at + size])
        at += size
    return (
        stream, grad_stream, pieces[0],
        jnp.stack([c[0] for c in collected]),
        pieces[7].reshape(layers, -1, heads),
        pieces[1].reshape(layers, taps_len, -1),
        pieces[2], pieces[3], pieces[4], pieces[5], pieces[6],
        jnp.stack([c[1] for c in collected]),
    )


def solution(mesh):
    split = P("fsdp", "seq", None)
    vector = P(None, "fsdp")
    matrix = P(None, "fsdp", None)
    taps = P(None, None, "fsdp")
    return jax.shard_map(
        on_device,
        mesh=mesh,
        in_specs=(
            split, P("fsdp", "seq"), vector, matrix, matrix, taps, vector, vector, vector, vector, vector, matrix, split,
        ),
        out_specs=(
            split, split, vector, matrix, matrix, taps, vector, vector, vector, vector, vector, matrix,
        ),
        check_vma=False,
    )
```

time: 1690 us -> 1230 us (0.73)
  matrix products: 375 us -> 98.1 us
  blocking collectives: 242 us -> 16.2 us
  waiting for transfers between devices: 601 us -> 765 us
  other arithmetic: 218 us -> 65.2 us
  Pallas kernels: 0 us -> 144 us
  local copies, waits for them, and re-layouts: 213 us -> 72.5 us
  starting transfers between devices: 10.6 us -> 45.6 us
    dot_general x44 -> x24, matrix products: 375 us -> 98.1 us  [the longest x8 35.5 us: dot(): return jnp.dot(a, b, preferred_element_type=F32)]
    all_gather x12 -> x1, blocking collectives: 173 us -> 16.2 us  [on_device(): packed = lax.all_gather(jnp.concatenate(small, axis=1), 'fsdp', axis=0)]
    pallas_call x0 -> x12, Pallas kernels: none -> 144 us  [call(): pl.pallas_call(kernel, grid=(batch,), in_specs=[spec(a.shape, whole) for...]
    ppermute x5 -> x25, waiting for transfers between devices: 2.35 us -> 121 us  [the longest x12 115 us: exchange(): got = lax.ppermute(joined, 'seq', route).astype(F32)]
    slice x27 -> x45, local copies, waits for them, and re-layouts: 126 us -> 21.4 us  [the longest x1 3.95 us: on_device(): in_all = [gathered(in_weight[layer]) for layer in range(layers)]]
    reduce_sum x19 -> x5, other arithmetic: 81 us -> 2.43 us  [the longest x2 1.92 us: on_device(): gain_grad = jnp.sum(grad_rows * entry * norm_scale, axis=(0, 1))]
    all_gather x8, waiting for transfers between devices: 161 us -> 233 us  [the longest x4 130 us: gathered(): return lax.all_gather(share, ('fsdp', 'seq'), axis=0, tiled=True)]
    reduce_scatter x6 -> x4, waiting for transfers between devices: 356 us -> 289 us  [reduced(): lax.psum_scatter(grad, ('fsdp', 'seq'), scatter_dimension=0, tiled=True)]
  transfers between devices with their start and end apart: 22 -> 38, of which waited for: 12 -> 20; matrix products, arithmetic and copies ran while one was open for 33% -> 16% of each run, Pallas kernels for 0% -> 10%
where the time goes in v1:
time: 1230 us; the launch traced here: 1220 us
  waiting for transfers between devices  765 us (62%)
  Pallas kernels  144 us (12%)
  matrix products  98.1 us (8%)
  local copies, waits for them, and re-layouts  72.5 us (6%)
  other arithmetic  65.2 us (5%)
  starting transfers between devices  45.6 us (4%)
  between operations  16.7 us (1%)
  blocking collectives  16.2 us (1%)
    reduce_scatter x4, waiting for transfers between devices, reduced(): lax.psum_scatter(grad, ('fsdp', 'seq'), scatter_dimension=0, tiled=True)  289 us
    pallas_call x12, Pallas kernels, call(): pl.pallas_call(kernel, grid=(batch,), in_specs=[spec(a.shape, whole) for...  144 us
    all_gather x4, waiting for transfers between devices, gathered(): return lax.all_gather(share, ('fsdp', 'seq'), axis=0, tiled=True)  130 us
    psum x1, waiting for transfers between devices, on_device(): lax.psum(jnp.stack([c[2] for c in collected], axis=1), ('fsdp', 'seq'))  120 us
    ppermute x12, waiting for transfers between devices, exchange(): got = lax.ppermute(joined, 'seq', route).astype(F32)  115 us
    all_gather x4, waiting for transfers between devices, reduced(): return lax.all_gather(share, 'seq', axis=0, tiled=True).astype(F32)  102 us
    dot_general x8, matrix products, dot(): return jnp.dot(a, b, preferred_element_type=F32)  35.5 us
    dot_general x8, matrix products, dot_nt(): return lax.dot_general(a, b, NT, preferred_element_type=F32)  32.1 us
  transfers between devices with their start and end apart: 38, of which 20 were waited for; matrix products, arithmetic and copies ran while one was open for 16% of the time, Pallas kernels for 10%

profile of v1, /device:TPU:0, one launch (start us, length us, event | category | flops | bytes accessed | tf_op | source)
XLA Modules:
  0.0 1222.7 jit_solution(4992750049678430838)
XLA Ops:
  20.5 16.2 %all-gather.5 = bf16[4,2,11864]{2,1,0:T(2,128)(2,1)S(1)} all-gather(bf16[1,2,11864]{2,1,0:T(2,128)(2,1)S(1)} %bitcast.333), channel_id=2, replica_groups=mesh['fsdp'=4,'seq'=8] {'fsdp'}, dimensions={0}, use_global_device_ids=true | all-gather | bytes 237280 | tf_op jit(solution)/shard_map/all_gather | solution.py:460
  43.4 53.7 %all-gather.23.cloned.1.call-done = bf16[1,1024,4352]{2,1,0:T(8,128)(2,1)} async-done(((bf16[1,32,4352]{2,1,0:T(8,128)(2,1)}), bf16[1,1024,4352]{2,1,0:T(8,128)(2,1)}) %all-gather.23.cloned.1.call-update) | async-done | bytes 8912912 | tf_op jit(solution)/shard_map/all_gather | solution.py:430
  147.7 21.6 %collective-permute-done.4 = bf16[144,2048]{1,0:T(8,128)(2,1)} collective-permute-done((bf16[144,2048]{1,0:T(8,128)(2,1)}, bf16[144,2048]{1,0:T(8,128)(2,1)}, u32[]{:S(2)}, u32[]{:S(2)}) %collective-permute-start.4) | collective-permute-done | bytes 589856 | tf_op jit(solution)/shard_map/ppermute | solution.py:416
  181.7 11.8 mix_within.2.part_mixed
  211.8 46.4 %all-gather.27.cloned.1.call-done = bf16[1,1024,4352]{2,1,0:T(8,128)(2,1)} async-done(((bf16[1,32,4352]{2,1,0:T(8,128)(2,1)}), bf16[1,1024,4352]{2,1,0:T(8,128)(2,1)}) %all-gather.27.cloned.1.call-update) | async-done | bytes 8912912 | tf_op jit(solution)/shard_map/all_gather | solution.py:430
  296.1 30.2 %all-gather.29.cloned.1.call-done = bf16[1,2048,1024]{2,1,0:T(8,128)(2,1)} async-done(((bf16[1,64,1024]{2,1,0:T(8,128)(2,1)}), bf16[1,2048,1024]{2,1,0:T(8,128)(2,1)}) %all-gather.29.cloned.1.call-update) | async-done | bytes 4194320 | tf_op jit(solution)/shard_map/all_gather | solution.py:430
  344.8 11.9 mix_within.3.part_mixed
  366.5 11.2 gate_back.2
  391.3 22.0 %collective-permute-done.15 = bf16[144,2048]{1,0:T(8,128)(2,1)S(1)} collective-permute-done((bf16[144,2048]{1,0:T(8,128)(2,1)S(1)}, bf16[144,2048]{1,0:T(8,128)(2,1)S(1)}, u32[]{:S(2)}, u32[]{:S(2)}) %collective-permute-start.15) | collective-permute-done | bytes 589856 | tf_op jit(solution)/shard_map/ppermute | solution.py:416
  413.9 28.5 %collective-permute-done.16 = bf16[144,2048]{1,0:T(8,128)(2,1)S(1)} collective-permute-done((bf16[144,2048]{1,0:T(8,128)(2,1)S(1)}, bf16[144,2048]{1,0:T(8,128)(2,1)S(1)}, u32[]{:S(2)}, u32[]{:S(2)}) %collective-permute-start.16) | collective-permute-done | bytes 589856 | tf_op jit(solution)/shard_map/ppermute | solution.py:416
  443.9 17.4 %mix_within_back.2 = (bf16[2,256,2048]{2,1,0:T(8,128)(2,1)S(1)}, f32[2,256,256]{2,1,0:T(8,128)S(1)}, f32[2,256,128]{2,1,0:T(8,128)S(1)}) custom-call(bf16[2,256,2048]{2,1,0:T(8,128)(2,1)} %get-tuple-element.72.d_mixed, bf16[2,256,2304]{2,1,0:T(8,128)(2,1)} %copy-done.1, f32[2,256,128]{2,1,0:T(8,128)S(1)} %copy-done.26, f32[2,256,128]{2,1,0:T(8,128)S(1)} %copy-done.14, ...), custom_call_target="tpu_custom_call" | custom-call | tf_op jit(solution)/shard_map/mix_within_back/pallas_call | solution.py:385
  465.4 17.7 %conv_back.2 = (bf16[2,256,2304]{2,1,0:T(8,128)(2,1)}, f32[2,8,2304]{2,1,0:T(8,128)S(1)}, bf16[2,256,128]{2,1,0:T(8,128)(2,1)S(1)}, f32[8,2304]{1,0:T(8,128)S(1)}, f32[8,128]{1,0:T(8,128)S(1)}) custom-call(bf16[2,256,2048]{2,1,0:T(8,128)(2,1)} %copy-done.28, bf16[2,256,2048]{2,1,0:T(8,128)(2,1)} %get-tuple-element.72.d_mixed, ...), custom_call_target="tpu_custom_call" | custom-call | tf_op jit(solution)/shard_map/conv_back/pallas_call | solution.py:385
  528.5 11.1 gate_back.3
  548.0 16.2 %collective-permute-done.21 = bf16[144,2048]{1,0:T(8,128)(2,1)S(1)} collective-permute-done((bf16[144,2048]{1,0:T(8,128)(2,1)S(1)}, bf16[144,2048]{1,0:T(8,128)(2,1)S(1)}, u32[]{:S(2)}, u32[]{:S(2)}) %collective-permute-start.21) | collective-permute-done | bytes 589856 | tf_op jit(solution)/shard_map/ppermute | solution.py:416
  569.8 21.3 %collective-permute-done.22 = bf16[144,2048]{1,0:T(8,128)(2,1)S(1)} collective-permute-done((bf16[144,2048]{1,0:T(8,128)(2,1)S(1)}, bf16[144,2048]{1,0:T(8,128)(2,1)S(1)}, u32[]{:S(2)}, u32[]{:S(2)}) %collective-permute-start.22) | collective-permute-done | bytes 589856 | tf_op jit(solution)/shard_map/ppermute | solution.py:416
  592.1 17.2 %mix_within_back.3 = (bf16[2,256,2048]{2,1,0:T(8,128)(2,1)S(1)}, f32[2,256,256]{2,1,0:T(8,128)S(1)}, f32[2,256,128]{2,1,0:T(8,128)S(1)}) custom-call(bf16[2,256,2048]{2,1,0:T(8,128)(2,1)} %get-tuple-element.84.d_mixed, bf16[2,256,2304]{2,1,0:T(8,128)(2,1)} %copy-done, f32[2,256,128]{2,1,0:T(8,128)S(1)} %copy-done.23, f32[2,256,128]{2,1,0:T(8,128)S(1)} %copy-done.11, ...), custom_call_target="tpu_custom_call" | custom-call | tf_op jit(solution)/shard_map/mix_within_back/pallas_call | solution.py:385
  611.7 17.5 %conv_back.3 = (bf16[2,256,2304]{2,1,0:T(8,128)(2,1)}, f32[2,8,2304]{2,1,0:T(8,128)S(1)}, bf16[2,256,128]{2,1,0:T(8,128)(2,1)S(1)}, f32[8,2304]{1,0:T(8,128)S(1)}, f32[8,128]{1,0:T(8,128)S(1)}) custom-call(bf16[2,256,2048]{2,1,0:T(8,128)(2,1)} %copy-done.27, bf16[2,256,2048]{2,1,0:T(8,128)(2,1)} %get-tuple-element.84.d_mixed, bf16[2,256,2304]{2,1,0:T(8,128)(2,1)} %copy-done, ...), custom_call_target="tpu_custom_call" | custom-call | tf_op jit(solution)/shard_map/conv_back/pallas_call | solution.py:385
  679.2 141.6 %reduce-scatter.7.cloned.1.call-done = bf16[32,4352]{1,0:T(8,128)(2,1)} async-done(((bf16[1024,4352]{1,0:T(8,128)(2,1)}), bf16[32,4352]{1,0:T(8,128)(2,1)}) %reduce-scatter.7.cloned.1.call-update) | async-done | bytes 278544 | tf_op jit(solution)/shard_map/reduce_scatter | solution.py:434
  821.2 147.6 %reduce-scatter.5.cloned.1.call-done = bf16[32,4352]{1,0:T(8,128)(2,1)} async-done(((bf16[1024,4352]{1,0:T(8,128)(2,1)}), bf16[32,4352]{1,0:T(8,128)(2,1)}) %reduce-scatter.5.cloned.1.call-update) | async-done | bytes 278544 | tf_op jit(solution)/shard_map/reduce_scatter | solution.py:434
  977.9 119.7 %all-reduce.7.cloned.1.call-done = f32[4,2,11864]{2,0,1:T(4,128)} async-done(((f32[4,2,11864]{2,0,1:T(4,128)}), f32[4,2,11864]{2,0,1:T(4,128)}) %all-reduce.7.cloned.1.call-update) | async-done | bytes 379664 | tf_op jit(solution)/shard_map/psum | solution.py:609
  1103.0 19.7 %all-gather.21.cloned.1.call-done = bf16[512,1024]{1,0:T(8,128)(2,1)} async-done(((bf16[64,1024]{1,0:T(8,128)(2,1)}), bf16[512,1024]{1,0:T(8,128)(2,1)}) %all-gather.21.cloned.1.call-update) | async-done | bytes 1048592 | tf_op jit(solution)/shard_map/all_gather | solution.py:435
  1122.7 25.6 %all-gather.19.cloned.1.call-done = bf16[512,1024]{1,0:T(8,128)(2,1)} async-done(((bf16[64,1024]{1,0:T(8,128)(2,1)}), bf16[512,1024]{1,0:T(8,128)(2,1)}) %all-gather.19.cloned.1.call-update) | async-done | bytes 1048592 | tf_op jit(solution)/shard_map/all_gather | solution.py:435
  1152.1 26.6 %all-gather.17.cloned.1.call-done = bf16[256,4352]{1,0:T(8,128)(2,1)} async-done(((bf16[32,4352]{1,0:T(8,128)(2,1)}), bf16[256,4352]{1,0:T(8,128)(2,1)}) %all-gather.17.cloned.1.call-update) | async-done | bytes 2228240 | tf_op jit(solution)/shard_map/all_gather | solution.py:435
  1178.7 30.5 %all-gather.15.cloned.1.call-done = bf16[256,4352]{1,0:T(8,128)(2,1)} async-done(((bf16[32,4352]{1,0:T(8,128)(2,1)}), bf16[256,4352]{1,0:T(8,128)(2,1)}) %all-gather.15.cloned.1.call-update) | async-done | bytes 2228240 | tf_op jit(solution)/shard_map/all_gather | solution.py:435
  (579 shorter events, 322.7 us)
Async XLA Ops:
  7.2 89.9 %all-gather.23.cloned.1.call-start = ((), (), s32[]{:S(2)}) async-start(), calls=%async_computation.13 | async-start | bytes 9191424 | tf_op jit(solution)/shard_map/all_gather | solution.py:430
  12.9 192.1 %all-gather.25.cloned.1.call-start = ((), (), s32[]{:S(2)}) async-start(), calls=%async_computation.14 | async-start | bytes 4325376 | tf_op jit(solution)/shard_map/all_gather | solution.py:430
  16.4 241.8 %all-gather.27.cloned.1.call-start = ((), (), s32[]{:S(2)}) async-start(), calls=%async_computation.15 | async-start | bytes 9191424 | tf_op jit(solution)/shard_map/all_gather | solution.py:430
  17.3 309.1 %all-gather.29.cloned.1.call-start = ((), (), s32[]{:S(2)}) async-start(), calls=%async_computation.16 | async-start | bytes 4325376 | tf_op jit(solution)/shard_map/all_gather | solution.py:430
  17.4 25.4 %collective-permute-start.1 = (f32[2,8]{1,0:T(2,128)S(1)}, f32[2,8]{1,0:T(2,128)S(1)}, u32[]{:S(2)}, u32[]{:S(2)}) collective-permute-start(f32[2,8]{1,0:T(2,128)S(1)} %slice.534), channel_id=1, source_target_pairs={{0,1},{1,2},{2,3},{3,4},{4,5},{5,6},{6,7},{8,9},{9,10},{10,11},{11... | collective-permute-start | bytes 200 | tf_op jit(solution)/shard_map/ppermute | solution.py:488
  129.1 44.2 %collective-permute-start.5 = (bf16[144,2048]{1,0:T(8,128)(2,1)}, bf16[144,2048]{1,0:T(8,128)(2,1)}, u32[]{:S(2)}, u32[]{:S(2)}) collective-permute-start(bf16[144,2048]{1,0:T(8,128)(2,1)} %pad_maximum_fusion.8), channel_id=1, source_target_pairs={{0,6},{1,7},{8,14},{9,15},{16,22},{17,23},{24,30},{25,31}} | collective-permute-start | bytes 1769480 | tf_op jit(solution)/shard_map/ppermute | solution.py:416
  133.7 35.7 %collective-permute-start.4 = (bf16[144,2048]{1,0:T(8,128)(2,1)}, bf16[144,2048]{1,0:T(8,128)(2,1)}, u32[]{:S(2)}, u32[]{:S(2)}) collective-permute-start(bf16[144,2048]{1,0:T(8,128)(2,1)} %pad_maximum_fusion.8), channel_id=1, source_target_pairs={{0,4},{1,5},{2,6},{3,7},{8,12},{9,13},{10,14},{11,15},{16,20},{17,... | collective-permute-start | bytes 1769480 | tf_op jit(solution)/shard_map/ppermute | solution.py:416
  137.1 34.3 %collective-permute-start.3 = (bf16[144,2048]{1,0:T(8,128)(2,1)}, bf16[144,2048]{1,0:T(8,128)(2,1)}, u32[]{:S(2)}, u32[]{:S(2)}) collective-permute-start(bf16[144,2048]{1,0:T(8,128)(2,1)} %pad_maximum_fusion.8), channel_id=1, source_target_pairs={{0,2},{1,3},{2,4},{3,5},{4,6},{5,7},{8,10},{9,11},{10,12},{11,13},... | collective-permute-start | bytes 1769480 | tf_op jit(solution)/shard_map/ppermute | solution.py:416
  140.7 537.1 %reduce-scatter.11.cloned.1.call-start = ((), (), s32[]{:S(2)}) async-start(), calls=%async_computation.11 | async-start | bytes 4325376 | tf_op jit(solution)/shard_map/reduce_scatter | solution.py:434
  286.3 48.2 %collective-permute-start.11 = (bf16[144,2048]{1,0:T(8,128)(2,1)}, bf16[144,2048]{1,0:T(8,128)(2,1)}, u32[]{:S(2)}, u32[]{:S(2)}) collective-permute-start(bf16[144,2048]{1,0:T(8,128)(2,1)} %pad_maximum_fusion.9), channel_id=1, source_target_pairs={{0,6},{1,7},{8,14},{9,15},{16,22},{17,23},{24,30},{25,31}} | collective-permute-start | bytes 1769480 | tf_op jit(solution)/shard_map/ppermute | solution.py:416
  291.5 41.0 %collective-permute-start.10 = (bf16[144,2048]{1,0:T(8,128)(2,1)}, bf16[144,2048]{1,0:T(8,128)(2,1)}, u32[]{:S(2)}, u32[]{:S(2)}) collective-permute-start(bf16[144,2048]{1,0:T(8,128)(2,1)} %pad_maximum_fusion.9), channel_id=1, source_target_pairs={{0,4},{1,5},{2,6},{3,7},{8,12},{9,13},{10,14},{11,15},{16,20},{17,... | collective-permute-start | bytes 1769480 | tf_op jit(solution)/shard_map/ppermute | solution.py:416
  294.0 41.8 %collective-permute-start.9 = (bf16[144,2048]{1,0:T(8,128)(2,1)}, bf16[144,2048]{1,0:T(8,128)(2,1)}, u32[]{:S(2)}, u32[]{:S(2)}) collective-permute-start(bf16[144,2048]{1,0:T(8,128)(2,1)} %pad_maximum_fusion.9), channel_id=1, source_target_pairs={{0,2},{1,3},{2,4},{3,5},{4,6},{5,7},{8,10},{9,11},{10,12},{11,13},... | collective-permute-start | bytes 1769480 | tf_op jit(solution)/shard_map/ppermute | solution.py:416
  385.8 292.7 %reduce-scatter.9.cloned.1.call-start = ((), (), s32[]{:S(2)}) async-start(), calls=%async_computation.9 | async-start | bytes 4325376 | tf_op jit(solution)/shard_map/reduce_scatter | solution.py:434
  387.4 25.9 %collective-permute-start.15 = (bf16[144,2048]{1,0:T(8,128)(2,1)S(1)}, bf16[144,2048]{1,0:T(8,128)(2,1)S(1)}, u32[]{:S(2)}, u32[]{:S(2)}) collective-permute-start(bf16[144,2048]{1,0:T(8,128)(2,1)S(1)} %pad_maximum_fusion.10), channel_id=1, source_target_pairs={{4,0},{5,1},{6,2},{7,3},{12,8},{13,9},{14,10},{15,11},{20,16},{21,... | collective-permute-start | bytes 1769480 | tf_op jit(solution)/shard_map/ppermute | solution.py:416
  388.7 25.1 %collective-permute-start.14 = (bf16[144,2048]{1,0:T(8,128)(2,1)S(1)}, bf16[144,2048]{1,0:T(8,128)(2,1)S(1)}, u32[]{:S(2)}, u32[]{:S(2)}) collective-permute-start(bf16[144,2048]{1,0:T(8,128)(2,1)S(1)} %pad_maximum_fusion.10), channel_id=1, source_target_pairs={{2,0},{3,1},{4,2},{5,3},{6,4},{7,5},{10,8},{11,9},{12,10},{13,11},... | collective-permute-start | bytes 1769480 | tf_op jit(solution)/shard_map/ppermute | solution.py:416
  390.0 52.5 %collective-permute-start.16 = (bf16[144,2048]{1,0:T(8,128)(2,1)S(1)}, bf16[144,2048]{1,0:T(8,128)(2,1)S(1)}, u32[]{:S(2)}, u32[]{:S(2)}) collective-permute-start(bf16[144,2048]{1,0:T(8,128)(2,1)S(1)} %pad_maximum_fusion.10), channel_id=1, source_target_pairs={{6,0},{7,1},{14,8},{15,9},{22,16},{23,17},{30,24},{31,25}} | collective-permute-start | bytes 1769480 | tf_op jit(solution)/shard_map/ppermute | solution.py:416
  503.1 317.7 %reduce-scatter.7.cloned.1.call-start = ((), (), s32[]{:S(2)}) async-start(), calls=%async_computation.7 | async-start | bytes 9191424 | tf_op jit(solution)/shard_map/reduce_scatter | solution.py:434
  521.9 446.9 %reduce-scatter.5.cloned.1.call-start = ((), (), s32[]{:S(2)}) async-start(), calls=%async_computation.5 | async-start | bytes 9191424 | tf_op jit(solution)/shard_map/reduce_scatter | solution.py:434
  546.5 44.6 %collective-permute-start.22 = (bf16[144,2048]{1,0:T(8,128)(2,1)S(1)}, bf16[144,2048]{1,0:T(8,128)(2,1)S(1)}, u32[]{:S(2)}, u32[]{:S(2)}) collective-permute-start(bf16[144,2048]{1,0:T(8,128)(2,1)S(1)} %pad_maximum_fusion.11), channel_id=1, source_target_pairs={{6,0},{7,1},{14,8},{15,9},{22,16},{23,17},{30,24},{31,25}} | collective-permute-start | bytes 1769480 | tf_op jit(solution)/shard_map/ppermute | solution.py:416
  650.4 447.2 %all-reduce.7.cloned.1.call-start = ((), (), s32[]{:S(2)}) async-start(), calls=%async_computation.4 | async-start | bytes 761856 | tf_op jit(solution)/shard_map/psum | solution.py:609
  677.8 444.9 %all-gather.21.cloned.1.call-start = ((), (), s32[]{:S(2)}) async-start(), calls=%async_computation.12 | async-start | bytes 1179648 | tf_op jit(solution)/shard_map/all_gather | solution.py:435
  678.4 469.9 %all-gather.19.cloned.1.call-start = ((), (), s32[]{:S(2)}) async-start(), calls=%async_computation.10 | async-start | bytes 1179648 | tf_op jit(solution)/shard_map/all_gather | solution.py:435
  679.1 499.6 %all-gather.17.cloned.1.call-start = ((), (), s32[]{:S(2)}) async-start(), calls=%async_computation.8 | async-start | bytes 2506752 | tf_op jit(solution)/shard_map/all_gather | solution.py:435
  820.8 388.4 %all-gather.15.cloned.1.call-start = ((), (), s32[]{:S(2)}) async-start(), calls=%async_computation.6 | async-start | bytes 2506752 | tf_op jit(solution)/shard_map/all_gather | solution.py:435
  (149 other events, 1426.2 us)
Sparse Core Ops, SparseCore 0:
  13.0 83.9 all-gather.22
  99.9 68.0 all-gather.24
  171.4 86.7 all-gather.26
  261.0 65.3 all-gather.28
  385.9 147.0 reduce-scatter.10
  535.1 137.2 reduce-scatter.8
  675.3 145.5 reduce-scatter.6
  823.2 145.5 reduce-scatter.4
  974.7 122.8 all-reduce.6
  1099.5 23.1 all-gather.20
  1124.8 23.4 all-gather.18
  1150.2 28.4 all-gather.16
  1180.7 28.4 all-gather.14

commit v2 on v1

--- a/solution.py
+++ b/solution.py
@@ -65,17 +65,17 @@
     return total
 
 
-def conv_kernel(inner, mixed, edge, marks, taps, raw, rates, spread, act, sizes, sums, sums_t, state, factor, padded):
-    width, channels = mixed.shape[1:]
-    padded[0:EDGE, :] = edge[0].astype(F32)
-    padded[EDGE:EDGE + width, :] = mixed[0].astype(F32)
+def conv_kernel(inner, mixed, edge, marks, taps, rates, spread, act, sizes, sums, sums_t, state, factor, padded):
+    width, channels = mixed.shape[1], padded.shape[1]
+    padded[0:EDGE, :] = edge[0, :, 0:channels].astype(F32)
+    padded[EDGE:EDGE + width, :] = mixed[0, :, 0:channels].astype(F32)
     marks_now = marks[0]
     masks = [marks_now[:, back:back + 1] for back in range(3)]
     wide = 256
     for at in range(0, channels, wide):
         total = conv_total(padded, taps, masks, at, wide, width)
         act[0, :, pl.ds(at, wide)] = (total * sigmoid(total)).astype(BF16)
-    size = softplus(raw[0] + rates[0:1, :])
+    size = softplus(mixed[0, :, channels:].astype(F32) + rates[0:1, :])
     tri = jnp.where(below(width), 1.0, 0.0).astype(F32)
     total_sum = dot_exact(tri, size * rates[1:2, :])
     last = total_sum[width - 1:width]
@@ -90,8 +90,10 @@
     for at in range(0, inner, wide):
         part = spread[:, pl.ds(at, wide)]
         weighted = (dot(weight, part) * act[0, :, pl.ds(at, wide)].astype(F32)).astype(BF16)
-        state[0, :, pl.ds(at, wide)] = dot(keys_t, weighted).astype(BF16)
-        factor[0, :, pl.ds(at, wide)] = dot(gone, part)
+        state[0, 0:states, pl.ds(at, wide)] = dot(keys_t, weighted).astype(BF16)
+        fade = dot(gone, part).astype(BF16)
+        state[0, states:, pl.ds(at, wide)] = fade
+        factor[0, :, pl.ds(at, wide)] = fade
 
 
 def intra_kernel(inner, heads, act, sizes, sums, sums_t, marks, row_marks, skip, spread, out, scores, stepped):
@@ -135,15 +137,26 @@
     lax.fori_loop(0, inner // LANES, group, 0, unroll=2)
 
 
-def post_kernel(inner, part_mixed, act, state, sums, marks, gate, gain, spread, mixed, gated, kept):
+def entered_part(at, later_core, before, partner, other, place):
+    states = before.shape[0]
+    chip = before[:, place]
+    core = jnp.full(chip.shape, at[0], jnp.int32)
+    chip = jnp.where(core == pl.program_id(0), chip.astype(F32), partner[:, place].astype(F32))
+    through = other[0, states:states + 1, place].astype(F32) * chip + other[0, 0:states, place].astype(F32)
+    return jnp.where(core == later_core, through, chip).astype(BF16)
+
+
+def post_kernel(inner, at, part_mixed, act, before, partner, other, sums, marks, gate, gain, spread, mixed, gated, entering, kept):
     states = (act.shape[2] - inner) // 2
     queries = act[0, :, inner + states:]
     enter = halves(marks[0][:, 3:4] * jnp.exp(sums[0]))
     wide = 256
     square = None
-    for at in range(0, inner, wide):
-        place = pl.ds(at, wide)
-        whole = part_mixed[0, :, place].astype(F32) + dot(enter, spread[:, place]) * dot(queries, state[0, :, place])
+    for start in range(0, inner, wide):
+        place = pl.ds(start, wide)
+        state = entered_part(at, 1, before, partner, other, place)
+        entering[0, :, place] = state
+        whole = part_mixed[0, :, place].astype(F32) + dot(enter, spread[:, place]) * dot(queries, state)
         g = gate[0, :, place].astype(F32)
         w = whole * (g * sigmoid(g))
         mixed[0, :, place] = whole.astype(BF16)
@@ -156,7 +169,7 @@
 
 
 def gate_back_kernel(
-    inner, grad, mixed, gate, gain, act, state, sums, marks, spread,
+    inner, grad, grad_low, factor, mixed, gate, gain, act, state, sums, marks, spread,
     d_mixed, d_gate, d_state, d_queries, d_sums, row_grads, kept,
 ):
     states = (act.shape[2] - inner) // 2
@@ -200,7 +213,7 @@
         part = spread[:, place]
         st = state[0, :, place]
         e = (dm * dot(enter, part)).astype(BF16)
-        d_state[0, :, place] = dot(queries_t, e).astype(BF16)
+        d_state[0, 0:states, place] = dot(queries_t, e).astype(BF16)
         more_q = dot_nt(e, st)
         dq = more_q if dq is None else dq + more_q
         through = (dm * dot(queries, st)).astype(BF16)
@@ -208,6 +221,8 @@
         grad_enter = more_e if grad_enter is None else grad_enter + more_e
     d_queries[0] = dq
     d_sums[0] = grad_enter * entered
+    d_gate[0, :, inner:] = grad_low[0]
+    d_state[0, states:, :] = factor[0]
 
 
 def intra_back_kernel(
@@ -284,11 +299,11 @@
 
 
 def conv_back_kernel(
-    inner, d_stepped, d_mixed, act, mixed_in, edge, marks, taps, raw, rates, skip, sizes, sums, spread,
-    d_pair, d_total, d_state, state,
-    d_mixed_in, d_edge, d_raw, tap_grads, head_grads, padded, shifted,
+    inner, here, d_stepped, d_mixed, act, mixed_in, edge, marks, taps, rates, skip, sizes, sums, spread,
+    d_pair, d_total, before, partner, other, state,
+    d_mixed_in, d_edge, tap_grads, head_grads, padded, shifted,
 ):
-    width, channels = mixed_in.shape[1:]
+    width, channels = mixed_in.shape[1], padded.shape[1]
     states = (channels - inner) // 2
     wide = 256
 
@@ -297,8 +312,8 @@
         tap_grads[...] = jnp.zeros_like(tap_grads)
         head_grads[...] = jnp.zeros_like(head_grads)
 
-    padded[0:EDGE, :] = edge[0].astype(F32)
-    padded[EDGE:EDGE + width, :] = mixed_in[0].astype(F32)
+    padded[0:EDGE, :] = edge[0, :, 0:channels].astype(F32)
+    padded[EDGE:EDGE + width, :] = mixed_in[0, :, 0:channels].astype(F32)
     marks_now = marks[0]
     masks = [marks_now[:, back:back + 1] for back in range(3)]
     total_sum = sums[0]
@@ -340,7 +355,7 @@
         place = pl.ds(at, wide)
         values = act[0, :, place].astype(F32)
         part = spread[:, place]
-        ds = d_state[0, :, place]
+        ds = entered_part(here, 0, before, partner, other, place)
         wide_weight = dot(weight_pair, part)
         d_weighted = dot(keys, ds)
         dx = d_stepped[0, :, place].astype(F32)
@@ -364,8 +379,8 @@
     order = lax.broadcasted_iota(jnp.int32, (width, width), 0) <= lax.broadcasted_iota(jnp.int32, (width, width), 1)
     d_rate = dot_exact(jnp.where(order, 1.0, 0.0).astype(F32), d_sum)
     d_size = d_size + d_rate * rates[1:2, :]
-    d_step = d_size * sigmoid(raw[0] + rates[0:1, :])
-    d_raw[0] = d_step.astype(BF16)
+    d_step = d_size * sigmoid(mixed_in[0, :, channels:].astype(F32) + rates[0:1, :])
+    d_mixed_in[0, :, channels:] = d_step.astype(BF16)
     head_grads[0:1, :] += jnp.sum(d_step, axis=0, keepdims=True)
     head_grads[1:2, :] += jnp.sum(d_rate * size * rates[1:2, :], axis=0, keepdims=True)
 
@@ -374,7 +389,14 @@
     return v.astype(BF16)
 
 
-def call(kernel, batch, ins, outs, scratch, name):
+def without(kernel, first, count):
+    def run(*refs):
+        return kernel(*refs[:first], *refs[first + count:])
+
+    return run
+
+
+def call(kernel, batch, ins, outs, scratch, name, micros, at=None, after=()):
     def spec(shape, whole):
         block = tuple(shape) if whole else (1,) + tuple(shape[1:])
         if whole:
@@ -382,45 +404,91 @@
         return pl.BlockSpec(block, lambda b: (b,) + (0,) * (len(block) - 1))
 
     arrays = [a for a, _ in ins]
+    in_specs = [spec(a.shape, whole) for a, whole in ins]
+    if at is not None:
+        arrays, in_specs = [at] + arrays, [pl.BlockSpec(memory_space=pltpu.SMEM)] + in_specs
     return pl.pallas_call(
-        kernel,
+        without(kernel, len(arrays), len(after)),
         grid=(batch,),
-        in_specs=[spec(a.shape, whole) for a, whole in ins],
+        in_specs=in_specs + [pl.BlockSpec(memory_space=pl.ANY)] * len(after),
         out_specs=[spec(shape, whole) for shape, _, whole in outs],
         out_shape=[jax.ShapeDtypeStruct(shape, kind) for shape, kind, _ in outs],
         scratch_shapes=[pltpu.VMEM(shape, kind) for shape, kind in scratch],
         compiler_params=pltpu.CompilerParams(vmem_limit_bytes=VMEM),
+        cost_estimate=cost(micros),
         name=name,
-    )(*arrays)
-
-
-def exchange(state, factor, later_is_odd):
+    )(*arrays, *after)
+
+
+def cost(micros):
+    return pl.CostEstimate(flops=int(micros * 1.1e9), bytes_accessed=int(micros * 1e6), transcendentals=0)
+
+
+def whole_call(kernel, arrays, outs, micros, name, at=None, after=(), scratch=()):
+    spec = pl.BlockSpec(memory_space=pltpu.VMEM)
+    arrays, in_specs = list(arrays), [spec] * len(arrays)
+    if at is not None:
+        arrays, in_specs = [at] + arrays, [pl.BlockSpec(memory_space=pltpu.SMEM)] + in_specs
+    return pl.pallas_call(
+        without(kernel, len(arrays), len(after)),
+        in_specs=in_specs + [pl.BlockSpec(memory_space=pl.ANY)] * len(after),
+        out_specs=[spec] * len(outs),
+        out_shape=[jax.ShapeDtypeStruct(shape, kind) for shape, kind in outs],
+        scratch_shapes=[pltpu.VMEM(shape, kind) for shape, kind in scratch],
+        compiler_params=pltpu.CompilerParams(vmem_limit_bytes=VMEM),
+        cost_estimate=cost(micros),
+        name=name,
+    )(*arrays, *after)
+
+
+def swap(x, axis, bits):
+    return lax.ppermute(x, axis, [(i, i ^ bits) for i in range(lax.axis_size(axis))])
+
+
+def join_kernel(later_core, at, own, other, joined):
+    core = at[0]
+    states = own.shape[1] - FACTOR_ROWS
+    for start in range(0, own.shape[2], 512):
+        place = pl.ds(start, 512)
+        mine = own[core, :, place].astype(F32)
+        theirs = other[core, :, place].astype(F32)
+        later = jnp.full(mine.shape, core, jnp.int32) == later_core
+        second = jnp.where(later, mine, theirs)
+        first = jnp.where(later, theirs, mine)
+        gain = second[states:states + 1]
+        joined[0:states, place] = (gain * first[0:states] + second[0:states]).astype(BF16)
+        joined[states:, place] = (gain * first[states:]).astype(BF16)
+
+
+def enter_kernel(count, *refs):
+    out = refs[count]
+    states = out.shape[0]
+    for start in range(0, out.shape[1], 512):
+        place = pl.ds(start, 512)
+        before = refs[0][0:states, place].astype(F32)
+        for got in refs[1:count]:
+            before = got[states:states + 1, place].astype(F32) * before + got[0:states, place].astype(F32)
+        out[:, place] = before.astype(BF16)
+
+
+def exchange(own, at, later_core):
     peers = lax.axis_size("seq")
-    odd = lax.axis_index("seq") % 2
-    later = odd == 1 if later_is_odd else odd == 0
-    states = state.shape[1]
-    own = jnp.concatenate([state, factor.astype(BF16)], axis=1)
-    other = lax.ppermute(own, "seq", [(i, i ^ 1) for i in range(peers)])
-    mine = lax.dynamic_index_in_dim(own, odd, 0, keepdims=False).astype(F32)
-    theirs = lax.dynamic_index_in_dim(other, odd, 0, keepdims=False).astype(F32)
-    second = jnp.where(later, mine, theirs)
-    first = jnp.where(later, theirs, mine)
-    gain = second[states:states + 1]
-    joined = jnp.concatenate(
-        [gain * first[:states] + second[:states], gain * first[states:]], axis=0
-    ).astype(BF16)
-    before = jnp.zeros(joined[:states].shape, F32)
+    other = swap(own, "seq", 1)
+    joined = whole_call(functools.partial(join_kernel, later_core), [own, other], [(own.shape[1:], BF16)], 2.0, "join_states", at)[0]
+    got = []
     for distance in range(peers // 2 - 1, 0, -1):
-        step = 2 * distance if later_is_odd else -2 * distance
+        step = 2 * distance if later_core == 1 else -2 * distance
         route = [(i, i + step) for i in range(peers) if 0 <= i + step < peers]
-        got = lax.ppermute(joined, "seq", route).astype(F32)
-        before = got[states:states + 1] * before + got[:states]
-    before = before.astype(BF16)
-    partner = lax.ppermute(before, "seq", [(i, i ^ 1) for i in range(peers)])
-    entering = jnp.where(odd == 0, jnp.stack([before, partner]), jnp.stack([partner, before])).astype(F32)
-    gain = other[:, states:states + 1].astype(F32)
-    through = gain * entering + other[:, :states].astype(F32)
-    return jnp.where(later, through, entering).astype(BF16)
+        got.append(lax.ppermute(joined, "seq", route))
+    return got, other
+
+
+def entered(got, after):
+    shape = (got[0].shape[0] - FACTOR_ROWS, got[0].shape[1])
+    before = whole_call(
+        functools.partial(enter_kernel, len(got)), got, [(shape, BF16)], 2.0, "enter_states", after=after
+    )[0]
+    return before, swap(before, "seq", 1)
 
 
 def gathered(block):
@@ -430,9 +498,328 @@
     return lax.all_gather(share, ("fsdp", "seq"), axis=0, tiled=True)
 
 
+def take_in_kernel(columns, block, steps, out):
+    first, last, with_steps = columns
+    wide = last - first
+    out[:, 0:wide] = block[0, :, first:last]
+    if with_steps:
+        heads = steps.shape[2]
+        out[:, wide:] = jnp.zeros((out.shape[0], LANES), BF16)
+        out[:, wide:wide + heads] = steps[0]
+
+
+def take_share(weight, steps, layer, columns, at, share, parts, after):
+    first, last, with_steps = columns
+    wide = last - first + (LANES if with_steps else 0)
+
+    def rows(i, where):
+        return (layer, where[1] * 2 + where[0] if parts > 2 else where[0], 0)
+
+    arrays = [weight] if steps is None else [weight, steps]
+    specs = [pl.BlockSpec((1, share, a.shape[2]), rows) for a in arrays]
+    kernel = functools.partial(take_in_kernel, columns)
+    if steps is None:
+        kernel = lambda block, out: take_in_kernel(columns, block, None, out)
+    inner_kernel = without(kernel, len(arrays), len(after))
+    return pl.pallas_call(
+        lambda where, *refs: inner_kernel(*refs),
+        grid_spec=pltpu.PrefetchScalarGridSpec(
+            num_scalar_prefetch=1,
+            grid=(1,),
+            in_specs=specs + [pl.BlockSpec(memory_space=pl.ANY)] * len(after),
+            out_specs=pl.BlockSpec((share, wide), lambda i, where: (0, 0)),
+        ),
+        out_shape=jax.ShapeDtypeStruct((share, wide), BF16),
+        compiler_params=pltpu.CompilerParams(vmem_limit_bytes=VMEM),
+        cost_estimate=cost(1.0),
+        name="take_share",
+    )(at, *arrays, *after)
+
+
+def place_rows_kernel(starts, columns, many, at, *refs):
+    weight, steps = refs[0], refs[1] if many == 2 else None
+    sources, out = refs[many:-1], refs[-1]
+    core, chip, group = at[0], at[1], at[2]
+    rows = weight.shape[1]
+    own = pl.ds(pl.multiple_of(group * rows, rows), rows)
+    first, last, with_steps = columns
+    wide = last - first
+    out[own, 0:wide] = weight[0, :, first:last]
+    if with_steps:
+        out[own, wide:] = jnp.concatenate([steps[0], jnp.zeros((rows, LANES - steps.shape[2]), BF16)], axis=1)
+    for source, index, rows, place in starts:
+        start = pl.multiple_of(place(core, chip, group), rows)
+        out[pl.ds(start, rows), :] = sources[source][index]
+
+
+def placed_rows(at, weight, steps, layer, columns, sources, starts, groups, micros):
+    whole = pl.BlockSpec(memory_space=pltpu.VMEM)
+    own = [weight] if steps is None else [weight, steps]
+    first, last, with_steps = columns
+    shape = (weight.shape[1] * groups, last - first + (LANES if with_steps else 0))
+    return pl.pallas_call(
+        functools.partial(place_rows_kernel, starts, columns, len(own)),
+        grid=(1,),
+        in_specs=[pl.BlockSpec(memory_space=pltpu.SMEM)]
+        + [pl.BlockSpec((1,) + a.shape[1:], lambda i: (layer, 0, 0)) for a in own] + [whole] * len(sources),
+        out_specs=whole,
+        out_shape=jax.ShapeDtypeStruct(shape, BF16),
+        compiler_params=pltpu.CompilerParams(vmem_limit_bytes=VMEM),
+        cost_estimate=cost(micros),
+        name="place_rows",
+    )(at, *own, *sources)
+
+
+def fetched_by_all(weight, steps, layer, columns, at, groups, chips, after):
+    rows = weight.shape[1]
+    share = rows // (2 * chips)
+    mine = take_share(weight, steps, layer, columns, at, share, 2 * chips, after)
+    from_z = jnp.stack([swap(mine, "fsdp", e) for e in range(1, groups)])
+    sources = [from_z] + [swap(from_z, "seq", 2 * d) for d in range(1, chips)]
+    sources.append(swap(jnp.stack(sources), "seq", 1))
+
+    def place_of(d, e, other):
+        return lambda core, chip, group: (group ^ e) * rows + (chip ^ d) * (2 * share) + (core ^ other) * share
+
+    starts = []
+    for d in range(chips):
+        for e in range(1, groups):
+            starts.append((d, (e - 1,), share, place_of(d, e, 0)))
+            starts.append((chips, (d, e - 1), share, place_of(d, e, 1)))
+    return placed_rows(at, weight, steps, layer, columns, sources, starts, groups, 4.0), from_z
+
+
+def fetched_along_z(weight, layer, at, groups, after):
+    rows = weight.shape[1]
+    share = rows // 2
+    columns = (0, weight.shape[2], False)
+    mine = take_share(weight, None, layer, columns, at, share, 2, after)
+    from_z = jnp.stack([swap(mine, "fsdp", e) for e in range(1, groups)])
+    sources = [from_z, swap(from_z, "seq", 1)]
+
+    def place_of(e, other):
+        return lambda core, chip, group: (group ^ e) * rows + (core ^ other) * share
+
+    starts = [(other, (e - 1,), share, place_of(e, other)) for e in range(1, groups) for other in range(2)]
+    return placed_rows(at, weight, None, layer, columns, sources, starts, groups, 3.0), from_z
+
+
 def reduced(grad):
     share = lax.psum_scatter(grad, ("fsdp", "seq"), scatter_dimension=0, tiled=True)
     return lax.all_gather(share, "seq", axis=0, tiled=True).astype(F32)
+
+
+def turn_kernel(groups, chips, at, gated, low, own, send, turned):
+    core, chip, group = at[0], at[1], at[2]
+    base = 0
+    for x in (gated, low):
+        if x is None:
+            continue
+        total = x.shape[1]
+        share = total // (2 * groups * chips)
+        for start in range(0, total, 256):
+            turned[start:start + 256, :] = x[:, start:start + 256].T
+        for other, out in ((0, own), (1, send)):
+            for d in range(chips):
+                for e in range(groups):
+                    start = (group ^ e) * (total // groups) + (chip ^ d) * (2 * share) + (core ^ other) * share
+                    to = base + (d * groups + e) * share
+                    out[to:to + share, :] = turned[pl.ds(pl.multiple_of(start, share), share), :]
+        base += total // 2
+
+
+def turned_halves(gated, low, at, groups, chips):
+    rows = low.shape[0]
+    if gated is None:
+        def kernel(where, low_ref, *refs):
+            turn_kernel(groups, chips, where, None, low_ref, *refs)
+
+        return whole_call(kernel, [low], [((low.shape[1] // 2, rows), BF16)] * 2, 2.0, "turn", at, scratch=[(low.shape[::-1], BF16)])
+    half = ((gated.shape[1] + low.shape[1]) // 2, rows)
+    return whole_call(
+        functools.partial(turn_kernel, groups, chips), [gated, low], [(half, BF16)] * 2, 4.0, "turn", at,
+        scratch=[((gated.shape[1], rows), BF16)],
+    )
+
+
+def first_grads_kernel(groups, chips, inner, own, other, grad, grad_other, *outs):
+    wide = grad.shape[1] - inner
+    total_big = inner // 2
+    big = total_big // (groups * chips)
+    small = (own.shape[0] - total_big) // (groups * chips)
+
+    def put(total, share, start, at):
+        for d in range(chips):
+            for e in range(groups):
+                block = (d * groups + e) * share
+                outs[d][e, start:start + share, pl.ds(at, 512)] = total[block:block + share]
+
+    for at in range(0, wide, 512):
+        place = pl.ds(inner + at, 512)
+        total = dot(own[0:total_big, :], grad[:, place]) + dot(other[0:total_big, :], grad_other[:, place])
+        put(total.astype(BF16), big, 0, at)
+    for at in range(0, inner, 512):
+        place = pl.ds(at, 512)
+        total = dot(own[total_big:, :], grad[:, place]) + dot(other[total_big:, :], grad_other[:, place])
+        put(total.astype(BF16), small, big + at // wide * small, at % wide)
+
+
+def wide_grads_kernel(low, gated, grad, out):
+    turned = jnp.where(pl.program_id(1) * jnp.ones(low.shape, jnp.int32) < 2, low[...], gated[...])
+    out[...] = dot_tn(turned, grad[...]).astype(BF16)
+
+
+def wide_grads(low, gated, both, groups):
+    rows, model = low.shape
+    inner = gated.shape[1]
+    cut = model // groups
+    halves_of = inner // model
+    return pl.pallas_call(
+        wide_grads_kernel,
+        grid=(groups, 2 * halves_of),
+        in_specs=[
+            pl.BlockSpec((rows, cut), lambda z, j: (0, z)),
+            pl.BlockSpec((rows, cut), lambda z, j: (0, halves_of * z + jnp.maximum(j - halves_of, 0))),
+            pl.BlockSpec((rows, model), lambda z, j: (0, jnp.minimum(j, halves_of))),
+        ],
+        out_specs=pl.BlockSpec((cut, model), lambda z, j: (z, j)),
+        out_shape=jax.ShapeDtypeStruct((model, 2 * inner), BF16),
+        compiler_params=pltpu.CompilerParams(vmem_limit_bytes=VMEM),
+        cost_estimate=cost(10.0),
+        name="wide_grads",
+    )(low, gated, both)
+
+
+def second_grads_kernel(groups, chips, channels, heads, here, own, other, grad, grad_other, extra, extra_other, *outs):
+    rows = extra.shape[0] // 2
+    base = own.shape[0] - rows
+    share = rows // (groups * chips)
+    core, chip, group = here[0], here[1], here[2]
+    lane = lax.broadcasted_iota(jnp.int32, (share, LANES), 1)
+    total_wide = channels + LANES
+    edges = list(range(0, channels, 512)) + [channels, total_wide]
+    for at, end in zip(edges[:-1], edges[1:]):
+        place = pl.ds(at, end - at)
+        total = dot(own[base:, :], grad[:, place]) + dot(other[base:, :], grad_other[:, place])
+        for d in range(chips):
+            for e in range(groups):
+                block = (d * groups + e) * share
+                part = total[block:block + share]
+                if at == channels:
+                    start = (group ^ e) * (2 * rows // groups) + (chip ^ d) * (2 * share) + core * share
+                    here_rows = pl.ds(pl.multiple_of(start, share), share)
+                    part = jnp.where(lane < heads, part, extra[here_rows, :] + extra_other[here_rows, :])
+                outs[d][e, :, place] = part.astype(BF16)
+
+
+def add_kernel(count, *refs):
+    ins, outs = refs[:count], refs[count:]
+    for i, out in enumerate(outs):
+        total = ins[0][i].astype(F32)
+        for more in ins[1:]:
+            total = total + more[i].astype(F32)
+        out[...] = total.astype(out.dtype)
+
+
+def add_last_kernel(first, second, *refs):
+    out = refs[-1]
+    rows, wide = refs[0].shape[0] if first else 0, out.shape[1]
+
+    def total_of(group, place):
+        total = group[0][:, place].astype(F32)
+        for more in group[1:]:
+            total = total + more[:, place].astype(F32)
+        return total.astype(BF16)
+
+    if first:
+        out[0:rows, :] = total_of(refs[:first], pl.ds(0, wide))
+    seconds = refs[first:first + second]
+    share, columns = seconds[0].shape
+    for i, at in enumerate(range(0, columns, wide)):
+        width = min(wide, columns - at)
+        out[rows + i * share:rows + (i + 1) * share, 0:width] = total_of(seconds, pl.ds(at, width))
+        if width < wide:
+            out[rows + i * share:rows + (i + 1) * share, width:] = jnp.zeros((share, wide - width), BF16)
+
+
+def first_sums(blocks, axis, after=()):
+    parts, rows, columns = blocks[0].shape
+    unit = 2 if axis == "seq" else 1
+    got = [blocks[0]] + [swap(blocks[i], axis, unit * i) for i in range(1, len(blocks))]
+    return whole_call(
+        functools.partial(add_kernel, len(got)), got, [((rows, columns), BF16)] * parts, 2.5, "add_first", after=after
+    )
+
+
+def second_parts(shares, axis):
+    unit = 2 if axis == "seq" else 1
+    return [shares[0]] + [swap(shares[i], axis, unit * i) for i in range(1, len(shares))]
+
+
+def last_sums(first, second, wide):
+    rows = first[0].shape[0] if first else 0
+    share, columns = second[0].shape
+    total = rows + -(-columns // wide) * share
+    return whole_call(
+        functools.partial(add_last_kernel, len(first), len(second)), first + second, [((total, wide), BF16)], 2.0, "add_last"
+    )[0]
+
+
+def place_kernel(chips, inner, joined, at, *refs):
+    mine, other = refs[:chips], refs[chips]
+    in_out, extra_out, out_out = refs[-3:]
+    core, chip = at[0], at[1]
+    model = other.shape[2]
+    big = out_out.shape[1] // (2 * chips)
+    share = in_out.shape[1] // (2 * chips)
+    channels = in_out.shape[2] - inner
+    if joined:
+        scattered = refs[chips + 1]
+        in_out[0, :, 0:inner] = scattered[:, 0:inner].astype(F32)
+        rows = in_out.shape[1]
+        for i in range(inner // model):
+            out_out[0, i * rows:(i + 1) * rows, :] = scattered[:, inner + i * model:inner + (i + 1) * model].astype(F32)
+    for d in range(chips):
+        for is_other, part in ((0, mine[d]), (1, other.at[d])):
+            start = (chip ^ d) * (2 * share) + (core ^ is_other) * share
+            rows = pl.ds(pl.multiple_of(start, share), share)
+            at_row = 0
+            if not joined:
+                big_start = (chip ^ d) * (2 * big) + (core ^ is_other) * big
+                out_out[0, pl.ds(pl.multiple_of(big_start, big), big), :] = part[0:big, :].astype(F32)
+                at_row = big
+                for i in range(inner // model):
+                    in_out[0, rows, i * model:(i + 1) * model] = part[at_row:at_row + share, :].astype(F32)
+                    at_row += share
+            for start_column in range(0, channels, model):
+                wide = min(model, channels - start_column)
+                to = pl.ds(inner + start_column, wide)
+                in_out[0, rows, to] = part[at_row:at_row + share, 0:wide].astype(F32)
+                if start_column + model >= channels:
+                    extra_out[0, rows, :] = part[at_row:at_row + share, wide:wide + LANES].astype(F32)
+                at_row += share
+
+
+def placed_grads(at, share, scattered, before, layer, layers, shapes, chips, inner):
+    mine = [share] + [swap(share, "seq", 2 * d) for d in range(1, chips)]
+    pieces = mine + [swap(jnp.stack(mine), "seq", 1)]
+    joined = scattered is not None
+    pieces += [scattered] if joined else []
+    whole = pl.BlockSpec(memory_space=pltpu.VMEM)
+    anywhere = pl.BlockSpec(memory_space=pl.ANY)
+    before = [] if before is None else list(before)
+    outs = [jax.ShapeDtypeStruct((layers,) + shape, F32) for shape in shapes]
+    return pl.pallas_call(
+        functools.partial(place_kernel, chips, inner, joined),
+        grid=(1,),
+        in_specs=[pl.BlockSpec(memory_space=pltpu.SMEM)] + [whole] * len(pieces) + [anywhere] * len(before),
+        out_specs=[pl.BlockSpec((1,) + shape, lambda i: (layer, 0, 0)) for shape in shapes],
+        out_shape=outs,
+        input_output_aliases={1 + len(pieces) + i: i for i in range(len(before))},
+        compiler_params=pltpu.CompilerParams(vmem_limit_bytes=VMEM),
+        cost_estimate=cost(6.0),
+        name="place_grads",
+    )(at, *pieces, *before)
 
 
 def norm_scale_of(stream):
@@ -454,10 +841,19 @@
     channels = in_weight.shape[2] - inner
     states = (channels - inner) // 2
     span = inner // heads
-
-    small = [norm_gain, conv_weight.reshape(layers, -1), conv_bias, dt_bias, a_log, d_skip, gate_gain, dt_weight.reshape(layers, -1)]
+    chips = peers // 2
+    direct = model % (32 * groups * peers) == 0 and chips == 4 and groups == 4
+    seq_at = lax.axis_index("seq")
+    here = jnp.stack([seq_at % 2, seq_at // 2, lax.axis_index("fsdp")]).astype(jnp.int32)
+
+    small = [norm_gain, conv_weight.reshape(layers, -1), conv_bias, dt_bias, a_log, d_skip, gate_gain]
     sizes = [a.shape[1] for a in small]
-    packed = lax.all_gather(jnp.concatenate(small, axis=1), "fsdp", axis=0)
+    own = jnp.concatenate(small, axis=1)
+    if direct:
+        by_partner = jnp.stack([own] + [swap(own, "fsdp", e) for e in range(1, groups)])
+        packed = jnp.stack([lax.dynamic_index_in_dim(by_partner, here[2] ^ z, 0, keepdims=False) for z in range(groups)])
+    else:
+        packed = lax.all_gather(own, "fsdp", axis=0)
     pieces, at = [], 0
     for size in sizes:
         pieces.append(packed[:, :, at:at + size])
@@ -478,11 +874,28 @@
     rates_all = jnp.pad(rates_all, ((0, 0), (0, 6), (0, 0)))
     skip_all = jnp.broadcast_to(jnp.repeat(joined(pieces[5]).astype(F32), span, axis=1)[:, None], (layers, 8, inner))
     gain_all = jnp.broadcast_to(joined(pieces[6]).astype(F32)[:, None], (layers, 8, inner))
-    dt_all = jnp.moveaxis(pieces[7].reshape(groups, layers, -1, heads), 0, 1).reshape(layers, model, heads)
-    dt_all = jnp.pad(dt_all, ((0, 0), (0, 0), (0, LANES - heads)))
-
-    in_all = [gathered(in_weight[layer]) for layer in range(layers)]
-    out_all = [gathered(out_weight[layer]) for layer in range(layers)]
+
+    gate_columns, mix_columns, all_columns = (0, inner, False), (inner, inner + channels, True), (0, inner + channels, True)
+    gate_all, mix_all, out_all = [], [], []
+    for layer in range(layers):
+        if direct and layer == 0:
+            mixes, _ = fetched_by_all(in_weight, dt_weight, layer, mix_columns, here, groups, chips, ())
+            gates, from_z = fetched_by_all(in_weight, None, layer, gate_columns, here, groups, chips, ())
+            outs, _ = fetched_along_z(out_weight, layer, here, groups, (from_z,))
+        elif direct:
+            share = take_share(in_weight, dt_weight, layer, all_columns, here, model // (groups * peers), peers, ())
+            whole = lax.all_gather(share, ("fsdp", "seq"), axis=0, tiled=True)
+            gates, mixes = whole[:, :inner], whole[:, inner:]
+            share = take_share(out_weight, None, layer, (0, model, False), here, inner // (groups * peers), peers, ())
+            outs = lax.all_gather(share, ("fsdp", "seq"), axis=0, tiled=True)
+        else:
+            steps = jnp.pad(dt_weight[layer], ((0, 0), (0, LANES - heads)))
+            whole = gathered(jnp.concatenate([in_weight[layer], steps], axis=1))
+            gates, mixes = whole[:, :inner], whole[:, inner:]
+            outs = gathered(out_weight[layer])
+        gate_all.append(gates)
+        mix_all.append(mixes)
+        out_all.append(outs)
 
     numbers = (segments + 1).astype(F32)
     before = lax.ppermute(numbers[:, width - EDGE:], "seq", [(i, i + 1) for i in range(peers - 1)])
@@ -500,58 +913,83 @@
     for layer in range(layers):
         norm_scale = norm_scale_of(stream)
         low = (stream * norm_scale * norm_all[layer]).astype(BF16).reshape(rows, model)
-        w_in, w_out = in_all[layer], out_all[layer]
-        mixed_in = dot(low, w_in[:, inner:]).astype(BF16).reshape(batch, width, channels)
-        raw = dot(low, dt_all[layer]).reshape(batch, width, LANES)
+        w_gate, w_mix, w_out = gate_all[layer], mix_all[layer], out_all[layer]
+        mixed_in = dot(low, w_mix).astype(BF16).reshape(batch, width, channels + LANES)
         edge = lax.ppermute(mixed_in[:, width - EDGE:], "seq", [(i, i + 1) for i in range(peers - 1)])
-        gate = dot(low, w_in[:, :inner]).astype(BF16).reshape(batch, width, inner)
+        gate = dot(low, w_gate).astype(BF16).reshape(batch, width, inner)
         taps, rates, skip, gain = taps_all[layer], rates_all[layer], skip_all[layer], gain_all[layer]
         act, size, sums, sums_t, state, factor = call(
             functools.partial(conv_kernel, inner), batch,
-            [(mixed_in, 0), (edge, 0), (marks, 0), (taps, 1), (raw, 0), (rates, 1), (spread, 1)],
+            [(mixed_in, 0), (edge, 0), (marks, 0), (taps, 1), (rates, 1), (spread, 1)],
             [
                 ((batch, width, channels), BF16, 0), ((batch, width, LANES), F32, 0), ((batch, width, LANES), F32, 0),
-                ((batch, heads, width), F32, 0), ((batch, states, inner), BF16, 0), ((batch, FACTOR_ROWS, inner), F32, 0),
+                ((batch, heads, width), F32, 0), ((batch, states + FACTOR_ROWS, inner), BF16, 0),
+                ((batch, FACTOR_ROWS, inner), BF16, 0),
             ],
-            [((EDGE + width, channels), F32)], "conv_states",
+            [((EDGE + width, channels), F32)], "conv_states", 8.0,
         )
-        entering = exchange(state, factor, True)
+        got, other = exchange(state, here, 1)
         (part,) = call(
             functools.partial(intra_kernel, inner, heads), batch,
             [(act, 0), (size, 0), (sums, 0), (sums_t, 0), (marks, 0), (row_marks, 0), (skip, 1), (spread, 1)],
             [((batch, width, inner), F32, 0)],
-            [((width, width), F32), ((width, inner), BF16)], "mix_within",
+            [((width, width), F32), ((width, inner), BF16)], "mix_within", 12.0,
         )
-        mixed, gated = call(
+        before, partner = entered(got, (part,))
+        mixed, gated, entering = call(
             functools.partial(post_kernel, inner), batch,
-            [(part, 0), (act, 0), (entering, 0), (sums, 0), (marks, 0), (gate, 0), (gain, 1), (spread, 1)],
-            [((batch, width, inner), BF16, 0), ((batch, width, inner), BF16, 0)],
-            [((width, inner), F32)], "mix_gate",
+            [
+                (part, 0), (act, 0), (before, 1), (partner, 1), (other, 0), (sums, 0), (marks, 0), (gate, 0), (gain, 1), (spread, 1),
+            ],
+            [((batch, width, inner), BF16, 0), ((batch, width, inner), BF16, 0), ((batch, states, inner), BF16, 0)],
+            [((width, inner), F32)], "mix_gate", 6.0, here,
         )
         gated = gated.reshape(rows, inner)
-        kept.append((stream, norm_scale, low, mixed_in, raw, edge, gate, act, size, sums, sums_t, factor, entering, mixed, gated))
+        turned = None
+        if direct:
+            mine, send = turned_halves(gated if layer == 0 else None, low, here, groups, chips)
+            turned = (mine, swap(send, "seq", 1))
+        kept.append((turned, stream, norm_scale, low, mixed_in, edge, gate, act, size, sums, sums_t, factor, entering, mixed, gated))
         stream = stream + dot(gated, w_out).reshape(batch, width, model)
 
     grad_stream = cotangent.astype(F32)
-    collected = []
+    collected, collected_grads, placed, chains = [], [], None, []
+    started = ()
     for layer in reversed(range(layers)):
-        (entry, norm_scale, low, mixed_in, raw, edge, gate, act, size, sums, sums_t, factor, entering, mixed, gated) = kept[layer]
-        w_in, w_out = in_all[layer], out_all[layer]
+        (turned, entry, norm_scale, low, mixed_in, edge, gate, act, size, sums, sums_t, factor, entering, mixed, gated) = kept[layer]
+        w_gate, w_mix, w_out = gate_all[layer], mix_all[layer], out_all[layer]
         taps, rates, skip, gain = taps_all[layer], rates_all[layer], skip_all[layer], gain_all[layer]
         grad_low = grad_stream.astype(BF16).reshape(rows, model)
         grad_gated = dot_nt(grad_low, w_out).astype(BF16).reshape(batch, width, inner)
         d_mixed, d_gate, d_state, d_queries, d_sums, row_grads = call(
             functools.partial(gate_back_kernel, inner), batch,
-            [(grad_gated, 0), (mixed, 0), (gate, 0), (gain, 1), (act, 0), (entering, 0), (sums, 0), (marks, 0), (spread, 1)],
             [
-                ((batch, width, inner), BF16, 0), ((batch, width, inner), BF16, 0), ((batch, states, inner), BF16, 0),
-                ((batch, width, states), F32, 0), ((batch, width, LANES), F32, 0), ((8, inner), F32, 1),
+                (grad_gated, 0), (grad_low.reshape(batch, width, model), 0), (factor, 0), (mixed, 0), (gate, 0), (gain, 1), (act, 0),
+                (entering, 0), (sums, 0), (marks, 0), (spread, 1),
             ],
-            [((width, inner), F32)], "gate_back",
+            [
+                ((batch, width, inner), BF16, 0), ((batch, width, inner + model), BF16, 0),
+                ((batch, states + FACTOR_ROWS, inner), BF16, 0), ((batch, width, states), F32, 0), ((batch, width, LANES), F32, 0), ((8, inner), F32, 1),
+            ],
+            [((width, inner), F32)], "gate_back", 11.0, after=started,
         )
-        leaving = exchange(d_state, factor, False)
-        out_grad = dot_tn(gated, grad_low).astype(BF16)
-        out_share = reduced(out_grad)
+        got, other = exchange(d_state, here, 0)
+        both = d_gate.reshape(rows, inner + model)
+        d_gate = both[:, :inner]
+        started, arrived = (), ()
+        if direct:
+            big, small = inner // (groups * peers), model // (groups * peers)
+            mine, theirs = turned
+            both_other = swap(both, "seq", 1) if layer == 0 else None
+            if layer > 0:
+                wide = wide_grads(low, gated, both, groups)
+                share = lax.psum_scatter(wide, ("fsdp", "seq"), scatter_dimension=0, tiled=True)
+                scattered = lax.all_gather(share, "seq", axis=0, tiled=True)
+                started = (wide,)
+            else:
+                scattered = None
+        else:
+            out_share = reduced(dot_tn(gated, grad_low).astype(BF16))
         d_stepped, d_pair, d_total = call(
             functools.partial(intra_back_kernel, inner, heads), batch,
             [
@@ -561,33 +999,34 @@
             [((batch, width, inner), BF16, 0), ((batch, width, 2 * states), F32, 0), ((batch, width, LANES), F32, 0)],
             [
                 ((width, width), F32), ((width, width), F32), ((width, inner), BF16), ((LANES, width), F32), ((width, LANES), F32),
-            ], "mix_within_back",
+            ], "mix_within_back", 17.0, after=started,
         )
-        d_gate = d_gate.reshape(rows, inner)
-        d_mixed_in, d_edge, d_raw, tap_grads, head_grads = call(
+        before, partner = entered(got, (d_stepped,))
+        if direct and layer == 0:
+            first_blocks = whole_call(
+                functools.partial(first_grads_kernel, groups, chips, inner), [mine, theirs, both, both_other],
+                [((groups, big + inner // model * small, model), BF16)] * chips, 10.0, "first_grads", after=(before,),
+            )
+            arrived = tuple(first_blocks)
+            for chain in chains:
+                arrived += tuple(chain)
+        d_mixed_in, d_edge, tap_grads, head_grads = call(
             functools.partial(conv_back_kernel, inner), batch,
             [
-                (d_stepped, 0), (d_mixed, 0), (act, 0), (mixed_in, 0), (edge, 0), (marks, 0), (taps, 1), (raw, 0), (rates, 1),
-                (skip, 1), (size, 0), (sums, 0), (spread, 1), (d_pair, 0), (d_total, 0), (leaving, 0), (entering, 0),
+                (d_stepped, 0), (d_mixed, 0), (act, 0), (mixed_in, 0), (edge, 0), (marks, 0), (taps, 1), (rates, 1),
+                (skip, 1), (size, 0), (sums, 0), (spread, 1), (d_pair, 0), (d_total, 0), (before, 1), (partner, 1), (other, 0),
+                (entering, 0),
             ],
             [
-                ((batch, width, channels), BF16, 0), ((batch, EDGE, channels), F32, 0), ((batch, width, LANES), BF16, 0),
+                ((batch, width, channels + LANES), BF16, 0), ((batch, EDGE, channels), F32, 0),
                 ((8, channels), F32, 1), ((8, LANES), F32, 1),
             ],
-            [((EDGE + width, channels), F32), ((3, width + 2 * EDGE, 256), F32)], "conv_back",
+            [((EDGE + width, channels), F32), ((3, width + 2 * EDGE, 256), F32)], "conv_back", 17.0, here, arrived,
         )
         from_next = lax.ppermute(d_edge.astype(BF16), "seq", [(i + 1, i) for i in range(peers - 1)])
-        d_mixed_in = jnp.concatenate(
-            [
-                d_mixed_in[:, :width - EDGE],
-                (d_mixed_in[:, width - EDGE:].astype(F32) + from_next.astype(F32)).astype(BF16),
-            ], axis=1,
-        ).reshape(rows, channels)
-        d_raw = d_raw.reshape(rows, LANES)
-        in_grad = jnp.concatenate([dot_tn(low, d_gate).astype(BF16), dot_tn(low, d_mixed_in).astype(BF16)], axis=1)
-        in_share = reduced(in_grad)
-        dt_grad = dot_tn(low, d_raw)[:, :heads]
-        grad_rows = dot_nt(d_gate, w_in[:, :inner]) + dot_nt(d_mixed_in, w_in[:, inner:]) + dot_nt(d_raw, dt_all[layer])
+        tail = (d_mixed_in[:, width - EDGE:, :channels].astype(F32) + from_next.astype(F32)).astype(BF16)
+        grad_mixed = lax.dynamic_update_slice(d_mixed_in, tail, (0, width - EDGE, 0)).reshape(rows, channels + LANES)
+        grad_rows = dot_nt(d_gate, w_gate) + dot_nt(grad_mixed, w_mix)
         grad_rows = grad_rows.reshape(batch, width, model)
         scaled = grad_rows * norm_all[layer]
         inward = jnp.mean(scaled * entry, axis=-1, keepdims=True)
@@ -602,23 +1041,47 @@
             head_grads[1, :heads].reshape(groups, -1),
             skip_grad.reshape(groups, -1),
             row_grads[0].reshape(groups, -1),
-            dt_grad.reshape(groups, -1),
         ]
-        collected.append((in_share, out_share, jnp.concatenate(small_grads, axis=1)))
-    collected = collected[::-1]
-    small_sum = lax.psum(jnp.stack([c[2] for c in collected], axis=1), ("fsdp", "seq"))
-    small_sum = lax.dynamic_index_in_dim(small_sum, lax.axis_index("fsdp"), 0, keepdims=False)
+        small_sums = jnp.concatenate(small_grads, axis=1)
+        if direct:
+            per_row = -(-small_sums.shape[1] * groups // model)
+            extra = jnp.pad(small_sums, ((0, 0), (0, per_row * model // groups - small_sums.shape[1]))).reshape(model, per_row)
+            extra = jnp.pad(extra, ((0, 0), (heads, LANES - heads - per_row)))
+            second_blocks = whole_call(
+                functools.partial(second_grads_kernel, groups, chips, channels, heads),
+                [mine, theirs, grad_mixed, swap(grad_mixed, "seq", 1), extra, swap(extra, "seq", 1)],
+                [((groups, small, channels + LANES), BF16)] * chips, 6.0, "second_grads", here,
+            )
+            started = tuple(second_blocks)
+            second = first_sums(second_blocks, "seq")
+            first_last = second_parts(first_sums(first_blocks, "seq"), "fsdp") if layer == 0 else []
+            chains.append(second)
+            share = last_sums(first_last, second_parts(second, "fsdp"), model)
+            shapes = [(model // groups, inner + channels), (model // groups, LANES), (inner // groups, model)]
+            placed = placed_grads(here, share, scattered, placed, layer, layers, shapes, chips, inner)
+        else:
+            mixed_grad = dot_tn(low, grad_mixed)
+            in_share = reduced(jnp.concatenate([dot_tn(low, d_gate).astype(BF16), mixed_grad[:, :channels].astype(BF16)], axis=1))
+            dt_share = reduced(mixed_grad[:, channels:].astype(BF16))
+            collected_grads.append((in_share, dt_share, out_share))
+            collected.append(small_sums)
+    if direct:
+        small_sum = placed[1][:, :, heads:heads + per_row].reshape(layers, -1)
+    else:
+        placed = [jnp.stack([c[i] for c in collected_grads[::-1]]) for i in range(3)]
+        small_sum = lax.psum(jnp.stack(collected[::-1], axis=1), ("fsdp", "seq"))
+        small_sum = lax.dynamic_index_in_dim(small_sum, lax.axis_index("fsdp"), 0, keepdims=False)
     pieces, at = [], 0
     for size in sizes:
         pieces.append(small_sum[:, at:at + size])
         at += size
     return (
         stream, grad_stream, pieces[0],
-        jnp.stack([c[0] for c in collected]),
-        pieces[7].reshape(layers, -1, heads),
+        placed[0],
+        placed[1][:, :, :heads],
         pieces[1].reshape(layers, taps_len, -1),
         pieces[2], pieces[3], pieces[4], pieces[5], pieces[6],
-        jnp.stack([c[1] for c in collected]),
+        placed[2],
     )
 
 

time: 1230 us -> 802 us (0.65)
  waiting for transfers between devices: 765 us -> 286 us
  Pallas kernels: 144 us -> 231 us
  starting transfers between devices: 45.6 us -> 113 us
  other arithmetic: 65.2 us -> 21.2 us
  matrix products: 98.1 us -> 59.3 us
  blocking collectives: 16.2 us -> 0 us
    reduce_scatter x4 -> x1, waiting for transfers between devices: 289 us -> 0.01 us  [on_device(): lax.psum_scatter(wide, ('fsdp', 'seq'), scatter_dimension=0, tiled=True)]
    all_gather x8 -> x3, waiting for transfers between devices: 233 us -> 0.02 us  [the longest x1 0.02 us: on_device(): whole = lax.all_gather(share, ('fsdp', 'seq'), axis=0, tiled=True)]
    ppermute x20 -> x74, waiting for transfers between devices: 121 us -> 283 us  [the longest x62 241 us: swap(): lax.ppermute(x, axis, [(i, i ^ bits) for i in range(lax.axis_size(axis))])]
    psum x1 -> x0, waiting for transfers between devices: 120 us -> none  [on_device(): lax.psum(jnp.stack([c[2] for c in collected], axis=1), ('fsdp', 'seq'))]
    pallas_call x12 -> x41, Pallas kernels: 144 us -> 231 us  [the longest x12 153 us: call(): pl.pallas_call(without(kernel, len(arrays), len(after)), grid=(batch,), i...]
    ppermute x20 -> x74, starting transfers between devices: 33.9 us -> 105 us  [the longest x62 80.7 us: swap(): lax.ppermute(x, axis, [(i, i ^ bits) for i in range(lax.axis_size(axis))])]
    dot_general x8 -> x0, matrix products: 30.6 us -> none  [dot_tn(): return lax.dot_general(a, b, TN, preferred_element_type=F32)]
    concatenate x12 -> x0, other arithmetic: 23.2 us -> none  [the longest x2 15.6 us: on_device(): jnp.concatenate([dot_tn(low, d_gate).astype(BF16), dot_tn(low, d_mixed_in...]
  transfers between devices with their start and end apart: 38 -> 83, of which waited for: 20 -> 25; matrix products, arithmetic and copies ran while one was open for 16% -> 12% of each run, Pallas kernels for 10% -> 26%
where the time goes in v2:
time: 802 us; the launch traced here: 789 us
  waiting for transfers between devices  286 us (36%)
  Pallas kernels  231 us (29%)
  starting transfers between devices  113 us (14%)
  local copies, waits for them, and re-layouts  61.8 us (8%)
  matrix products  59.3 us (7%)
  other arithmetic  21.2 us (3%)
  between operations  16.7 us (2%)
    ppermute x62, waiting for transfers between devices, swap(): lax.ppermute(x, axis, [(i, i ^ bits) for i in range(lax.axis_size(axis))])  241 us
    pallas_call x12, Pallas kernels, call(): pl.pallas_call(without(kernel, len(arrays), len(after)), grid=(batch,), i...  153 us
    ppermute x62, starting transfers between devices, swap(): lax.ppermute(x, axis, [(i, i ^ bits) for i in range(lax.axis_size(axis))])  80.7 us
    unnamed x352, local copies, waits for them, and re-layouts  44.2 us
    ppermute x12, waiting for transfers between devices, exchange(): got.append(lax.ppermute(joined, 'seq', route))  41.5 us
    pallas_call x18, Pallas kernels, whole_call(): pl.pallas_call(without(kernel, len(arrays), len(after)), in_specs=in_spec...  35.5 us
    dot_general x6, matrix products, dot_nt(): return lax.dot_general(a, b, NT, preferred_element_type=F32)  30.7 us
    dot_general x6, matrix products, dot(): return jnp.dot(a, b, preferred_element_type=F32)  28.6 us
  transfers between devices with their start and end apart: 83, of which 25 were waited for; matrix products, arithmetic and copies ran while one was open for 12% of the time, Pallas kernels for 26%

profile of v2, /device:TPU:0, one launch (start us, length us, event | category | flops | bytes accessed | tf_op | source)
XLA Modules:
  0.0 789.5 jit_solution(5621136413769788370)
XLA Ops:
  54.7 10.3 %collective-permute-done.6.refs_3_ = bf16[3,32,2432]{2,1,0:T(8,128)(2,1)S(1)} collective-permute-done((bf16[3,32,2432]{2,1,0:T(8,128)(2,1)S(1)}, bf16[3,32,2432]{2,1,0:T(8,128)(2,1)S(1)}, u32[]{:S(2)}, u32[]{:S(2)}) %collective-permute-start.6) | collective-permute-done | bytes 466976 | tf_op jit(solution)/shard_map/ppermute | solution.py:445
  65.0 11.8 %collective-permute-done.8.refs_5_ = bf16[3,32,2432]{2,1,0:T(8,128)(2,1)S(1)} collective-permute-done((bf16[3,32,2432]{2,1,0:T(8,128)(2,1)S(1)}, bf16[3,32,2432]{2,1,0:T(8,128)(2,1)S(1)}, u32[]{:S(2)}, u32[]{:S(2)}) %collective-permute-start.8) | collective-permute-done | bytes 466976 | tf_op jit(solution)/shard_map/ppermute | solution.py:445
  103.5 11.7 %collective-permute-done.22.refs_4_ = bf16[3,32,2048]{2,1,0:T(8,128)(2,1)S(1)} collective-permute-done((bf16[3,32,2048]{2,1,0:T(8,128)(2,1)S(1)}, bf16[3,32,2048]{2,1,0:T(8,128)(2,1)S(1)}, u32[]{:S(2)}, u32[]{:S(2)}) %collective-permute-start.22) | collective-permute-done | bytes 393248 | tf_op jit(solution)/shard_map/ppermute | solution.py:445
  136.0 12.3 %collective-permute-done.26 = bf16[256,1024]{1,0:T(8,128)(2,1)} collective-permute-done((bf16[256,1024]{1,0:T(8,128)(2,1)}, bf16[256,1024]{1,0:T(8,128)(2,1)}, u32[]{:S(2)}, u32[]{:S(2)}) %collective-permute-start.26) | collective-permute-done | bytes 524320 | tf_op jit(solution)/shard_map/ppermute | solution.py:445
  148.3 39.0 %collective-permute-done.25 = bf16[256,1024]{1,0:T(8,128)(2,1)} collective-permute-done((bf16[256,1024]{1,0:T(8,128)(2,1)}, bf16[256,1024]{1,0:T(8,128)(2,1)}, u32[]{:S(2)}, u32[]{:S(2)}) %collective-permute-start.25) | collective-permute-done | bytes 524320 | tf_op jit(solution)/shard_map/ppermute | solution.py:445
  202.5 11.8 %mix_within.2.refs_3_.refs_1_ = f32[2,256,2048]{2,1,0:T(8,128)} custom-call(bf16[2,256,2304]{2,1,0:T(8,128)(2,1)S(1)} %copy-done.70, f32[2,256,128]{2,1,0:T(8,128)S(1)} %copy-done.93, f32[2,256,128]{2,1,0:T(8,128)S(1)} %copy-done.87, f32[2,32,256]{2,1,0:T(8,128)S(1)} %get-tuple-element.93.refs_3_.refs_4_, f32[2,256,128]{2,1,0:T(8,128)S(1)} %copy-done.19, ...), custom_call_target="tpu_custom_call" | custom-call | flops 13200000000 | bytes 12000000 | tf_op jit(solution)/shard_map/mix_within/pallas_call | solution.py:410
  214.3 11.1 %collective-permute-done.14.refs_1_ = bf16[144,2048]{1,0:T(8,128)(2,1)S(1)} collective-permute-done((bf16[144,2048]{1,0:T(8,128)(2,1)S(1)}, bf16[144,2048]{1,0:T(8,128)(2,1)S(1)}, u32[]{:S(2)}, u32[]{:S(2)}) %collective-permute-start.14) | collective-permute-done | bytes 589856 | tf_op jit(solution)/shard_map/ppermute | solution.py:482
  286.5 11.8 %mix_within.3.refs_3_.refs_1_ = f32[2,256,2048]{2,1,0:T(8,128)} custom-call(bf16[2,256,2304]{2,1,0:T(8,128)(2,1)S(1)} %copy-done.72, f32[2,256,128]{2,1,0:T(8,128)S(1)} %copy-done.97, f32[2,256,128]{2,1,0:T(8,128)S(1)} %copy-done.90, f32[2,32,256]{2,1,0:T(8,128)S(1)} %copy-done.115, f32[2,256,128]{2,1,0:T(8,128)S(1)} %copy-done.19, ...), custom_call_target="tpu_custom_call" | custom-call | flops 13200000000 | bytes 12000000 | tf_op jit(solution)/shard_map/mix_within/pallas_call | solution.py:410
  298.3 11.6 %collective-permute-done.31.refs_1_ = bf16[144,2048]{1,0:T(8,128)(2,1)S(1)} collective-permute-done((bf16[144,2048]{1,0:T(8,128)(2,1)S(1)}, bf16[144,2048]{1,0:T(8,128)(2,1)S(1)}, u32[]{:S(2)}, u32[]{:S(2)}) %collective-permute-start.31) | collective-permute-done | bytes 589856 | tf_op jit(solution)/shard_map/ppermute | solution.py:482
  322.8 11.7 %gate_back.2 = (bf16[2,256,2048]{2,1,0:T(8,128)(2,1)}, bf16[2,256,3072]{2,1,0:T(8,128)(2,1)}, bf16[2,144,2048]{2,1,0:T(8,128)(2,1)}, f32[2,256,128]{2,1,0:T(8,12...) custom-call(bf16[2,256,2048]{2,1,0:T(8,128)(2,1)} %bitcast.208, bf16[2,256,1024]{2,1,0:T(8,128)(2,1)S(1)} %copy-done.3, ...), custom_call_target="tpu_custom_call" | custom-call | flops 12099999744 | bytes 11000000 | tf_op jit(solution)/shard_map/gate_back/pallas_call | solution.py:410
  338.2 16.5 %wide_grads.1.refs_10_ = bf16[1024,4096]{1,0:T(8,128)(2,1)} custom-call(bf16[512,1024]{1,0:T(8,128)(2,1)S(1)} %bitcast.148, bf16[512,2048]{1,0:T(8,128)(2,1)S(1)} %bitcast.164, bf16[512,3072]{1,0:T(8,128)(2,1)} %bitcast.203), custom_call_target="tpu_custom_call" | custom-call | flops 11000000512 | bytes 10000000 | tf_op jit(solution)/shard_map/wide_grads/pallas_call | solution.py:677
  361.0 17.3 %mix_within_back.2 = (bf16[2,256,2048]{2,1,0:T(8,128)(2,1)S(1)}, f32[2,256,256]{2,1,0:T(8,128)S(1)}, f32[2,256,128]{2,1,0:T(8,128)S(1)}) custom-call(bf16[2,256,2048]{2,1,0:T(8,128)(2,1)} %get-tuple-element.106.refs_0_.refs_2_, bf16[2,256,2304]{2,1,0:T(8,128)(2,1)} %copy-done.71, f32[2,256,128]{2,1,0:T(8,128)S(1)} %copy-done.98, ...), custom_call_target="tpu_custom_call" | custom-call | flops 18699999232 | bytes 17000000 | tf_op jit(solution)/shard_map/mix_within_back/pallas_call | solution.py:410
  411.5 19.9 %conv_back.2 = (bf16[2,256,2432]{2,1,0:T(8,128)(2,1)}, f32[2,8,2304]{2,1,0:T(8,128)S(1)}, f32[8,2304]{1,0:T(8,128)S(1)}, f32[8,128]{1,0:T(8,128)S(1)}) custom-call(s32[3]{0:T(128)S(1)} %copy-done.34, bf16[2,256,2048]{2,1,0:T(8,128)(2,1)} %copy-done.66, bf16[2,256,2048]{2,1,0:T(8,128)(2,1)} %get-tuple-element.106.refs_0_.refs_2_, ...), custom_call_target="tpu_custom_call" | custom-call | flops 18699999232 | bytes 17000000 | tf_op jit(solution)/shard_map/conv_back/pallas_call | solution.py:410
  467.5 12.8 %gate_back.3 = (bf16[2,256,2048]{2,1,0:T(8,128)(2,1)}, bf16[2,256,3072]{2,1,0:T(8,128)(2,1)}, bf16[2,144,2048]{2,1,0:T(8,128)(2,1)}, f32[2,256,128]{2,1,0:T(8,12...) custom-call(bf16[2,256,2048]{2,1,0:T(8,128)(2,1)} %bitcast.209, bf16[2,256,1024]{2,1,0:T(8,128)(2,1)S(1)} %fusion.47.refs_1_, ...), custom_call_target="tpu_custom_call" | custom-call | flops 12099999744 | bytes 11000000 | tf_op jit(solution)/shard_map/gate_back/pallas_call | solution.py:410
  481.0 14.6 %collective-permute-start.50 = (bf16[4,32,2432]{2,1,0:T(8,128)(2,1)S(1)}, bf16[4,32,2432]{2,1,0:T(8,128)(2,1)S(1)}, u32[]{:S(2)}, u32[]{:S(2)}) collective-permute-start(bf16[4,32,2432]{2,1,0:T(8,128)(2,1)S(1)} %get-tuple-element.124.refs_12_), channel_id=1, source_target_pairs={{0,2},{1,3},{2,0},{3,1},{4,6},{5,7},{6,4},{7,5},{8,10},{9,11},{10,... | collective-permute-start | bytes 1867784 | tf_op jit(solution)/shard_map/ppermute | solution.py:445
  501.4 13.5 %collective-permute-done.50.refs_1_ = bf16[4,32,2432]{2,1,0:T(8,128)(2,1)S(1)} collective-permute-done((bf16[4,32,2432]{2,1,0:T(8,128)(2,1)S(1)}, bf16[4,32,2432]{2,1,0:T(8,128)(2,1)S(1)}, u32[]{:S(2)}, u32[]{:S(2)}) %collective-permute-start.50) | collective-permute-done | bytes 622624 | tf_op jit(solution)/shard_map/ppermute | solution.py:445
  516.1 25.9 %collective-permute-done.51.refs_2_ = bf16[4,32,2432]{2,1,0:T(8,128)(2,1)S(1)} collective-permute-done((bf16[4,32,2432]{2,1,0:T(8,128)(2,1)S(1)}, bf16[4,32,2432]{2,1,0:T(8,128)(2,1)S(1)}, u32[]{:S(2)}, u32[]{:S(2)}) %collective-permute-start.51) | collective-permute-done | bytes 622624 | tf_op jit(solution)/shard_map/ppermute | solution.py:445
  544.7 17.3 %mix_within_back.3 = (bf16[2,256,2048]{2,1,0:T(8,128)(2,1)S(1)}, f32[2,256,256]{2,1,0:T(8,128)S(1)}, f32[2,256,128]{2,1,0:T(8,128)S(1)}) custom-call(bf16[2,256,2048]{2,1,0:T(8,128)(2,1)} %get-tuple-element.128.refs_0_.refs_2_, bf16[2,256,2304]{2,1,0:T(8,128)(2,1)} %copy-done.69, f32[2,256,128]{2,1,0:T(8,128)S(1)} %copy-done.94, ...), custom_call_target="tpu_custom_call" | custom-call | flops 18699999232 | bytes 17000000 | tf_op jit(solution)/shard_map/mix_within_back/pallas_call | solution.py:410
  577.6 19.1 %conv_back.3 = (bf16[2,256,2432]{2,1,0:T(8,128)(2,1)}, f32[2,8,2304]{2,1,0:T(8,128)S(1)}, f32[8,2304]{1,0:T(8,128)S(1)}, f32[8,128]{1,0:T(8,128)S(1)}) custom-call(s32[3]{0:T(128)S(1)} %copy-done.35, bf16[2,256,2048]{2,1,0:T(8,128)(2,1)} %copy-done.64, bf16[2,256,2048]{2,1,0:T(8,128)(2,1)} %get-tuple-element.128.refs_0_.refs_2_, ...), custom_call_target="tpu_custom_call" | custom-call | flops 18699999232 | bytes 17000000 | tf_op jit(solution)/shard_map/conv_back/pallas_call | solution.py:410
  630.2 16.1 %collective-permute-done.54.refs_1_ = bf16[4,128,1024]{2,1,0:T(8,128)(2,1)} collective-permute-done((bf16[4,128,1024]{2,1,0:T(8,128)(2,1)}, bf16[4,128,1024]{2,1,0:T(8,128)(2,1)}, u32[]{:S(2)}, u32[]{:S(2)}) %collective-permute-start.54) | collective-permute-done | bytes 1048608 | tf_op jit(solution)/shard_map/ppermute | solution.py:445
  647.7 22.7 %collective-permute-done.55.refs_2_ = bf16[4,128,1024]{2,1,0:T(8,128)(2,1)} collective-permute-done((bf16[4,128,1024]{2,1,0:T(8,128)(2,1)}, bf16[4,128,1024]{2,1,0:T(8,128)(2,1)}, u32[]{:S(2)}, u32[]{:S(2)}) %collective-permute-start.55) | collective-permute-done | bytes 1048608 | tf_op jit(solution)/shard_map/ppermute | solution.py:445
  687.7 14.5 %collective-permute-done.63.refs_2_ = bf16[4,32,2432]{2,1,0:T(8,128)(2,1)S(1)} collective-permute-done((bf16[4,32,2432]{2,1,0:T(8,128)(2,1)S(1)}, bf16[4,32,2432]{2,1,0:T(8,128)(2,1)S(1)}, u32[]{:S(2)}, u32[]{:S(2)}) %collective-permute-start.63) | collective-permute-done | bytes 622624 | tf_op jit(solution)/shard_map/ppermute | solution.py:445
  708.6 16.5 %collective-permute-done.58.refs_2_ = bf16[128,1024]{1,0:T(8,128)(2,1)S(1)} collective-permute-done((bf16[128,1024]{1,0:T(8,128)(2,1)S(1)}, bf16[128,1024]{1,0:T(8,128)(2,1)S(1)}, u32[]{:S(2)}, u32[]{:S(2)}) %collective-permute-start.58) | collective-permute-done | bytes 262176 | tf_op jit(solution)/shard_map/ppermute | solution.py:445
  735.6 20.6 %collective-permute-done.76.refs_2_ = bf16[96,1024]{1,0:T(8,128)(2,1)S(1)} collective-permute-done((bf16[96,1024]{1,0:T(8,128)(2,1)S(1)}, bf16[96,1024]{1,0:T(8,128)(2,1)S(1)}, u32[]{:S(2)}, u32[]{:S(2)}) %collective-permute-start.76) | collective-permute-done | bytes 196640 | tf_op jit(solution)/shard_map/ppermute | solution.py:445
  (679 shorter events, 382.3 us)
Async XLA Ops:
  7.2 238.1 %all-gather.4.cloned.1.call-start = ((), (), s32[]{:S(2)}) async-start(), calls=%async_computation.1 | async-start | bytes 9461760 | tf_op jit(solution)/shard_map/all_gather | solution.py:887
  11.8 257.3 %all-gather.6.cloned.1.call-start = ((), (), s32[]{:S(2)}) async-start(), calls=%async_computation.2 | async-start | bytes 4325376 | tf_op jit(solution)/shard_map/all_gather | solution.py:890
  27.2 593.5 %reduce-scatter.2.cloned.1.call-start = ((), (), s32[]{:S(2)}) async-start(), calls=%async_computation.3 | async-start | bytes 8650752 | tf_op jit(solution)/shard_map/reduce_scatter | solution.py:986
  33.8 47.1 %collective-permute-start.19 = (bf16[32,2048]{1,0:T(8,128)(2,1)S(1)}, bf16[32,2048]{1,0:T(8,128)(2,1)}, u32[]{:S(2)}, u32[]{:S(2)}) collective-permute-start(bf16[32,2048]{1,0:T(8,128)(2,1)S(1)} %take_share.6), channel_id=1, source_target_pairs={{0,24},{8,16},{16,8},{24,0},{1,25},{9,17},{17,9},{25,1},{2,26},{10... | collective-permute-start | bytes 393224 | tf_op jit(solution)/shard_map/ppermute | solution.py:445
  37.5 43.4 %collective-permute-start.18 = (bf16[32,2048]{1,0:T(8,128)(2,1)S(1)}, bf16[32,2048]{1,0:T(8,128)(2,1)}, u32[]{:S(2)}, u32[]{:S(2)}) collective-permute-start(bf16[32,2048]{1,0:T(8,128)(2,1)S(1)} %take_share.6), channel_id=1, source_target_pairs={{0,16},{8,24},{16,0},{24,8},{1,17},{9,25},{17,1},{25,9},{2,18},{10... | collective-permute-start | bytes 393224 | tf_op jit(solution)/shard_map/ppermute | solution.py:445
  117.3 71.6 %collective-permute-start.23 = (bf16[4,3,32,2048]{3,2,1,0:T(8,128)(2,1)}, bf16[4,3,32,2048]{3,2,1,0:T(8,128)(2,1)}, u32[]{:S(2)}, u32[]{:S(2)}) collective-permute-start(bf16[4,3,32,2048]{3,2,1,0:T(8,128)(2,1)} %pad_maximum_fusion.2), channel_id=1, source_target_pairs={{0,1},{1,0},{2,3},{3,2},{4,5},{5,4},{6,7},{7,6},{8,9},{9,8},{10,11... | collective-permute-start | bytes 4718600 | tf_op jit(solution)/shard_map/ppermute | solution.py:445
  128.2 65.2 %collective-permute-start.12 = (bf16[2,144,2048]{2,1,0:T(8,128)(2,1)}, bf16[2,144,2048]{2,1,0:T(8,128)(2,1)}, u32[]{:S(2)}, u32[]{:S(2)}) collective-permute-start(bf16[2,144,2048]{2,1,0:T(8,128)(2,1)} %get-tuple-element.94.refs_1_), channel_id=1, source_target_pairs={{0,1},{1,0},{2,3},{3,2},{4,5},{5,4},{6,7},{7,6},{8,9},{9,8},{10,11... | collective-permute-start | bytes 3538952 | tf_op jit(solution)/shard_map/ppermute | solution.py:445
  133.4 53.9 %collective-permute-start.25 = (bf16[256,1024]{1,0:T(8,128)(2,1)}, bf16[256,1024]{1,0:T(8,128)(2,1)}, u32[]{:S(2)}, u32[]{:S(2)}) collective-permute-start(bf16[256,1024]{1,0:T(8,128)(2,1)} %take_share.7), channel_id=1, source_target_pairs={{0,16},{8,24},{16,0},{24,8},{1,17},{9,25},{17,1},{25,9},{2,18},{10... | collective-permute-start | bytes 1572872 | tf_op jit(solution)/shard_map/ppermute | solution.py:445
  133.4 53.9 %collective-permute-start.24 = (bf16[256,1024]{1,0:T(8,128)(2,1)}, bf16[256,1024]{1,0:T(8,128)(2,1)}, u32[]{:S(2)}, u32[]{:S(2)}) collective-permute-start(bf16[256,1024]{1,0:T(8,128)(2,1)} %take_share.7), channel_id=1, source_target_pairs={{0,8},{8,0},{16,24},{24,16},{1,9},{9,1},{17,25},{25,17},{2,10},{10... | collective-permute-start | bytes 1572872 | tf_op jit(solution)/shard_map/ppermute | solution.py:445
  188.9 40.6 %collective-permute-start.27 = (bf16[3,256,1024]{2,1,0:T(8,128)(2,1)S(1)}, bf16[3,256,1024]{2,1,0:T(8,128)(2,1)S(1)}, u32[]{:S(2)}, u32[]{:S(2)}) collective-permute-start(bf16[3,256,1024]{2,1,0:T(8,128)(2,1)S(1)} %pad_maximum_fusion.3.refs_1_), channel_id=1, source_target_pairs={{0,1},{1,0},{2,3},{3,2},{4,5},{5,4},{6,7},{7,6},{8,9},{9,8},{10,11... | collective-permute-start | bytes 4718600 | tf_op jit(solution)/shard_map/ppermute | solution.py:445
  338.2 123.5 %collective-permute-start.40 = (bf16[512,512]{1,0:T(8,128)(2,1)}, bf16[512,512]{1,0:T(8,128)(2,1)}, u32[]{:S(2)}, u32[]{:S(2)}) collective-permute-start(bf16[512,512]{1,0:T(8,128)(2,1)} %get-tuple-element.119), channel_id=1, source_target_pairs={{0,1},{1,0},{2,3},{3,2},{4,5},{5,4},{6,7},{7,6},{8,9},{9,8},{10,11... | collective-permute-start | bytes 1572872 | tf_op jit(solution)/shard_map/ppermute | solution.py:445
  354.7 411.4 %all-gather.8.cloned.1.call-start = ((), (), s32[]{:S(2)}) async-start(), calls=%async_computation.4 | async-start | bytes 2359296 | tf_op jit(solution)/shard_map/all_gather | solution.py:987
  358.1 39.0 %collective-permute-start.36 = (bf16[144,2048]{1,0:T(8,128)(2,1)S(1)}, bf16[144,2048]{1,0:T(8,128)(2,1)S(1)}, u32[]{:S(2)}, u32[]{:S(2)}) collective-permute-start(bf16[144,2048]{1,0:T(8,128)(2,1)S(1)} %join_states.6), channel_id=1, source_target_pairs={{4,0},{5,1},{6,2},{7,3},{12,8},{13,9},{14,10},{15,11},{20,16},{21,... | collective-permute-start | bytes 1769480 | tf_op jit(solution)/shard_map/ppermute | solution.py:482
  359.4 37.7 %collective-permute-start.37 = (bf16[144,2048]{1,0:T(8,128)(2,1)S(1)}, bf16[144,2048]{1,0:T(8,128)(2,1)S(1)}, u32[]{:S(2)}, u32[]{:S(2)}) collective-permute-start(bf16[144,2048]{1,0:T(8,128)(2,1)S(1)} %join_states.6), channel_id=1, source_target_pairs={{2,0},{3,1},{4,2},{5,3},{6,4},{7,5},{10,8},{11,9},{12,10},{13,11},... | collective-permute-start | bytes 1769480 | tf_op jit(solution)/shard_map/ppermute | solution.py:482
  480.9 84.9 %collective-permute-start.49 = (bf16[512,3072]{1,0:T(8,128)(2,1)}, bf16[512,3072]{1,0:T(8,128)(2,1)}, u32[]{:S(2)}, u32[]{:S(2)}) collective-permute-start(bf16[512,3072]{1,0:T(8,128)(2,1)} %bitcast.200), channel_id=1, source_target_pairs={{0,1},{1,0},{2,3},{3,2},{4,5},{5,4},{6,7},{7,6},{8,9},{9,8},{10,11... | collective-permute-start | bytes 9437192 | tf_op jit(solution)/shard_map/ppermute | solution.py:445
  495.6 46.5 %collective-permute-start.51 = (bf16[4,32,2432]{2,1,0:T(8,128)(2,1)S(1)}, bf16[4,32,2432]{2,1,0:T(8,128)(2,1)S(1)}, u32[]{:S(2)}, u32[]{:S(2)}) collective-permute-start(bf16[4,32,2432]{2,1,0:T(8,128)(2,1)S(1)} %get-tuple-element.125.refs_13_), channel_id=1, source_target_pairs={{0,4},{1,5},{2,6},{3,7},{4,0},{5,1},{6,2},{7,3},{8,12},{9,13},{10,... | collective-permute-start | bytes 1867784 | tf_op jit(solution)/shard_map/ppermute | solution.py:445
  495.6 47.8 %collective-permute-start.52 = (bf16[4,32,2432]{2,1,0:T(8,128)(2,1)S(1)}, bf16[4,32,2432]{2,1,0:T(8,128)(2,1)S(1)}, u32[]{:S(2)}, u32[]{:S(2)}) collective-permute-start(bf16[4,32,2432]{2,1,0:T(8,128)(2,1)S(1)} %get-tuple-element.126.refs_14_), channel_id=1, source_target_pairs={{0,6},{1,7},{2,4},{3,5},{4,2},{5,3},{6,0},{7,1},{8,14},{9,15},{10,... | collective-permute-start | bytes 1867784 | tf_op jit(solution)/shard_map/ppermute | solution.py:445
  499.9 65.9 %collective-permute-start.48 = (bf16[1536,512]{1,0:T(8,128)(2,1)S(1)}, bf16[1536,512]{1,0:T(8,128)(2,1)}, u32[]{:S(2)}, u32[]{:S(2)}) collective-permute-start(bf16[1536,512]{1,0:T(8,128)(2,1)S(1)} %get-tuple-element.136), channel_id=1, source_target_pairs={{0,1},{1,0},{2,3},{3,2},{4,5},{5,4},{6,7},{7,6},{8,9},{9,8},{10,11... | collective-permute-start | bytes 4718600 | tf_op jit(solution)/shard_map/ppermute | solution.py:445
  514.9 48.8 %collective-permute-start.44 = (bf16[144,2048]{1,0:T(8,128)(2,1)S(1)}, bf16[144,2048]{1,0:T(8,128)(2,1)S(1)}, u32[]{:S(2)}, u32[]{:S(2)}) collective-permute-start(bf16[144,2048]{1,0:T(8,128)(2,1)S(1)} %join_states.7), channel_id=1, source_target_pairs={{6,0},{7,1},{14,8},{15,9},{22,16},{23,17},{30,24},{31,25}} | collective-permute-start | bytes 1769480 | tf_op jit(solution)/shard_map/ppermute | solution.py:482
  619.2 51.3 %collective-permute-start.55 = (bf16[4,128,1024]{2,1,0:T(8,128)(2,1)}, bf16[4,128,1024]{2,1,0:T(8,128)(2,1)}, u32[]{:S(2)}, u32[]{:S(2)}) collective-permute-start(bf16[4,128,1024]{2,1,0:T(8,128)(2,1)} %copy-done.48), channel_id=1, source_target_pairs={{0,4},{1,5},{2,6},{3,7},{4,0},{5,1},{6,2},{7,3},{8,12},{9,13},{10,... | collective-permute-start | bytes 3145736 | tf_op jit(solution)/shard_map/ppermute | solution.py:445
  619.2 54.9 %collective-permute-start.56 = (bf16[4,128,1024]{2,1,0:T(8,128)(2,1)S(1)}, bf16[4,128,1024]{2,1,0:T(8,128)(2,1)}, u32[]{:S(2)}, u32[]{:S(2)}) collective-permute-start(bf16[4,128,1024]{2,1,0:T(8,128)(2,1)S(1)} %copy-done.47), channel_id=1, source_target_pairs={{0,6},{1,7},{2,4},{3,5},{4,2},{5,3},{6,0},{7,1},{8,14},{9,15},{10,... | collective-permute-start | bytes 3145736 | tf_op jit(solution)/shard_map/ppermute | solution.py:445
  628.1 59.5 %collective-permute-start.62 = (bf16[4,32,2432]{2,1,0:T(8,128)(2,1)S(1)}, bf16[4,32,2432]{2,1,0:T(8,128)(2,1)S(1)}, u32[]{:S(2)}, u32[]{:S(2)}) collective-permute-start(bf16[4,32,2432]{2,1,0:T(8,128)(2,1)S(1)} %get-tuple-element.155), channel_id=1, source_target_pairs={{0,2},{1,3},{2,0},{3,1},{4,6},{5,7},{6,4},{7,5},{8,10},{9,11},{10,... | collective-permute-start | bytes 1867784 | tf_op jit(solution)/shard_map/ppermute | solution.py:445
  630.2 72.0 %collective-permute-start.63 = (bf16[4,32,2432]{2,1,0:T(8,128)(2,1)S(1)}, bf16[4,32,2432]{2,1,0:T(8,128)(2,1)S(1)}, u32[]{:S(2)}, u32[]{:S(2)}) collective-permute-start(bf16[4,32,2432]{2,1,0:T(8,128)(2,1)S(1)} %get-tuple-element.156), channel_id=1, source_target_pairs={{0,4},{1,5},{2,6},{3,7},{4,0},{5,1},{6,2},{7,3},{8,12},{9,13},{10,... | collective-permute-start | bytes 1867784 | tf_op jit(solution)/shard_map/ppermute | solution.py:445
  646.3 55.9 %collective-permute-start.64 = (bf16[4,32,2432]{2,1,0:T(8,128)(2,1)S(1)}, bf16[4,32,2432]{2,1,0:T(8,128)(2,1)S(1)}, u32[]{:S(2)}, u32[]{:S(2)}) collective-permute-start(bf16[4,32,2432]{2,1,0:T(8,128)(2,1)S(1)} %get-tuple-element.157), channel_id=1, source_target_pairs={{0,6},{1,7},{2,4},{3,5},{4,2},{5,3},{6,0},{7,1},{8,14},{9,15},{10,... | collective-permute-start | bytes 1867784 | tf_op jit(solution)/shard_map/ppermute | solution.py:445
  (234 other events, 3411.9 us)
Sparse Core Ops, SparseCore 0:
  12.0 112.5 all-gather.3
  127.4 83.7 all-gather.5
  354.8 157.0 reduce-scatter.1
  620.9 61.5 all-gather.7

commit v3 on v2

--- a/solution.py
+++ b/solution.py
@@ -12,6 +12,7 @@
 LANES = 128
 EDGE = 8
 FACTOR_ROWS = 16
+SCALE = 0.25
 VMEM = 48 * 1024 * 1024
 NT = (((1,), (1,)), ((), ()))
 TN = (((0,), (0,)), ((), ()))
@@ -421,6 +422,7 @@
 
 
 def cost(micros):
+    micros = micros * SCALE
     return pl.CostEstimate(flops=int(micros * 1.1e9), bytes_accessed=int(micros * 1e6), transcendentals=0)
 
 
@@ -471,16 +473,16 @@
         out[:, place] = before.astype(BF16)
 
 
-def exchange(own, at, later_core):
+def exchange(own, at, later_core, after=()):
     peers = lax.axis_size("seq")
     other = swap(own, "seq", 1)
-    joined = whole_call(functools.partial(join_kernel, later_core), [own, other], [(own.shape[1:], BF16)], 2.0, "join_states", at)[0]
+    joined = whole_call(functools.partial(join_kernel, later_core), [own, other], [(own.shape[1:], BF16)], 2.0, "join_states", at, after)[0]
     got = []
     for distance in range(peers // 2 - 1, 0, -1):
         step = 2 * distance if later_core == 1 else -2 * distance
         route = [(i, i + step) for i in range(peers) if 0 <= i + step < peers]
         got.append(lax.ppermute(joined, "seq", route))
-    return got, other
+    return got, other, joined
 
 
 def entered(got, after):
@@ -552,31 +554,75 @@
         out[pl.ds(start, rows), :] = sources[source][index]
 
 
-def placed_rows(at, weight, steps, layer, columns, sources, starts, groups, micros):
+def placed_rows(at, weight, steps, layer, columns, sources, starts, groups, micros, after=()):
     whole = pl.BlockSpec(memory_space=pltpu.VMEM)
     own = [weight] if steps is None else [weight, steps]
     first, last, with_steps = columns
     shape = (weight.shape[1] * groups, last - first + (LANES if with_steps else 0))
     return pl.pallas_call(
-        functools.partial(place_rows_kernel, starts, columns, len(own)),
+        without(functools.partial(place_rows_kernel, starts, columns, len(own)), 1 + len(own) + len(sources), len(after)),
         grid=(1,),
         in_specs=[pl.BlockSpec(memory_space=pltpu.SMEM)]
-        + [pl.BlockSpec((1,) + a.shape[1:], lambda i: (layer, 0, 0)) for a in own] + [whole] * len(sources),
+        + [pl.BlockSpec((1,) + a.shape[1:], lambda i: (layer, 0, 0)) for a in own] + [whole] * len(sources)
+        + [pl.BlockSpec(memory_space=pl.ANY)] * len(after),
         out_specs=whole,
         out_shape=jax.ShapeDtypeStruct(shape, BF16),
         compiler_params=pltpu.CompilerParams(vmem_limit_bytes=VMEM),
         cost_estimate=cost(micros),
         name="place_rows",
-    )(at, *own, *sources)
-
-
-def fetched_by_all(weight, steps, layer, columns, at, groups, chips, after):
+    )(at, *own, *sources, *after)
+
+
+def stack_kernel(count, *refs):
+    out, row = refs[count], 0
+    for ref in refs[:count]:
+        if len(ref.shape) == 2:
+            out[row] = ref[...]
+            row += 1
+        else:
+            out[row:row + ref.shape[0]] = ref[...]
+            row += ref.shape[0]
+
+
+def stacked(blocks, after=()):
+    many = sum(1 if b.ndim == 2 else b.shape[0] for b in blocks)
+    return whole_call(
+        functools.partial(stack_kernel, len(blocks)), blocks, [((many,) + blocks[0].shape[-2:], BF16)], 1.0, "stack", after=after
+    )[0]
+
+
+def unfold_kernel(share, folded, out):
+    many = folded.shape[1] // out.shape[1]
+    model = out.shape[1]
+    for block in range(folded.shape[0] // share):
+        for i in range(many):
+            to = (block * many + i) * share
+            out[to:to + share, :] = folded[block * share:(block + 1) * share, i * model:(i + 1) * model]
+
+
+def unfolded(whole, inner, model, share):
+    rows = whole.shape[0] // 4
+    return pl.pallas_call(
+        functools.partial(unfold_kernel, share),
+        grid=(4,),
+        in_specs=[pl.BlockSpec((rows, inner), lambda i: (i, 0))],
+        out_specs=pl.BlockSpec((rows * inner // model, model), lambda i: (i, 0)),
+        out_shape=jax.ShapeDtypeStruct((inner, model), BF16),
+        compiler_params=pltpu.CompilerParams(vmem_limit_bytes=VMEM),
+        cost_estimate=cost(3.0),
+        name="unfold",
+    )(whole)
+
+
+def from_along_z(mine, groups, after=()):
+    return stacked([swap(mine, "fsdp", e) for e in range(1, groups)], after)
+
+
+def fetched_by_all(weight, steps, layer, columns, at, groups, chips, from_z, place_after=()):
     rows = weight.shape[1]
     share = rows // (2 * chips)
-    mine = take_share(weight, steps, layer, columns, at, share, 2 * chips, after)
-    from_z = jnp.stack([swap(mine, "fsdp", e) for e in range(1, groups)])
     sources = [from_z] + [swap(from_z, "seq", 2 * d) for d in range(1, chips)]
-    sources.append(swap(jnp.stack(sources), "seq", 1))
+    sources.append(swap(stacked([a.reshape(-1, a.shape[2]) for a in sources]), "seq", 1))
 
     def place_of(d, e, other):
         return lambda core, chip, group: (group ^ e) * rows + (chip ^ d) * (2 * share) + (core ^ other) * share
@@ -584,24 +630,10 @@
     starts = []
     for d in range(chips):
         for e in range(1, groups):
-            starts.append((d, (e - 1,), share, place_of(d, e, 0)))
-            starts.append((chips, (d, e - 1), share, place_of(d, e, 1)))
-    return placed_rows(at, weight, steps, layer, columns, sources, starts, groups, 4.0), from_z
-
-
-def fetched_along_z(weight, layer, at, groups, after):
-    rows = weight.shape[1]
-    share = rows // 2
-    columns = (0, weight.shape[2], False)
-    mine = take_share(weight, None, layer, columns, at, share, 2, after)
-    from_z = jnp.stack([swap(mine, "fsdp", e) for e in range(1, groups)])
-    sources = [from_z, swap(from_z, "seq", 1)]
-
-    def place_of(e, other):
-        return lambda core, chip, group: (group ^ e) * rows + (core ^ other) * share
-
-    starts = [(other, (e - 1,), share, place_of(e, other)) for e in range(1, groups) for other in range(2)]
-    return placed_rows(at, weight, None, layer, columns, sources, starts, groups, 3.0), from_z
+            index = e - 1
+            starts.append((d, (index,), share, place_of(d, e, 0)))
+            starts.append((chips, (d, slice(index * share, (index + 1) * share)), share, place_of(d, e, 1)))
+    return placed_rows(at, weight, steps, layer, columns, sources, starts, groups, 4.0, place_after)
 
 
 def reduced(grad):
@@ -665,29 +697,35 @@
 
 
 def wide_grads_kernel(low, gated, grad, out):
-    turned = jnp.where(pl.program_id(1) * jnp.ones(low.shape, jnp.int32) < 2, low[...], gated[...])
-    out[...] = dot_tn(turned, grad[...]).astype(BF16)
-
-
-def wide_grads(low, gated, both, groups):
+    cut, model = low.shape[1], grad.shape[1] - out.shape[1] // 2
+    inner = out.shape[1] // 2
+    turned = low[...].T
+    for at in range(0, inner, 512):
+        out[:, pl.ds(at, 512)] = dot(turned, grad[:, pl.ds(at, 512)]).astype(BF16)
+    for i in range(inner // model):
+        turned = gated[:, i * cut:(i + 1) * cut].T
+        for at in range(0, model, 512):
+            out[:, pl.ds(inner + i * model + at, 512)] = dot(turned, grad[:, pl.ds(inner + at, 512)]).astype(BF16)
+
+
+def wide_grads(low, gated, both, groups, after):
     rows, model = low.shape
     inner = gated.shape[1]
     cut = model // groups
-    halves_of = inner // model
     return pl.pallas_call(
-        wide_grads_kernel,
-        grid=(groups, 2 * halves_of),
+        without(wide_grads_kernel, 3, len(after)),
+        grid=(groups,),
         in_specs=[
-            pl.BlockSpec((rows, cut), lambda z, j: (0, z)),
-            pl.BlockSpec((rows, cut), lambda z, j: (0, halves_of * z + jnp.maximum(j - halves_of, 0))),
-            pl.BlockSpec((rows, model), lambda z, j: (0, jnp.minimum(j, halves_of))),
-        ],
-        out_specs=pl.BlockSpec((cut, model), lambda z, j: (z, j)),
+            pl.BlockSpec((rows, cut), lambda z: (0, z)),
+            pl.BlockSpec((rows, inner // groups), lambda z: (0, z)),
+            pl.BlockSpec(both.shape, lambda z: (0, 0)),
+        ] + [pl.BlockSpec(memory_space=pl.ANY)] * len(after),
+        out_specs=pl.BlockSpec((cut, 2 * inner), lambda z: (z, 0)),
         out_shape=jax.ShapeDtypeStruct((model, 2 * inner), BF16),
         compiler_params=pltpu.CompilerParams(vmem_limit_bytes=VMEM),
         cost_estimate=cost(10.0),
         name="wide_grads",
-    )(low, gated, both)
+    )(low, gated, both, *after)
 
 
 def second_grads_kernel(groups, chips, channels, heads, here, own, other, grad, grad_other, extra, extra_other, *outs):
@@ -712,6 +750,35 @@
                 outs[d][e, :, place] = part.astype(BF16)
 
 
+def gather_small_kernel(groups, taps, heads, gain, tap_grads, head_grads, row_grads, spread, out):
+    cut = out.shape[0] // groups
+    channels, inner = tap_grads.shape[1], row_grads.shape[1]
+    skip = row_grads[1:2, :]
+    high = skip.astype(BF16)
+    low = (skip - high.astype(F32)).astype(BF16)
+    ones = spread[0:LANES, :]
+    skip = dot_nt(jnp.broadcast_to(high, (8, inner)), ones) + dot_nt(jnp.broadcast_to(low, (8, inner)), ones)
+    span, part, few = channels // groups, inner // groups, heads // groups
+    for z in range(groups):
+        rows = [jnp.zeros((heads, cut), F32), gain[0:1, z * cut:(z + 1) * cut]]
+        for at in range(0, part, cut):
+            rows.append(row_grads[0:1, z * part + at:z * part + at + cut])
+        for at in range(0, span, cut):
+            wide = min(cut, span - at)
+            block = tap_grads[0:taps + 1, z * span + at:z * span + at + wide]
+            if wide < cut:
+                block = jnp.concatenate([block, jnp.zeros((taps + 1, cut - wide), F32)], axis=1)
+            rows.append(block)
+        lane = lax.broadcasted_iota(jnp.int32, (1, LANES), 1)
+        for row in (head_grads[0:1, :], head_grads[1:2, :], skip[0:1, :]):
+            row = pltpu.roll(row, (LANES - z * few) % LANES, axis=1) if z else row
+            row = jnp.where(lane < few, row, 0.0)
+            rows.append(jnp.concatenate([row] + [jnp.zeros((1, cut - LANES), F32)], axis=1))
+        table = jnp.concatenate(rows, axis=0)
+        table = jnp.concatenate([table, jnp.zeros((LANES - table.shape[0], cut), F32)], axis=0)
+        out[z * cut:(z + 1) * cut, :] = table.T
+
+
 def add_kernel(count, *refs):
     ins, outs = refs[:count], refs[count:]
     for i, out in enumerate(outs):
@@ -721,105 +788,142 @@
         out[...] = total.astype(out.dtype)
 
 
-def add_last_kernel(first, second, *refs):
+def halve_kernel(count, *refs):
+    ins, (near, far) = refs[:count], refs[count:]
+    half = near.shape[0]
+    for i in range(2 * half):
+        total = ins[0][i].astype(F32)
+        for more in ins[1:]:
+            total = total + more[i].astype(F32)
+        if i < half:
+            near[i] = total.astype(BF16)
+        else:
+            far[i - half] = total.astype(BF16)
+
+
+def lay_kernel(count, layers, *refs):
     out = refs[-1]
-    rows, wide = refs[0].shape[0] if first else 0, out.shape[1]
-
-    def total_of(group, place):
-        total = group[0][:, place].astype(F32)
-        for more in group[1:]:
-            total = total + more[:, place].astype(F32)
-        return total.astype(BF16)
-
-    if first:
-        out[0:rows, :] = total_of(refs[:first], pl.ds(0, wide))
-    seconds = refs[first:first + second]
-    share, columns = seconds[0].shape
-    for i, at in enumerate(range(0, columns, wide)):
-        width = min(wide, columns - at)
-        out[rows + i * share:rows + (i + 1) * share, 0:width] = total_of(seconds, pl.ds(at, width))
-        if width < wide:
-            out[rows + i * share:rows + (i + 1) * share, width:] = jnp.zeros((share, wide - width), BF16)
-
-
-def first_sums(blocks, axis, after=()):
-    parts, rows, columns = blocks[0].shape
-    unit = 2 if axis == "seq" else 1
-    got = [blocks[0]] + [swap(blocks[i], axis, unit * i) for i in range(1, len(blocks))]
-    return whole_call(
-        functools.partial(add_kernel, len(got)), got, [((rows, columns), BF16)] * parts, 2.5, "add_first", after=after
-    )
-
-
-def second_parts(shares, axis):
-    unit = 2 if axis == "seq" else 1
-    return [shares[0]] + [swap(shares[i], axis, unit * i) for i in range(1, len(shares))]
-
-
-def last_sums(first, second, wide):
-    rows = first[0].shape[0] if first else 0
-    share, columns = second[0].shape
-    total = rows + -(-columns // wide) * share
-    return whole_call(
-        functools.partial(add_last_kernel, len(first), len(second)), first + second, [((total, wide), BF16)], 2.0, "add_last"
-    )[0]
-
-
-def place_kernel(chips, inner, joined, at, *refs):
-    mine, other = refs[:chips], refs[chips]
-    in_out, extra_out, out_out = refs[-3:]
+    wide = out.shape[1]
+    share, columns = refs[0].shape[0] // layers, refs[0].shape[1]
+    row = 0
+    for layer in range(layers):
+        rows = slice(layer * share, (layer + 1) * share)
+        for at in range(0, columns, wide):
+            width = min(wide, columns - at)
+            total = refs[0][rows, at:at + width].astype(F32)
+            for more in refs[1:count]:
+                total = total + more[rows, at:at + width].astype(F32)
+            out[row:row + share, 0:width] = total.astype(BF16)
+            if width < wide:
+                out[row:row + share, width:] = jnp.zeros((share, wide - width), BF16)
+            row += share
+
+
+def plane_parts(blocks):
+    return [blocks[0]] + [swap(blocks[i], "seq", 2 * i) for i in range(1, len(blocks))]
+
+
+def halved_sums(got, groups):
+    parts, rows, columns = got[0].shape
+    after = ()
+    while parts > 1:
+        half = parts // 2
+        near, far = whole_call(
+            functools.partial(halve_kernel, len(got)), got, [((half, rows, columns), BF16)] * 2, 2.0, "add_halves"
+        )
+        if parts == groups:
+            after = (near,)
+        got = [near, swap(far, "fsdp", half)]
+        parts = half
+    return whole_call(functools.partial(add_kernel, 2), got, [((rows, columns), BF16)], 1.0, "add_halves")[0], after
+
+
+def laid(got, wide, after):
+    rows, columns = got[0].shape
+    shape = (-(-columns // wide) * rows, wide)
+    return whole_call(functools.partial(lay_kernel, len(got), 1), got, [(shape, BF16)], 2.0, "lay_sums", after=after)[0]
+
+
+def layer_sums(got, groups, wide, after):
+    parts, rows, columns = got[0].shape
+    shares = whole_call(functools.partial(add_kernel, len(got)), got, [((rows, columns), BF16)] * parts, 2.0, "add_plane")
+    return laid([shares[0]] + [swap(shares[e], "fsdp", e) for e in range(1, groups)], wide, after)
+
+
+def spread_in_plane(share, chips):
+    mine = [share] + [swap(share, "seq", 2 * d) for d in range(1, chips)]
+    return mine, swap(stacked(mine), "seq", 1)
+
+
+def place_kernel(chips, inner, layers, at, *refs):
+    mine_a, other_a = refs[:chips], refs[chips]
+    mine_b, other_b = refs[chips + 1:2 * chips + 1], refs[2 * chips + 1]
+    scattered = refs[2 * chips + 2:2 * chips + 1 + layers]
+    in_out, extra_out, out_out, norm_out, taps_out, bias_out, heads_out, gain_out, extra = refs[-9:]
     core, chip = at[0], at[1]
-    model = other.shape[2]
-    big = out_out.shape[1] // (2 * chips)
-    share = in_out.shape[1] // (2 * chips)
+    model = other_a.shape[2]
+    rows_in, rows_out = in_out.shape[1], out_out.shape[1]
+    big, share = rows_out // (2 * chips), rows_in // (2 * chips)
     channels = in_out.shape[2] - inner
-    if joined:
-        scattered = refs[chips + 1]
-        in_out[0, :, 0:inner] = scattered[:, 0:inner].astype(F32)
-        rows = in_out.shape[1]
-        for i in range(inner // model):
-            out_out[0, i * rows:(i + 1) * rows, :] = scattered[:, inner + i * model:inner + (i + 1) * model].astype(F32)
-    for d in range(chips):
-        for is_other, part in ((0, mine[d]), (1, other.at[d])):
-            start = (chip ^ d) * (2 * share) + (core ^ is_other) * share
-            rows = pl.ds(pl.multiple_of(start, share), share)
-            at_row = 0
-            if not joined:
-                big_start = (chip ^ d) * (2 * big) + (core ^ is_other) * big
-                out_out[0, pl.ds(pl.multiple_of(big_start, big), big), :] = part[0:big, :].astype(F32)
-                at_row = big
+    for layer in range(layers):
+        @pl.when(pl.program_id(0) == layer)
+        def _():
+            if layer:
+                wide = scattered[layer - 1]
+                in_out[0, :, 0:inner] = wide[:, 0:inner].astype(F32)
                 for i in range(inner // model):
-                    in_out[0, rows, i * model:(i + 1) * model] = part[at_row:at_row + share, :].astype(F32)
-                    at_row += share
-            for start_column in range(0, channels, model):
-                wide = min(model, channels - start_column)
-                to = pl.ds(inner + start_column, wide)
-                in_out[0, rows, to] = part[at_row:at_row + share, 0:wide].astype(F32)
-                if start_column + model >= channels:
-                    extra_out[0, rows, :] = part[at_row:at_row + share, wide:wide + LANES].astype(F32)
-                at_row += share
-
-
-def placed_grads(at, share, scattered, before, layer, layers, shapes, chips, inner):
-    mine = [share] + [swap(share, "seq", 2 * d) for d in range(1, chips)]
-    pieces = mine + [swap(jnp.stack(mine), "seq", 1)]
-    joined = scattered is not None
-    pieces += [scattered] if joined else []
+                    out_out[0, i * rows_in:(i + 1) * rows_in, :] = wide[:, inner + i * model:inner + (i + 1) * model].astype(F32)
+            for d in range(chips):
+                for is_other in range(2):
+                    a, b = (other_a.at[d], other_b.at[d]) if is_other else (mine_a[d], mine_b[d])
+                    start = (chip ^ d) * (2 * share) + (core ^ is_other) * share
+                    rows = pl.ds(pl.multiple_of(start, share), share)
+                    if not layer:
+                        start = (chip ^ d) * (2 * big) + (core ^ is_other) * big
+                        out_out[0, pl.ds(pl.multiple_of(start, big), big), :] = a[0:big, :].astype(F32)
+                        for i in range(inner // model):
+                            first = big + i * share
+                            in_out[0, rows, i * model:(i + 1) * model] = a[first:first + share, :].astype(F32)
+                    first = layer * (b.shape[0] // layers)
+                    for column in range(0, channels + LANES, model):
+                        wide = min(model, channels - column)
+                        in_out[0, rows, pl.ds(inner + column, wide)] = b[first:first + share, 0:wide].astype(F32)
+                        if column + model >= channels:
+                            extra[rows, :] = b[first:first + share, wide:wide + LANES].astype(F32)
+                        first += share
+            extra_out[0] = extra[:, 0:extra_out.shape[2]]
+            table = extra[...].T
+            heads = extra_out.shape[2]
+            taps, span, part = taps_out.shape[1], taps_out.shape[2], gain_out.shape[1]
+            norm_out[layer:layer + 1, :] = table[heads:heads + 1]
+            row = heads + 1
+            for start in range(0, part, rows_in):
+                gain_out[layer:layer + 1, start:start + rows_in] = table[row:row + 1]
+                row += 1
+            for start in range(0, span, rows_in):
+                wide = min(rows_in, span - start)
+                taps_out[layer, :, start:start + wide] = table[row:row + taps, 0:wide]
+                bias_out[layer:layer + 1, start:start + wide] = table[row + taps:row + taps + 1, 0:wide]
+                row += taps + 1
+            few = heads_out.shape[2]
+            heads_out[layer] = table[row:row + 3, 0:few]
+
+
+def placed_grads(at, pieces, layers, shapes, smalls, chips, inner, after):
     whole = pl.BlockSpec(memory_space=pltpu.VMEM)
-    anywhere = pl.BlockSpec(memory_space=pl.ANY)
-    before = [] if before is None else list(before)
-    outs = [jax.ShapeDtypeStruct((layers,) + shape, F32) for shape in shapes]
     return pl.pallas_call(
-        functools.partial(place_kernel, chips, inner, joined),
-        grid=(1,),
-        in_specs=[pl.BlockSpec(memory_space=pltpu.SMEM)] + [whole] * len(pieces) + [anywhere] * len(before),
-        out_specs=[pl.BlockSpec((1,) + shape, lambda i: (layer, 0, 0)) for shape in shapes],
-        out_shape=outs,
-        input_output_aliases={1 + len(pieces) + i: i for i in range(len(before))},
+        without(functools.partial(place_kernel, chips, inner, layers), 1 + len(pieces), len(after)),
+        grid=(layers,),
+        in_specs=[pl.BlockSpec(memory_space=pltpu.SMEM)] + [whole] * len(pieces)
+        + [pl.BlockSpec(memory_space=pl.ANY)] * len(after),
+        out_specs=[pl.BlockSpec((1,) + shape, lambda i: (i, 0, 0)) for shape in shapes]
+        + [pl.BlockSpec(shape, lambda i, n=len(shape): (0,) * n) for shape in smalls],
+        out_shape=[jax.ShapeDtypeStruct((layers,) + shape, F32) for shape in shapes] + [jax.ShapeDtypeStruct(shape, F32) for shape in smalls],
+        scratch_shapes=[pltpu.VMEM((shapes[0][0], LANES), F32)],
         compiler_params=pltpu.CompilerParams(vmem_limit_bytes=VMEM),
-        cost_estimate=cost(6.0),
+        cost_estimate=cost(8.0),
         name="place_grads",
-    )(at, *pieces, *before)
+    )(at, *pieces, *after)
 
 
 def norm_scale_of(stream):
@@ -850,7 +954,10 @@
     sizes = [a.shape[1] for a in small]
     own = jnp.concatenate(small, axis=1)
     if direct:
-        by_partner = jnp.stack([own] + [swap(own, "fsdp", e) for e in range(1, groups)])
+        by_partner, bits = own[None], 1
+        while bits < groups:
+            by_partner = jnp.concatenate([by_partner, swap(by_partner, "fsdp", bits)])
+            bits *= 2
         packed = jnp.stack([lax.dynamic_index_in_dim(by_partner, here[2] ^ z, 0, keepdims=False) for z in range(groups)])
     else:
         packed = lax.all_gather(own, "fsdp", axis=0)
@@ -872,22 +979,34 @@
         [jnp.pad(joined(pieces[3]).astype(F32), pad_heads), jnp.pad(-jnp.exp(joined(pieces[4]).astype(F32)), pad_heads)], axis=1
     )
     rates_all = jnp.pad(rates_all, ((0, 0), (0, 6), (0, 0)))
-    skip_all = jnp.broadcast_to(jnp.repeat(joined(pieces[5]).astype(F32), span, axis=1)[:, None], (layers, 8, inner))
-    gain_all = jnp.broadcast_to(joined(pieces[6]).astype(F32)[:, None], (layers, 8, inner))
-
-    gate_columns, mix_columns, all_columns = (0, inner, False), (inner, inner + channels, True), (0, inner + channels, True)
+    skip_all = jnp.repeat(joined(pieces[5]).astype(F32), span, axis=1)[:, None]
+    gain_all = joined(pieces[6]).astype(F32)[:, None]
+
+    all_columns = (0, inner + channels, True)
     gate_all, mix_all, out_all = [], [], []
     for layer in range(layers):
-        if direct and layer == 0:
-            mixes, _ = fetched_by_all(in_weight, dt_weight, layer, mix_columns, here, groups, chips, ())
-            gates, from_z = fetched_by_all(in_weight, None, layer, gate_columns, here, groups, chips, ())
-            outs, _ = fetched_along_z(out_weight, layer, here, groups, (from_z,))
-        elif direct:
-            share = take_share(in_weight, dt_weight, layer, all_columns, here, model // (groups * peers), peers, ())
-            whole = lax.all_gather(share, ("fsdp", "seq"), axis=0, tiled=True)
-            gates, mixes = whole[:, :inner], whole[:, inner:]
-            share = take_share(out_weight, None, layer, (0, model, False), here, inner // (groups * peers), peers, ())
-            outs = lax.all_gather(share, ("fsdp", "seq"), axis=0, tiled=True)
+        if direct:
+            share_in, share_out = model // (groups * peers), inner // (groups * peers)
+            if layer == 0:
+                mix_z = from_along_z(take_share(in_weight, dt_weight, 0, all_columns, here, share_in, peers, ()), groups, (by_partner,))
+                whole = fetched_by_all(
+                    in_weight, dt_weight, 0, all_columns, here, groups, chips, mix_z, (norm_all, taps_all, rates_all, skip_all, gain_all)
+                )
+                gates, mixes = whole[:, :inner], whole[:, inner:]
+                outs = None
+            else:
+                share = take_share(in_weight, dt_weight, layer, all_columns, here, share_in, peers, (mix_z,))
+                taken, first = [share], 0
+                if layer == 1:
+                    share = take_share(out_weight, None, 0, (0, model, False), here, share_out, peers, (mix_z,))
+                    taken = [share[i * share_in:(i + 1) * share_in] for i in range(inner // model)] + taken
+                    first = inner
+                whole = lax.all_gather(jnp.concatenate(taken, axis=1), ("fsdp", "seq"), axis=0, tiled=True)
+                gates, mixes = whole[:, first:first + inner], whole[:, first + inner:]
+                if layer == 1:
+                    out_all[0] = unfolded(whole, inner, model, share_in)
+                share = take_share(out_weight, None, layer, (0, model, False), here, share_out, peers, (mix_z,))
+                outs = lax.all_gather(share, ("fsdp", "seq"), axis=0, tiled=True)
         else:
             steps = jnp.pad(dt_weight[layer], ((0, 0), (0, LANES - heads)))
             whole = gathered(jnp.concatenate([in_weight[layer], steps], axis=1))
@@ -909,7 +1028,7 @@
     spread = (jnp.arange(2 * LANES)[:, None] % LANES == lane_head[None, :]).astype(BF16)
 
     stream = tokens.astype(F32)
-    kept = []
+    kept, sent = [], ()
     for layer in range(layers):
         norm_scale = norm_scale_of(stream)
         low = (stream * norm_scale * norm_all[layer]).astype(BF16).reshape(rows, model)
@@ -926,9 +1045,9 @@
                 ((batch, heads, width), F32, 0), ((batch, states + FACTOR_ROWS, inner), BF16, 0),
                 ((batch, FACTOR_ROWS, inner), BF16, 0),
             ],
-            [((EDGE + width, channels), F32)], "conv_states", 8.0,
+            [((EDGE + width, channels), F32)], "conv_states", 8.0, after=sent,
         )
-        got, other = exchange(state, here, 1)
+        got, other, _ = exchange(state, here, 1)
         (part,) = call(
             functools.partial(intra_kernel, inner, heads), batch,
             [(act, 0), (size, 0), (sums, 0), (sums_t, 0), (marks, 0), (row_marks, 0), (skip, 1), (spread, 1)],
@@ -949,11 +1068,12 @@
         if direct:
             mine, send = turned_halves(gated if layer == 0 else None, low, here, groups, chips)
             turned = (mine, swap(send, "seq", 1))
+            sent = (send,)
         kept.append((turned, stream, norm_scale, low, mixed_in, edge, gate, act, size, sums, sums_t, factor, entering, mixed, gated))
         stream = stream + dot(gated, w_out).reshape(batch, width, model)
 
     grad_stream = cotangent.astype(F32)
-    collected, collected_grads, placed, chains = [], [], None, []
+    collected, collected_grads, scattered, second_shares, waiting = [], [], [], [], []
     started = ()
     for layer in reversed(range(layers)):
         (turned, entry, norm_scale, low, mixed_in, edge, gate, act, size, sums, sums_t, factor, entering, mixed, gated) = kept[layer]
@@ -973,7 +1093,7 @@
             ],
             [((width, inner), F32)], "gate_back", 11.0, after=started,
         )
-        got, other = exchange(d_state, here, 0)
+        got, other, joined_state = exchange(d_state, here, 0)
         both = d_gate.reshape(rows, inner + model)
         d_gate = both[:, :inner]
         started, arrived = (), ()
@@ -982,12 +1102,9 @@
             mine, theirs = turned
             both_other = swap(both, "seq", 1) if layer == 0 else None
             if layer > 0:
-                wide = wide_grads(low, gated, both, groups)
-                share = lax.psum_scatter(wide, ("fsdp", "seq"), scatter_dimension=0, tiled=True)
-                scattered = lax.all_gather(share, "seq", axis=0, tiled=True)
+                wide = wide_grads(low, gated, both, groups, (joined_state,))
+                scattered.append(lax.psum_scatter(wide, ("fsdp", "seq"), scatter_dimension=0, tiled=True))
                 started = (wide,)
-            else:
-                scattered = None
         else:
             out_share = reduced(dot_tn(gated, grad_low).astype(BF16))
         d_stepped, d_pair, d_total = call(
@@ -1008,8 +1125,10 @@
                 [((groups, big + inner // model * small, model), BF16)] * chips, 10.0, "first_grads", after=(before,),
             )
             arrived = tuple(first_blocks)
-            for chain in chains:
-                arrived += tuple(chain)
+            for later in waiting:
+                share, _ = halved_sums(plane_parts(later((first_blocks[0],))), groups)
+                second_shares.append(laid([share], model, ()))
+            first_share, halved = halved_sums(plane_parts(first_blocks), groups)
         d_mixed_in, d_edge, tap_grads, head_grads = call(
             functools.partial(conv_back_kernel, inner), batch,
             [
@@ -1032,53 +1151,63 @@
         inward = jnp.mean(scaled * entry, axis=-1, keepdims=True)
         gain_grad = jnp.sum(grad_rows * entry * norm_scale, axis=(0, 1))
         grad_stream = grad_stream + norm_scale * scaled - (norm_scale * norm_scale * norm_scale * inward) * entry
-        skip_grad = jnp.sum(row_grads[1].reshape(heads, span), axis=1)
-        small_grads = [
-            gain_grad.reshape(groups, -1),
-            jnp.moveaxis(tap_grads[:taps_len].reshape(taps_len, groups, -1), 1, 0).reshape(groups, -1),
-            tap_grads[taps_len].reshape(groups, -1),
-            head_grads[0, :heads].reshape(groups, -1),
-            head_grads[1, :heads].reshape(groups, -1),
-            skip_grad.reshape(groups, -1),
-            row_grads[0].reshape(groups, -1),
-        ]
-        small_sums = jnp.concatenate(small_grads, axis=1)
         if direct:
-            per_row = -(-small_sums.shape[1] * groups // model)
-            extra = jnp.pad(small_sums, ((0, 0), (0, per_row * model // groups - small_sums.shape[1]))).reshape(model, per_row)
-            extra = jnp.pad(extra, ((0, 0), (heads, LANES - heads - per_row)))
-            second_blocks = whole_call(
-                functools.partial(second_grads_kernel, groups, chips, channels, heads),
-                [mine, theirs, grad_mixed, swap(grad_mixed, "seq", 1), extra, swap(extra, "seq", 1)],
-                [((groups, small, channels + LANES), BF16)] * chips, 6.0, "second_grads", here,
-            )
-            started = tuple(second_blocks)
-            second = first_sums(second_blocks, "seq")
-            first_last = second_parts(first_sums(first_blocks, "seq"), "fsdp") if layer == 0 else []
-            chains.append(second)
-            share = last_sums(first_last, second_parts(second, "fsdp"), model)
-            shapes = [(model // groups, inner + channels), (model // groups, LANES), (inner // groups, model)]
-            placed = placed_grads(here, share, scattered, placed, layer, layers, shapes, chips, inner)
+            extra = whole_call(
+                functools.partial(gather_small_kernel, groups, taps_len, heads), [gain_grad[None], tap_grads, head_grads, row_grads, spread],
+                [((model, LANES), F32)], 3.0, "gather_small",
+            )[0]
+            operands = [mine, theirs, grad_mixed, swap(grad_mixed, "seq", 1), extra, swap(extra, "seq", 1)]
+            kernel = functools.partial(second_grads_kernel, groups, chips, channels, heads)
+            outs = [((groups, small, channels + LANES), BF16)] * chips
+            if layer > 0:
+                waiting.append(functools.partial(whole_call, kernel, operands, outs, 6.0, "second_grads", here))
+                started = (operands[3], operands[5])
+            else:
+                got = plane_parts(whole_call(kernel, operands, outs, 6.0, "second_grads", here, halved))
+                second_shares.append(layer_sums(got, groups, model, (stream, grad_stream)))
         else:
             mixed_grad = dot_tn(low, grad_mixed)
             in_share = reduced(jnp.concatenate([dot_tn(low, d_gate).astype(BF16), mixed_grad[:, :channels].astype(BF16)], axis=1))
             dt_share = reduced(mixed_grad[:, channels:].astype(BF16))
             collected_grads.append((in_share, dt_share, out_share))
-            collected.append(small_sums)
+            small_grads = [
+                gain_grad.reshape(groups, -1),
+                jnp.moveaxis(tap_grads[:taps_len].reshape(taps_len, groups, -1), 1, 0).reshape(groups, -1),
+                tap_grads[taps_len].reshape(groups, -1),
+                head_grads[0, :heads].reshape(groups, -1),
+                head_grads[1, :heads].reshape(groups, -1),
+                jnp.sum(row_grads[1].reshape(heads, span), axis=1).reshape(groups, -1),
+                row_grads[0].reshape(groups, -1),
+            ]
+            collected.append(jnp.concatenate(small_grads, axis=1))
     if direct:
-        small_sum = placed[1][:, :, heads:heads + per_row].reshape(layers, -1)
+        mine_a, other_a = spread_in_plane(first_share, chips)
+        second_share = stacked(second_shares[::-1]).reshape(-1, model)
+        held = [stacked([share], (first_blocks[0],))[0] for share in scattered]
+        scattered = [lax.all_gather(share, "seq", axis=0, tiled=True) for share in held]
+        mine_b, other_b = spread_in_plane(second_share, chips)
+        shapes = [(model // groups, inner + channels), (model // groups, heads), (inner // groups, model)]
+        smalls = [
+            (layers, model // groups), (layers, taps_len, channels // groups), (layers, channels // groups), (layers, 3, heads // groups),
+            (layers, inner // groups),
+        ]
+        blocks = mine_a + [other_a] + mine_b + [other_b] + scattered[::-1]
+        placed = placed_grads(here, blocks, layers, shapes, smalls, chips, inner, ())
+        by_head = placed[6]
+        pieces = [placed[3], placed[4], placed[5], by_head[:, 0], by_head[:, 1], by_head[:, 2], placed[7]]
     else:
         placed = [jnp.stack([c[i] for c in collected_grads[::-1]]) for i in range(3)]
+        placed[1] = placed[1][:, :, :heads]
         small_sum = lax.psum(jnp.stack(collected[::-1], axis=1), ("fsdp", "seq"))
         small_sum = lax.dynamic_index_in_dim(small_sum, lax.axis_index("fsdp"), 0, keepdims=False)
-    pieces, at = [], 0
-    for size in sizes:
-        pieces.append(small_sum[:, at:at + size])
-        at += size
+        pieces, at = [], 0
+        for size in sizes:
+            pieces.append(small_sum[:, at:at + size])
+            at += size
     return (
         stream, grad_stream, pieces[0],
         placed[0],
-        placed[1][:, :, :heads],
+        placed[1],
         pieces[1].reshape(layers, taps_len, -1),
         pieces[2], pieces[3], pieces[4], pieces[5], pieces[6],
         placed[2],

time: 802 us -> 724 us (0.903)
  waiting for transfers between devices: 286 us -> 246 us
  local copies, waits for them, and re-layouts: 61.8 us -> 49.4 us
  Pallas kernels: 231 us -> 222 us
  other arithmetic: 21.2 us -> 12.5 us
    ppermute x62 -> x48, waiting for transfers between devices: 241 us -> 188 us  [swap(): lax.ppermute(x, axis, [(i, i ^ bits) for i in range(lax.axis_size(axis))])]
    ppermute x62 -> x48, starting transfers between devices: 80.7 us -> 66.7 us  [swap(): lax.ppermute(x, axis, [(i, i ^ bits) for i in range(lax.axis_size(axis))])]
    ppermute x12, waiting for transfers between devices: 41.5 us -> 54.6 us  [exchange(): got.append(lax.ppermute(joined, 'seq', route))]
    pallas_call x6 -> x4, Pallas kernels: 36.9 us -> 26.3 us  [the longest x1 8.6 us: wide_grads(): pl.pallas_call(without(wide_grads_kernel, 3, len(after)), grid=(groups,),...]
    pallas_call x18 -> x30, Pallas kernels: 35.5 us -> 42.7 us  [whole_call(): pl.pallas_call(without(kernel, len(arrays), len(after)), in_specs=in_spec...]
    unnamed x352 -> x244, local copies, waits for them, and re-layouts: 44.2 us -> 42.4 us
  transfers between devices with their start and end apart: 83 -> 69, of which waited for: 25 -> 34; matrix products, arithmetic and copies ran while one was open for 12% -> 11% of each run, Pallas kernels for 26% -> 26%
where the time goes in v3:
time: 724 us; the launch traced here: 713 us
  waiting for transfers between devices  246 us (34%)
  Pallas kernels  222 us (31%)
  starting transfers between devices  105 us (15%)
  matrix products  62 us (9%)
  local copies, waits for them, and re-layouts  49.4 us (7%)
  between operations  15.6 us (2%)
  other arithmetic  12.5 us (2%)
    ppermute x48, waiting for transfers between devices, swap(): lax.ppermute(x, axis, [(i, i ^ bits) for i in range(lax.axis_size(axis))])  188 us
    pallas_call x12, Pallas kernels, call(): pl.pallas_call(without(kernel, len(arrays), len(after)), grid=(batch,), i...  150 us
    ppermute x48, starting transfers between devices, swap(): lax.ppermute(x, axis, [(i, i ^ bits) for i in range(lax.axis_size(axis))])  66.7 us
    ppermute x12, waiting for transfers between devices, exchange(): got.append(lax.ppermute(joined, 'seq', route))  54.6 us
    pallas_call x30, Pallas kernels, whole_call(): pl.pallas_call(without(kernel, len(arrays), len(after)), in_specs=in_spec...  42.7 us
    unnamed x244, local copies, waits for them, and re-layouts  42.4 us
    dot_general x6, matrix products, dot(): return jnp.dot(a, b, preferred_element_type=F32)  31.8 us
    dot_general x6, matrix products, dot_nt(): return lax.dot_general(a, b, NT, preferred_element_type=F32)  30.2 us
  transfers between devices with their start and end apart: 69, of which 34 were waited for; matrix products, arithmetic and copies ran while one was open for 11% of the time, Pallas kernels for 26%

profile of v3, /device:TPU:0, one launch (start us, length us, event | category | flops | bytes accessed | tf_op | source)
XLA Modules:
  0.0 712.7 jit_solution(3178286412933857003)
XLA Ops:
  31.7 12.8 %collective-permute-done.3.refs_1_ = bf16[32,4480]{1,0:T(8,128)(2,1)S(1)} collective-permute-done((bf16[32,4480]{1,0:T(8,128)(2,1)S(1)}, bf16[32,4480]{1,0:T(8,128)(2,1)S(1)}, u32[]{:S(2)}, u32[]{:S(2)}) %collective-permute-start.3) | collective-permute-done | bytes 286752 | tf_op jit(solution)/shard_map/ppermute | solution.py:447
  58.0 20.1 %collective-permute-done.5.refs_4_ = bf16[3,32,4480]{2,1,0:T(8,128)(2,1)S(1)} collective-permute-done((bf16[3,32,4480]{2,1,0:T(8,128)(2,1)S(1)}, bf16[3,32,4480]{2,1,0:T(8,128)(2,1)S(1)}, u32[]{:S(2)}, u32[]{:S(2)}) %collective-permute-start.5) | collective-permute-done | bytes 860192 | tf_op jit(solution)/shard_map/ppermute | solution.py:447
  84.3 25.7 %collective-permute-done.7.refs_6_ = bf16[3,32,4480]{2,1,0:T(8,128)(2,1)S(1)} collective-permute-done((bf16[3,32,4480]{2,1,0:T(8,128)(2,1)S(1)}, bf16[3,32,4480]{2,1,0:T(8,128)(2,1)S(1)}, u32[]{:S(2)}, u32[]{:S(2)}) %collective-permute-start.7) | collective-permute-done | bytes 860192 | tf_op jit(solution)/shard_map/ppermute | solution.py:447
  121.2 7.3 %place_rows.1 = bf16[1024,4480]{1,0:T(8,128)(2,1)} custom-call(s32[3]{0:T(128)S(1)} %pad_add_fusion.where.refs_0_, bf16[2,256,4352]{2,1,0:T(8,128)(2,1)} %refs_0_.6, bf16[2,256,32]{2,1,0:T(8,128)(2,1)S(1)} %copy.138.refs_1_.refs_2_, bf16[3,32,4480]{2,1,0:T(8,128)(2,1)S(1)} %stack.122.refs_3_.refs_1_.refs_2_, ...), custom_call_target="tpu_custom_call" | custom-call | flops 1100000000 | bytes 1000000 | tf_op jit(solution)/shard_map/place_rows/pallas_call | solution.py:562
  137.3 8.2 %conv_states.2 = (bf16[2,256,2304]{2,1,0:T(8,128)(2,1)S(1)}, f32[2,256,128]{2,1,0:T(8,128)S(1)}, f32[2,256,128]{2,1,0:T(8,128)S(1)}, f32[2,32,256]{2,1,0:T(8,128...) custom-call(bf16[2,256,2432]{2,1,0:T(8,128)(2,1)} %bitcast.151, ...), custom_call_target="tpu_custom_call" | custom-call | flops 2200000000 | bytes 2000000 | tf_op jit(solution)/shard_map/conv_states/pallas_call | solution.py:411
  171.0 11.7 %mix_within.2.refs_3_.refs_1_ = f32[2,256,2048]{2,1,0:T(8,128)} custom-call(bf16[2,256,2304]{2,1,0:T(8,128)(2,1)S(1)} %get-tuple-element.92.refs_0_.refs_2_.refs_6_.refs_1_.refs_3_, f32[2,256,128]{2,1,0:T(8,128)S(1)} %copy-done.56, f32[2,256,128]{2,1,0:T(8,128)S(1)} %copy-done.27, f32[2,32,256]{2,1,0:T(8,128)S(1)} %copy-done.96, ...), custom_call_target="tpu_custom_call" | custom-call | flops 3300000000 | bytes 3000000 | tf_op jit(solution)/shard_map/mix_within/pallas_call | solution.py:411
  182.7 7.3 %collective-permute-done.13.refs_1_ = bf16[144,2048]{1,0:T(8,128)(2,1)} collective-permute-done((bf16[144,2048]{1,0:T(8,128)(2,1)}, bf16[144,2048]{1,0:T(8,128)(2,1)}, u32[]{:S(2)}, u32[]{:S(2)}) %collective-permute-start.13) | collective-permute-done | bytes 589856 | tf_op jit(solution)/shard_map/ppermute | solution.py:484
  224.2 9.5 %conv_states.3 = (bf16[2,256,2304]{2,1,0:T(8,128)(2,1)}, f32[2,256,128]{2,1,0:T(8,128)S(1)}, f32[2,256,128]{2,1,0:T(8,128)S(1)}, f32[2,32,256]{2,1,0:T(8,128)S(1...) custom-call(bf16[2,256,2432]{2,1,0:T(8,128)(2,1)} %bitcast.174, ...), custom_call_target="tpu_custom_call" | custom-call | flops 2200000000 | bytes 2000000 | tf_op jit(solution)/shard_map/conv_states/pallas_call | solution.py:411
  258.1 12.0 %mix_within.3.refs_3_.refs_1_ = f32[2,256,2048]{2,1,0:T(8,128)} custom-call(bf16[2,256,2304]{2,1,0:T(8,128)(2,1)S(1)} %copy-done.6, f32[2,256,128]{2,1,0:T(8,128)S(1)} %copy-done.90, f32[2,256,128]{2,1,0:T(8,128)S(1)} %copy-done.43, f32[2,32,256]{2,1,0:T(8,128)S(1)} %copy-done.93, f32[2,256,128]{2,1,0:T(8,128)S(1)} %copy-done.5, ...), custom_call_target="tpu_custom_call" | custom-call | flops 3300000000 | bytes 3000000 | tf_op jit(solution)/shard_map/mix_within/pallas_call | solution.py:411
  288.3 11.4 %gate_back.2 = (bf16[2,256,2048]{2,1,0:T(8,128)(2,1)}, bf16[2,256,3072]{2,1,0:T(8,128)(2,1)}, bf16[2,144,2048]{2,1,0:T(8,128)(2,1)S(1)}, f32[2,256,128]{2,1,0:T(...) custom-call(bf16[2,256,2048]{2,1,0:T(8,128)(2,1)} %bitcast.160, bf16[2,256,1024]{2,1,0:T(8,128)(2,1)S(1)} %copy-done.7, ...), custom_call_target="tpu_custom_call" | custom-call | flops 3024999936 | bytes 2750000 | tf_op jit(solution)/shard_map/gate_back/pallas_call | solution.py:411
  307.5 8.6 %wide_grads.1.refs_10_ = bf16[1024,4096]{1,0:T(8,128)(2,1)} custom-call(bf16[512,1024]{1,0:T(8,128)(2,1)S(1)} %bitcast.121, bf16[512,2048]{1,0:T(8,128)(2,1)S(1)} %bitcast.126, bf16[512,3072]{1,0:T(8,128)(2,1)} %bitcast.148, bf16[144,2048]{1,0:T(8,128)(2,1)S(1)} %join_states.6.refs_3_), custom_call_target="tpu_custom_call" | custom-call | flops 2750000128 | bytes 2500000 | tf_op jit(solution)/shard_map/wide_grads/pallas_call | solution.py:715
  325.6 17.6 %mix_within_back.2 = (bf16[2,256,2048]{2,1,0:T(8,128)(2,1)S(1)}, f32[2,256,256]{2,1,0:T(8,128)S(1)}, f32[2,256,128]{2,1,0:T(8,128)S(1)}) custom-call(bf16[2,256,2048]{2,1,0:T(8,128)(2,1)} %get-tuple-element.109.refs_0_.refs_2_, bf16[2,256,2304]{2,1,0:T(8,128)(2,1)} %get-tuple-element.99.refs_0_.refs_2_.refs_6_.refs_1_.refs_3_, ...), custom_call_target="tpu_custom_call" | custom-call | flops 4674999808 | bytes 4250000 | tf_op jit(solution)/shard_map/mix_within_back/pallas_call | solution.py:411
  346.1 10.6 %collective-permute-done.24.refs_1_ = bf16[144,2048]{1,0:T(8,128)(2,1)S(1)} collective-permute-done((bf16[144,2048]{1,0:T(8,128)(2,1)}, bf16[144,2048]{1,0:T(8,128)(2,1)S(1)}, u32[]{:S(2)}, u32[]{:S(2)}) %collective-permute-start.24) | collective-permute-done | bytes 589856 | tf_op jit(solution)/shard_map/ppermute | solution.py:484
  359.0 19.1 %conv_back.2 = (bf16[2,256,2432]{2,1,0:T(8,128)(2,1)}, f32[2,8,2304]{2,1,0:T(8,128)S(1)}, f32[8,2304]{1,0:T(8,128)S(1)}, f32[8,128]{1,0:T(8,128)S(1)}) custom-call(s32[3]{0:T(128)S(1)} %pad_add_fusion.where.refs_0_, bf16[2,256,2048]{2,1,0:T(8,128)(2,1)} %copy-done.31, bf16[2,256,2048]{2,1,0:T(8,128)(2,1)} %get-tuple-element.109.refs_0_.refs_2_, ...), custom_call_target="tpu_custom_call" | custom-call | flops 4674999808 | bytes 4250000 | tf_op jit(solution)/shard_map/conv_back/pallas_call | solution.py:411
  404.6 11.5 %gate_back.3 = (bf16[2,256,2048]{2,1,0:T(8,128)(2,1)}, bf16[2,256,3072]{2,1,0:T(8,128)(2,1)}, bf16[2,144,2048]{2,1,0:T(8,128)(2,1)S(1)}, f32[2,256,128]{2,1,0:T(...) custom-call(bf16[2,256,2048]{2,1,0:T(8,128)(2,1)} %bitcast.159, bf16[2,256,1024]{2,1,0:T(8,128)(2,1)S(1)} %fusion.58.refs_1_, ...), custom_call_target="tpu_custom_call" | custom-call | flops 3024999936 | bytes 2750000 | tf_op jit(solution)/shard_map/gate_back/pallas_call | solution.py:411
  429.0 17.6 %mix_within_back.3 = (bf16[2,256,2048]{2,1,0:T(8,128)(2,1)S(1)}, f32[2,256,256]{2,1,0:T(8,128)S(1)}, f32[2,256,128]{2,1,0:T(8,128)S(1)}) custom-call(bf16[2,256,2048]{2,1,0:T(8,128)(2,1)} %get-tuple-element.125.refs_0_.refs_2_, bf16[2,256,2304]{2,1,0:T(8,128)(2,1)} %copy-done.2, f32[2,256,128]{2,1,0:T(8,128)S(1)} %copy-done.57, ...), custom_call_target="tpu_custom_call" | custom-call | flops 4674999808 | bytes 4250000 | tf_op jit(solution)/shard_map/mix_within_back/pallas_call | solution.py:411
  446.6 22.8 %collective-permute-done.31.refs_0_ = bf16[144,2048]{1,0:T(8,128)(2,1)S(1)} collective-permute-done((bf16[144,2048]{1,0:T(8,128)(2,1)S(1)}, bf16[144,2048]{1,0:T(8,128)(2,1)S(1)}, u32[]{:S(2)}, u32[]{:S(2)}) %collective-permute-start.31) | collective-permute-done | bytes 589856 | tf_op jit(solution)/shard_map/ppermute | solution.py:484
  476.9 8.3 %first_grads.1 = (bf16[4,128,1024]{2,1,0:T(8,128)(2,1)S(1)}, bf16[4,128,1024]{2,1,0:T(8,128)(2,1)S(1)}, bf16[4,128,1024]{2,1,0:T(8,128)(2,1)S(1)}, bf16[4,128,1024]{2,1,0:T(8,128)(2,1)S(1)}) custom-call(bf16[1536,512]{1,0:T(8,128)(2,1)} %copy-done.33, bf16[1536,512]{1,0:T(8,128)(2,1)} %collective-permute-done.35.refs_1_.refs_2_, ...), custom_call_target="tpu_custom_call" | custom-call | flops 2750000128 | bytes 2500000 | tf_op jit(solution)/shard_map/first_grads/pallas_call | solution.py:434
  488.2 18.7 %conv_back.3 = (bf16[2,256,2432]{2,1,0:T(8,128)(2,1)}, f32[2,8,2304]{2,1,0:T(8,128)S(1)}, f32[8,2304]{1,0:T(8,128)S(1)}, f32[8,128]{1,0:T(8,128)S(1)}) custom-call(s32[3]{0:T(128)S(1)} %pad_add_fusion.where.refs_0_, bf16[2,256,2048]{2,1,0:T(8,128)(2,1)} %copy-done.11, bf16[2,256,2048]{2,1,0:T(8,128)(2,1)} %get-tuple-element.125.refs_0_.refs_2_, ...), custom_call_target="tpu_custom_call" | custom-call | flops 4674999808 | bytes 4250000 | tf_op jit(solution)/shard_map/conv_back/pallas_call | solution.py:411
  512.2 7.6 %collective-permute-start.39 = (bf16[4,128,1024]{2,1,0:T(8,128)(2,1)S(1)}, bf16[4,128,1024]{2,1,0:T(8,128)(2,1)S(1)}, u32[]{:S(2)}, u32[]{:S(2)}) collective-permute-start(bf16[4,128,1024]{2,1,0:T(8,128)(2,1)S(1)} %copy-done.39), channel_id=1, source_target_pairs={{0,4},{1,5},{2,6},{3,7},{4,0},{5,1},{6,2},{7,3},{8,12},{9,13},{10,... | collective-permute-start | bytes 3145736 | tf_op jit(solution)/shard_map/ppermute | solution.py:447
  534.0 15.3 %collective-permute-done.56.refs_1_ = bf16[4,32,2432]{2,1,0:T(8,128)(2,1)S(1)} collective-permute-done((bf16[4,32,2432]{2,1,0:T(8,128)(2,1)S(1)}, bf16[4,32,2432]{2,1,0:T(8,128)(2,1)S(1)}, u32[]{:S(2)}, u32[]{:S(2)}) %collective-permute-start.56) | collective-permute-done | bytes 622624 | tf_op jit(solution)/shard_map/ppermute | solution.py:447
  549.3 8.7 %collective-permute-start.40 = (bf16[4,128,1024]{2,1,0:T(8,128)(2,1)S(1)}, bf16[4,128,1024]{2,1,0:T(8,128)(2,1)S(1)}, u32[]{:S(2)}, u32[]{:S(2)}) collective-permute-start(bf16[4,128,1024]{2,1,0:T(8,128)(2,1)S(1)} %copy-done.37), channel_id=1, source_target_pairs={{0,6},{1,7},{2,4},{3,5},{4,2},{5,3},{6,0},{7,1},{8,14},{9,15},{10,... | collective-permute-start | bytes 3145736 | tf_op jit(solution)/shard_map/ppermute | solution.py:447
  564.7 29.7 %collective-permute-done.58.refs_3_ = bf16[4,32,2432]{2,1,0:T(8,128)(2,1)S(1)} collective-permute-done((bf16[4,32,2432]{2,1,0:T(8,128)(2,1)S(1)}, bf16[4,32,2432]{2,1,0:T(8,128)(2,1)S(1)}, u32[]{:S(2)}, u32[]{:S(2)}) %collective-permute-start.58) | collective-permute-done | bytes 622624 | tf_op jit(solution)/shard_map/ppermute | solution.py:447
  622.7 14.8 %collective-permute-done.50.refs_2_ = bf16[4,32,2432]{2,1,0:T(8,128)(2,1)} collective-permute-done((bf16[4,32,2432]{2,1,0:T(8,128)(2,1)}, bf16[4,32,2432]{2,1,0:T(8,128)(2,1)}, u32[]{:S(2)}, u32[]{:S(2)}) %collective-permute-start.50) | collective-permute-done | bytes 622624 | tf_op jit(solution)/shard_map/ppermute | solution.py:447
  (506 shorter events, 360.1 us)
Async XLA Ops:
  7.2 197.1 %all-gather.5.cloned.1.call-start = ((), (), s32[]{:S(2)}) async-start(), calls=%async_computation.1 | async-start | bytes 13787136 | tf_op jit(solution)/shard_map/all_gather | solution.py:1004
  47.5 204.5 %all-gather.7.cloned.1.call-start = ((), (), s32[]{:S(2)}) async-start(), calls=%async_computation.2 | async-start | bytes 4325376 | tf_op jit(solution)/shard_map/all_gather | solution.py:1009
  55.4 28.9 %collective-permute-start.6 = (bf16[3,32,4480]{2,1,0:T(8,128)(2,1)S(1)}, bf16[3,32,4480]{2,1,0:T(8,128)(2,1)S(1)}, u32[]{:S(2)}, u32[]{:S(2)}) collective-permute-start(bf16[3,32,4480]{2,1,0:T(8,128)(2,1)S(1)} %stack.122.refs_3_.refs_1_.refs_2_), channel_id=1, source_target_pairs={{0,4},{1,5},{2,6},{3,7},{4,0},{5,1},{6,2},{7,3},{8,12},{9,13},{10,... | collective-permute-start | bytes 2580488 | tf_op jit(solution)/shard_map/ppermute | solution.py:447
  56.9 53.1 %collective-permute-start.7 = (bf16[3,32,4480]{2,1,0:T(8,128)(2,1)S(1)}, bf16[3,32,4480]{2,1,0:T(8,128)(2,1)S(1)}, u32[]{:S(2)}, u32[]{:S(2)}) collective-permute-start(bf16[3,32,4480]{2,1,0:T(8,128)(2,1)S(1)} %stack.122.refs_3_.refs_1_.refs_2_), channel_id=1, source_target_pairs={{0,6},{1,7},{2,4},{3,5},{4,2},{5,3},{6,0},{7,1},{8,14},{9,15},{10,... | collective-permute-start | bytes 2580488 | tf_op jit(solution)/shard_map/ppermute | solution.py:447
  117.1 490.6 %reduce-scatter.2.cloned.1.call-start = ((), (), s32[]{:S(2)}) async-start(), calls=%async_computation.3 | async-start | bytes 8650752 | tf_op jit(solution)/shard_map/reduce_scatter | solution.py:1106
  317.0 376.3 %all-gather.9.cloned.1.call-start = ((), (), s32[]{:S(2)}) async-start(), calls=%async_computation.4 | async-start | bytes 2359296 | tf_op jit(solution)/shard_map/all_gather | solution.py:1187
  317.0 29.1 %collective-permute-start.23 = (bf16[144,2048]{1,0:T(8,128)(2,1)}, bf16[144,2048]{1,0:T(8,128)(2,1)S(1)}, u32[]{:S(2)}, u32[]{:S(2)}) collective-permute-start(bf16[144,2048]{1,0:T(8,128)(2,1)} %copy-done.29), channel_id=1, source_target_pairs={{6,0},{7,1},{14,8},{15,9},{22,16},{23,17},{30,24},{31,25}} | collective-permute-start | bytes 1769480 | tf_op jit(solution)/shard_map/ppermute | solution.py:484
  318.3 38.4 %collective-permute-start.24 = (bf16[144,2048]{1,0:T(8,128)(2,1)}, bf16[144,2048]{1,0:T(8,128)(2,1)S(1)}, u32[]{:S(2)}, u32[]{:S(2)}) collective-permute-start(bf16[144,2048]{1,0:T(8,128)(2,1)} %copy-done.29), channel_id=1, source_target_pairs={{4,0},{5,1},{6,2},{7,3},{12,8},{13,9},{14,10},{15,11},{20,16},{21,... | collective-permute-start | bytes 1769480 | tf_op jit(solution)/shard_map/ppermute | solution.py:484
  319.6 37.1 %collective-permute-start.25 = (bf16[144,2048]{1,0:T(8,128)(2,1)}, bf16[144,2048]{1,0:T(8,128)(2,1)S(1)}, u32[]{:S(2)}, u32[]{:S(2)}) collective-permute-start(bf16[144,2048]{1,0:T(8,128)(2,1)} %copy-done.29), channel_id=1, source_target_pairs={{2,0},{3,1},{4,2},{5,3},{6,4},{7,5},{10,8},{11,9},{12,10},{13,11},... | collective-permute-start | bytes 1769480 | tf_op jit(solution)/shard_map/ppermute | solution.py:484
  416.2 60.7 %collective-permute-start.36 = (bf16[512,3072]{1,0:T(8,128)(2,1)}, bf16[512,3072]{1,0:T(8,128)(2,1)}, u32[]{:S(2)}, u32[]{:S(2)}) collective-permute-start(bf16[512,3072]{1,0:T(8,128)(2,1)} %bitcast.180), channel_id=1, source_target_pairs={{0,1},{1,0},{2,3},{3,2},{4,5},{5,4},{6,7},{7,6},{8,9},{9,8},{10,11... | collective-permute-start | bytes 9437192 | tf_op jit(solution)/shard_map/ppermute | solution.py:447
  416.7 60.1 %collective-permute-start.35 = (bf16[1536,512]{1,0:T(8,128)(2,1)S(1)}, bf16[1536,512]{1,0:T(8,128)(2,1)}, u32[]{:S(2)}, u32[]{:S(2)}) collective-permute-start(bf16[1536,512]{1,0:T(8,128)(2,1)S(1)} %copy-done.72), channel_id=1, source_target_pairs={{0,1},{1,0},{2,3},{3,2},{4,5},{5,4},{6,7},{7,6},{8,9},{9,8},{10,11... | collective-permute-start | bytes 4718600 | tf_op jit(solution)/shard_map/ppermute | solution.py:447
  425.1 44.4 %collective-permute-start.31 = (bf16[144,2048]{1,0:T(8,128)(2,1)S(1)}, bf16[144,2048]{1,0:T(8,128)(2,1)S(1)}, u32[]{:S(2)}, u32[]{:S(2)}) collective-permute-start(bf16[144,2048]{1,0:T(8,128)(2,1)S(1)} %join_states.7), channel_id=1, source_target_pairs={{6,0},{7,1},{14,8},{15,9},{22,16},{23,17},{30,24},{31,25}} | collective-permute-start | bytes 1769480 | tf_op jit(solution)/shard_map/ppermute | solution.py:484
  426.4 50.1 %collective-permute-start.32 = (bf16[144,2048]{1,0:T(8,128)(2,1)S(1)}, bf16[144,2048]{1,0:T(8,128)(2,1)S(1)}, u32[]{:S(2)}, u32[]{:S(2)}) collective-permute-start(bf16[144,2048]{1,0:T(8,128)(2,1)S(1)} %join_states.7), channel_id=1, source_target_pairs={{4,0},{5,1},{6,2},{7,3},{12,8},{13,9},{14,10},{15,11},{20,16},{21,... | collective-permute-start | bytes 1769480 | tf_op jit(solution)/shard_map/ppermute | solution.py:484
  427.7 48.8 %collective-permute-start.33 = (bf16[144,2048]{1,0:T(8,128)(2,1)S(1)}, bf16[144,2048]{1,0:T(8,128)(2,1)S(1)}, u32[]{:S(2)}, u32[]{:S(2)}) collective-permute-start(bf16[144,2048]{1,0:T(8,128)(2,1)S(1)} %join_states.7), channel_id=1, source_target_pairs={{2,0},{3,1},{4,2},{5,3},{6,4},{7,5},{10,8},{11,9},{12,10},{13,11},... | collective-permute-start | bytes 1769480 | tf_op jit(solution)/shard_map/ppermute | solution.py:484
  510.5 84.2 %collective-permute-start.38 = (bf16[4,128,1024]{2,1,0:T(8,128)(2,1)S(1)}, bf16[4,128,1024]{2,1,0:T(8,128)(2,1)S(1)}, u32[]{:S(2)}, u32[]{:S(2)}) collective-permute-start(bf16[4,128,1024]{2,1,0:T(8,128)(2,1)S(1)} %copy-done.41), channel_id=1, source_target_pairs={{0,2},{1,3},{2,0},{3,1},{4,6},{5,7},{6,4},{7,5},{8,10},{9,11},{10,... | collective-permute-start | bytes 3145736 | tf_op jit(solution)/shard_map/ppermute | solution.py:447
  512.2 82.6 %collective-permute-start.39 = (bf16[4,128,1024]{2,1,0:T(8,128)(2,1)S(1)}, bf16[4,128,1024]{2,1,0:T(8,128)(2,1)S(1)}, u32[]{:S(2)}, u32[]{:S(2)}) collective-permute-start(bf16[4,128,1024]{2,1,0:T(8,128)(2,1)S(1)} %copy-done.39), channel_id=1, source_target_pairs={{0,4},{1,5},{2,6},{3,7},{4,0},{5,1},{6,2},{7,3},{8,12},{9,13},{10,... | collective-permute-start | bytes 3145736 | tf_op jit(solution)/shard_map/ppermute | solution.py:447
  521.3 75.0 %collective-permute-start.47 = (bf16[512,2432]{1,0:T(8,128)(2,1)}, bf16[512,2432]{1,0:T(8,128)(2,1)}, u32[]{:S(2)}, u32[]{:S(2)}) collective-permute-start(bf16[512,2432]{1,0:T(8,128)(2,1)} %bitcast.153), channel_id=1, source_target_pairs={{0,1},{1,0},{2,3},{3,2},{4,5},{5,4},{6,7},{7,6},{8,9},{9,8},{10,11... | collective-permute-start | bytes 7471112 | tf_op jit(solution)/shard_map/ppermute | solution.py:447
  527.2 30.9 %collective-permute-start.57 = (bf16[4,32,2432]{2,1,0:T(8,128)(2,1)S(1)}, bf16[4,32,2432]{2,1,0:T(8,128)(2,1)S(1)}, u32[]{:S(2)}, u32[]{:S(2)}) collective-permute-start(bf16[4,32,2432]{2,1,0:T(8,128)(2,1)S(1)} %get-tuple-element.158), channel_id=1, source_target_pairs={{0,4},{1,5},{2,6},{3,7},{4,0},{5,1},{6,2},{7,3},{8,12},{9,13},{10,... | collective-permute-start | bytes 1867784 | tf_op jit(solution)/shard_map/ppermute | solution.py:447
  549.3 45.5 %collective-permute-start.40 = (bf16[4,128,1024]{2,1,0:T(8,128)(2,1)S(1)}, bf16[4,128,1024]{2,1,0:T(8,128)(2,1)S(1)}, u32[]{:S(2)}, u32[]{:S(2)}) collective-permute-start(bf16[4,128,1024]{2,1,0:T(8,128)(2,1)S(1)} %copy-done.37), channel_id=1, source_target_pairs={{0,6},{1,7},{2,4},{3,5},{4,2},{5,3},{6,0},{7,1},{8,14},{9,15},{10,... | collective-permute-start | bytes 3145736 | tf_op jit(solution)/shard_map/ppermute | solution.py:447
  558.1 36.3 %collective-permute-start.58 = (bf16[4,32,2432]{2,1,0:T(8,128)(2,1)S(1)}, bf16[4,32,2432]{2,1,0:T(8,128)(2,1)S(1)}, u32[]{:S(2)}, u32[]{:S(2)}) collective-permute-start(bf16[4,32,2432]{2,1,0:T(8,128)(2,1)S(1)} %get-tuple-element.159), channel_id=1, source_target_pairs={{0,6},{1,7},{2,4},{3,5},{4,2},{5,3},{6,0},{7,1},{8,14},{9,15},{10,... | collective-permute-start | bytes 1867784 | tf_op jit(solution)/shard_map/ppermute | solution.py:447
  604.3 33.2 %collective-permute-start.50 = (bf16[4,32,2432]{2,1,0:T(8,128)(2,1)}, bf16[4,32,2432]{2,1,0:T(8,128)(2,1)}, u32[]{:S(2)}, u32[]{:S(2)}) collective-permute-start(bf16[4,32,2432]{2,1,0:T(8,128)(2,1)} %get-tuple-element.148), channel_id=1, source_target_pairs={{0,4},{1,5},{2,6},{3,7},{4,0},{5,1},{6,2},{7,3},{8,12},{9,13},{10,... | collective-permute-start | bytes 1867784 | tf_op jit(solution)/shard_map/ppermute | solution.py:447
  607.4 30.6 %collective-permute-start.51 = (bf16[4,32,2432]{2,1,0:T(8,128)(2,1)}, bf16[4,32,2432]{2,1,0:T(8,128)(2,1)}, u32[]{:S(2)}, u32[]{:S(2)}) collective-permute-start(bf16[4,32,2432]{2,1,0:T(8,128)(2,1)} %get-tuple-element.149), channel_id=1, source_target_pairs={{0,6},{1,7},{2,4},{3,5},{4,2},{5,3},{6,0},{7,1},{8,14},{9,15},{10,... | collective-permute-start | bytes 1867784 | tf_op jit(solution)/shard_map/ppermute | solution.py:447
  617.1 28.1 %collective-permute-start.60 = (bf16[1,32,2432]{2,1,0:T(8,128)(2,1)S(1)}, bf16[1,32,2432]{2,1,0:T(8,128)(2,1)S(1)}, u32[]{:S(2)}, u32[]{:S(2)}) collective-permute-start(bf16[1,32,2432]{2,1,0:T(8,128)(2,1)S(1)} %get-tuple-element.163), channel_id=1, source_target_pairs={{0,8},{8,0},{16,24},{24,16},{1,9},{9,1},{17,25},{25,17},{2,10},{10... | collective-permute-start | bytes 466952 | tf_op jit(solution)/shard_map/ppermute | solution.py:447
  617.2 40.9 %collective-permute-start.41 = (bf16[2,128,1024]{2,1,0:T(8,128)(2,1)S(1)}, bf16[2,128,1024]{2,1,0:T(8,128)(2,1)S(1)}, u32[]{:S(2)}, u32[]{:S(2)}) collective-permute-start(bf16[2,128,1024]{2,1,0:T(8,128)(2,1)S(1)} %copy-done.78), channel_id=1, source_target_pairs={{0,16},{8,24},{16,0},{24,8},{1,17},{9,25},{17,1},{25,9},{2,18},{10... | collective-permute-start | bytes 1572872 | tf_op jit(solution)/shard_map/ppermute | solution.py:447
  (166 other events, 1776.1 us)
Sparse Core Ops, SparseCore 0:
  47.7 117.4 all-gather.4
  168.1 62.6 all-gather.6
  317.1 155.9 reduce-scatter.1
  609.5 42.2 all-gather.8

commit v4 on v3

--- a/solution.py
+++ b/solution.py
@@ -424,6 +424,30 @@
 def cost(micros):
     micros = micros * SCALE
     return pl.CostEstimate(flops=int(micros * 1.1e9), bytes_accessed=int(micros * 1e6), transcendentals=0)
+
+
+def edge_kernel(grad, more, out):
+    size, channels = grad.shape[1], more.shape[2]
+    out[0, :, channels:] = grad[0, :, channels:]
+    last = jnp.concatenate([jnp.zeros((size - EDGE, channels), F32), more[0].astype(F32)], axis=0)
+    out[0, :, 0:channels] = (grad[0, :, 0:channels].astype(F32) + last).astype(BF16)
+
+
+def with_edges(grad, more, after):
+    batch, width, wide = grad.shape
+    size = 2 * EDGE
+    block = pl.BlockSpec((1, size, wide), lambda b: (b, width // size - 1, 0))
+    return pl.pallas_call(
+        without(edge_kernel, 2, len(after)),
+        grid=(batch,),
+        in_specs=[block, pl.BlockSpec((1,) + more.shape[1:], lambda b: (b, 0, 0))] + [pl.BlockSpec(memory_space=pl.ANY)] * len(after),
+        out_specs=block,
+        out_shape=jax.ShapeDtypeStruct(grad.shape, grad.dtype),
+        input_output_aliases={0: 0},
+        compiler_params=pltpu.CompilerParams(vmem_limit_bytes=VMEM),
+        cost_estimate=cost(1.0),
+        name="with_edges",
+    )(grad, more, *after)
 
 
 def whole_call(kernel, arrays, outs, micros, name, at=None, after=(), scratch=()):
@@ -988,7 +1012,7 @@
         if direct:
             share_in, share_out = model // (groups * peers), inner // (groups * peers)
             if layer == 0:
-                mix_z = from_along_z(take_share(in_weight, dt_weight, 0, all_columns, here, share_in, peers, ()), groups, (by_partner,))
+                mix_z = from_along_z(take_share(in_weight, dt_weight, 0, all_columns, here, share_in, peers, ()), groups)
                 whole = fetched_by_all(
                     in_weight, dt_weight, 0, all_columns, here, groups, chips, mix_z, (norm_all, taps_all, rates_all, skip_all, gain_all)
                 )
@@ -1047,14 +1071,14 @@
             ],
             [((EDGE + width, channels), F32)], "conv_states", 8.0, after=sent,
         )
-        got, other, _ = exchange(state, here, 1)
+        got, other, joined_state = exchange(state, here, 1)
         (part,) = call(
             functools.partial(intra_kernel, inner, heads), batch,
             [(act, 0), (size, 0), (sums, 0), (sums_t, 0), (marks, 0), (row_marks, 0), (skip, 1), (spread, 1)],
             [((batch, width, inner), F32, 0)],
-            [((width, width), F32), ((width, inner), BF16)], "mix_within", 12.0,
+            [((width, width), F32), ((width, inner), BF16)], "mix_within", 12.0, after=(joined_state,),
         )
-        before, partner = entered(got, (part,))
+        before, partner = entered(got, (part, gate, w_out) if direct else (part,))
         mixed, gated, entering = call(
             functools.partial(post_kernel, inner), batch,
             [
@@ -1096,15 +1120,11 @@
         got, other, joined_state = exchange(d_state, here, 0)
         both = d_gate.reshape(rows, inner + model)
         d_gate = both[:, :inner]
-        started, arrived = (), ()
+        started, arrived, ordered = (), (), ()
         if direct:
             big, small = inner // (groups * peers), model // (groups * peers)
             mine, theirs = turned
             both_other = swap(both, "seq", 1) if layer == 0 else None
-            if layer > 0:
-                wide = wide_grads(low, gated, both, groups, (joined_state,))
-                scattered.append(lax.psum_scatter(wide, ("fsdp", "seq"), scatter_dimension=0, tiled=True))
-                started = (wide,)
         else:
             out_share = reduced(dot_tn(gated, grad_low).astype(BF16))
         d_stepped, d_pair, d_total = call(
@@ -1116,19 +1136,28 @@
             [((batch, width, inner), BF16, 0), ((batch, width, 2 * states), F32, 0), ((batch, width, LANES), F32, 0)],
             [
                 ((width, width), F32), ((width, width), F32), ((width, inner), BF16), ((LANES, width), F32), ((width, LANES), F32),
-            ], "mix_within_back", 17.0, after=started,
+            ], "mix_within_back", 17.0, after=(joined_state,),
         )
         before, partner = entered(got, (d_stepped,))
+        if direct and layer > 0:
+            wide = wide_grads(low, gated, both, groups, (before,))
+            scattered.append(lax.psum_scatter(wide, ("fsdp", "seq"), scatter_dimension=0, tiled=True))
+            arrived = (wide,)
         if direct and layer == 0:
             first_blocks = whole_call(
                 functools.partial(first_grads_kernel, groups, chips, inner), [mine, theirs, both, both_other],
                 [((groups, big + inner // model * small, model), BF16)] * chips, 10.0, "first_grads", after=(before,),
             )
             arrived = tuple(first_blocks)
+            first_share, halved = halved_sums(plane_parts(first_blocks), groups)
+            ordered = halved
             for later in waiting:
-                share, _ = halved_sums(plane_parts(later((first_blocks[0],))), groups)
+                blocks = later((first_blocks[0],))
+                share, more = halved_sums(plane_parts(blocks), groups)
+                ordered += (blocks[0],)
+                halved += more
                 second_shares.append(laid([share], model, ()))
-            first_share, halved = halved_sums(plane_parts(first_blocks), groups)
+            mine_a, other_a = spread_in_plane(first_share, chips)
         d_mixed_in, d_edge, tap_grads, head_grads = call(
             functools.partial(conv_back_kernel, inner), batch,
             [
@@ -1143,8 +1172,7 @@
             [((EDGE + width, channels), F32), ((3, width + 2 * EDGE, 256), F32)], "conv_back", 17.0, here, arrived,
         )
         from_next = lax.ppermute(d_edge.astype(BF16), "seq", [(i + 1, i) for i in range(peers - 1)])
-        tail = (d_mixed_in[:, width - EDGE:, :channels].astype(F32) + from_next.astype(F32)).astype(BF16)
-        grad_mixed = lax.dynamic_update_slice(d_mixed_in, tail, (0, width - EDGE, 0)).reshape(rows, channels + LANES)
+        grad_mixed = with_edges(d_mixed_in, from_next, ordered).reshape(rows, channels + LANES)
         grad_rows = dot_nt(d_gate, w_gate) + dot_nt(grad_mixed, w_mix)
         grad_rows = grad_rows.reshape(batch, width, model)
         scaled = grad_rows * norm_all[layer]
@@ -1164,7 +1192,7 @@
                 started = (operands[3], operands[5])
             else:
                 got = plane_parts(whole_call(kernel, operands, outs, 6.0, "second_grads", here, halved))
-                second_shares.append(layer_sums(got, groups, model, (stream, grad_stream)))
+                second_shares.append(layer_sums(got, groups, model, (stream, grad_stream) + tuple(mine_a)))
         else:
             mixed_grad = dot_tn(low, grad_mixed)
             in_share = reduced(jnp.concatenate([dot_tn(low, d_gate).astype(BF16), mixed_grad[:, :channels].astype(BF16)], axis=1))
@@ -1181,7 +1209,6 @@
             ]
             collected.append(jnp.concatenate(small_grads, axis=1))
     if direct:
-        mine_a, other_a = spread_in_plane(first_share, chips)
         second_share = stacked(second_shares[::-1]).reshape(-1, model)
         held = [stacked([share], (first_blocks[0],))[0] for share in scattered]
         scattered = [lax.all_gather(share, "seq", axis=0, tiled=True) for share in held]

time: 724 us -> 696 us (0.961)
  waiting for transfers between devices: 246 us -> 207 us
  local copies, waits for them, and re-layouts: 49.4 us -> 58 us
    ppermute x12, waiting for transfers between devices: 54.6 us -> 33.4 us  [exchange(): got.append(lax.ppermute(joined, 'seq', route))]
    ppermute x48, waiting for transfers between devices: 188 us -> 171 us  [swap(): lax.ppermute(x, axis, [(i, i ^ bits) for i in range(lax.axis_size(axis))])]
    unnamed x244 -> x336, local copies, waits for them, and re-layouts: 42.4 us -> 48.2 us
  transfers between devices with their start and end apart: 69 -> 69, of which waited for: 34 -> 30; matrix products, arithmetic and copies ran while one was open for 11% -> 12% of each run, Pallas kernels for 26% -> 28%
where the time goes in v4:
time: 696 us; the launch traced here: 686 us
  Pallas kernels  227 us (33%)
  waiting for transfers between devices  207 us (30%)
  starting transfers between devices  107 us (15%)
  matrix products  61.4 us (9%)
  local copies, waits for them, and re-layouts  58 us (8%)
  between operations  16.3 us (2%)
  other arithmetic  9.94 us (1%)
    ppermute x48, waiting for transfers between devices, swap(): lax.ppermute(x, axis, [(i, i ^ bits) for i in range(lax.axis_size(axis))])  171 us
    pallas_call x12, Pallas kernels, call(): pl.pallas_call(without(kernel, len(arrays), len(after)), grid=(batch,), i...  150 us
    ppermute x48, starting transfers between devices, swap(): lax.ppermute(x, axis, [(i, i ^ bits) for i in range(lax.axis_size(axis))])  69.1 us
    unnamed x336, local copies, waits for them, and re-layouts  48.2 us
    pallas_call x30, Pallas kernels, whole_call(): pl.pallas_call(without(kernel, len(arrays), len(after)), in_specs=in_spec...  45.9 us
    dot_general x6, matrix products, dot(): return jnp.dot(a, b, preferred_element_type=F32)  34.1 us
    ppermute x12, waiting for transfers between devices, exchange(): got.append(lax.ppermute(joined, 'seq', route))  33.4 us
    ppermute x12, starting transfers between devices, exchange(): got.append(lax.ppermute(joined, 'seq', route))  28.7 us
  transfers between devices with their start and end apart: 69, of which 30 were waited for; matrix products, arithmetic and copies ran while one was open for 12% of the time, Pallas kernels for 28%

profile of v4, /device:TPU:0, one launch (start us, length us, event | category | flops | bytes accessed | tf_op | source)
XLA Modules:
  0.0 685.9 jit_solution(2125471481544241612)
XLA Ops:
  16.7 9.6 %collective-permute-done.2.refs_0_ = bf16[32,4480]{1,0:T(8,128)(2,1)S(1)} collective-permute-done((bf16[32,4480]{1,0:T(8,128)(2,1)S(1)}, bf16[32,4480]{1,0:T(8,128)(2,1)S(1)}, u32[]{:S(2)}, u32[]{:S(2)}) %collective-permute-start.2) | collective-permute-done | bytes 286752 | tf_op jit(solution)/shard_map/ppermute | solution.py:471
  26.4 10.7 %collective-permute-done.3.refs_1_ = bf16[32,4480]{1,0:T(8,128)(2,1)S(1)} collective-permute-done((bf16[32,4480]{1,0:T(8,128)(2,1)S(1)}, bf16[32,4480]{1,0:T(8,128)(2,1)S(1)}, u32[]{:S(2)}, u32[]{:S(2)}) %collective-permute-start.3) | collective-permute-done | bytes 286752 | tf_op jit(solution)/shard_map/ppermute | solution.py:471
  61.2 20.8 %collective-permute-done.5.refs_4_ = bf16[3,32,4480]{2,1,0:T(8,128)(2,1)S(1)} collective-permute-done((bf16[3,32,4480]{2,1,0:T(8,128)(2,1)S(1)}, bf16[3,32,4480]{2,1,0:T(8,128)(2,1)S(1)}, u32[]{:S(2)}, u32[]{:S(2)}) %collective-permute-start.5) | collective-permute-done | bytes 860192 | tf_op jit(solution)/shard_map/ppermute | solution.py:471
  84.0 24.3 %collective-permute-done.7.refs_6_ = bf16[3,32,4480]{2,1,0:T(8,128)(2,1)S(1)} collective-permute-done((bf16[3,32,4480]{2,1,0:T(8,128)(2,1)S(1)}, bf16[3,32,4480]{2,1,0:T(8,128)(2,1)S(1)}, u32[]{:S(2)}, u32[]{:S(2)}) %collective-permute-start.7) | collective-permute-done | bytes 860192 | tf_op jit(solution)/shard_map/ppermute | solution.py:471
  136.6 9.0 %conv_states.2 = (bf16[2,256,2304]{2,1,0:T(8,128)(2,1)S(1)}, f32[2,256,128]{2,1,0:T(8,128)S(1)}, f32[2,256,128]{2,1,0:T(8,128)S(1)}, f32[2,32,256]{2,1,0:T(8,128...) custom-call(bf16[2,256,2432]{2,1,0:T(8,128)(2,1)} %bitcast.159, ...), custom_call_target="tpu_custom_call" | custom-call | flops 2200000000 | bytes 2000000 | tf_op jit(solution)/shard_map/conv_states/pallas_call | solution.py:411
  171.9 11.8 %mix_within.2.refs_3_.refs_1_ = f32[2,256,2048]{2,1,0:T(8,128)} custom-call(bf16[2,256,2304]{2,1,0:T(8,128)(2,1)S(1)} %get-tuple-element.92.refs_0_.refs_2_.refs_6_.refs_1_.refs_3_, f32[2,256,128]{2,1,0:T(8,128)S(1)} %copy-done.75, f32[2,256,128]{2,1,0:T(8,128)S(1)} %copy-done.38, f32[2,32,256]{2,1,0:T(8,128)S(1)} %copy-done.124, ...), custom_call_target="tpu_custom_call" | custom-call | flops 3300000000 | bytes 3000000 | tf_op jit(solution)/shard_map/mix_within/pallas_call | solution.py:411
  217.0 9.5 %conv_states.3 = (bf16[2,256,2304]{2,1,0:T(8,128)(2,1)}, f32[2,256,128]{2,1,0:T(8,128)S(1)}, f32[2,256,128]{2,1,0:T(8,128)S(1)}, f32[2,32,256]{2,1,0:T(8,128)S(1...) custom-call(bf16[2,256,2432]{2,1,0:T(8,128)(2,1)} %bitcast.156, ...), custom_call_target="tpu_custom_call" | custom-call | flops 2200000000 | bytes 2000000 | tf_op jit(solution)/shard_map/conv_states/pallas_call | solution.py:411
  252.6 11.8 %mix_within.3.refs_3_.refs_1_ = f32[2,256,2048]{2,1,0:T(8,128)} custom-call(bf16[2,256,2304]{2,1,0:T(8,128)(2,1)S(1)} %copy-done.2, f32[2,256,128]{2,1,0:T(8,128)S(1)} %copy-done.78, f32[2,256,128]{2,1,0:T(8,128)S(1)} %copy-done.42, f32[2,32,256]{2,1,0:T(8,128)S(1)} %copy-done.121, f32[2,256,128]{2,1,0:T(8,128)S(1)} %copy-done.12, ...), custom_call_target="tpu_custom_call" | custom-call | flops 3300000000 | bytes 3000000 | tf_op jit(solution)/shard_map/mix_within/pallas_call | solution.py:411
  287.4 11.7 %gate_back.2 = (bf16[2,256,2048]{2,1,0:T(8,128)(2,1)}, bf16[2,256,3072]{2,1,0:T(8,128)(2,1)}, bf16[2,144,2048]{2,1,0:T(8,128)(2,1)S(1)}, f32[2,256,128]{2,1,0:T(...) custom-call(bf16[2,256,2048]{2,1,0:T(8,128)(2,1)} %bitcast.162, bf16[2,256,1024]{2,1,0:T(8,128)(2,1)S(1)} %copy-done.16, ...), custom_call_target="tpu_custom_call" | custom-call | flops 3024999936 | bytes 2750000 | tf_op jit(solution)/shard_map/gate_back/pallas_call | solution.py:411
  307.5 17.2 %mix_within_back.2 = (bf16[2,256,2048]{2,1,0:T(8,128)(2,1)S(1)}, f32[2,256,256]{2,1,0:T(8,128)S(1)}, f32[2,256,128]{2,1,0:T(8,128)S(1)}) custom-call(bf16[2,256,2048]{2,1,0:T(8,128)(2,1)} %get-tuple-element.109.refs_0_.refs_2_, bf16[2,256,2304]{2,1,0:T(8,128)(2,1)} %get-tuple-element.99.refs_0_.refs_2_.refs_6_.refs_1_.refs_3_, ...), custom_call_target="tpu_custom_call" | custom-call | flops 4674999808 | bytes 4250000 | tf_op jit(solution)/shard_map/mix_within_back/pallas_call | solution.py:411
  326.3 7.9 %collective-permute-done.24.refs_1_ = bf16[144,2048]{1,0:T(8,128)(2,1)S(1)} collective-permute-done((bf16[144,2048]{1,0:T(8,128)(2,1)S(1)}, bf16[144,2048]{1,0:T(8,128)(2,1)S(1)}, u32[]{:S(2)}, u32[]{:S(2)}) %collective-permute-start.24) | collective-permute-done | bytes 589856 | tf_op jit(solution)/shard_map/ppermute | solution.py:508
  336.1 8.6 %wide_grads.1.refs_19_ = bf16[1024,4096]{1,0:T(8,128)(2,1)} custom-call(bf16[512,1024]{1,0:T(8,128)(2,1)S(1)} %bitcast.130, bf16[512,2048]{1,0:T(8,128)(2,1)S(1)} %bitcast.135, bf16[512,3072]{1,0:T(8,128)(2,1)} %bitcast.153, bf16[128,2048]{1,0:T(8,128)(2,1)S(1)} %enter_states.6.refs_3_.refs_15_), custom_call_target="tpu_custom_call" | custom-call | flops 2750000128 | bytes 2500000 | tf_op jit(solution)/shard_map/wide_grads/pallas_call | solution.py:739
  351.9 18.6 %conv_back.2 = (bf16[2,256,2432]{2,1,0:T(8,128)(2,1)}, f32[2,8,2304]{2,1,0:T(8,128)S(1)}, f32[8,2304]{1,0:T(8,128)S(1)}, f32[8,128]{1,0:T(8,128)S(1)}) custom-call(s32[3]{0:T(128)S(1)} %pad_add_fusion.where.refs_0_, bf16[2,256,2048]{2,1,0:T(8,128)(2,1)} %copy-done.18, bf16[2,256,2048]{2,1,0:T(8,128)(2,1)} %get-tuple-element.109.refs_0_.refs_2_, ...), custom_call_target="tpu_custom_call" | custom-call | flops 4674999808 | bytes 4250000 | tf_op jit(solution)/shard_map/conv_back/pallas_call | solution.py:411
  398.4 11.5 %gate_back.3 = (bf16[2,256,2048]{2,1,0:T(8,128)(2,1)}, bf16[2,256,3072]{2,1,0:T(8,128)(2,1)}, bf16[2,144,2048]{2,1,0:T(8,128)(2,1)S(1)}, f32[2,256,128]{2,1,0:T(...) custom-call(bf16[2,256,2048]{2,1,0:T(8,128)(2,1)} %bitcast.161, bf16[2,256,1024]{2,1,0:T(8,128)(2,1)S(1)} %fusion.56.refs_1_, ...), custom_call_target="tpu_custom_call" | custom-call | flops 3024999936 | bytes 2750000 | tf_op jit(solution)/shard_map/gate_back/pallas_call | solution.py:411
  422.3 17.3 %mix_within_back.3 = (bf16[2,256,2048]{2,1,0:T(8,128)(2,1)S(1)}, f32[2,256,256]{2,1,0:T(8,128)S(1)}, f32[2,256,128]{2,1,0:T(8,128)S(1)}) custom-call(bf16[2,256,2048]{2,1,0:T(8,128)(2,1)} %get-tuple-element.125.refs_0_.refs_2_, bf16[2,256,2304]{2,1,0:T(8,128)(2,1)} %copy-done.3, f32[2,256,128]{2,1,0:T(8,128)S(1)} %copy-done.76, ...), custom_call_target="tpu_custom_call" | custom-call | flops 4674999808 | bytes 4250000 | tf_op jit(solution)/shard_map/mix_within_back/pallas_call | solution.py:411
  440.2 10.6 %collective-permute-done.31.refs_0_ = bf16[144,2048]{1,0:T(8,128)(2,1)S(1)} collective-permute-done((bf16[144,2048]{1,0:T(8,128)(2,1)S(1)}, bf16[144,2048]{1,0:T(8,128)(2,1)S(1)}, u32[]{:S(2)}, u32[]{:S(2)}) %collective-permute-start.31) | collective-permute-done | bytes 589856 | tf_op jit(solution)/shard_map/ppermute | solution.py:508
  450.8 9.7 %collective-permute-done.32.refs_1_ = bf16[144,2048]{1,0:T(8,128)(2,1)S(1)} collective-permute-done((bf16[144,2048]{1,0:T(8,128)(2,1)S(1)}, bf16[144,2048]{1,0:T(8,128)(2,1)S(1)}, u32[]{:S(2)}, u32[]{:S(2)}) %collective-permute-start.32) | collective-permute-done | bytes 589856 | tf_op jit(solution)/shard_map/ppermute | solution.py:508
  462.1 8.4 %first_grads.1 = (bf16[4,128,1024]{2,1,0:T(8,128)(2,1)S(1)}, bf16[4,128,1024]{2,1,0:T(8,128)(2,1)S(1)}, bf16[4,128,1024]{2,1,0:T(8,128)(2,1)S(1)}, bf16[4,128,1024]{2,1,0:T(8,128)(2,1)S(1)}) custom-call(bf16[1536,512]{1,0:T(8,128)(2,1)} %copy-done.46, bf16[1536,512]{1,0:T(8,128)(2,1)} %copy-done.140, bf16[512,3072]{1,0:T(8,128)(2,1)} %bitcast.180, ...), custom_call_target="tpu_custom_call" | custom-call | flops 2750000128 | bytes 2500000 | tf_op jit(solution)/shard_map/first_grads/pallas_call | solution.py:458
  470.7 16.6 %collective-permute-start.39 = (bf16[4,128,1024]{2,1,0:T(8,128)(2,1)S(1)}, bf16[4,128,1024]{2,1,0:T(8,128)(2,1)S(1)}, u32[]{:S(2)}, u32[]{:S(2)}) collective-permute-start(bf16[4,128,1024]{2,1,0:T(8,128)(2,1)S(1)} %get-tuple-element.135.refs_21_), channel_id=1, source_target_pairs={{0,4},{1,5},{2,6},{3,7},{4,0},{5,1},{6,2},{7,3},{8,12},{9,13},{10,... | collective-permute-start | bytes 3145736 | tf_op jit(solution)/shard_map/ppermute | solution.py:471
  490.5 18.8 %conv_back.3 = (bf16[2,256,2432]{2,1,0:T(8,128)(2,1)}, f32[2,8,2304]{2,1,0:T(8,128)S(1)}, f32[8,2304]{1,0:T(8,128)S(1)}, f32[8,128]{1,0:T(8,128)S(1)}) custom-call(s32[3]{0:T(128)S(1)} %pad_add_fusion.where.refs_0_, bf16[2,256,2048]{2,1,0:T(8,128)(2,1)} %copy-done.21, bf16[2,256,2048]{2,1,0:T(8,128)(2,1)} %get-tuple-element.125.refs_0_.refs_2_, ...), custom_call_target="tpu_custom_call" | custom-call | flops 4674999808 | bytes 4250000 | tf_op jit(solution)/shard_map/conv_back/pallas_call | solution.py:411
  519.6 14.3 %collective-permute-done.39.refs_2_ = bf16[4,128,1024]{2,1,0:T(8,128)(2,1)S(1)} collective-permute-done((bf16[4,128,1024]{2,1,0:T(8,128)(2,1)S(1)}, bf16[4,128,1024]{2,1,0:T(8,128)(2,1)S(1)}, u32[]{:S(2)}, u32[]{:S(2)}) %collective-permute-start.39) | collective-permute-done | bytes 1048608 | tf_op jit(solution)/shard_map/ppermute | solution.py:471
  557.2 12.9 %collective-permute-done.51.refs_2_ = bf16[4,32,2432]{2,1,0:T(8,128)(2,1)S(1)} collective-permute-done((bf16[4,32,2432]{2,1,0:T(8,128)(2,1)}, bf16[4,32,2432]{2,1,0:T(8,128)(2,1)S(1)}, u32[]{:S(2)}, u32[]{:S(2)}) %collective-permute-start.51) | collective-permute-done | bytes 622624 | tf_op jit(solution)/shard_map/ppermute | solution.py:471
  570.4 16.8 %collective-permute-done.42.refs_1_ = bf16[2,128,1024]{2,1,0:T(8,128)(2,1)S(1)} collective-permute-done((bf16[2,128,1024]{2,1,0:T(8,128)(2,1)S(1)}, bf16[2,128,1024]{2,1,0:T(8,128)(2,1)S(1)}, u32[]{:S(2)}, u32[]{:S(2)}) %collective-permute-start.42) | collective-permute-done | bytes 524320 | tf_op jit(solution)/shard_map/ppermute | solution.py:471
  616.7 12.2 %collective-permute-done.54.refs_2_ = bf16[4,32,2432]{2,1,0:T(8,128)(2,1)} collective-permute-done((bf16[4,32,2432]{2,1,0:T(8,128)(2,1)}, bf16[4,32,2432]{2,1,0:T(8,128)(2,1)}, u32[]{:S(2)}, u32[]{:S(2)}) %collective-permute-start.54) | collective-permute-done | bytes 622624 | tf_op jit(solution)/shard_map/ppermute | solution.py:471
  (598 shorter events, 348.9 us)
Async XLA Ops:
  7.2 176.4 %all-gather.5.cloned.1.call-start = ((), (), s32[]{:S(2)}) async-start(), calls=%async_computation.1 | async-start | bytes 13787136 | tf_op jit(solution)/shard_map/all_gather | solution.py:1028
  40.2 224.1 %all-gather.7.cloned.1.call-start = ((), (), s32[]{:S(2)}) async-start(), calls=%async_computation.2 | async-start | bytes 4325376 | tf_op jit(solution)/shard_map/all_gather | solution.py:1033
  59.7 48.7 %collective-permute-start.7 = (bf16[3,32,4480]{2,1,0:T(8,128)(2,1)S(1)}, bf16[3,32,4480]{2,1,0:T(8,128)(2,1)S(1)}, u32[]{:S(2)}, u32[]{:S(2)}) collective-permute-start(bf16[3,32,4480]{2,1,0:T(8,128)(2,1)S(1)} %stack.122.refs_3_.refs_1_.refs_2_), channel_id=1, source_target_pairs={{0,6},{1,7},{2,4},{3,5},{4,2},{5,3},{6,0},{7,1},{8,14},{9,15},{10,... | collective-permute-start | bytes 2580488 | tf_op jit(solution)/shard_map/ppermute | solution.py:471
  118.2 481.3 %reduce-scatter.2.cloned.1.call-start = ((), (), s32[]{:S(2)}) async-start(), calls=%async_computation.3 | async-start | bytes 8650752 | tf_op jit(solution)/shard_map/reduce_scatter | solution.py:1144
  155.2 33.7 %collective-permute-start.12 = (bf16[144,2048]{1,0:T(8,128)(2,1)}, bf16[144,2048]{1,0:T(8,128)(2,1)}, u32[]{:S(2)}, u32[]{:S(2)}) collective-permute-start(bf16[144,2048]{1,0:T(8,128)(2,1)} %join_states.4.refs_8_), channel_id=1, source_target_pairs={{0,6},{1,7},{8,14},{9,15},{16,22},{17,23},{24,30},{25,31}} | collective-permute-start | bytes 1769480 | tf_op jit(solution)/shard_map/ppermute | solution.py:508
  304.7 29.5 %collective-permute-start.24 = (bf16[144,2048]{1,0:T(8,128)(2,1)S(1)}, bf16[144,2048]{1,0:T(8,128)(2,1)S(1)}, u32[]{:S(2)}, u32[]{:S(2)}) collective-permute-start(bf16[144,2048]{1,0:T(8,128)(2,1)S(1)} %join_states.6.refs_10_), channel_id=1, source_target_pairs={{4,0},{5,1},{6,2},{7,3},{12,8},{13,9},{14,10},{15,11},{20,16},{21,... | collective-permute-start | bytes 1769480 | tf_op jit(solution)/shard_map/ppermute | solution.py:508
  344.8 323.4 %all-gather.9.cloned.1.call-start = ((), (), s32[]{:S(2)}) async-start(), calls=%async_computation.4 | async-start | bytes 2359296 | tf_op jit(solution)/shard_map/all_gather | solution.py:1214
  410.0 51.0 %collective-permute-start.36 = (bf16[512,3072]{1,0:T(8,128)(2,1)}, bf16[512,3072]{1,0:T(8,128)(2,1)}, u32[]{:S(2)}, u32[]{:S(2)}) collective-permute-start(bf16[512,3072]{1,0:T(8,128)(2,1)} %bitcast.179), channel_id=1, source_target_pairs={{0,1},{1,0},{2,3},{3,2},{4,5},{5,4},{6,7},{7,6},{8,9},{9,8},{10,11... | collective-permute-start | bytes 9437192 | tf_op jit(solution)/shard_map/ppermute | solution.py:471
  410.6 50.4 %collective-permute-start.35 = (bf16[1536,512]{1,0:T(8,128)(2,1)S(1)}, bf16[1536,512]{1,0:T(8,128)(2,1)S(1)}, u32[]{:S(2)}, u32[]{:S(2)}) collective-permute-start(bf16[1536,512]{1,0:T(8,128)(2,1)S(1)} %copy-done.105), channel_id=1, source_target_pairs={{0,1},{1,0},{2,3},{3,2},{4,5},{5,4},{6,7},{7,6},{8,9},{9,8},{10,11... | collective-permute-start | bytes 4718600 | tf_op jit(solution)/shard_map/ppermute | solution.py:471
  418.2 32.7 %collective-permute-start.31 = (bf16[144,2048]{1,0:T(8,128)(2,1)S(1)}, bf16[144,2048]{1,0:T(8,128)(2,1)S(1)}, u32[]{:S(2)}, u32[]{:S(2)}) collective-permute-start(bf16[144,2048]{1,0:T(8,128)(2,1)S(1)} %join_states.7.refs_10_), channel_id=1, source_target_pairs={{6,0},{7,1},{14,8},{15,9},{22,16},{23,17},{30,24},{31,25}} | collective-permute-start | bytes 1769480 | tf_op jit(solution)/shard_map/ppermute | solution.py:508
  419.5 41.1 %collective-permute-start.32 = (bf16[144,2048]{1,0:T(8,128)(2,1)S(1)}, bf16[144,2048]{1,0:T(8,128)(2,1)S(1)}, u32[]{:S(2)}, u32[]{:S(2)}) collective-permute-start(bf16[144,2048]{1,0:T(8,128)(2,1)S(1)} %join_states.7.refs_10_), channel_id=1, source_target_pairs={{4,0},{5,1},{6,2},{7,3},{12,8},{13,9},{14,10},{15,11},{20,16},{21,... | collective-permute-start | bytes 1769480 | tf_op jit(solution)/shard_map/ppermute | solution.py:508
  420.8 39.8 %collective-permute-start.33 = (bf16[144,2048]{1,0:T(8,128)(2,1)S(1)}, bf16[144,2048]{1,0:T(8,128)(2,1)S(1)}, u32[]{:S(2)}, u32[]{:S(2)}) collective-permute-start(bf16[144,2048]{1,0:T(8,128)(2,1)S(1)} %join_states.7.refs_10_), channel_id=1, source_target_pairs={{2,0},{3,1},{4,2},{5,3},{6,4},{7,5},{10,8},{11,9},{12,10},{13,11},... | collective-permute-start | bytes 1769480 | tf_op jit(solution)/shard_map/ppermute | solution.py:508
  460.8 29.5 %collective-permute-start.34 = (bf16[128,2048]{1,0:T(8,128)(2,1)S(1)}, bf16[128,2048]{1,0:T(8,128)(2,1)S(1)}, u32[]{:S(2)}, u32[]{:S(2)}) collective-permute-start(bf16[128,2048]{1,0:T(8,128)(2,1)S(1)} %enter_states.7.refs_4_.refs_15_), channel_id=1, source_target_pairs={{0,1},{1,0},{2,3},{3,2},{4,5},{5,4},{6,7},{7,6},{8,9},{9,8},{10,11... | collective-permute-start | bytes 1572872 | tf_op jit(solution)/shard_map/ppermute | solution.py:471
  470.6 49.0 %collective-permute-start.38 = (bf16[4,128,1024]{2,1,0:T(8,128)(2,1)S(1)}, bf16[4,128,1024]{2,1,0:T(8,128)(2,1)S(1)}, u32[]{:S(2)}, u32[]{:S(2)}) collective-permute-start(bf16[4,128,1024]{2,1,0:T(8,128)(2,1)S(1)} %get-tuple-element.134.refs_20_), channel_id=1, source_target_pairs={{0,2},{1,3},{2,0},{3,1},{4,6},{5,7},{6,4},{7,5},{8,10},{9,11},{10,... | collective-permute-start | bytes 3145736 | tf_op jit(solution)/shard_map/ppermute | solution.py:471
  470.7 63.2 %collective-permute-start.39 = (bf16[4,128,1024]{2,1,0:T(8,128)(2,1)S(1)}, bf16[4,128,1024]{2,1,0:T(8,128)(2,1)S(1)}, u32[]{:S(2)}, u32[]{:S(2)}) collective-permute-start(bf16[4,128,1024]{2,1,0:T(8,128)(2,1)S(1)} %get-tuple-element.135.refs_21_), channel_id=1, source_target_pairs={{0,4},{1,5},{2,6},{3,7},{4,0},{5,1},{6,2},{7,3},{8,12},{9,13},{10,... | collective-permute-start | bytes 3145736 | tf_op jit(solution)/shard_map/ppermute | solution.py:471
  487.2 50.6 %collective-permute-start.40 = (bf16[4,128,1024]{2,1,0:T(8,128)(2,1)S(1)}, bf16[4,128,1024]{2,1,0:T(8,128)(2,1)}, u32[]{:S(2)}, u32[]{:S(2)}) collective-permute-start(bf16[4,128,1024]{2,1,0:T(8,128)(2,1)S(1)} %get-tuple-element.136.refs_22_), channel_id=1, source_target_pairs={{0,6},{1,7},{2,4},{3,5},{4,2},{5,3},{6,0},{7,1},{8,14},{9,15},{10,... | collective-permute-start | bytes 3145736 | tf_op jit(solution)/shard_map/ppermute | solution.py:471
  509.3 30.3 %collective-permute-start.37 = (bf16[2,8,2304]{2,1,0:T(8,128)(2,1)S(1)}, bf16[2,8,2304]{2,1,0:T(8,128)(2,1)S(1)}, u32[]{:S(2)}, u32[]{:S(2)}) collective-permute-start(bf16[2,8,2304]{2,1,0:T(8,128)(2,1)S(1)} %convert_element_type.198), channel_id=1, source_target_pairs={{1,0},{2,1},{3,2},{4,3},{5,4},{6,5},{7,6},{9,8},{10,9},{11,10},{12... | collective-permute-start | bytes 221192 | tf_op jit(solution)/shard_map/ppermute | solution.py:1174
  540.0 48.1 %collective-permute-start.48 = (bf16[512,2432]{1,0:T(8,128)(2,1)S(1)}, bf16[512,2432]{1,0:T(8,128)(2,1)}, u32[]{:S(2)}, u32[]{:S(2)}) collective-permute-start(bf16[512,2432]{1,0:T(8,128)(2,1)S(1)} %bitcast.123), channel_id=1, source_target_pairs={{0,1},{1,0},{2,3},{3,2},{4,5},{5,4},{6,7},{7,6},{8,9},{9,8},{10,11... | collective-permute-start | bytes 7471112 | tf_op jit(solution)/shard_map/ppermute | solution.py:471
  540.1 29.9 %collective-permute-start.51 = (bf16[4,32,2432]{2,1,0:T(8,128)(2,1)}, bf16[4,32,2432]{2,1,0:T(8,128)(2,1)S(1)}, u32[]{:S(2)}, u32[]{:S(2)}) collective-permute-start(bf16[4,32,2432]{2,1,0:T(8,128)(2,1)} %get-tuple-element.150), channel_id=1, source_target_pairs={{0,4},{1,5},{2,6},{3,7},{4,0},{5,1},{6,2},{7,3},{8,12},{9,13},{10,... | collective-permute-start | bytes 1867784 | tf_op jit(solution)/shard_map/ppermute | solution.py:471
  554.5 32.8 %collective-permute-start.42 = (bf16[2,128,1024]{2,1,0:T(8,128)(2,1)S(1)}, bf16[2,128,1024]{2,1,0:T(8,128)(2,1)S(1)}, u32[]{:S(2)}, u32[]{:S(2)}) collective-permute-start(bf16[2,128,1024]{2,1,0:T(8,128)(2,1)S(1)} %get-tuple-element.143), channel_id=1, source_target_pairs={{0,16},{8,24},{16,0},{24,8},{1,17},{9,25},{17,1},{25,9},{2,18},{10... | collective-permute-start | bytes 1572872 | tf_op jit(solution)/shard_map/ppermute | solution.py:471
  557.2 30.9 %collective-permute-start.49 = (f32[1024,128]{1,0:T(8,128)S(1)}, f32[1024,128]{1,0:T(8,128)S(1)}, u32[]{:S(2)}, u32[]{:S(2)}) collective-permute-start(f32[1024,128]{1,0:T(8,128)S(1)} %gather_small.3.refs_5_), channel_id=1, source_target_pairs={{0,1},{1,0},{2,3},{3,2},{4,5},{5,4},{6,7},{7,6},{8,9},{9,8},{10,11... | collective-permute-start | bytes 1572872 | tf_op jit(solution)/shard_map/ppermute | solution.py:471
  570.4 36.8 %collective-permute-start.59 = (bf16[2,32,2432]{2,1,0:T(8,128)(2,1)S(1)}, bf16[2,32,2432]{2,1,0:T(8,128)(2,1)S(1)}, u32[]{:S(2)}, u32[]{:S(2)}) collective-permute-start(bf16[2,32,2432]{2,1,0:T(8,128)(2,1)S(1)} %get-tuple-element.161), channel_id=1, source_target_pairs={{0,16},{8,24},{16,0},{24,8},{1,17},{9,25},{17,1},{25,9},{2,18},{10... | collective-permute-start | bytes 933896 | tf_op jit(solution)/shard_map/ppermute | solution.py:471
  596.9 32.0 %collective-permute-start.54 = (bf16[4,32,2432]{2,1,0:T(8,128)(2,1)}, bf16[4,32,2432]{2,1,0:T(8,128)(2,1)}, u32[]{:S(2)}, u32[]{:S(2)}) collective-permute-start(bf16[4,32,2432]{2,1,0:T(8,128)(2,1)} %get-tuple-element.155), channel_id=1, source_target_pairs={{0,4},{1,5},{2,6},{3,7},{4,0},{5,1},{6,2},{7,3},{8,12},{9,13},{10,... | collective-permute-start | bytes 1867784 | tf_op jit(solution)/shard_map/ppermute | solution.py:471
  597.6 34.1 %collective-permute-start.55 = (bf16[4,32,2432]{2,1,0:T(8,128)(2,1)}, bf16[4,32,2432]{2,1,0:T(8,128)(2,1)}, u32[]{:S(2)}, u32[]{:S(2)}) collective-permute-start(bf16[4,32,2432]{2,1,0:T(8,128)(2,1)} %get-tuple-element.156), channel_id=1, source_target_pairs={{0,6},{1,7},{2,4},{3,5},{4,2},{5,3},{6,0},{7,1},{8,14},{9,15},{10,... | collective-permute-start | bytes 1867784 | tf_op jit(solution)/shard_map/ppermute | solution.py:471
  (212 other events, 2252.8 us)
Sparse Core Ops, SparseCore 0:
  40.4 117.6 all-gather.4
  160.9 71.0 all-gather.6
  344.9 155.5 reduce-scatter.1
  601.3 46.0 all-gather.8

commit v5 on v4

--- a/solution.py
+++ b/solution.py
@@ -698,58 +698,35 @@
     )
 
 
-def first_grads_kernel(groups, chips, inner, own, other, grad, grad_other, *outs):
+def first_grads_kernel(groups, chips, inner, joined, at, own, other, grad, grad_other, *refs):
     wide = grad.shape[1] - inner
     total_big = inner // 2
     big = total_big // (groups * chips)
     small = (own.shape[0] - total_big) // (groups * chips)
-
-    def put(total, share, start, at):
+    outs = refs[1:] if joined else refs
+    group = at[2]
+
+    def put(total, share, start, column):
         for d in range(chips):
             for e in range(groups):
                 block = (d * groups + e) * share
-                outs[d][e, start:start + share, pl.ds(at, 512)] = total[block:block + share]
-
-    for at in range(0, wide, 512):
-        place = pl.ds(inner + at, 512)
+                rows, columns = slice(start, start + share), pl.ds(column, 512)
+                if joined:
+                    outs[d][e, rows, columns] = total[block:block + share]
+                else:
+                    outs[0][group ^ e, d, rows, columns] = total[block:block + share]
+
+    if joined:
+        for d in range(chips):
+            outs[d][groups] = refs[0][d]
+    for start in range(0, wide, 512):
+        place = pl.ds(inner + start, 512)
         total = dot(own[0:total_big, :], grad[:, place]) + dot(other[0:total_big, :], grad_other[:, place])
-        put(total.astype(BF16), big, 0, at)
-    for at in range(0, inner, 512):
-        place = pl.ds(at, 512)
+        put(total.astype(BF16), big, 0, start)
+    for start in range(0, inner, 512):
+        place = pl.ds(start, 512)
         total = dot(own[total_big:, :], grad[:, place]) + dot(other[total_big:, :], grad_other[:, place])
-        put(total.astype(BF16), small, big + at // wide * small, at % wide)
-
-
-def wide_grads_kernel(low, gated, grad, out):
-    cut, model = low.shape[1], grad.shape[1] - out.shape[1] // 2
-    inner = out.shape[1] // 2
-    turned = low[...].T
-    for at in range(0, inner, 512):
-        out[:, pl.ds(at, 512)] = dot(turned, grad[:, pl.ds(at, 512)]).astype(BF16)
-    for i in range(inner // model):
-        turned = gated[:, i * cut:(i + 1) * cut].T
-        for at in range(0, model, 512):
-            out[:, pl.ds(inner + i * model + at, 512)] = dot(turned, grad[:, pl.ds(inner + at, 512)]).astype(BF16)
-
-
-def wide_grads(low, gated, both, groups, after):
-    rows, model = low.shape
-    inner = gated.shape[1]
-    cut = model // groups
-    return pl.pallas_call(
-        without(wide_grads_kernel, 3, len(after)),
-        grid=(groups,),
-        in_specs=[
-            pl.BlockSpec((rows, cut), lambda z: (0, z)),
-            pl.BlockSpec((rows, inner // groups), lambda z: (0, z)),
-            pl.BlockSpec(both.shape, lambda z: (0, 0)),
-        ] + [pl.BlockSpec(memory_space=pl.ANY)] * len(after),
-        out_specs=pl.BlockSpec((cut, 2 * inner), lambda z: (z, 0)),
-        out_shape=jax.ShapeDtypeStruct((model, 2 * inner), BF16),
-        compiler_params=pltpu.CompilerParams(vmem_limit_bytes=VMEM),
-        cost_estimate=cost(10.0),
-        name="wide_grads",
-    )(low, gated, both, *after)
+        put(total.astype(BF16), small, big + start // wide * small, start % wide)
 
 
 def second_grads_kernel(groups, chips, channels, heads, here, own, other, grad, grad_other, extra, extra_other, *outs):
@@ -813,16 +790,18 @@
 
 
 def halve_kernel(count, *refs):
-    ins, (near, far) = refs[:count], refs[count:]
+    ins, (near, far, *more_outs) = refs[:count], refs[count:]
     half = near.shape[0]
-    for i in range(2 * half):
+    for i in range(2 * half + len(more_outs)):
         total = ins[0][i].astype(F32)
         for more in ins[1:]:
             total = total + more[i].astype(F32)
         if i < half:
             near[i] = total.astype(BF16)
+        elif i < 2 * half:
+            far[i - half] = total.astype(BF16)
         else:
-            far[i - half] = total.astype(BF16)
+            more_outs[0][...] = total.astype(BF16)
 
 
 def lay_kernel(count, layers, *refs):
@@ -847,19 +826,20 @@
     return [blocks[0]] + [swap(blocks[i], "seq", 2 * i) for i in range(1, len(blocks))]
 
 
-def halved_sums(got, groups):
+def halved(got, after=()):
     parts, rows, columns = got[0].shape
-    after = ()
+    outs = [((parts // 2, rows, columns), BF16)] * 2 + [((rows, columns), BF16)] * (parts % 2)
+    return whole_call(functools.partial(halve_kernel, len(got)), got, outs, 2.0, "add_halves", after=after)
+
+
+def halved_sums(near, far, after):
+    parts, rows, columns = near.shape
+    got = [near, swap(far, "fsdp", parts)]
     while parts > 1:
-        half = parts // 2
-        near, far = whole_call(
-            functools.partial(halve_kernel, len(got)), got, [((half, rows, columns), BF16)] * 2, 2.0, "add_halves"
-        )
-        if parts == groups:
-            after = (near,)
-        got = [near, swap(far, "fsdp", half)]
-        parts = half
-    return whole_call(functools.partial(add_kernel, 2), got, [((rows, columns), BF16)], 1.0, "add_halves")[0], after
+        near, far = halved(got, after)
+        parts //= 2
+        got = [near, swap(far, "fsdp", parts)]
+    return whole_call(functools.partial(add_kernel, 2), got, [((rows, columns), BF16)], 1.0, "add_halves", after=after)[0]
 
 
 def laid(got, wide, after):
@@ -882,7 +862,6 @@
 def place_kernel(chips, inner, layers, at, *refs):
     mine_a, other_a = refs[:chips], refs[chips]
     mine_b, other_b = refs[chips + 1:2 * chips + 1], refs[2 * chips + 1]
-    scattered = refs[2 * chips + 2:2 * chips + 1 + layers]
     in_out, extra_out, out_out, norm_out, taps_out, bias_out, heads_out, gain_out, extra = refs[-9:]
     core, chip = at[0], at[1]
     model = other_a.shape[2]
@@ -892,22 +871,18 @@
     for layer in range(layers):
         @pl.when(pl.program_id(0) == layer)
         def _():
-            if layer:
-                wide = scattered[layer - 1]
-                in_out[0, :, 0:inner] = wide[:, 0:inner].astype(F32)
-                for i in range(inner // model):
-                    out_out[0, i * rows_in:(i + 1) * rows_in, :] = wide[:, inner + i * model:inner + (i + 1) * model].astype(F32)
             for d in range(chips):
                 for is_other in range(2):
                     a, b = (other_a.at[d], other_b.at[d]) if is_other else (mine_a[d], mine_b[d])
                     start = (chip ^ d) * (2 * share) + (core ^ is_other) * share
                     rows = pl.ds(pl.multiple_of(start, share), share)
-                    if not layer:
-                        start = (chip ^ d) * (2 * big) + (core ^ is_other) * big
-                        out_out[0, pl.ds(pl.multiple_of(start, big), big), :] = a[0:big, :].astype(F32)
-                        for i in range(inner // model):
-                            first = big + i * share
-                            in_out[0, rows, i * model:(i + 1) * model] = a[first:first + share, :].astype(F32)
+                    start = (chip ^ d) * (2 * big) + (core ^ is_other) * big
+                    first = layer * (a.shape[0] // layers)
+                    out_out[0, pl.ds(pl.multiple_of(start, big), big), :] = a[first:first + big, :].astype(F32)
+                    first += big
+                    for i in range(inner // model):
+                        in_out[0, rows, i * model:(i + 1) * model] = a[first:first + share, :].astype(F32)
+                        first += share
                     first = layer * (b.shape[0] // layers)
                     for column in range(0, channels + LANES, model):
                         wide = min(model, channels - column)
@@ -970,7 +945,7 @@
     states = (channels - inner) // 2
     span = inner // heads
     chips = peers // 2
-    direct = model % (32 * groups * peers) == 0 and chips == 4 and groups == 4
+    direct = model % (32 * groups * peers) == 0 and chips == 4 and groups == 4 and layers == 2
     seq_at = lax.axis_index("seq")
     here = jnp.stack([seq_at % 2, seq_at // 2, lax.axis_index("fsdp")]).astype(jnp.int32)
 
@@ -1090,14 +1065,14 @@
         gated = gated.reshape(rows, inner)
         turned = None
         if direct:
-            mine, send = turned_halves(gated if layer == 0 else None, low, here, groups, chips)
+            mine, send = turned_halves(gated, low, here, groups, chips)
             turned = (mine, swap(send, "seq", 1))
             sent = (send,)
         kept.append((turned, stream, norm_scale, low, mixed_in, edge, gate, act, size, sums, sums_t, factor, entering, mixed, gated))
         stream = stream + dot(gated, w_out).reshape(batch, width, model)
 
     grad_stream = cotangent.astype(F32)
-    collected, collected_grads, scattered, second_shares, waiting = [], [], [], [], []
+    collected, collected_grads, far_sums, second_shares, waiting = [], [], [], [], []
     started = ()
     for layer in reversed(range(layers)):
         (turned, entry, norm_scale, low, mixed_in, edge, gate, act, size, sums, sums_t, factor, entering, mixed, gated) = kept[layer]
@@ -1124,7 +1099,7 @@
         if direct:
             big, small = inner // (groups * peers), model // (groups * peers)
             mine, theirs = turned
-            both_other = swap(both, "seq", 1) if layer == 0 else None
+            both_other = swap(both, "seq", 1)
         else:
             out_share = reduced(dot_tn(gated, grad_low).astype(BF16))
         d_stepped, d_pair, d_total = call(
@@ -1140,24 +1115,25 @@
         )
         before, partner = entered(got, (d_stepped,))
         if direct and layer > 0:
-            wide = wide_grads(low, gated, both, groups, (before,))
-            scattered.append(lax.psum_scatter(wide, ("fsdp", "seq"), scatter_dimension=0, tiled=True))
-            arrived = (wide,)
+            (parts,) = whole_call(
+                functools.partial(first_grads_kernel, groups, chips, inner, False), [mine, theirs, both, both_other],
+                [((groups, chips, big + inner // model * small, model), BF16)], 10.0, "first_grads", here, (before,),
+            )
+            far_sums.append(lax.psum_scatter(parts, "fsdp", scatter_dimension=0, tiled=True)[0])
+            arrived = (parts,)
         if direct and layer == 0:
             first_blocks = whole_call(
-                functools.partial(first_grads_kernel, groups, chips, inner), [mine, theirs, both, both_other],
-                [((groups, big + inner // model * small, model), BF16)] * chips, 10.0, "first_grads", after=(before,),
+                functools.partial(first_grads_kernel, groups, chips, inner, True), [mine, theirs, both, both_other] + far_sums,
+                [((groups + 1, big + inner // model * small, model), BF16)] * chips, 10.0, "first_grads", here, (before,),
             )
             arrived = tuple(first_blocks)
-            first_share, halved = halved_sums(plane_parts(first_blocks), groups)
-            ordered = halved
+            near, far, *passed = halved(plane_parts(first_blocks))
+            ordered = (near,)
+            gots = []
             for later in waiting:
                 blocks = later((first_blocks[0],))
-                share, more = halved_sums(plane_parts(blocks), groups)
+                gots.append(plane_parts(blocks))
                 ordered += (blocks[0],)
-                halved += more
-                second_shares.append(laid([share], model, ()))
-            mine_a, other_a = spread_in_plane(first_share, chips)
         d_mixed_in, d_edge, tap_grads, head_grads = call(
             functools.partial(conv_back_kernel, inner), batch,
             [
@@ -1191,8 +1167,14 @@
                 waiting.append(functools.partial(whole_call, kernel, operands, outs, 6.0, "second_grads", here))
                 started = (operands[3], operands[5])
             else:
-                got = plane_parts(whole_call(kernel, operands, outs, 6.0, "second_grads", here, halved))
-                second_shares.append(layer_sums(got, groups, model, (stream, grad_stream) + tuple(mine_a)))
+                blocks = whole_call(kernel, operands, outs, 6.0, "second_grads", here)
+                after = (blocks[0],)
+                first_share = stacked([halved_sums(near, far, after)] + passed).reshape(-1, model)
+                mine_a, other_a = spread_in_plane(first_share, chips)
+                for got in gots:
+                    near, far = halved(got, after)
+                    second_shares.append(laid([halved_sums(near, far, ())], model, ()))
+                second_shares.append(layer_sums(plane_parts(blocks), groups, model, (stream, grad_stream) + tuple(mine_a)))
         else:
             mixed_grad = dot_tn(low, grad_mixed)
             in_share = reduced(jnp.concatenate([dot_tn(low, d_gate).astype(BF16), mixed_grad[:, :channels].astype(BF16)], axis=1))
@@ -1210,15 +1192,13 @@
             collected.append(jnp.concatenate(small_grads, axis=1))
     if direct:
         second_share = stacked(second_shares[::-1]).reshape(-1, model)
-        held = [stacked([share], (first_blocks[0],))[0] for share in scattered]
-        scattered = [lax.all_gather(share, "seq", axis=0, tiled=True) for share in held]
         mine_b, other_b = spread_in_plane(second_share, chips)
         shapes = [(model // groups, inner + channels), (model // groups, heads), (inner // groups, model)]
         smalls = [
             (layers, model // groups), (layers, taps_len, channels // groups), (layers, channels // groups), (layers, 3, heads // groups),
             (layers, inner // groups),
         ]
-        blocks = mine_a + [other_a] + mine_b + [other_b] + scattered[::-1]
+        blocks = mine_a + [other_a] + mine_b + [other_b]
         placed = placed_grads(here, blocks, layers, shapes, smalls, chips, inner, ())
         by_head = placed[6]
         pieces = [placed[3], placed[4], placed[5], by_head[:, 0], by_head[:, 1], by_head[:, 2], placed[7]]

time: 696 us -> 668 us (0.960)
  starting transfers between devices: 107 us -> 83.8 us
  local copies, waits for them, and re-layouts: 58 us -> 38.7 us
  waiting for transfers between devices: 207 us -> 217 us
    ppermute x48 -> x49, starting transfers between devices: 69.1 us -> 44.6 us  [swap(): lax.ppermute(x, axis, [(i, i ^ bits) for i in range(lax.axis_size(axis))])]
    ppermute x48 -> x49, waiting for transfers between devices: 171 us -> 190 us  [swap(): lax.ppermute(x, axis, [(i, i ^ bits) for i in range(lax.axis_size(axis))])]
    unnamed x336 -> x314, local copies, waits for them, and re-layouts: 48.2 us -> 33.8 us
    pallas_call x30 -> x31, Pallas kernels: 45.9 us -> 57.2 us  [whole_call(): pl.pallas_call(without(kernel, len(arrays), len(after)), in_specs=in_spec...]
    pallas_call x1 -> x0, Pallas kernels: 8.6 us -> none  [wide_grads(): pl.pallas_call(without(wide_grads_kernel, 3, len(after)), grid=(groups,),...]
    ppermute x12, waiting for transfers between devices: 33.4 us -> 25.1 us  [exchange(): got.append(lax.ppermute(joined, 'seq', route))]
where the time goes in v5:
time: 668 us; the launch traced here: 659 us
  Pallas kernels  230 us (34%)
  waiting for transfers between devices  217 us (32%)
  starting transfers between devices  83.8 us (13%)
  matrix products  61.6 us (9%)
  local copies, waits for them, and re-layouts  38.7 us (6%)
  between operations  16.3 us (2%)
  other arithmetic  12.2 us (2%)
    ppermute x49, waiting for transfers between devices, swap(): lax.ppermute(x, axis, [(i, i ^ bits) for i in range(lax.axis_size(axis))])  190 us
    pallas_call x12, Pallas kernels, call(): pl.pallas_call(without(kernel, len(arrays), len(after)), grid=(batch,), i...  150 us
    pallas_call x31, Pallas kernels, whole_call(): pl.pallas_call(without(kernel, len(arrays), len(after)), in_specs=in_spec...  57.2 us
    ppermute x49, starting transfers between devices, swap(): lax.ppermute(x, axis, [(i, i ^ bits) for i in range(lax.axis_size(axis))])  44.6 us
    unnamed x314, local copies, waits for them, and re-layouts  33.8 us
    dot_general x6, matrix products, dot(): return jnp.dot(a, b, preferred_element_type=F32)  33.3 us
    ppermute x12, starting transfers between devices, exchange(): got.append(lax.ppermute(joined, 'seq', route))  30.1 us
    dot_general x6, matrix products, dot_nt(): return lax.dot_general(a, b, NT, preferred_element_type=F32)  28.3 us
  transfers between devices with their start and end apart: 69, of which 30 were waited for; matrix products, arithmetic and copies ran while one was open for 12% of the time, Pallas kernels for 28%

profile of v5, /device:TPU:0, one launch (start us, length us, event | category | flops | bytes accessed | tf_op | source)
XLA Modules:
  0.0 659.4 jit_solution(6063271314413750159)
XLA Ops:
  16.8 7.2 %collective-permute-done.4.refs_2_ = bf16[32,4480]{1,0:T(8,128)(2,1)S(1)} collective-permute-done((bf16[32,4480]{1,0:T(8,128)(2,1)S(1)}, bf16[32,4480]{1,0:T(8,128)(2,1)S(1)}, u32[]{:S(2)}, u32[]{:S(2)}) %collective-permute-start.4) | collective-permute-done | bytes 286752 | tf_op jit(solution)/shard_map/ppermute | solution.py:471
  24.0 16.6 %collective-permute-done.3.refs_1_ = bf16[32,4480]{1,0:T(8,128)(2,1)S(1)} collective-permute-done((bf16[32,4480]{1,0:T(8,128)(2,1)S(1)}, bf16[32,4480]{1,0:T(8,128)(2,1)S(1)}, u32[]{:S(2)}, u32[]{:S(2)}) %collective-permute-start.3) | collective-permute-done | bytes 286752 | tf_op jit(solution)/shard_map/ppermute | solution.py:471
  58.7 19.3 %collective-permute-done.7.refs_6_ = bf16[3,32,4480]{2,1,0:T(8,128)(2,1)S(1)} collective-permute-done((bf16[3,32,4480]{2,1,0:T(8,128)(2,1)S(1)}, bf16[3,32,4480]{2,1,0:T(8,128)(2,1)S(1)}, u32[]{:S(2)}, u32[]{:S(2)}) %collective-permute-start.7) | collective-permute-done | bytes 860192 | tf_op jit(solution)/shard_map/ppermute | solution.py:471
  78.0 20.6 %collective-permute-done.6.refs_5_ = bf16[3,32,4480]{2,1,0:T(8,128)(2,1)} collective-permute-done((bf16[3,32,4480]{2,1,0:T(8,128)(2,1)S(1)}, bf16[3,32,4480]{2,1,0:T(8,128)(2,1)}, u32[]{:S(2)}, u32[]{:S(2)}) %collective-permute-start.6) | collective-permute-done | bytes 860192 | tf_op jit(solution)/shard_map/ppermute | solution.py:471
  109.2 7.4 %place_rows.1 = bf16[1024,4480]{1,0:T(8,128)(2,1)} custom-call(s32[3]{0:T(128)S(1)} %pad_add_fusion.where.refs_0_, bf16[2,256,4352]{2,1,0:T(8,128)(2,1)} %refs_0_.6, bf16[2,256,32]{2,1,0:T(8,128)(2,1)S(1)} %copy.135.refs_1_.refs_2_, bf16[3,32,4480]{2,1,0:T(8,128)(2,1)S(1)} %stack.122.refs_3_.refs_1_.refs_2_, ...), custom_call_target="tpu_custom_call" | custom-call | flops 1100000000 | bytes 1000000 | tf_op jit(solution)/shard_map/place_rows/pallas_call | solution.py:586
  125.5 9.0 %conv_states.2 = (bf16[2,256,2304]{2,1,0:T(8,128)(2,1)S(1)}, f32[2,256,128]{2,1,0:T(8,128)S(1)}, f32[2,256,128]{2,1,0:T(8,128)S(1)}, f32[2,32,256]{2,1,0:T(8,128...) custom-call(bf16[2,256,2432]{2,1,0:T(8,128)(2,1)} %bitcast.164, ...), custom_call_target="tpu_custom_call" | custom-call | flops 2200000000 | bytes 2000000 | tf_op jit(solution)/shard_map/conv_states/pallas_call | solution.py:411
  163.3 11.8 %mix_within.2.refs_3_.refs_1_ = f32[2,256,2048]{2,1,0:T(8,128)} custom-call(bf16[2,256,2304]{2,1,0:T(8,128)(2,1)S(1)} %get-tuple-element.93.refs_0_.refs_2_.refs_6_.refs_1_.refs_3_, f32[2,256,128]{2,1,0:T(8,128)S(1)} %copy-done.67, f32[2,256,128]{2,1,0:T(8,128)S(1)} %copy-done.37, f32[2,32,256]{2,1,0:T(8,128)S(1)} %copy-done.111, ...), custom_call_target="tpu_custom_call" | custom-call | flops 3300000000 | bytes 3000000 | tf_op jit(solution)/shard_map/mix_within/pallas_call | solution.py:411
  208.3 9.3 %conv_states.3 = (bf16[2,256,2304]{2,1,0:T(8,128)(2,1)}, f32[2,256,128]{2,1,0:T(8,128)S(1)}, f32[2,256,128]{2,1,0:T(8,128)S(1)}, f32[2,32,256]{2,1,0:T(8,128)S(1...) custom-call(bf16[2,256,2432]{2,1,0:T(8,128)(2,1)} %bitcast.167, ...), custom_call_target="tpu_custom_call" | custom-call | flops 2200000000 | bytes 2000000 | tf_op jit(solution)/shard_map/conv_states/pallas_call | solution.py:411
  243.2 11.8 %mix_within.3.refs_3_.refs_1_ = f32[2,256,2048]{2,1,0:T(8,128)} custom-call(bf16[2,256,2304]{2,1,0:T(8,128)(2,1)S(1)} %copy-done.3, f32[2,256,128]{2,1,0:T(8,128)S(1)} %copy-done.71, f32[2,256,128]{2,1,0:T(8,128)S(1)} %copy-done.42, f32[2,32,256]{2,1,0:T(8,128)S(1)} %copy-done.108, f32[2,256,128]{2,1,0:T(8,128)S(1)} %copy-done.12, ...), custom_call_target="tpu_custom_call" | custom-call | flops 3300000000 | bytes 3000000 | tf_op jit(solution)/shard_map/mix_within/pallas_call | solution.py:411
  273.3 11.8 %gate_back.2 = (bf16[2,256,2048]{2,1,0:T(8,128)(2,1)}, bf16[2,256,3072]{2,1,0:T(8,128)(2,1)}, bf16[2,144,2048]{2,1,0:T(8,128)(2,1)S(1)}, f32[2,256,128]{2,1,0:T(...) custom-call(bf16[2,256,2048]{2,1,0:T(8,128)(2,1)} %bitcast.170, bf16[2,256,1024]{2,1,0:T(8,128)(2,1)S(1)} %copy-done.18, ...), custom_call_target="tpu_custom_call" | custom-call | flops 3024999936 | bytes 2750000 | tf_op jit(solution)/shard_map/gate_back/pallas_call | solution.py:411
  299.3 17.2 %mix_within_back.2 = (bf16[2,256,2048]{2,1,0:T(8,128)(2,1)S(1)}, f32[2,256,256]{2,1,0:T(8,128)S(1)}, f32[2,256,128]{2,1,0:T(8,128)S(1)}) custom-call(bf16[2,256,2048]{2,1,0:T(8,128)(2,1)} %get-tuple-element.110.refs_0_.refs_2_, bf16[2,256,2304]{2,1,0:T(8,128)(2,1)} %get-tuple-element.100.refs_0_.refs_2_.refs_6_.refs_1_.refs_3_, ...), custom_call_target="tpu_custom_call" | custom-call | flops 4674999808 | bytes 4250000 | tf_op jit(solution)/shard_map/mix_within_back/pallas_call | solution.py:411
  316.6 11.5 %collective-permute-done.24.refs_1_ = bf16[144,2048]{1,0:T(8,128)(2,1)S(1)} collective-permute-done((bf16[144,2048]{1,0:T(8,128)(2,1)S(1)}, bf16[144,2048]{1,0:T(8,128)(2,1)S(1)}, u32[]{:S(2)}, u32[]{:S(2)}) %collective-permute-start.24) | collective-permute-done | bytes 589856 | tf_op jit(solution)/shard_map/ppermute | solution.py:508
  328.5 9.4 %first_grads.2.refs_19_ = bf16[4,4,128,1024]{3,2,1,0:T(8,128)(2,1)} custom-call(s32[3]{0:T(128)S(1)} %copy-done.81, bf16[1536,512]{1,0:T(8,128)(2,1)S(1)} %get-tuple-element.117.refs_1_, bf16[1536,512]{1,0:T(8,128)(2,1)S(1)} %collective-permute-done.27.refs_2_, bf16[512,3072]{1,0:T(8,128)(2,1)} %bitcast.161, ...), custom_call_target="tpu_custom_call" | custom-call | flops 2750000128 | bytes 2500000 | tf_op jit(solution)/shard_map/first_grads/pallas_call | solution.py:458
  345.2 18.7 %conv_back.2 = (bf16[2,256,2432]{2,1,0:T(8,128)(2,1)}, f32[2,8,2304]{2,1,0:T(8,128)S(1)}, f32[8,2304]{1,0:T(8,128)S(1)}, f32[8,128]{1,0:T(8,128)S(1)}) custom-call(s32[3]{0:T(128)S(1)} %copy-done.81, bf16[2,256,2048]{2,1,0:T(8,128)(2,1)} %copy-done.22, bf16[2,256,2048]{2,1,0:T(8,128)(2,1)} %get-tuple-element.110.refs_0_.refs_2_, ...), custom_call_target="tpu_custom_call" | custom-call | flops 4674999808 | bytes 4250000 | tf_op jit(solution)/shard_map/conv_back/pallas_call | solution.py:411
  391.9 11.5 %gate_back.3 = (bf16[2,256,2048]{2,1,0:T(8,128)(2,1)}, bf16[2,256,3072]{2,1,0:T(8,128)(2,1)}, bf16[2,144,2048]{2,1,0:T(8,128)(2,1)S(1)}, f32[2,256,128]{2,1,0:T(...) custom-call(bf16[2,256,2048]{2,1,0:T(8,128)(2,1)} %bitcast.169, bf16[2,256,1024]{2,1,0:T(8,128)(2,1)S(1)} %fusion.56.refs_1_, ...), custom_call_target="tpu_custom_call" | custom-call | flops 3024999936 | bytes 2750000 | tf_op jit(solution)/shard_map/gate_back/pallas_call | solution.py:411
  415.8 17.2 %mix_within_back.3 = (bf16[2,256,2048]{2,1,0:T(8,128)(2,1)S(1)}, f32[2,256,256]{2,1,0:T(8,128)S(1)}, f32[2,256,128]{2,1,0:T(8,128)S(1)}) custom-call(bf16[2,256,2048]{2,1,0:T(8,128)(2,1)} %get-tuple-element.128.refs_0_.refs_2_, bf16[2,256,2304]{2,1,0:T(8,128)(2,1)} %copy-done.2, f32[2,256,128]{2,1,0:T(8,128)S(1)} %copy-done.68, ...), custom_call_target="tpu_custom_call" | custom-call | flops 4674999808 | bytes 4250000 | tf_op jit(solution)/shard_map/mix_within_back/pallas_call | solution.py:411
  433.1 10.2 %collective-permute-done.34.refs_1_ = bf16[144,2048]{1,0:T(8,128)(2,1)S(1)} collective-permute-done((bf16[144,2048]{1,0:T(8,128)(2,1)S(1)}, bf16[144,2048]{1,0:T(8,128)(2,1)S(1)}, u32[]{:S(2)}, u32[]{:S(2)}) %collective-permute-start.34) | collective-permute-done | bytes 589856 | tf_op jit(solution)/shard_map/ppermute | solution.py:508
  446.0 9.8 %first_grads.3 = (bf16[5,128,1024]{2,1,0:T(8,128)(2,1)S(1)}, bf16[5,128,1024]{2,1,0:T(8,128)(2,1)}, bf16[5,128,1024]{2,1,0:T(8,128)(2,1)S(1)}, bf16[5,128,1024]{2,1,0:T(8,128)(2,1)}) custom-call(s32[3]{0:T(128)S(1)} %copy-done.81, bf16[1536,512]{1,0:T(8,128)(2,1)} %copy-done.23, bf16[1536,512]{1,0:T(8,128)(2,1)} %copy-done.123, bf16[512,3072]{1,0:T(8,128)(2,1)} %bitcast.158, ...), custom_call_target="tpu_custom_call" | custom-call | flops 2750000128 | bytes 2500000 | tf_op jit(solution)/shard_map/first_grads/pallas_call | solution.py:458
  462.4 18.8 %conv_back.3 = (bf16[2,256,2432]{2,1,0:T(8,128)(2,1)}, f32[2,8,2304]{2,1,0:T(8,128)S(1)}, f32[8,2304]{1,0:T(8,128)S(1)}, f32[8,128]{1,0:T(8,128)S(1)}) custom-call(s32[3]{0:T(128)S(1)} %copy-done.81, bf16[2,256,2048]{2,1,0:T(8,128)(2,1)} %copy-done.19, bf16[2,256,2048]{2,1,0:T(8,128)(2,1)} %get-tuple-element.128.refs_0_.refs_2_, ...), custom_call_target="tpu_custom_call" | custom-call | flops 4674999808 | bytes 4250000 | tf_op jit(solution)/shard_map/conv_back/pallas_call | solution.py:411
  489.6 26.0 %collective-permute-done.41.refs_2_ = bf16[5,128,1024]{2,1,0:T(8,128)(2,1)} collective-permute-done((bf16[5,128,1024]{2,1,0:T(8,128)(2,1)S(1)}, bf16[5,128,1024]{2,1,0:T(8,128)(2,1)}, u32[]{:S(2)}, u32[]{:S(2)}) %collective-permute-start.41) | collective-permute-done | bytes 1310752 | tf_op jit(solution)/shard_map/ppermute | solution.py:471
  541.6 16.2 %collective-permute-done.43.refs_1_ = bf16[2,128,1024]{2,1,0:T(8,128)(2,1)S(1)} collective-permute-done((bf16[2,128,1024]{2,1,0:T(8,128)(2,1)S(1)}, bf16[2,128,1024]{2,1,0:T(8,128)(2,1)S(1)}, u32[]{:S(2)}, u32[]{:S(2)}) %collective-permute-start.43) | collective-permute-done | bytes 524320 | tf_op jit(solution)/shard_map/ppermute | solution.py:471
  583.3 23.2 %collective-permute-done.52.refs_2_ = bf16[4,32,2432]{2,1,0:T(8,128)(2,1)S(1)} collective-permute-done((bf16[4,32,2432]{2,1,0:T(8,128)(2,1)S(1)}, bf16[4,32,2432]{2,1,0:T(8,128)(2,1)S(1)}, u32[]{:S(2)}, u32[]{:S(2)}) %collective-permute-start.52) | collective-permute-done | bytes 622624 | tf_op jit(solution)/shard_map/ppermute | solution.py:471
  622.5 9.3 %collective-permute-done.64.refs_3_.refs_9_ = bf16[192,1024]{1,0:T(8,128)(2,1)S(1)} collective-permute-done((bf16[192,1024]{1,0:T(8,128)(2,1)S(1)}, bf16[192,1024]{1,0:T(8,128)(2,1)S(1)}, u32[]{:S(2)}, u32[]{:S(2)}) %collective-permute-start.64) | collective-permute-done | bytes 393248 | tf_op jit(solution)/shard_map/ppermute | solution.py:471
  631.8 7.5 %collective-permute-done.63.refs_2_.refs_8_ = bf16[192,1024]{1,0:T(8,128)(2,1)S(1)} collective-permute-done((bf16[192,1024]{1,0:T(8,128)(2,1)S(1)}, bf16[192,1024]{1,0:T(8,128)(2,1)S(1)}, u32[]{:S(2)}, u32[]{:S(2)}) %collective-permute-start.63) | collective-permute-done | bytes 393248 | tf_op jit(solution)/shard_map/ppermute | solution.py:471
  (575 shorter events, 311.7 us)
Async XLA Ops:
  7.2 167.9 %all-gather.3.cloned.1.call-start = ((), (), s32[]{:S(2)}) async-start(), calls=%async_computation.1 | async-start | bytes 13787136 | tf_op jit(solution)/shard_map/all_gather | solution.py:1003
  43.7 211.3 %all-gather.5.cloned.1.call-start = ((), (), s32[]{:S(2)}) async-start(), calls=%async_computation.2 | async-start | bytes 4325376 | tf_op jit(solution)/shard_map/all_gather | solution.py:1008
  57.3 41.3 %collective-permute-start.6 = (bf16[3,32,4480]{2,1,0:T(8,128)(2,1)S(1)}, bf16[3,32,4480]{2,1,0:T(8,128)(2,1)}, u32[]{:S(2)}, u32[]{:S(2)}) collective-permute-start(bf16[3,32,4480]{2,1,0:T(8,128)(2,1)S(1)} %stack.122.refs_3_.refs_1_.refs_2_), channel_id=1, source_target_pairs={{0,4},{1,5},{2,6},{3,7},{4,0},{5,1},{6,2},{7,3},{8,12},{9,13},{10,... | collective-permute-start | bytes 2580488 | tf_op jit(solution)/shard_map/ppermute | solution.py:471
  58.3 41.0 %collective-permute-start.5 = (bf16[3,32,4480]{2,1,0:T(8,128)(2,1)S(1)}, bf16[3,32,4480]{2,1,0:T(8,128)(2,1)}, u32[]{:S(2)}, u32[]{:S(2)}) collective-permute-start(bf16[3,32,4480]{2,1,0:T(8,128)(2,1)S(1)} %stack.122.refs_3_.refs_1_.refs_2_), channel_id=1, source_target_pairs={{0,2},{1,3},{2,0},{3,1},{4,6},{5,7},{6,4},{7,5},{8,10},{9,11},{10,... | collective-permute-start | bytes 2580488 | tf_op jit(solution)/shard_map/ppermute | solution.py:471
  109.1 335.6 %reduce-scatter.2.cloned.1.call-start = ((), (), s32[]{:S(2)}) async-start(), calls=%async_computation.3 | async-start | bytes 5242880 | tf_op jit(solution)/shard_map/reduce_scatter | solution.py:1122
  145.7 34.6 %collective-permute-start.14 = (bf16[144,2048]{1,0:T(8,128)(2,1)}, bf16[144,2048]{1,0:T(8,128)(2,1)}, u32[]{:S(2)}, u32[]{:S(2)}) collective-permute-start(bf16[144,2048]{1,0:T(8,128)(2,1)} %join_states.4.refs_8_), channel_id=1, source_target_pairs={{0,2},{1,3},{2,4},{3,5},{4,6},{5,7},{8,10},{9,11},{10,12},{11,13},... | collective-permute-start | bytes 1769480 | tf_op jit(solution)/shard_map/ppermute | solution.py:508
  151.3 29.0 %collective-permute-start.13 = (bf16[144,2048]{1,0:T(8,128)(2,1)}, bf16[144,2048]{1,0:T(8,128)(2,1)}, u32[]{:S(2)}, u32[]{:S(2)}) collective-permute-start(bf16[144,2048]{1,0:T(8,128)(2,1)} %join_states.4.refs_8_), channel_id=1, source_target_pairs={{0,4},{1,5},{2,6},{3,7},{8,12},{9,13},{10,14},{11,15},{16,20},{17,... | collective-permute-start | bytes 1769480 | tf_op jit(solution)/shard_map/ppermute | solution.py:508
  285.7 42.7 %collective-permute-start.28 = (bf16[512,3072]{1,0:T(8,128)(2,1)}, bf16[512,3072]{1,0:T(8,128)(2,1)}, u32[]{:S(2)}, u32[]{:S(2)}) collective-permute-start(bf16[512,3072]{1,0:T(8,128)(2,1)} %bitcast.160), channel_id=1, source_target_pairs={{0,1},{1,0},{2,3},{3,2},{4,5},{5,4},{6,7},{7,6},{8,9},{9,8},{10,11... | collective-permute-start | bytes 9437192 | tf_op jit(solution)/shard_map/ppermute | solution.py:471
  290.0 38.4 %collective-permute-start.27 = (bf16[1536,512]{1,0:T(8,128)(2,1)}, bf16[1536,512]{1,0:T(8,128)(2,1)S(1)}, u32[]{:S(2)}, u32[]{:S(2)}) collective-permute-start(bf16[1536,512]{1,0:T(8,128)(2,1)} %get-tuple-element.118), channel_id=1, source_target_pairs={{0,1},{1,0},{2,3},{3,2},{4,5},{5,4},{6,7},{7,6},{8,9},{9,8},{10,11... | collective-permute-start | bytes 4718600 | tf_op jit(solution)/shard_map/ppermute | solution.py:471
  296.7 31.4 %collective-permute-start.24 = (bf16[144,2048]{1,0:T(8,128)(2,1)S(1)}, bf16[144,2048]{1,0:T(8,128)(2,1)S(1)}, u32[]{:S(2)}, u32[]{:S(2)}) collective-permute-start(bf16[144,2048]{1,0:T(8,128)(2,1)S(1)} %join_states.6.refs_10_), channel_id=1, source_target_pairs={{4,0},{5,1},{6,2},{7,3},{12,8},{13,9},{14,10},{15,11},{20,16},{21,... | collective-permute-start | bytes 1769480 | tf_op jit(solution)/shard_map/ppermute | solution.py:508
  298.0 30.1 %collective-permute-start.23 = (bf16[144,2048]{1,0:T(8,128)(2,1)S(1)}, bf16[144,2048]{1,0:T(8,128)(2,1)S(1)}, u32[]{:S(2)}, u32[]{:S(2)}) collective-permute-start(bf16[144,2048]{1,0:T(8,128)(2,1)S(1)} %join_states.6.refs_10_), channel_id=1, source_target_pairs={{6,0},{7,1},{14,8},{15,9},{22,16},{23,17},{30,24},{31,25}} | collective-permute-start | bytes 1769480 | tf_op jit(solution)/shard_map/ppermute | solution.py:508
  403.4 41.2 %collective-permute-start.38 = (bf16[512,3072]{1,0:T(8,128)(2,1)}, bf16[512,3072]{1,0:T(8,128)(2,1)}, u32[]{:S(2)}, u32[]{:S(2)}) collective-permute-start(bf16[512,3072]{1,0:T(8,128)(2,1)} %bitcast.157), channel_id=1, source_target_pairs={{0,1},{1,0},{2,3},{3,2},{4,5},{5,4},{6,7},{7,6},{8,9},{9,8},{10,11... | collective-permute-start | bytes 9437192 | tf_op jit(solution)/shard_map/ppermute | solution.py:471
  404.0 39.5 %collective-permute-start.37 = (bf16[1536,512]{1,0:T(8,128)(2,1)S(1)}, bf16[1536,512]{1,0:T(8,128)(2,1)S(1)}, u32[]{:S(2)}, u32[]{:S(2)}) collective-permute-start(bf16[1536,512]{1,0:T(8,128)(2,1)S(1)} %copy-done.102), channel_id=1, source_target_pairs={{0,1},{1,0},{2,3},{3,2},{4,5},{5,4},{6,7},{7,6},{8,9},{9,8},{10,11... | collective-permute-start | bytes 4718600 | tf_op jit(solution)/shard_map/ppermute | solution.py:471
  413.0 30.3 %collective-permute-start.34 = (bf16[144,2048]{1,0:T(8,128)(2,1)S(1)}, bf16[144,2048]{1,0:T(8,128)(2,1)S(1)}, u32[]{:S(2)}, u32[]{:S(2)}) collective-permute-start(bf16[144,2048]{1,0:T(8,128)(2,1)S(1)} %join_states.7.refs_10_), channel_id=1, source_target_pairs={{4,0},{5,1},{6,2},{7,3},{12,8},{13,9},{14,10},{15,11},{20,16},{21,... | collective-permute-start | bytes 1769480 | tf_op jit(solution)/shard_map/ppermute | solution.py:508
  456.9 32.7 %collective-permute-start.40 = (bf16[5,128,1024]{2,1,0:T(8,128)(2,1)}, bf16[5,128,1024]{2,1,0:T(8,128)(2,1)}, u32[]{:S(2)}, u32[]{:S(2)}) collective-permute-start(bf16[5,128,1024]{2,1,0:T(8,128)(2,1)} %get-tuple-element.137.refs_20_), channel_id=1, source_target_pairs={{0,2},{1,3},{2,0},{3,1},{4,6},{5,7},{6,4},{7,5},{8,10},{9,11},{10,... | collective-permute-start | bytes 3932168 | tf_op jit(solution)/shard_map/ppermute | solution.py:471
  457.1 58.6 %collective-permute-start.41 = (bf16[5,128,1024]{2,1,0:T(8,128)(2,1)S(1)}, bf16[5,128,1024]{2,1,0:T(8,128)(2,1)}, u32[]{:S(2)}, u32[]{:S(2)}) collective-permute-start(bf16[5,128,1024]{2,1,0:T(8,128)(2,1)S(1)} %get-tuple-element.138.refs_21_), channel_id=1, source_target_pairs={{0,4},{1,5},{2,6},{3,7},{4,0},{5,1},{6,2},{7,3},{8,12},{9,13},{10,... | collective-permute-start | bytes 3932168 | tf_op jit(solution)/shard_map/ppermute | solution.py:471
  457.1 58.6 %collective-permute-start.42 = (bf16[5,128,1024]{2,1,0:T(8,128)(2,1)}, bf16[5,128,1024]{2,1,0:T(8,128)(2,1)}, u32[]{:S(2)}, u32[]{:S(2)}) collective-permute-start(bf16[5,128,1024]{2,1,0:T(8,128)(2,1)} %get-tuple-element.139.refs_22_), channel_id=1, source_target_pairs={{0,6},{1,7},{2,4},{3,5},{4,2},{5,3},{6,0},{7,1},{8,14},{9,15},{10,... | collective-permute-start | bytes 3932168 | tf_op jit(solution)/shard_map/ppermute | solution.py:471
  481.3 37.2 %collective-permute-start.39 = (bf16[2,8,2304]{2,1,0:T(8,128)(2,1)S(1)}, bf16[2,8,2304]{2,1,0:T(8,128)(2,1)S(1)}, u32[]{:S(2)}, u32[]{:S(2)}) collective-permute-start(bf16[2,8,2304]{2,1,0:T(8,128)(2,1)S(1)} %convert_element_type.198), channel_id=1, source_target_pairs={{1,0},{2,1},{3,2},{4,3},{5,4},{6,5},{7,6},{9,8},{10,9},{11,10},{12... | collective-permute-start | bytes 221192 | tf_op jit(solution)/shard_map/ppermute | solution.py:1150
  534.3 29.2 %collective-permute-start.58 = (bf16[4,32,2432]{2,1,0:T(8,128)(2,1)S(1)}, bf16[4,32,2432]{2,1,0:T(8,128)(2,1)S(1)}, u32[]{:S(2)}, u32[]{:S(2)}) collective-permute-start(bf16[4,32,2432]{2,1,0:T(8,128)(2,1)S(1)} %get-tuple-element.160), channel_id=1, source_target_pairs={{0,4},{1,5},{2,6},{3,7},{4,0},{5,1},{6,2},{7,3},{8,12},{9,13},{10,... | collective-permute-start | bytes 1867784 | tf_op jit(solution)/shard_map/ppermute | solution.py:471
  534.3 29.2 %collective-permute-start.59 = (bf16[4,32,2432]{2,1,0:T(8,128)(2,1)S(1)}, bf16[4,32,2432]{2,1,0:T(8,128)(2,1)S(1)}, u32[]{:S(2)}, u32[]{:S(2)}) collective-permute-start(bf16[4,32,2432]{2,1,0:T(8,128)(2,1)S(1)} %get-tuple-element.161), channel_id=1, source_target_pairs={{0,6},{1,7},{2,4},{3,5},{4,2},{5,3},{6,0},{7,1},{8,14},{9,15},{10,... | collective-permute-start | bytes 1867784 | tf_op jit(solution)/shard_map/ppermute | solution.py:471
  566.4 40.1 %collective-permute-start.52 = (bf16[4,32,2432]{2,1,0:T(8,128)(2,1)S(1)}, bf16[4,32,2432]{2,1,0:T(8,128)(2,1)S(1)}, u32[]{:S(2)}, u32[]{:S(2)}) collective-permute-start(bf16[4,32,2432]{2,1,0:T(8,128)(2,1)S(1)} %get-tuple-element.153), channel_id=1, source_target_pairs={{0,4},{1,5},{2,6},{3,7},{4,0},{5,1},{6,2},{7,3},{8,12},{9,13},{10,... | collective-permute-start | bytes 1867784 | tf_op jit(solution)/shard_map/ppermute | solution.py:471
  568.0 38.6 %collective-permute-start.53 = (bf16[4,32,2432]{2,1,0:T(8,128)(2,1)S(1)}, bf16[4,32,2432]{2,1,0:T(8,128)(2,1)S(1)}, u32[]{:S(2)}, u32[]{:S(2)}) collective-permute-start(bf16[4,32,2432]{2,1,0:T(8,128)(2,1)S(1)} %get-tuple-element.154), channel_id=1, source_target_pairs={{0,6},{1,7},{2,4},{3,5},{4,2},{5,3},{6,0},{7,1},{8,14},{9,15},{10,... | collective-permute-start | bytes 1867784 | tf_op jit(solution)/shard_map/ppermute | solution.py:471
  569.7 40.5 %collective-permute-start.49 = (bf16[256,1024]{1,0:T(8,128)(2,1)S(1)}, bf16[256,1024]{1,0:T(8,128)(2,1)S(1)}, u32[]{:S(2)}, u32[]{:S(2)}) collective-permute-start(bf16[256,1024]{1,0:T(8,128)(2,1)S(1)} %bitcast.128), channel_id=1, source_target_pairs={{0,6},{1,7},{2,4},{3,5},{4,2},{5,3},{6,0},{7,1},{8,14},{9,15},{10,... | collective-permute-start | bytes 1572872 | tf_op jit(solution)/shard_map/ppermute | solution.py:471
  583.0 33.8 %collective-permute-start.48 = (bf16[256,1024]{1,0:T(8,128)(2,1)S(1)}, bf16[256,1024]{1,0:T(8,128)(2,1)S(1)}, u32[]{:S(2)}, u32[]{:S(2)}) collective-permute-start(bf16[256,1024]{1,0:T(8,128)(2,1)S(1)} %bitcast.129), channel_id=1, source_target_pairs={{0,4},{1,5},{2,6},{3,7},{4,0},{5,1},{6,2},{7,3},{8,12},{9,13},{10,... | collective-permute-start | bytes 1572872 | tf_op jit(solution)/shard_map/ppermute | solution.py:471
  (201 other events, 2281.5 us)
Sparse Core Ops, SparseCore 0:
  43.8 121.8 all-gather.2
  168.6 60.0 all-gather.4
  339.1 74.9 reduce-scatter.1

commit v6 on v5

--- a/solution.py
+++ b/solution.py
@@ -953,7 +953,10 @@
     sizes = [a.shape[1] for a in small]
     own = jnp.concatenate(small, axis=1)
     if direct:
-        by_partner, bits = own[None], 1
+        share_in, share_out = model // (groups * peers), inner // (groups * peers)
+        all_columns = (0, inner + channels, True)
+        mix_z = from_along_z(take_share(in_weight, dt_weight, 0, all_columns, here, share_in, peers, ()), groups)
+        by_partner, bits = stacked([own], (mix_z,)), 1
         while bits < groups:
             by_partner = jnp.concatenate([by_partner, swap(by_partner, "fsdp", bits)])
             bits *= 2
@@ -981,13 +984,10 @@
     skip_all = jnp.repeat(joined(pieces[5]).astype(F32), span, axis=1)[:, None]
     gain_all = joined(pieces[6]).astype(F32)[:, None]
 
-    all_columns = (0, inner + channels, True)
     gate_all, mix_all, out_all = [], [], []
     for layer in range(layers):
         if direct:
-            share_in, share_out = model // (groups * peers), inner // (groups * peers)
             if layer == 0:
-                mix_z = from_along_z(take_share(in_weight, dt_weight, 0, all_columns, here, share_in, peers, ()), groups)
                 whole = fetched_by_all(
                     in_weight, dt_weight, 0, all_columns, here, groups, chips, mix_z, (norm_all, taps_all, rates_all, skip_all, gain_all)
                 )

time: 668 us -> 662 us (level)
    unnamed x314 -> x304, local copies, waits for them, and re-layouts: 33.8 us -> 33.9 us
    pallas_call x31 -> x32, Pallas kernels: 57.2 us -> 57.2 us  [whole_call(): pl.pallas_call(without(kernel, len(arrays), len(after)), in_specs=in_spec...]
  transfers between devices with their start and end apart: 69 -> 69, of which waited for: 30 -> 28; matrix products, arithmetic and copies ran while one was open for 12% -> 12% of each run, Pallas kernels for 28% -> 28%
where the time goes in v6:
time: 662 us; the launch traced here: 654 us
  Pallas kernels  230 us (35%)
  waiting for transfers between devices  212 us (32%)
  starting transfers between devices  84.1 us (13%)
  matrix products  61.5 us (9%)
  local copies, waits for them, and re-layouts  38.1 us (6%)
  between operations  16.3 us (2%)
  other arithmetic  11.3 us (2%)
    ppermute x49, waiting for transfers between devices, swap(): lax.ppermute(x, axis, [(i, i ^ bits) for i in range(lax.axis_size(axis))])  184 us
    pallas_call x12, Pallas kernels, call(): pl.pallas_call(without(kernel, len(arrays), len(after)), grid=(batch,), i...  150 us
    pallas_call x32, Pallas kernels, whole_call(): pl.pallas_call(without(kernel, len(arrays), len(after)), in_specs=in_spec...  57.2 us
    ppermute x49, starting transfers between devices, swap(): lax.ppermute(x, axis, [(i, i ^ bits) for i in range(lax.axis_size(axis))])  46.1 us
    unnamed x304, local copies, waits for them, and re-layouts  33.9 us
    dot_general x6, matrix products, dot(): return jnp.dot(a, b, preferred_element_type=F32)  33.2 us
    ppermute x12, starting transfers between devices, exchange(): got.append(lax.ppermute(joined, 'seq', route))  29.5 us
    dot_general x6, matrix products, dot_nt(): return lax.dot_general(a, b, NT, preferred_element_type=F32)  28.3 us
  transfers between devices with their start and end apart: 69, of which 28 were waited for; matrix products, arithmetic and copies ran while one was open for 12% of the time, Pallas kernels for 28%

profile of v6, /device:TPU:0, one launch (start us, length us, event | category | flops | bytes accessed | tf_op | source)
XLA Modules:
  0.0 653.9 jit_solution(11846126624814788358)
XLA Ops:
  16.8 7.2 %collective-permute-done.2.refs_2_ = bf16[32,4480]{1,0:T(8,128)(2,1)S(1)} collective-permute-done((bf16[32,4480]{1,0:T(8,128)(2,1)S(1)}, bf16[32,4480]{1,0:T(8,128)(2,1)S(1)}, u32[]{:S(2)}, u32[]{:S(2)}) %collective-permute-start.2) | collective-permute-done | bytes 286752 | tf_op jit(solution)/shard_map/ppermute | solution.py:471
  24.0 16.6 %collective-permute-done.1.refs_1_ = bf16[32,4480]{1,0:T(8,128)(2,1)S(1)} collective-permute-done((bf16[32,4480]{1,0:T(8,128)(2,1)S(1)}, bf16[32,4480]{1,0:T(8,128)(2,1)S(1)}, u32[]{:S(2)}, u32[]{:S(2)}) %collective-permute-start.1) | collective-permute-done | bytes 286752 | tf_op jit(solution)/shard_map/ppermute | solution.py:471
  62.6 15.5 %collective-permute-done.7.refs_6_ = bf16[3,32,4480]{2,1,0:T(8,128)(2,1)S(1)} collective-permute-done((bf16[3,32,4480]{2,1,0:T(8,128)(2,1)S(1)}, bf16[3,32,4480]{2,1,0:T(8,128)(2,1)S(1)}, u32[]{:S(2)}, u32[]{:S(2)}) %collective-permute-start.7) | collective-permute-done | bytes 860192 | tf_op jit(solution)/shard_map/ppermute | solution.py:471
  78.1 19.0 %collective-permute-done.6.refs_5_ = bf16[3,32,4480]{2,1,0:T(8,128)(2,1)} collective-permute-done((bf16[3,32,4480]{2,1,0:T(8,128)(2,1)S(1)}, bf16[3,32,4480]{2,1,0:T(8,128)(2,1)}, u32[]{:S(2)}, u32[]{:S(2)}) %collective-permute-start.6) | collective-permute-done | bytes 860192 | tf_op jit(solution)/shard_map/ppermute | solution.py:471
  107.0 7.4 %place_rows.1 = bf16[1024,4480]{1,0:T(8,128)(2,1)} custom-call(s32[3]{0:T(128)S(1)} %pad_add_fusion.where.refs_0_, bf16[2,256,4352]{2,1,0:T(8,128)(2,1)} %refs_0_.6, bf16[2,256,32]{2,1,0:T(8,128)(2,1)S(1)} %copy.133.refs_1_.refs_2_, bf16[3,32,4480]{2,1,0:T(8,128)(2,1)S(1)} %stack.123.refs_1_.refs_3_.refs_2_, ...), custom_call_target="tpu_custom_call" | custom-call | flops 1100000000 | bytes 1000000 | tf_op jit(solution)/shard_map/place_rows/pallas_call | solution.py:586
  123.1 9.0 %conv_states.2 = (bf16[2,256,2304]{2,1,0:T(8,128)(2,1)S(1)}, f32[2,256,128]{2,1,0:T(8,128)S(1)}, f32[2,256,128]{2,1,0:T(8,128)S(1)}, f32[2,32,256]{2,1,0:T(8,128...) custom-call(bf16[2,256,2432]{2,1,0:T(8,128)(2,1)} %bitcast.163, ...), custom_call_target="tpu_custom_call" | custom-call | flops 2200000000 | bytes 2000000 | tf_op jit(solution)/shard_map/conv_states/pallas_call | solution.py:411
  160.2 11.8 %mix_within.2.refs_3_.refs_1_ = f32[2,256,2048]{2,1,0:T(8,128)} custom-call(bf16[2,256,2304]{2,1,0:T(8,128)(2,1)S(1)} %get-tuple-element.93.refs_0_.refs_2_.refs_6_.refs_1_.refs_3_, f32[2,256,128]{2,1,0:T(8,128)S(1)} %copy-done.67, f32[2,256,128]{2,1,0:T(8,128)S(1)} %copy-done.37, f32[2,32,256]{2,1,0:T(8,128)S(1)} %copy-done.105, ...), custom_call_target="tpu_custom_call" | custom-call | flops 3300000000 | bytes 3000000 | tf_op jit(solution)/shard_map/mix_within/pallas_call | solution.py:411
  204.9 9.2 %conv_states.3 = (bf16[2,256,2304]{2,1,0:T(8,128)(2,1)}, f32[2,256,128]{2,1,0:T(8,128)S(1)}, f32[2,256,128]{2,1,0:T(8,128)S(1)}, f32[2,32,256]{2,1,0:T(8,128)S(1...) custom-call(bf16[2,256,2432]{2,1,0:T(8,128)(2,1)} %bitcast.166, ...), custom_call_target="tpu_custom_call" | custom-call | flops 2200000000 | bytes 2000000 | tf_op jit(solution)/shard_map/conv_states/pallas_call | solution.py:411
  238.9 11.8 %mix_within.3.refs_3_.refs_1_ = f32[2,256,2048]{2,1,0:T(8,128)} custom-call(bf16[2,256,2304]{2,1,0:T(8,128)(2,1)S(1)} %copy-done.3, f32[2,256,128]{2,1,0:T(8,128)S(1)} %copy-done.71, f32[2,256,128]{2,1,0:T(8,128)S(1)} %copy-done.42, f32[2,32,256]{2,1,0:T(8,128)S(1)} %copy-done.102, f32[2,256,128]{2,1,0:T(8,128)S(1)} %copy-done.12, ...), custom_call_target="tpu_custom_call" | custom-call | flops 3300000000 | bytes 3000000 | tf_op jit(solution)/shard_map/mix_within/pallas_call | solution.py:411
  269.3 11.8 %gate_back.2 = (bf16[2,256,2048]{2,1,0:T(8,128)(2,1)}, bf16[2,256,3072]{2,1,0:T(8,128)(2,1)}, bf16[2,144,2048]{2,1,0:T(8,128)(2,1)S(1)}, f32[2,256,128]{2,1,0:T(...) custom-call(bf16[2,256,2048]{2,1,0:T(8,128)(2,1)} %bitcast.169, bf16[2,256,1024]{2,1,0:T(8,128)(2,1)S(1)} %copy-done.18, ...), custom_call_target="tpu_custom_call" | custom-call | flops 3024999936 | bytes 2750000 | tf_op jit(solution)/shard_map/gate_back/pallas_call | solution.py:411
  294.6 17.4 %mix_within_back.2 = (bf16[2,256,2048]{2,1,0:T(8,128)(2,1)S(1)}, f32[2,256,256]{2,1,0:T(8,128)S(1)}, f32[2,256,128]{2,1,0:T(8,128)S(1)}) custom-call(bf16[2,256,2048]{2,1,0:T(8,128)(2,1)} %get-tuple-element.110.refs_0_.refs_2_, bf16[2,256,2304]{2,1,0:T(8,128)(2,1)} %get-tuple-element.100.refs_0_.refs_2_.refs_6_.refs_1_.refs_3_, ...), custom_call_target="tpu_custom_call" | custom-call | flops 4674999808 | bytes 4250000 | tf_op jit(solution)/shard_map/mix_within_back/pallas_call | solution.py:411
  312.0 11.3 %collective-permute-done.24.refs_1_ = bf16[144,2048]{1,0:T(8,128)(2,1)S(1)} collective-permute-done((bf16[144,2048]{1,0:T(8,128)(2,1)S(1)}, bf16[144,2048]{1,0:T(8,128)(2,1)S(1)}, u32[]{:S(2)}, u32[]{:S(2)}) %collective-permute-start.24) | collective-permute-done | bytes 589856 | tf_op jit(solution)/shard_map/ppermute | solution.py:508
  323.7 9.4 %first_grads.2.refs_19_ = bf16[4,4,128,1024]{3,2,1,0:T(8,128)(2,1)} custom-call(s32[3]{0:T(128)S(1)} %pad_add_fusion.where.refs_0_, bf16[1536,512]{1,0:T(8,128)(2,1)S(1)} %get-tuple-element.117.refs_1_, bf16[1536,512]{1,0:T(8,128)(2,1)S(1)} %collective-permute-done.27.refs_2_, bf16[512,3072]{1,0:T(8,128)(2,1)} %bitcast.160, ...), custom_call_target="tpu_custom_call" | custom-call | flops 2750000128 | bytes 2500000 | tf_op jit(solution)/shard_map/first_grads/pallas_call | solution.py:458
  340.6 18.7 %conv_back.2 = (bf16[2,256,2432]{2,1,0:T(8,128)(2,1)}, f32[2,8,2304]{2,1,0:T(8,128)S(1)}, f32[8,2304]{1,0:T(8,128)S(1)}, f32[8,128]{1,0:T(8,128)S(1)}) custom-call(s32[3]{0:T(128)S(1)} %pad_add_fusion.where.refs_0_, bf16[2,256,2048]{2,1,0:T(8,128)(2,1)} %copy-done.22, bf16[2,256,2048]{2,1,0:T(8,128)(2,1)} %get-tuple-element.110.refs_0_.refs_2_, ...), custom_call_target="tpu_custom_call" | custom-call | flops 4674999808 | bytes 4250000 | tf_op jit(solution)/shard_map/conv_back/pallas_call | solution.py:411
  387.4 11.5 %gate_back.3 = (bf16[2,256,2048]{2,1,0:T(8,128)(2,1)}, bf16[2,256,3072]{2,1,0:T(8,128)(2,1)}, bf16[2,144,2048]{2,1,0:T(8,128)(2,1)S(1)}, f32[2,256,128]{2,1,0:T(...) custom-call(bf16[2,256,2048]{2,1,0:T(8,128)(2,1)} %bitcast.168, bf16[2,256,1024]{2,1,0:T(8,128)(2,1)S(1)} %fusion.56.refs_1_, ...), custom_call_target="tpu_custom_call" | custom-call | flops 3024999936 | bytes 2750000 | tf_op jit(solution)/shard_map/gate_back/pallas_call | solution.py:411
  411.1 17.2 %mix_within_back.3 = (bf16[2,256,2048]{2,1,0:T(8,128)(2,1)S(1)}, f32[2,256,256]{2,1,0:T(8,128)S(1)}, f32[2,256,128]{2,1,0:T(8,128)S(1)}) custom-call(bf16[2,256,2048]{2,1,0:T(8,128)(2,1)} %get-tuple-element.128.refs_0_.refs_2_, bf16[2,256,2304]{2,1,0:T(8,128)(2,1)} %copy-done.2, f32[2,256,128]{2,1,0:T(8,128)S(1)} %copy-done.68, ...), custom_call_target="tpu_custom_call" | custom-call | flops 4674999808 | bytes 4250000 | tf_op jit(solution)/shard_map/mix_within_back/pallas_call | solution.py:411
  428.4 10.3 %collective-permute-done.34.refs_1_ = bf16[144,2048]{1,0:T(8,128)(2,1)S(1)} collective-permute-done((bf16[144,2048]{1,0:T(8,128)(2,1)S(1)}, bf16[144,2048]{1,0:T(8,128)(2,1)S(1)}, u32[]{:S(2)}, u32[]{:S(2)}) %collective-permute-start.34) | collective-permute-done | bytes 589856 | tf_op jit(solution)/shard_map/ppermute | solution.py:508
  441.5 9.9 %first_grads.3 = (bf16[5,128,1024]{2,1,0:T(8,128)(2,1)S(1)}, bf16[5,128,1024]{2,1,0:T(8,128)(2,1)}, bf16[5,128,1024]{2,1,0:T(8,128)(2,1)S(1)}, bf16[5,128,1024]{2,1,0:T(8,128)(2,1)}) custom-call(s32[3]{0:T(128)S(1)} %pad_add_fusion.where.refs_0_, bf16[1536,512]{1,0:T(8,128)(2,1)} %copy-done.23, bf16[1536,512]{1,0:T(8,128)(2,1)} %copy-done.117, ...), custom_call_target="tpu_custom_call" | custom-call | flops 2750000128 | bytes 2500000 | tf_op jit(solution)/shard_map/first_grads/pallas_call | solution.py:458
  458.0 18.8 %conv_back.3 = (bf16[2,256,2432]{2,1,0:T(8,128)(2,1)}, f32[2,8,2304]{2,1,0:T(8,128)S(1)}, f32[8,2304]{1,0:T(8,128)S(1)}, f32[8,128]{1,0:T(8,128)S(1)}) custom-call(s32[3]{0:T(128)S(1)} %pad_add_fusion.where.refs_0_, bf16[2,256,2048]{2,1,0:T(8,128)(2,1)} %copy-done.19, bf16[2,256,2048]{2,1,0:T(8,128)(2,1)} %get-tuple-element.128.refs_0_.refs_2_, ...), custom_call_target="tpu_custom_call" | custom-call | flops 4674999808 | bytes 4250000 | tf_op jit(solution)/shard_map/conv_back/pallas_call | solution.py:411
  485.2 26.1 %collective-permute-done.41.refs_2_ = bf16[5,128,1024]{2,1,0:T(8,128)(2,1)} collective-permute-done((bf16[5,128,1024]{2,1,0:T(8,128)(2,1)S(1)}, bf16[5,128,1024]{2,1,0:T(8,128)(2,1)}, u32[]{:S(2)}, u32[]{:S(2)}) %collective-permute-start.41) | collective-permute-done | bytes 1310752 | tf_op jit(solution)/shard_map/ppermute | solution.py:471
  538.0 15.3 %collective-permute-done.43.refs_1_ = bf16[2,128,1024]{2,1,0:T(8,128)(2,1)S(1)} collective-permute-done((bf16[2,128,1024]{2,1,0:T(8,128)(2,1)S(1)}, bf16[2,128,1024]{2,1,0:T(8,128)(2,1)S(1)}, u32[]{:S(2)}, u32[]{:S(2)}) %collective-permute-start.43) | collective-permute-done | bytes 524320 | tf_op jit(solution)/shard_map/ppermute | solution.py:471
  578.6 22.2 %collective-permute-done.52.refs_2_ = bf16[4,32,2432]{2,1,0:T(8,128)(2,1)S(1)} collective-permute-done((bf16[4,32,2432]{2,1,0:T(8,128)(2,1)S(1)}, bf16[4,32,2432]{2,1,0:T(8,128)(2,1)S(1)}, u32[]{:S(2)}, u32[]{:S(2)}) %collective-permute-start.52) | collective-permute-done | bytes 622624 | tf_op jit(solution)/shard_map/ppermute | solution.py:471
  617.2 9.4 %collective-permute-done.64.refs_3_.refs_9_ = bf16[192,1024]{1,0:T(8,128)(2,1)S(1)} collective-permute-done((bf16[192,1024]{1,0:T(8,128)(2,1)S(1)}, bf16[192,1024]{1,0:T(8,128)(2,1)S(1)}, u32[]{:S(2)}, u32[]{:S(2)}) %collective-permute-start.64) | collective-permute-done | bytes 393248 | tf_op jit(solution)/shard_map/ppermute | solution.py:471
  626.6 7.3 %collective-permute-done.63.refs_2_.refs_8_ = bf16[192,1024]{1,0:T(8,128)(2,1)S(1)} collective-permute-done((bf16[192,1024]{1,0:T(8,128)(2,1)S(1)}, bf16[192,1024]{1,0:T(8,128)(2,1)S(1)}, u32[]{:S(2)}, u32[]{:S(2)}) %collective-permute-start.63) | collective-permute-done | bytes 393248 | tf_op jit(solution)/shard_map/ppermute | solution.py:471
  (566 shorter events, 313.4 us)
Async XLA Ops:
  7.2 164.8 %all-gather.3.cloned.1.call-start = ((), (), s32[]{:S(2)}) async-start(), calls=%async_computation.1 | async-start | bytes 13787136 | tf_op jit(solution)/shard_map/all_gather | solution.py:1003
  43.7 207.0 %all-gather.5.cloned.1.call-start = ((), (), s32[]{:S(2)}) async-start(), calls=%async_computation.2 | async-start | bytes 4325376 | tf_op jit(solution)/shard_map/all_gather | solution.py:1008
  57.5 39.6 %collective-permute-start.6 = (bf16[3,32,4480]{2,1,0:T(8,128)(2,1)S(1)}, bf16[3,32,4480]{2,1,0:T(8,128)(2,1)}, u32[]{:S(2)}, u32[]{:S(2)}) collective-permute-start(bf16[3,32,4480]{2,1,0:T(8,128)(2,1)S(1)} %stack.123.refs_1_.refs_3_.refs_2_), channel_id=1, source_target_pairs={{0,4},{1,5},{2,6},{3,7},{4,0},{5,1},{6,2},{7,3},{8,12},{9,13},{10,... | collective-permute-start | bytes 2580488 | tf_op jit(solution)/shard_map/ppermute | solution.py:471
  58.0 39.1 %collective-permute-start.5 = (bf16[3,32,4480]{2,1,0:T(8,128)(2,1)S(1)}, bf16[3,32,4480]{2,1,0:T(8,128)(2,1)}, u32[]{:S(2)}, u32[]{:S(2)}) collective-permute-start(bf16[3,32,4480]{2,1,0:T(8,128)(2,1)S(1)} %stack.123.refs_1_.refs_3_.refs_2_), channel_id=1, source_target_pairs={{0,2},{1,3},{2,0},{3,1},{4,6},{5,7},{6,4},{7,5},{8,10},{9,11},{10,... | collective-permute-start | bytes 2580488 | tf_op jit(solution)/shard_map/ppermute | solution.py:471
  61.8 378.4 %reduce-scatter.2.cloned.1.call-start = ((), (), s32[]{:S(2)}) async-start(), calls=%async_computation.3 | async-start | bytes 5242880 | tf_op jit(solution)/shard_map/reduce_scatter | solution.py:1122
  143.0 34.2 %collective-permute-start.14 = (bf16[144,2048]{1,0:T(8,128)(2,1)}, bf16[144,2048]{1,0:T(8,128)(2,1)}, u32[]{:S(2)}, u32[]{:S(2)}) collective-permute-start(bf16[144,2048]{1,0:T(8,128)(2,1)} %join_states.4.refs_8_), channel_id=1, source_target_pairs={{0,2},{1,3},{2,4},{3,5},{4,6},{5,7},{8,10},{9,11},{10,12},{11,13},... | collective-permute-start | bytes 1769480 | tf_op jit(solution)/shard_map/ppermute | solution.py:508
  281.1 42.6 %collective-permute-start.28 = (bf16[512,3072]{1,0:T(8,128)(2,1)}, bf16[512,3072]{1,0:T(8,128)(2,1)}, u32[]{:S(2)}, u32[]{:S(2)}) collective-permute-start(bf16[512,3072]{1,0:T(8,128)(2,1)} %bitcast.159), channel_id=1, source_target_pairs={{0,1},{1,0},{2,3},{3,2},{4,5},{5,4},{6,7},{7,6},{8,9},{9,8},{10,11... | collective-permute-start | bytes 9437192 | tf_op jit(solution)/shard_map/ppermute | solution.py:471
  285.4 38.2 %collective-permute-start.27 = (bf16[1536,512]{1,0:T(8,128)(2,1)}, bf16[1536,512]{1,0:T(8,128)(2,1)S(1)}, u32[]{:S(2)}, u32[]{:S(2)}) collective-permute-start(bf16[1536,512]{1,0:T(8,128)(2,1)} %get-tuple-element.118), channel_id=1, source_target_pairs={{0,1},{1,0},{2,3},{3,2},{4,5},{5,4},{6,7},{7,6},{8,9},{9,8},{10,11... | collective-permute-start | bytes 4718600 | tf_op jit(solution)/shard_map/ppermute | solution.py:471
  291.9 31.4 %collective-permute-start.24 = (bf16[144,2048]{1,0:T(8,128)(2,1)S(1)}, bf16[144,2048]{1,0:T(8,128)(2,1)S(1)}, u32[]{:S(2)}, u32[]{:S(2)}) collective-permute-start(bf16[144,2048]{1,0:T(8,128)(2,1)S(1)} %join_states.6.refs_10_), channel_id=1, source_target_pairs={{4,0},{5,1},{6,2},{7,3},{12,8},{13,9},{14,10},{15,11},{20,16},{21,... | collective-permute-start | bytes 1769480 | tf_op jit(solution)/shard_map/ppermute | solution.py:508
  293.2 30.1 %collective-permute-start.23 = (bf16[144,2048]{1,0:T(8,128)(2,1)S(1)}, bf16[144,2048]{1,0:T(8,128)(2,1)S(1)}, u32[]{:S(2)}, u32[]{:S(2)}) collective-permute-start(bf16[144,2048]{1,0:T(8,128)(2,1)S(1)} %join_states.6.refs_10_), channel_id=1, source_target_pairs={{6,0},{7,1},{14,8},{15,9},{22,16},{23,17},{30,24},{31,25}} | collective-permute-start | bytes 1769480 | tf_op jit(solution)/shard_map/ppermute | solution.py:508
  399.0 41.2 %collective-permute-start.38 = (bf16[512,3072]{1,0:T(8,128)(2,1)}, bf16[512,3072]{1,0:T(8,128)(2,1)}, u32[]{:S(2)}, u32[]{:S(2)}) collective-permute-start(bf16[512,3072]{1,0:T(8,128)(2,1)} %bitcast.156), channel_id=1, source_target_pairs={{0,1},{1,0},{2,3},{3,2},{4,5},{5,4},{6,7},{7,6},{8,9},{9,8},{10,11... | collective-permute-start | bytes 9437192 | tf_op jit(solution)/shard_map/ppermute | solution.py:471
  399.6 39.5 %collective-permute-start.37 = (bf16[1536,512]{1,0:T(8,128)(2,1)S(1)}, bf16[1536,512]{1,0:T(8,128)(2,1)S(1)}, u32[]{:S(2)}, u32[]{:S(2)}) collective-permute-start(bf16[1536,512]{1,0:T(8,128)(2,1)S(1)} %copy-done.96), channel_id=1, source_target_pairs={{0,1},{1,0},{2,3},{3,2},{4,5},{5,4},{6,7},{7,6},{8,9},{9,8},{10,11... | collective-permute-start | bytes 4718600 | tf_op jit(solution)/shard_map/ppermute | solution.py:471
  408.3 30.4 %collective-permute-start.34 = (bf16[144,2048]{1,0:T(8,128)(2,1)S(1)}, bf16[144,2048]{1,0:T(8,128)(2,1)S(1)}, u32[]{:S(2)}, u32[]{:S(2)}) collective-permute-start(bf16[144,2048]{1,0:T(8,128)(2,1)S(1)} %join_states.7.refs_10_), channel_id=1, source_target_pairs={{4,0},{5,1},{6,2},{7,3},{12,8},{13,9},{14,10},{15,11},{20,16},{21,... | collective-permute-start | bytes 1769480 | tf_op jit(solution)/shard_map/ppermute | solution.py:508
  409.6 29.1 %collective-permute-start.33 = (bf16[144,2048]{1,0:T(8,128)(2,1)S(1)}, bf16[144,2048]{1,0:T(8,128)(2,1)S(1)}, u32[]{:S(2)}, u32[]{:S(2)}) collective-permute-start(bf16[144,2048]{1,0:T(8,128)(2,1)S(1)} %join_states.7.refs_10_), channel_id=1, source_target_pairs={{6,0},{7,1},{14,8},{15,9},{22,16},{23,17},{30,24},{31,25}} | collective-permute-start | bytes 1769480 | tf_op jit(solution)/shard_map/ppermute | solution.py:508
  452.5 32.7 %collective-permute-start.40 = (bf16[5,128,1024]{2,1,0:T(8,128)(2,1)}, bf16[5,128,1024]{2,1,0:T(8,128)(2,1)}, u32[]{:S(2)}, u32[]{:S(2)}) collective-permute-start(bf16[5,128,1024]{2,1,0:T(8,128)(2,1)} %get-tuple-element.137.refs_20_), channel_id=1, source_target_pairs={{0,2},{1,3},{2,0},{3,1},{4,6},{5,7},{6,4},{7,5},{8,10},{9,11},{10,... | collective-permute-start | bytes 3932168 | tf_op jit(solution)/shard_map/ppermute | solution.py:471
  452.6 58.6 %collective-permute-start.41 = (bf16[5,128,1024]{2,1,0:T(8,128)(2,1)S(1)}, bf16[5,128,1024]{2,1,0:T(8,128)(2,1)}, u32[]{:S(2)}, u32[]{:S(2)}) collective-permute-start(bf16[5,128,1024]{2,1,0:T(8,128)(2,1)S(1)} %get-tuple-element.138.refs_21_), channel_id=1, source_target_pairs={{0,4},{1,5},{2,6},{3,7},{4,0},{5,1},{6,2},{7,3},{8,12},{9,13},{10,... | collective-permute-start | bytes 3932168 | tf_op jit(solution)/shard_map/ppermute | solution.py:471
  452.6 58.6 %collective-permute-start.42 = (bf16[5,128,1024]{2,1,0:T(8,128)(2,1)}, bf16[5,128,1024]{2,1,0:T(8,128)(2,1)}, u32[]{:S(2)}, u32[]{:S(2)}) collective-permute-start(bf16[5,128,1024]{2,1,0:T(8,128)(2,1)} %get-tuple-element.139.refs_22_), channel_id=1, source_target_pairs={{0,6},{1,7},{2,4},{3,5},{4,2},{5,3},{6,0},{7,1},{8,14},{9,15},{10,... | collective-permute-start | bytes 3932168 | tf_op jit(solution)/shard_map/ppermute | solution.py:471
  476.8 37.2 %collective-permute-start.39 = (bf16[2,8,2304]{2,1,0:T(8,128)(2,1)S(1)}, bf16[2,8,2304]{2,1,0:T(8,128)(2,1)S(1)}, u32[]{:S(2)}, u32[]{:S(2)}) collective-permute-start(bf16[2,8,2304]{2,1,0:T(8,128)(2,1)S(1)} %convert_element_type.198), channel_id=1, source_target_pairs={{1,0},{2,1},{3,2},{4,3},{5,4},{6,5},{7,6},{9,8},{10,9},{11,10},{12... | collective-permute-start | bytes 221192 | tf_op jit(solution)/shard_map/ppermute | solution.py:1150
  530.7 29.2 %collective-permute-start.58 = (bf16[4,32,2432]{2,1,0:T(8,128)(2,1)S(1)}, bf16[4,32,2432]{2,1,0:T(8,128)(2,1)S(1)}, u32[]{:S(2)}, u32[]{:S(2)}) collective-permute-start(bf16[4,32,2432]{2,1,0:T(8,128)(2,1)S(1)} %get-tuple-element.160), channel_id=1, source_target_pairs={{0,4},{1,5},{2,6},{3,7},{4,0},{5,1},{6,2},{7,3},{8,12},{9,13},{10,... | collective-permute-start | bytes 1867784 | tf_op jit(solution)/shard_map/ppermute | solution.py:471
  530.7 29.2 %collective-permute-start.59 = (bf16[4,32,2432]{2,1,0:T(8,128)(2,1)S(1)}, bf16[4,32,2432]{2,1,0:T(8,128)(2,1)S(1)}, u32[]{:S(2)}, u32[]{:S(2)}) collective-permute-start(bf16[4,32,2432]{2,1,0:T(8,128)(2,1)S(1)} %get-tuple-element.161), channel_id=1, source_target_pairs={{0,6},{1,7},{2,4},{3,5},{4,2},{5,3},{6,0},{7,1},{8,14},{9,15},{10,... | collective-permute-start | bytes 1867784 | tf_op jit(solution)/shard_map/ppermute | solution.py:471
  561.7 39.2 %collective-permute-start.52 = (bf16[4,32,2432]{2,1,0:T(8,128)(2,1)S(1)}, bf16[4,32,2432]{2,1,0:T(8,128)(2,1)S(1)}, u32[]{:S(2)}, u32[]{:S(2)}) collective-permute-start(bf16[4,32,2432]{2,1,0:T(8,128)(2,1)S(1)} %get-tuple-element.153), channel_id=1, source_target_pairs={{0,4},{1,5},{2,6},{3,7},{4,0},{5,1},{6,2},{7,3},{8,12},{9,13},{10,... | collective-permute-start | bytes 1867784 | tf_op jit(solution)/shard_map/ppermute | solution.py:471
  563.3 37.5 %collective-permute-start.53 = (bf16[4,32,2432]{2,1,0:T(8,128)(2,1)S(1)}, bf16[4,32,2432]{2,1,0:T(8,128)(2,1)S(1)}, u32[]{:S(2)}, u32[]{:S(2)}) collective-permute-start(bf16[4,32,2432]{2,1,0:T(8,128)(2,1)S(1)} %get-tuple-element.154), channel_id=1, source_target_pairs={{0,6},{1,7},{2,4},{3,5},{4,2},{5,3},{6,0},{7,1},{8,14},{9,15},{10,... | collective-permute-start | bytes 1867784 | tf_op jit(solution)/shard_map/ppermute | solution.py:471
  565.0 39.8 %collective-permute-start.49 = (bf16[256,1024]{1,0:T(8,128)(2,1)S(1)}, bf16[256,1024]{1,0:T(8,128)(2,1)S(1)}, u32[]{:S(2)}, u32[]{:S(2)}) collective-permute-start(bf16[256,1024]{1,0:T(8,128)(2,1)S(1)} %bitcast.127), channel_id=1, source_target_pairs={{0,6},{1,7},{2,4},{3,5},{4,2},{5,3},{6,0},{7,1},{8,14},{9,15},{10,... | collective-permute-start | bytes 1572872 | tf_op jit(solution)/shard_map/ppermute | solution.py:471
  578.4 33.8 %collective-permute-start.48 = (bf16[256,1024]{1,0:T(8,128)(2,1)S(1)}, bf16[256,1024]{1,0:T(8,128)(2,1)S(1)}, u32[]{:S(2)}, u32[]{:S(2)}) collective-permute-start(bf16[256,1024]{1,0:T(8,128)(2,1)S(1)} %bitcast.128), channel_id=1, source_target_pairs={{0,4},{1,5},{2,6},{3,7},{4,0},{5,1},{6,2},{7,3},{8,12},{9,13},{10,... | collective-permute-start | bytes 1572872 | tf_op jit(solution)/shard_map/ppermute | solution.py:471
  (196 other events, 2378.1 us)
Sparse Core Ops, SparseCore 0:
  43.8 121.8 all-gather.2
  168.6 60.1 all-gather.4
  334.4 74.4 reduce-scatter.1

commit v7 on v6

--- a/solution.py
+++ b/solution.py
@@ -1113,14 +1113,15 @@
                 ((width, width), F32), ((width, width), F32), ((width, inner), BF16), ((LANES, width), F32), ((width, LANES), F32),
             ], "mix_within_back", 17.0, after=(joined_state,),
         )
-        before, partner = entered(got, (d_stepped,))
+        filled = (d_stepped,)
         if direct and layer > 0:
             (parts,) = whole_call(
                 functools.partial(first_grads_kernel, groups, chips, inner, False), [mine, theirs, both, both_other],
-                [((groups, chips, big + inner // model * small, model), BF16)], 10.0, "first_grads", here, (before,),
+                [((groups, chips, big + inner // model * small, model), BF16)], 10.0, "first_grads", here, (d_stepped,),
             )
             far_sums.append(lax.psum_scatter(parts, "fsdp", scatter_dimension=0, tiled=True)[0])
-            arrived = (parts,)
+            filled += (parts,)
+        before, partner = entered(got, filled)
         if direct and layer == 0:
             first_blocks = whole_call(
                 functools.partial(first_grads_kernel, groups, chips, inner, True), [mine, theirs, both, both_other] + far_sums,

time: 662 us -> 684 us (1.033)
  waiting for transfers between devices: 212 us -> 231 us
    ppermute x12, waiting for transfers between devices: 25.3 us -> 44.3 us  [exchange(): got.append(lax.ppermute(joined, 'seq', route))]
    unnamed x304 -> x248, local copies, waits for them, and re-layouts: 33.9 us -> 28.2 us
  transfers between devices with their start and end apart: 69 -> 69, of which waited for: 28 -> 30; matrix products, arithmetic and copies ran while one was open for 12% -> 12% of each run, Pallas kernels for 28% -> 27%
where the time goes in v7:
time: 684 us; the launch traced here: 671 us
  Pallas kernels  231 us (34%)
  waiting for transfers between devices  231 us (34%)
  starting transfers between devices  83.3 us (12%)
  matrix products  62.8 us (9%)
  local copies, waits for them, and re-layouts  32.6 us (5%)
  between operations  15.9 us (2%)
  other arithmetic  15.1 us (2%)
    ppermute x49, waiting for transfers between devices, swap(): lax.ppermute(x, axis, [(i, i ^ bits) for i in range(lax.axis_size(axis))])  183 us
    pallas_call x12, Pallas kernels, call(): pl.pallas_call(without(kernel, len(arrays), len(after)), grid=(batch,), i...  152 us
    pallas_call x32, Pallas kernels, whole_call(): pl.pallas_call(without(kernel, len(arrays), len(after)), in_specs=in_spec...  56.6 us
    ppermute x49, starting transfers between devices, swap(): lax.ppermute(x, axis, [(i, i ^ bits) for i in range(lax.axis_size(axis))])  46.5 us
    ppermute x12, waiting for transfers between devices, exchange(): got.append(lax.ppermute(joined, 'seq', route))  44.3 us
    dot_general x6, matrix products, dot(): return jnp.dot(a, b, preferred_element_type=F32)  32.8 us
    dot_general x6, matrix products, dot_nt(): return lax.dot_general(a, b, NT, preferred_element_type=F32)  30 us
    ppermute x12, starting transfers between devices, exchange(): got.append(lax.ppermute(joined, 'seq', route))  28.6 us
  transfers between devices with their start and end apart: 69, of which 30 were waited for; matrix products, arithmetic and copies ran while one was open for 12% of the time, Pallas kernels for 27%

profile of v7, /device:TPU:0, one launch (start us, length us, event | category | flops | bytes accessed | tf_op | source)
XLA Modules:
  0.0 671.3 jit_solution(12171964961136095709)
XLA Ops:
  24.0 16.6 %collective-permute-done.1.refs_1_ = bf16[32,4480]{1,0:T(8,128)(2,1)S(1)} collective-permute-done((bf16[32,4480]{1,0:T(8,128)(2,1)S(1)}, bf16[32,4480]{1,0:T(8,128)(2,1)S(1)}, u32[]{:S(2)}, u32[]{:S(2)}) %collective-permute-start.1) | collective-permute-done | bytes 286752 | tf_op jit(solution)/shard_map/ppermute | solution.py:471
  62.6 15.8 %collective-permute-done.7.refs_6_ = bf16[3,32,4480]{2,1,0:T(8,128)(2,1)S(1)} collective-permute-done((bf16[3,32,4480]{2,1,0:T(8,128)(2,1)S(1)}, bf16[3,32,4480]{2,1,0:T(8,128)(2,1)S(1)}, u32[]{:S(2)}, u32[]{:S(2)}) %collective-permute-start.7) | collective-permute-done | bytes 860192 | tf_op jit(solution)/shard_map/ppermute | solution.py:471
  78.3 18.9 %collective-permute-done.6.refs_5_ = bf16[3,32,4480]{2,1,0:T(8,128)(2,1)} collective-permute-done((bf16[3,32,4480]{2,1,0:T(8,128)(2,1)S(1)}, bf16[3,32,4480]{2,1,0:T(8,128)(2,1)}, u32[]{:S(2)}, u32[]{:S(2)}) %collective-permute-start.6) | collective-permute-done | bytes 860192 | tf_op jit(solution)/shard_map/ppermute | solution.py:471
  107.1 7.4 %place_rows.1 = bf16[1024,4480]{1,0:T(8,128)(2,1)} custom-call(s32[3]{0:T(128)S(1)} %pad_add_fusion.where.refs_0_, bf16[2,256,4352]{2,1,0:T(8,128)(2,1)} %refs_0_.6, bf16[2,256,32]{2,1,0:T(8,128)(2,1)S(1)} %copy.133.refs_1_.refs_2_, bf16[3,32,4480]{2,1,0:T(8,128)(2,1)S(1)} %stack.123.refs_1_.refs_3_.refs_2_, ...), custom_call_target="tpu_custom_call" | custom-call | flops 1100000000 | bytes 1000000 | tf_op jit(solution)/shard_map/place_rows/pallas_call | solution.py:586
  123.1 9.0 %conv_states.2 = (bf16[2,256,2304]{2,1,0:T(8,128)(2,1)S(1)}, f32[2,256,128]{2,1,0:T(8,128)S(1)}, f32[2,256,128]{2,1,0:T(8,128)S(1)}, f32[2,32,256]{2,1,0:T(8,128...) custom-call(bf16[2,256,2432]{2,1,0:T(8,128)(2,1)} %bitcast.162, ...), custom_call_target="tpu_custom_call" | custom-call | flops 2200000000 | bytes 2000000 | tf_op jit(solution)/shard_map/conv_states/pallas_call | solution.py:411
  160.0 11.8 %mix_within.2.refs_3_.refs_1_ = f32[2,256,2048]{2,1,0:T(8,128)} custom-call(bf16[2,256,2304]{2,1,0:T(8,128)(2,1)S(1)} %get-tuple-element.93.refs_0_.refs_2_.refs_6_.refs_1_.refs_3_, f32[2,256,128]{2,1,0:T(8,128)S(1)} %copy-done.58, f32[2,256,128]{2,1,0:T(8,128)S(1)} %copy-done.33, f32[2,32,256]{2,1,0:T(8,128)S(1)} %copy-done.91, ...), custom_call_target="tpu_custom_call" | custom-call | flops 3300000000 | bytes 3000000 | tf_op jit(solution)/shard_map/mix_within/pallas_call | solution.py:411
  204.8 9.5 %conv_states.3 = (bf16[2,256,2304]{2,1,0:T(8,128)(2,1)}, f32[2,256,128]{2,1,0:T(8,128)S(1)}, f32[2,256,128]{2,1,0:T(8,128)S(1)}, f32[2,32,256]{2,1,0:T(8,128)S(1...) custom-call(bf16[2,256,2432]{2,1,0:T(8,128)(2,1)} %bitcast.176, ...), custom_call_target="tpu_custom_call" | custom-call | flops 2200000000 | bytes 2000000 | tf_op jit(solution)/shard_map/conv_states/pallas_call | solution.py:411
  237.3 12.2 %mix_within.3.refs_3_.refs_1_ = f32[2,256,2048]{2,1,0:T(8,128)} custom-call(bf16[2,256,2304]{2,1,0:T(8,128)(2,1)S(1)} %copy-done.15, f32[2,256,128]{2,1,0:T(8,128)S(1)} %copy-done.82, f32[2,256,128]{2,1,0:T(8,128)S(1)} %copy-done.43, f32[2,32,256]{2,1,0:T(8,128)S(1)} %copy-done.88, f32[2,256,128]{2,1,0:T(8,128)S(1)} %copy-done.14, ...), custom_call_target="tpu_custom_call" | custom-call | flops 3300000000 | bytes 3000000 | tf_op jit(solution)/shard_map/mix_within/pallas_call | solution.py:411
  267.3 11.8 %gate_back.2 = (bf16[2,256,2048]{2,1,0:T(8,128)(2,1)}, bf16[2,256,3072]{2,1,0:T(8,128)(2,1)}, bf16[2,144,2048]{2,1,0:T(8,128)(2,1)S(1)}, f32[2,256,128]{2,1,0:T(...) custom-call(bf16[2,256,2048]{2,1,0:T(8,128)(2,1)} %bitcast.165, bf16[2,256,1024]{2,1,0:T(8,128)(2,1)S(1)} %copy-done.16, ...), custom_call_target="tpu_custom_call" | custom-call | flops 3024999936 | bytes 2750000 | tf_op jit(solution)/shard_map/gate_back/pallas_call | solution.py:411
  287.7 17.4 %mix_within_back.2 = (bf16[2,256,2048]{2,1,0:T(8,128)(2,1)S(1)}, f32[2,256,256]{2,1,0:T(8,128)S(1)}, f32[2,256,128]{2,1,0:T(8,128)S(1)}) custom-call(bf16[2,256,2048]{2,1,0:T(8,128)(2,1)} %get-tuple-element.110.refs_0_.refs_2_, bf16[2,256,2304]{2,1,0:T(8,128)(2,1)} %get-tuple-element.100.refs_0_.refs_2_.refs_6_.refs_1_.refs_3_, ...), custom_call_target="tpu_custom_call" | custom-call | flops 4674999808 | bytes 4250000 | tf_op jit(solution)/shard_map/mix_within_back/pallas_call | solution.py:411
  308.3 9.4 %first_grads.2.refs_4_ = bf16[4,4,128,1024]{3,2,1,0:T(8,128)(2,1)} custom-call(s32[3]{0:T(128)S(1)} %pad_add_fusion.where.refs_0_, bf16[1536,512]{1,0:T(8,128)(2,1)S(1)} %get-tuple-element.117.refs_1_, bf16[1536,512]{1,0:T(8,128)(2,1)S(1)} %collective-permute-done.26.refs_2_, bf16[512,3072]{1,0:T(8,128)(2,1)} %bitcast.159, bf16[512,3072]{1,0:T(8,128)(2,1)} %copy-done.103, ...), custom_call_target="tpu_custom_call" | custom-call | flops 2750000128 | bytes 2500000 | tf_op jit(solution)/shard_map/first_grads/pallas_call | solution.py:458
  323.1 13.9 %collective-permute-done.25.refs_2_ = bf16[144,2048]{1,0:T(8,128)(2,1)S(1)} collective-permute-done((bf16[144,2048]{1,0:T(8,128)(2,1)}, bf16[144,2048]{1,0:T(8,128)(2,1)S(1)}, u32[]{:S(2)}, u32[]{:S(2)}) %collective-permute-start.25) | collective-permute-done | bytes 589856 | tf_op jit(solution)/shard_map/ppermute | solution.py:508
  337.0 15.1 %collective-permute-done.24.refs_1_ = bf16[144,2048]{1,0:T(8,128)(2,1)S(1)} collective-permute-done((bf16[144,2048]{1,0:T(8,128)(2,1)}, bf16[144,2048]{1,0:T(8,128)(2,1)S(1)}, u32[]{:S(2)}, u32[]{:S(2)}) %collective-permute-start.24) | collective-permute-done | bytes 589856 | tf_op jit(solution)/shard_map/ppermute | solution.py:508
  354.4 19.0 %conv_back.2 = (bf16[2,256,2432]{2,1,0:T(8,128)(2,1)}, f32[2,8,2304]{2,1,0:T(8,128)S(1)}, f32[8,2304]{1,0:T(8,128)S(1)}, f32[8,128]{1,0:T(8,128)S(1)}) custom-call(s32[3]{0:T(128)S(1)} %pad_add_fusion.where.refs_0_, bf16[2,256,2048]{2,1,0:T(8,128)(2,1)} %copy-done.21, bf16[2,256,2048]{2,1,0:T(8,128)(2,1)} %get-tuple-element.110.refs_0_.refs_2_, ...), custom_call_target="tpu_custom_call" | custom-call | flops 4674999808 | bytes 4250000 | tf_op jit(solution)/shard_map/conv_back/pallas_call | solution.py:411
  386.4 7.5 %fusion.43 = f32[512,1024]{1,0:T(8,128)} fusion(f32[512,1024]{1,0:T(8,128)S(1)} %fusion.10, bf16[512,2432]{1,0:T(8,128)(2,1)} %bitcast.45.refs_3_, bf16[1024,6528]{1,0:T(8,128)(2,1)} %all-gather.3.cloned.1.call-done.folded), kind=kOutput, calls=%fused_computation.47 | convolution fusion | flops 2550661120 | bytes 11665408 | tf_op jit(solution)/shard_map/dot_general | solution.py:26
  404.6 11.6 %gate_back.3 = (bf16[2,256,2048]{2,1,0:T(8,128)(2,1)}, bf16[2,256,3072]{2,1,0:T(8,128)(2,1)}, bf16[2,144,2048]{2,1,0:T(8,128)(2,1)S(1)}, f32[2,256,128]{2,1,0:T(...) custom-call(bf16[2,256,2048]{2,1,0:T(8,128)(2,1)} %bitcast.164, bf16[2,256,1024]{2,1,0:T(8,128)(2,1)S(1)} %fusion.56.refs_1_, ...), custom_call_target="tpu_custom_call" | custom-call | flops 3024999936 | bytes 2750000 | tf_op jit(solution)/shard_map/gate_back/pallas_call | solution.py:411
  428.5 17.2 %mix_within_back.3 = (bf16[2,256,2048]{2,1,0:T(8,128)(2,1)S(1)}, f32[2,256,256]{2,1,0:T(8,128)S(1)}, f32[2,256,128]{2,1,0:T(8,128)S(1)}) custom-call(bf16[2,256,2048]{2,1,0:T(8,128)(2,1)} %get-tuple-element.128.refs_0_.refs_2_, bf16[2,256,2304]{2,1,0:T(8,128)(2,1)} %copy-done.2, f32[2,256,128]{2,1,0:T(8,128)S(1)} %copy-done.59, ...), custom_call_target="tpu_custom_call" | custom-call | flops 4674999808 | bytes 4250000 | tf_op jit(solution)/shard_map/mix_within_back/pallas_call | solution.py:411
  445.8 10.6 %collective-permute-done.34.refs_1_ = bf16[144,2048]{1,0:T(8,128)(2,1)S(1)} collective-permute-done((bf16[144,2048]{1,0:T(8,128)(2,1)S(1)}, bf16[144,2048]{1,0:T(8,128)(2,1)S(1)}, u32[]{:S(2)}, u32[]{:S(2)}) %collective-permute-start.34) | collective-permute-done | bytes 589856 | tf_op jit(solution)/shard_map/ppermute | solution.py:508
  459.1 9.9 %first_grads.3 = (bf16[5,128,1024]{2,1,0:T(8,128)(2,1)S(1)}, bf16[5,128,1024]{2,1,0:T(8,128)(2,1)}, bf16[5,128,1024]{2,1,0:T(8,128)(2,1)S(1)}, bf16[5,128,1024]{2,1,0:T(8,128)(2,1)}) custom-call(s32[3]{0:T(128)S(1)} %pad_add_fusion.where.refs_0_, bf16[1536,512]{1,0:T(8,128)(2,1)} %copy-done.22, bf16[1536,512]{1,0:T(8,128)(2,1)} %copy-done.99, ...), custom_call_target="tpu_custom_call" | custom-call | flops 2750000128 | bytes 2500000 | tf_op jit(solution)/shard_map/first_grads/pallas_call | solution.py:458
  475.6 18.9 %conv_back.3 = (bf16[2,256,2432]{2,1,0:T(8,128)(2,1)}, f32[2,8,2304]{2,1,0:T(8,128)S(1)}, f32[8,2304]{1,0:T(8,128)S(1)}, f32[8,128]{1,0:T(8,128)S(1)}) custom-call(s32[3]{0:T(128)S(1)} %pad_add_fusion.where.refs_0_, bf16[2,256,2048]{2,1,0:T(8,128)(2,1)} %copy-done.18, bf16[2,256,2048]{2,1,0:T(8,128)(2,1)} %get-tuple-element.128.refs_0_.refs_2_, ...), custom_call_target="tpu_custom_call" | custom-call | flops 4674999808 | bytes 4250000 | tf_op jit(solution)/shard_map/conv_back/pallas_call | solution.py:411
  502.2 26.7 %collective-permute-done.41.refs_2_ = bf16[5,128,1024]{2,1,0:T(8,128)(2,1)} collective-permute-done((bf16[5,128,1024]{2,1,0:T(8,128)(2,1)S(1)}, bf16[5,128,1024]{2,1,0:T(8,128)(2,1)}, u32[]{:S(2)}, u32[]{:S(2)}) %collective-permute-start.41) | collective-permute-done | bytes 1310752 | tf_op jit(solution)/shard_map/ppermute | solution.py:471
  556.2 14.8 %collective-permute-done.43.refs_1_ = bf16[2,128,1024]{2,1,0:T(8,128)(2,1)S(1)} collective-permute-done((bf16[2,128,1024]{2,1,0:T(8,128)(2,1)S(1)}, bf16[2,128,1024]{2,1,0:T(8,128)(2,1)S(1)}, u32[]{:S(2)}, u32[]{:S(2)}) %collective-permute-start.43) | collective-permute-done | bytes 524320 | tf_op jit(solution)/shard_map/ppermute | solution.py:471
  596.5 21.2 %collective-permute-done.52.refs_2_ = bf16[4,32,2432]{2,1,0:T(8,128)(2,1)S(1)} collective-permute-done((bf16[4,32,2432]{2,1,0:T(8,128)(2,1)S(1)}, bf16[4,32,2432]{2,1,0:T(8,128)(2,1)S(1)}, u32[]{:S(2)}, u32[]{:S(2)}) %collective-permute-start.52) | collective-permute-done | bytes 622624 | tf_op jit(solution)/shard_map/ppermute | solution.py:471
  634.7 9.4 %collective-permute-done.64.refs_3_.refs_9_ = bf16[192,1024]{1,0:T(8,128)(2,1)S(1)} collective-permute-done((bf16[192,1024]{1,0:T(8,128)(2,1)S(1)}, bf16[192,1024]{1,0:T(8,128)(2,1)S(1)}, u32[]{:S(2)}, u32[]{:S(2)}) %collective-permute-start.64) | collective-permute-done | bytes 393248 | tf_op jit(solution)/shard_map/ppermute | solution.py:471
  (510 shorter events, 319.8 us)
Async XLA Ops:
  7.2 164.6 %all-gather.3.cloned.1.call-start = ((), (), s32[]{:S(2)}) async-start(), calls=%async_computation.1 | async-start | bytes 13787136 | tf_op jit(solution)/shard_map/all_gather | solution.py:1003
  43.7 205.7 %all-gather.5.cloned.1.call-start = ((), (), s32[]{:S(2)}) async-start(), calls=%async_computation.2 | async-start | bytes 4325376 | tf_op jit(solution)/shard_map/all_gather | solution.py:1008
  57.5 39.7 %collective-permute-start.6 = (bf16[3,32,4480]{2,1,0:T(8,128)(2,1)S(1)}, bf16[3,32,4480]{2,1,0:T(8,128)(2,1)}, u32[]{:S(2)}, u32[]{:S(2)}) collective-permute-start(bf16[3,32,4480]{2,1,0:T(8,128)(2,1)S(1)} %stack.123.refs_1_.refs_3_.refs_2_), channel_id=1, source_target_pairs={{0,4},{1,5},{2,6},{3,7},{4,0},{5,1},{6,2},{7,3},{8,12},{9,13},{10,... | collective-permute-start | bytes 2580488 | tf_op jit(solution)/shard_map/ppermute | solution.py:471
  58.0 39.2 %collective-permute-start.5 = (bf16[3,32,4480]{2,1,0:T(8,128)(2,1)S(1)}, bf16[3,32,4480]{2,1,0:T(8,128)(2,1)}, u32[]{:S(2)}, u32[]{:S(2)}) collective-permute-start(bf16[3,32,4480]{2,1,0:T(8,128)(2,1)S(1)} %stack.123.refs_1_.refs_3_.refs_2_), channel_id=1, source_target_pairs={{0,2},{1,3},{2,0},{3,1},{4,6},{5,7},{6,4},{7,5},{8,10},{9,11},{10,... | collective-permute-start | bytes 2580488 | tf_op jit(solution)/shard_map/ppermute | solution.py:471
  61.8 396.1 %reduce-scatter.2.cloned.1.call-start = ((), (), s32[]{:S(2)}) async-start(), calls=%async_computation.3 | async-start | bytes 5242880 | tf_op jit(solution)/shard_map/reduce_scatter | solution.py:1122
  143.2 33.8 %collective-permute-start.14 = (bf16[144,2048]{1,0:T(8,128)(2,1)}, bf16[144,2048]{1,0:T(8,128)(2,1)}, u32[]{:S(2)}, u32[]{:S(2)}) collective-permute-start(bf16[144,2048]{1,0:T(8,128)(2,1)} %join_states.4.refs_8_), channel_id=1, source_target_pairs={{0,2},{1,3},{2,4},{3,5},{4,6},{5,7},{8,10},{9,11},{10,12},{11,13},... | collective-permute-start | bytes 1769480 | tf_op jit(solution)/shard_map/ppermute | solution.py:508
  148.9 28.1 %collective-permute-start.13 = (bf16[144,2048]{1,0:T(8,128)(2,1)}, bf16[144,2048]{1,0:T(8,128)(2,1)}, u32[]{:S(2)}, u32[]{:S(2)}) collective-permute-start(bf16[144,2048]{1,0:T(8,128)(2,1)} %join_states.4.refs_8_), channel_id=1, source_target_pairs={{0,4},{1,5},{2,6},{3,7},{8,12},{9,13},{10,14},{11,15},{16,20},{17,... | collective-permute-start | bytes 1769480 | tf_op jit(solution)/shard_map/ppermute | solution.py:508
  222.5 26.9 %collective-permute-start.20 = (bf16[144,2048]{1,0:T(8,128)(2,1)}, bf16[144,2048]{1,0:T(8,128)(2,1)}, u32[]{:S(2)}, u32[]{:S(2)}) collective-permute-start(bf16[144,2048]{1,0:T(8,128)(2,1)} %join_states.5.refs_8_), channel_id=1, source_target_pairs={{0,2},{1,3},{2,4},{3,5},{4,6},{5,7},{8,10},{9,11},{10,12},{11,13},... | collective-permute-start | bytes 1769480 | tf_op jit(solution)/shard_map/ppermute | solution.py:508
  320.5 31.6 %collective-permute-start.24 = (bf16[144,2048]{1,0:T(8,128)(2,1)}, bf16[144,2048]{1,0:T(8,128)(2,1)S(1)}, u32[]{:S(2)}, u32[]{:S(2)}) collective-permute-start(bf16[144,2048]{1,0:T(8,128)(2,1)} %copy-done.54), channel_id=1, source_target_pairs={{4,0},{5,1},{6,2},{7,3},{12,8},{13,9},{14,10},{15,11},{20,16},{21,... | collective-permute-start | bytes 1769480 | tf_op jit(solution)/shard_map/ppermute | solution.py:508
  321.8 30.3 %collective-permute-start.23 = (bf16[144,2048]{1,0:T(8,128)(2,1)}, bf16[144,2048]{1,0:T(8,128)(2,1)S(1)}, u32[]{:S(2)}, u32[]{:S(2)}) collective-permute-start(bf16[144,2048]{1,0:T(8,128)(2,1)} %copy-done.54), channel_id=1, source_target_pairs={{6,0},{7,1},{14,8},{15,9},{22,16},{23,17},{30,24},{31,25}} | collective-permute-start | bytes 1769480 | tf_op jit(solution)/shard_map/ppermute | solution.py:508
  416.8 41.0 %collective-permute-start.38 = (bf16[512,3072]{1,0:T(8,128)(2,1)}, bf16[512,3072]{1,0:T(8,128)(2,1)}, u32[]{:S(2)}, u32[]{:S(2)}) collective-permute-start(bf16[512,3072]{1,0:T(8,128)(2,1)} %bitcast.155), channel_id=1, source_target_pairs={{0,1},{1,0},{2,3},{3,2},{4,5},{5,4},{6,7},{7,6},{8,9},{9,8},{10,11... | collective-permute-start | bytes 9437192 | tf_op jit(solution)/shard_map/ppermute | solution.py:471
  417.4 39.4 %collective-permute-start.37 = (bf16[1536,512]{1,0:T(8,128)(2,1)S(1)}, bf16[1536,512]{1,0:T(8,128)(2,1)S(1)}, u32[]{:S(2)}, u32[]{:S(2)}) collective-permute-start(bf16[1536,512]{1,0:T(8,128)(2,1)S(1)} %copy-done.72), channel_id=1, source_target_pairs={{0,1},{1,0},{2,3},{3,2},{4,5},{5,4},{6,7},{7,6},{8,9},{9,8},{10,11... | collective-permute-start | bytes 4718600 | tf_op jit(solution)/shard_map/ppermute | solution.py:471
  425.9 30.5 %collective-permute-start.34 = (bf16[144,2048]{1,0:T(8,128)(2,1)S(1)}, bf16[144,2048]{1,0:T(8,128)(2,1)S(1)}, u32[]{:S(2)}, u32[]{:S(2)}) collective-permute-start(bf16[144,2048]{1,0:T(8,128)(2,1)S(1)} %join_states.7.refs_10_), channel_id=1, source_target_pairs={{4,0},{5,1},{6,2},{7,3},{12,8},{13,9},{14,10},{15,11},{20,16},{21,... | collective-permute-start | bytes 1769480 | tf_op jit(solution)/shard_map/ppermute | solution.py:508
  427.2 29.2 %collective-permute-start.33 = (bf16[144,2048]{1,0:T(8,128)(2,1)S(1)}, bf16[144,2048]{1,0:T(8,128)(2,1)S(1)}, u32[]{:S(2)}, u32[]{:S(2)}) collective-permute-start(bf16[144,2048]{1,0:T(8,128)(2,1)S(1)} %join_states.7.refs_10_), channel_id=1, source_target_pairs={{6,0},{7,1},{14,8},{15,9},{22,16},{23,17},{30,24},{31,25}} | collective-permute-start | bytes 1769480 | tf_op jit(solution)/shard_map/ppermute | solution.py:508
  470.1 32.0 %collective-permute-start.40 = (bf16[5,128,1024]{2,1,0:T(8,128)(2,1)}, bf16[5,128,1024]{2,1,0:T(8,128)(2,1)}, u32[]{:S(2)}, u32[]{:S(2)}) collective-permute-start(bf16[5,128,1024]{2,1,0:T(8,128)(2,1)} %get-tuple-element.137.refs_20_), channel_id=1, source_target_pairs={{0,2},{1,3},{2,0},{3,1},{4,6},{5,7},{6,4},{7,5},{8,10},{9,11},{10,... | collective-permute-start | bytes 3932168 | tf_op jit(solution)/shard_map/ppermute | solution.py:471
  470.3 58.6 %collective-permute-start.41 = (bf16[5,128,1024]{2,1,0:T(8,128)(2,1)S(1)}, bf16[5,128,1024]{2,1,0:T(8,128)(2,1)}, u32[]{:S(2)}, u32[]{:S(2)}) collective-permute-start(bf16[5,128,1024]{2,1,0:T(8,128)(2,1)S(1)} %get-tuple-element.138.refs_21_), channel_id=1, source_target_pairs={{0,4},{1,5},{2,6},{3,7},{4,0},{5,1},{6,2},{7,3},{8,12},{9,13},{10,... | collective-permute-start | bytes 3932168 | tf_op jit(solution)/shard_map/ppermute | solution.py:471
  470.3 58.6 %collective-permute-start.42 = (bf16[5,128,1024]{2,1,0:T(8,128)(2,1)}, bf16[5,128,1024]{2,1,0:T(8,128)(2,1)}, u32[]{:S(2)}, u32[]{:S(2)}) collective-permute-start(bf16[5,128,1024]{2,1,0:T(8,128)(2,1)} %get-tuple-element.139.refs_22_), channel_id=1, source_target_pairs={{0,6},{1,7},{2,4},{3,5},{4,2},{5,3},{6,0},{7,1},{8,14},{9,15},{10,... | collective-permute-start | bytes 3932168 | tf_op jit(solution)/shard_map/ppermute | solution.py:471
  494.5 37.1 %collective-permute-start.39 = (bf16[2,8,2304]{2,1,0:T(8,128)(2,1)S(1)}, bf16[2,8,2304]{2,1,0:T(8,128)(2,1)S(1)}, u32[]{:S(2)}, u32[]{:S(2)}) collective-permute-start(bf16[2,8,2304]{2,1,0:T(8,128)(2,1)S(1)} %convert_element_type.198), channel_id=1, source_target_pairs={{1,0},{2,1},{3,2},{4,3},{5,4},{6,5},{7,6},{9,8},{10,9},{11,10},{12... | collective-permute-start | bytes 221192 | tf_op jit(solution)/shard_map/ppermute | solution.py:1151
  548.9 29.2 %collective-permute-start.58 = (bf16[4,32,2432]{2,1,0:T(8,128)(2,1)S(1)}, bf16[4,32,2432]{2,1,0:T(8,128)(2,1)S(1)}, u32[]{:S(2)}, u32[]{:S(2)}) collective-permute-start(bf16[4,32,2432]{2,1,0:T(8,128)(2,1)S(1)} %get-tuple-element.160), channel_id=1, source_target_pairs={{0,4},{1,5},{2,6},{3,7},{4,0},{5,1},{6,2},{7,3},{8,12},{9,13},{10,... | collective-permute-start | bytes 1867784 | tf_op jit(solution)/shard_map/ppermute | solution.py:471
  549.0 29.2 %collective-permute-start.59 = (bf16[4,32,2432]{2,1,0:T(8,128)(2,1)S(1)}, bf16[4,32,2432]{2,1,0:T(8,128)(2,1)S(1)}, u32[]{:S(2)}, u32[]{:S(2)}) collective-permute-start(bf16[4,32,2432]{2,1,0:T(8,128)(2,1)S(1)} %get-tuple-element.161), channel_id=1, source_target_pairs={{0,6},{1,7},{2,4},{3,5},{4,2},{5,3},{6,0},{7,1},{8,14},{9,15},{10,... | collective-permute-start | bytes 1867784 | tf_op jit(solution)/shard_map/ppermute | solution.py:471
  579.5 38.2 %collective-permute-start.52 = (bf16[4,32,2432]{2,1,0:T(8,128)(2,1)S(1)}, bf16[4,32,2432]{2,1,0:T(8,128)(2,1)S(1)}, u32[]{:S(2)}, u32[]{:S(2)}) collective-permute-start(bf16[4,32,2432]{2,1,0:T(8,128)(2,1)S(1)} %get-tuple-element.153), channel_id=1, source_target_pairs={{0,4},{1,5},{2,6},{3,7},{4,0},{5,1},{6,2},{7,3},{8,12},{9,13},{10,... | collective-permute-start | bytes 1867784 | tf_op jit(solution)/shard_map/ppermute | solution.py:471
  581.0 37.2 %collective-permute-start.53 = (bf16[4,32,2432]{2,1,0:T(8,128)(2,1)S(1)}, bf16[4,32,2432]{2,1,0:T(8,128)(2,1)S(1)}, u32[]{:S(2)}, u32[]{:S(2)}) collective-permute-start(bf16[4,32,2432]{2,1,0:T(8,128)(2,1)S(1)} %get-tuple-element.154), channel_id=1, source_target_pairs={{0,6},{1,7},{2,4},{3,5},{4,2},{5,3},{6,0},{7,1},{8,14},{9,15},{10,... | collective-permute-start | bytes 1867784 | tf_op jit(solution)/shard_map/ppermute | solution.py:471
  582.9 39.4 %collective-permute-start.49 = (bf16[256,1024]{1,0:T(8,128)(2,1)S(1)}, bf16[256,1024]{1,0:T(8,128)(2,1)S(1)}, u32[]{:S(2)}, u32[]{:S(2)}) collective-permute-start(bf16[256,1024]{1,0:T(8,128)(2,1)S(1)} %bitcast.127), channel_id=1, source_target_pairs={{0,6},{1,7},{2,4},{3,5},{4,2},{5,3},{6,0},{7,1},{8,14},{9,15},{10,... | collective-permute-start | bytes 1572872 | tf_op jit(solution)/shard_map/ppermute | solution.py:471
  596.2 33.6 %collective-permute-start.48 = (bf16[256,1024]{1,0:T(8,128)(2,1)S(1)}, bf16[256,1024]{1,0:T(8,128)(2,1)S(1)}, u32[]{:S(2)}, u32[]{:S(2)}) collective-permute-start(bf16[256,1024]{1,0:T(8,128)(2,1)S(1)} %bitcast.128), channel_id=1, source_target_pairs={{0,4},{1,5},{2,6},{3,7},{4,0},{5,1},{6,2},{7,3},{8,12},{9,13},{10,... | collective-permute-start | bytes 1572872 | tf_op jit(solution)/shard_map/ppermute | solution.py:471
  (168 other events, 1888.2 us)
Sparse Core Ops, SparseCore 0:
  43.8 121.8 all-gather.2
  168.6 60.1 all-gather.4
  319.1 78.3 reduce-scatter.1
